TPU v7x, 256 devices: a whole 4x4x8 slice. The times are simulated.
256 devices in a mesh: seq: 32 (over x, y, core), user: 8 (over z).
Axes of the slice: x: 4, y: 4, z: 8, core: 2. Of those that a mesh axis runs over, the one named last changes fastest.
Arguments:
- tokens: bfloat16 [8, 8192, 1024], P('user', 'seq'), may hold values from -6 to 6
- w_query: bfloat16 [1024, 1024], replicated, may hold values from -0.1875 to 0.1875
- w_key: bfloat16 [1024, 1024], replicated, may hold values from -0.1875 to 0.1875
- w_value: bfloat16 [1024, 1024], replicated, may hold values from -0.1875 to 0.1875
- w_out: bfloat16 [1024, 1024], replicated, may hold values from -0.1875 to 0.1875
- norm_gain: float32 [1024], replicated, may hold values from 0.3 to 3
- lengths: int32 [8], P('user'), may hold values from 2048 to 8192, as said below
- d_mixed: bfloat16 [8, 8192, 1024], P('user', 'seq'), may hold values from -6 to 6
Outputs:
- mixed_out: bfloat16 [8, 8192, 1024], P('user', 'seq')
- d_tokens: bfloat16 [8, 8192, 1024], P('user', 'seq')
- d_weights: float32 [2, 1048576], P(None, ('seq', 'user'))
- d_gain: float32 [1024], replicated
Inputs may be any that keep to these rules, and one draw needn't show every extreme that they name: `lengths`: valid events come first in each history and padding follows; some user has all 8192 events and some user has 2048.
All inputs are finite; a program needn't handle non-finite values.
Results may differ from a plain program's by a relative error of at most 0.0058.
Values sent between devices are 32-bit elements; how exact they have to be, the bound alone decides.
No kernel may reach another device: no remote copies, remote signals or barrier semaphores. Data moves between devices by JAX's collectives and lax.ppermute only.
A program may use at most 128 MiB of HBM per device.

v0:
```python
import jax
import jax.numpy as jnp
from jax import lax
from jax.sharding import PartitionSpec as P

HEADS = 16


EPS = 1e-05
PRECISE = lax.Precision.HIGHEST
SPLIT_THREE = lax.Precision.HIGH


def entering(value, axis, join, neutral, backward):
    count, mine = (lax.axis_size(axis), lax.axis_index(axis))
    pieces = lax.all_gather(value, axis)
    if backward:
        pieces = pieces[::-1]
        mine = count - 1 - mine
    total = jnp.full_like(value, 0) + jnp.asarray(neutral, value.dtype)

    def lap(position, total):
        longer = join(total, pieces[position])
        return jnp.where(position < mine, longer, total)

    return lax.fori_loop(0, count - 1, lap, total)


def feature(raw_values):
    return jax.nn.elu(raw_values) + 1.0


def elu_slope(raw_values):
    return jnp.where(raw_values > 0, 1.0, jnp.exp(jnp.minimum(raw_values, 0.0)))


def add_states(earlier_part, later_part):
    return earlier_part + later_part


def on_device(tokens, w_query, w_key, w_value, w_out, norm_gain, lengths, d_mixed):
    user_count, row_count, model_width = tokens.shape
    head_count = HEADS
    head_size = model_width // head_count
    own_index = lax.axis_index("seq")
    positions = own_index * row_count + jnp.arange(row_count, dtype=jnp.int32)
    valid_mask = (positions[None, :] < lengths[:, None]).astype(jnp.float32)
    flat_tokens = tokens.reshape(user_count * row_count, model_width)

    def project(weight):
        return jnp.dot(flat_tokens, weight, preferred_element_type=jnp.float32).reshape(
            user_count, row_count, head_count, head_size
        )

    query_proj = project(w_query)
    key_proj = project(w_key)
    value_proj = project(w_value)
    query_bf = feature(query_proj).astype(jnp.bfloat16)
    key_bf = (feature(key_proj) * valid_mask[:, :, None, None]).astype(jnp.bfloat16)
    value_bf = value_proj.astype(jnp.bfloat16)
    local_state = jnp.einsum(
        "uthe,uthf->uhef", key_bf, value_bf, preferred_element_type=jnp.float32
    )
    earlier = entering(local_state, "seq", add_states, jnp.zeros_like(local_state), False)
    causal = jnp.arange(row_count)[:, None] >= jnp.arange(row_count)[None, :]
    scores = jnp.where(
        causal,
        jnp.einsum("uthe,ushe->uhts", query_bf, key_bf, preferred_element_type=jnp.float32),
        0.0,
    )
    numerator = jnp.einsum(
        "uhts,ushf->uthf",
        scores,
        value_bf,
        precision=SPLIT_THREE,
        preferred_element_type=jnp.float32,
    )
    numerator = numerator + jnp.einsum(
        "uthe,uhef->uthf",
        query_bf,
        earlier,
        precision=SPLIT_THREE,
        preferred_element_type=jnp.float32,
    )
    inv_rms = lax.rsqrt(jnp.mean(numerator * numerator, axis=-1, keepdims=True) + EPS)
    normed = (numerator * inv_rms).reshape(user_count, row_count, model_width)
    row_mask = valid_mask[:, :, None]
    attended = (normed * norm_gain * row_mask).astype(jnp.bfloat16)
    flat_attended = attended.reshape(user_count * row_count, model_width)
    mixed_out = jnp.dot(flat_attended, w_out, preferred_element_type=jnp.float32).astype(
        jnp.bfloat16
    )
    mixed_out = mixed_out.reshape(user_count, row_count, model_width)
    flat_grad = d_mixed.reshape(user_count * row_count, model_width)
    d_output = jnp.dot(flat_grad, w_out.T, preferred_element_type=jnp.float32).reshape(
        user_count, row_count, model_width
    )
    gain_part = jnp.sum(d_output * row_mask * normed, axis=(0, 1))
    gated_grad = (d_output * row_mask * norm_gain).reshape(
        user_count, row_count, head_count, head_size
    )
    d_numer = inv_rms * gated_grad - inv_rms**3 * numerator * jnp.mean(
        gated_grad * numerator, axis=-1, keepdims=True
    )
    grad_state = jnp.einsum(
        "uthe,uthf->uhef",
        query_bf,
        d_numer,
        precision=SPLIT_THREE,
        preferred_element_type=jnp.float32,
    )
    later_grad = entering(grad_state, "seq", add_states, jnp.zeros_like(grad_state), True)
    weights_p = jnp.where(
        causal,
        jnp.einsum(
            "uthf,ushf->uhts",
            d_numer,
            value_bf,
            precision=SPLIT_THREE,
            preferred_element_type=jnp.float32,
        ),
        0.0,
    )
    d_fq = jnp.einsum("uthf,uhef->uthe", d_numer, earlier, precision=PRECISE)
    d_fq = d_fq + jnp.einsum(
        "uhts,ushe->uthe",
        weights_p,
        key_bf,
        precision=SPLIT_THREE,
        preferred_element_type=jnp.float32,
    )
    d_fk = jnp.einsum(
        "uhts,uthe->ushe",
        weights_p,
        query_bf,
        precision=SPLIT_THREE,
        preferred_element_type=jnp.float32,
    )
    d_fk = d_fk + jnp.einsum(
        "ushf,uhef->ushe",
        value_bf,
        later_grad,
        precision=SPLIT_THREE,
        preferred_element_type=jnp.float32,
    )
    d_fv = jnp.einsum("uhts,uthf->ushf", scores, d_numer, precision=PRECISE)
    d_fv = d_fv + jnp.einsum(
        "ushe,uhef->ushf",
        key_bf,
        later_grad,
        precision=SPLIT_THREE,
        preferred_element_type=jnp.float32,
    )
    flat_shape = (user_count * row_count, model_width)
    d_query = (d_fq * elu_slope(query_proj)).astype(jnp.bfloat16).reshape(flat_shape)
    d_key = (
        (d_fk * valid_mask[:, :, None, None] * elu_slope(key_proj))
        .astype(jnp.bfloat16)
        .reshape(flat_shape)
    )
    d_value = d_fv.astype(jnp.bfloat16).reshape(flat_shape)
    d_tok = jnp.dot(d_query, w_query.T, preferred_element_type=jnp.float32)
    d_tok = d_tok + jnp.dot(d_key, w_key.T, preferred_element_type=jnp.float32)
    d_tok = d_tok + jnp.dot(d_value, w_value.T, preferred_element_type=jnp.float32)
    d_tokens = d_tok.astype(jnp.bfloat16).reshape(user_count, row_count, model_width)
    both_grads = jnp.concatenate([d_query, d_key], axis=1)
    weight_terms = jnp.dot(flat_tokens.T, both_grads, preferred_element_type=jnp.float32)
    weight_terms = (
        weight_terms.reshape(model_width, 2, model_width)
        .transpose(1, 0, 2)
        .reshape(2, model_width * model_width)
    )
    d_weights = lax.psum_scatter(weight_terms, ("seq", "user"), scatter_dimension=1, tiled=True)
    d_gain = lax.psum(gain_part, ("seq", "user"))
    return (mixed_out, d_tokens, d_weights, d_gain)


def solution(mesh):
    placed = (P("user", "seq", None), P(), P(), P(), P(), P(), P("user"), P("user", "seq", None))
    return jax.shard_map(
        on_device,
        mesh=mesh,
        in_specs=placed,
        out_specs=(P("user", "seq", None), P("user", "seq", None), P(None, ("seq", "user")), P()),
        check_vma=False,
    )
```

profile of v0, /device:TPU:1, one launch (start us, length us, event | category | flops | bytes accessed | tf_op | source)
XLA Modules:
  0.0 630.7 jit_solution(2568452253257711277)
XLA Ops:
  8.1 3.9 copy.42
  16.6 2.6 copy.43
  19.2 3.7 exponential_select_fusion
  22.8 2.6 copy.44
  25.4 3.2 fusion.63
  29.8 3.2 broadcast_multiply_fusion
  33.0 2.6 copy.48
  35.6 3.9 fusion.100
  39.5 72.2 %all-gather.5.cloned.1.call-done = f32[512,64,64]{2,1,0:T(8,128)} async-done(((f32[16,64,64]{2,1,0:T(8,128)}), f32[512,64,64]{2,1,0:T(8,128)}) %all-gather.5.cloned.1.call-update) | async-done | bytes 8388624 | tf_op jit(solution)/shard_map/all_gather | solution.py:16
  111.6 38.8 %while.28 = (s32[]{:T(128)}, f32[1,16,64,64]{3,2,1,0:T(8,128)S(1)}, s32[]{:T(128)}, f32[32,1,16,64,64]{4,3,2,1,0:T(8,128)}, s32[]{:T(128)}, /*index=5*/s32[]{:T(128)}) while((s32[]{:T(128)}, f32[1,16,64,64]{3,2,1,0:T(8,128)S(1)}, s32[]{:T(128)}, f32[32,1,16,64,64]{4,3,2,1,0:T(8,128)}, s32[]{:T(128)}, /*index=5*/s32[]{:T(128)}) %tuple.86), condition=%wide.region_1.2_spmd.clone, body=%wide.region_0.1_spmd.clone.sunk | while | flops 196612 | bytes 786533 | solution.py:26
  151.0 4.3 multiply_reduce_fusion.1
  158.2 2.6 copy.49
  172.1 63.0 %all-gather.7.cloned.1.call-done = f32[512,64,64]{2,1,0:T(8,128)} async-done(((f32[16,64,64]{2,1,0:T(8,128)}), f32[512,64,64]{2,1,0:T(8,128)}) %all-gather.7.cloned.1.call-update) | async-done | bytes 8388624 | tf_op jit(solution)/shard_map/all_gather | solution.py:16
  235.1 11.8 %rev.3 = f32[32,1,16,64,64]{4,3,2,1,0:T(8,128)} reverse(f32[32,1,16,64,64]{4,3,2,1,0:T(8,128)} %bitcast.138), dimensions={0} | reverse | bytes 16777216 | tf_op jit(solution)/shard_map/rev | solution.py:18
  247.0 64.4 %while.29 = (s32[]{:T(128)}, f32[1,16,64,64]{3,2,1,0:T(8,128)}, s32[]{:T(128)}, f32[32,1,16,64,64]{4,3,2,1,0:T(8,128)}, s32[]{:T(128)}, /*index=5*/s32[]{:T(128)}) while((s32[]{:T(128)}, f32[1,16,64,64]{3,2,1,0:T(8,128)}, s32[]{:T(128)}, f32[32,1,16,64,64]{4,3,2,1,0:T(8,128)}, s32[]{:T(128)}, /*index=5*/s32[]{:T(128)}) %tuple.77), condition=%wide.region_5.6_spmd.clone, body=%wide.region_4.5_spmd.clone.sunk | while | flops 196612 | bytes 786533 | solution.py:26
  313.0 3.9 fusion.52
  317.0 4.5 fusion.68
  321.5 8.7 %copy.53 = f32[2,1024,1024]{2,1,0:T(8,128)} copy(f32[2,1024,1024]{1,2,0:T(8,128)} %bitcast.135) | data formatting | bytes 16777216 | tf_op jit(solution)/shard_map/transpose | solution.py:170
  330.2 15.5 %copy.59 = f32[1,2,1024,1024]{3,1,2,0:T(2,128)} copy(f32[1,2,1024,1024]{3,2,1,0:T(8,128)} %bitcast.137) | data formatting | bytes 16777216
  345.7 2.6 copy.47
  349.9 76.9 %psum.7 = f32[1024]{0:T(1024)} all-reduce(f32[1024]{0:T(1024)S(1)} %multiply_reduce_fusion), channel_id=1, replica_groups=mesh['seq'=32,'user'=8] {'seq','user'}, use_global_device_ids=true, to_apply=%region_8.9 | all-reduce | flops 1024 | bytes 8192 | tf_op jit(solution)/shard_map/psum | solution.py:174
  426.8 2.9 fusion.60
  434.5 2.9 fusion.56
  439.0 183.8 %all-reduce.3.cloned.1.call-done = f32[2,1048576]{1,0:T(2,128)} async-done(((f32[2,1048576]{1,0:T(2,128)}), f32[2,1048576]{1,0:T(2,128)}) %all-reduce.3.cloned.1.call-update) | async-done | bytes 8388624
  (135 shorter events, 133.9 us)
Async XLA Ops:
  7.2 22.6 %copy-start = (bf16[1024,1024]{1,0:T(8,128)(2,1)S(1)}, bf16[1024,1024]{1,0:T(8,128)(2,1)}, u32[]{:S(2)}) copy-start(bf16[1024,1024]{1,0:T(8,128)(2,1)} %param.16) | copy-start | bytes 6291460
  7.2 4.8 copy-start.16
  7.2 104.4 %all-gather.5.cloned.1.call-start = ((), (), s32[]{:S(2)}) async-start(), calls=%async_computation | async-start | bytes 17301504 | tf_op jit(solution)/shard_map/all_gather | solution.py:16
  12.0 2.5 copy-start.11
  14.5 14.1 %copy-start.14 = (bf16[256,16,64]{0,2,1:T(8,128)(2,1)}, bf16[256,16,64]{0,2,1:T(8,128)(2,1)S(1)}, u32[]{:S(2)}) copy-start(bf16[256,16,64]{0,2,1:T(8,128)(2,1)S(1)} %convolution_convert_fusion.1) | copy-start | bytes 1572868
  22.8 7.0 %copy-start.21 = (f32[1024]{0:T(1024)S(1)}, f32[1024]{0:T(1024)}, u32[]{:S(2)}) copy-start(f32[1024]{0:T(1024)} %param.17) | copy-start | bytes 12292
  28.6 6.9 %copy-start.5 = (bf16[256,16,64]{0,2,1:T(8,128)(2,1)}, bf16[256,16,64]{0,2,1:T(8,128)(2,1)S(1)}, u32[]{:S(2)}) copy-start(bf16[256,16,64]{0,2,1:T(8,128)(2,1)S(1)} %get-tuple-element.236) | copy-start | bytes 1572868
  29.7 205.4 %all-gather.7.cloned.1.call-start = ((), (), s32[]{:S(2)}) async-start(), calls=%async_computation.1 | async-start | bytes 17301504 | tf_op jit(solution)/shard_map/all_gather | solution.py:16
  39.5 111.0 %copy-start.8 = (bf16[256,16,64]{0,2,1:T(8,128)(2,1)S(1)}, bf16[256,16,64]{0,2,1:T(8,128)(2,1)}, u32[]{:S(2)}) copy-start(bf16[256,16,64]{0,2,1:T(8,128)(2,1)} %get-tuple-element.235) | copy-start | bytes 1572868
  150.5 4.9 copy-start.4
  151.0 4.4 copy-start.10
  151.0 5.7 copy-start.9
  157.9 464.9 %all-reduce.3.cloned.1.call-start = ((), (), s32[]{:S(2)}) async-start(), calls=%async_computation.2 | async-start | bytes 16777216
  163.3 6.6 %copy-start.6 = (bf16[256,16,64]{0,2,1:T(8,128)(2,1)S(1)}, bf16[256,16,64]{0,2,1:T(8,128)(2,1)}, u32[]{:S(2)}) copy-start(bf16[256,16,64]{0,2,1:T(8,128)(2,1)} %copy-done.5) | copy-start | bytes 1572868
  163.3 6.6 %copy-start.20 = (f32[256,1024]{0,1:T(8,128)S(1)}, f32[256,1024]{0,1:T(8,128)}, u32[]{:S(2)}) copy-start(f32[256,1024]{0,1:T(8,128)} %copy.49) | copy-start | bytes 3145732
  313.0 4.0 copy-start.15
  313.0 4.0 copy-start.17
  317.0 4.6 copy-start.18
  426.8 5.5 copy-start.3
  426.8 5.5 copy-start.7
  426.8 6.0 copy-start.12
  426.8 6.0 copy-start.19
  432.3 2.2 copy-start.2
  434.5 2.9 copy-start.13
  (1 other events, 2.0 us)
Sparse Core Ops, SparseCore 0:
  29.9 81.7 all-gather.4
  158.1 77.0 all-gather.6
  345.8 276.9 all-reduce.2
where the time goes:
time: 635 us; the launch traced here: 631 us
  waiting for transfers between devices  319 us (50%)
  other arithmetic  109 us (17%)
  blocking collectives  76.9 us (12%)
  local copies, waits for them, and re-layouts  59.6 us (9%)
  matrix products  50.5 us (8%)
  between operations  14.9 us (2%)
    unnamed x4, waiting for transfers between devices  184 us
    all_gather x2, waiting for transfers between devices, entering(): pieces = lax.all_gather(value, axis)  135 us
    select_n x62, other arithmetic, lap(): return jnp.where(position < mine, longer, total)  103 us
    psum x1, blocking collectives, on_device(): d_gain = lax.psum(gain_part, ('seq', 'user'))  76.9 us
    unnamed x47, local copies, waits for them, and re-layouts  23.8 us
  transfers between devices with their start and end apart: 3, of which 3 were waited for; matrix products, arithmetic and copies ran while one was open for 6% of the time, Pallas kernels for 0%

commit v1 on v0

v1 whole, which is shorter than its diff:
```python
import functools

import jax
import jax.numpy as jnp
from jax import lax
from jax.experimental import pallas as pl
from jax.experimental.pallas import tpu as pltpu
from jax.sharding import Mesh, PartitionSpec as P

EPS = 1e-05
HD = 64
GL = 256
F32 = jnp.float32
BF = jnp.bfloat16
NN = (((1,), (0,)), ((), ()))
NT = (((1,), (1,)), ((), ()))
TN = (((0,), (0,)), ((), ()))
SEQ = ("x", "y", "c")
VMEM_LIMIT = 48 * 1024 * 1024


def dot(a, b, dims=NN):
    return lax.dot_general(a, b, dims, preferred_element_type=F32)


def split(v):
    hi = v.astype(BF)
    return hi, (v - hi.astype(F32)).astype(BF)


def lanes(shape):
    return lax.broadcasted_iota(jnp.int32, shape, 1)


def rows(shape):
    return lax.broadcasted_iota(jnp.int32, shape, 0)


def head_masks(shape):
    which = lanes(shape) // HD
    return [which == h for h in range(GL // HD)]


def pick(mask, v):
    return jnp.where(mask, v, jnp.zeros_like(v))


def pack_state(full):
    out = []
    for p in range(GL // 128):
        blk = full[128 * p:128 * p + 128, 128 * p:128 * p + 128]
        out.append(jnp.where(lanes((HD, 128)) < HD, blk[:HD], blk[HD:]))
    return jnp.concatenate(out, axis=0)


def unpack_state(st):
    zero = jnp.zeros((128, 128), st.dtype)
    blks = []
    for p in range(GL // 128):
        a = st[HD * p:HD * p + HD]
        first = lanes((HD, 128)) < HD
        blks.append(jnp.concatenate([pick(first, a), pick(~first, a)], axis=0))
    return jnp.concatenate(
        [
            jnp.concatenate([blks[0], zero], axis=1),
            jnp.concatenate([zero, blks[1]], axis=1),
        ],
        axis=0,
    )


def valid_rows(nv_ref, count):
    return (rows((count, 1)) < nv_ref[0]).astype(F32)


def features(raw):
    ex = jnp.exp(jnp.minimum(raw, 0.0))
    up = raw > 0
    return jnp.where(up, raw + 1.0, ex), jnp.where(up, 1.0, ex)


def head_mean(v):
    same = (rows((GL, GL)) // HD == lanes((GL, GL)) // HD).astype(BF)
    hi, lo = split(v)
    return (dot(hi, same) + dot(lo, same)) * (1.0 / HD)


def kv_kernel(nv_ref, tok, wk, wv, fk_o, fv_o, sk_o, st_o):
    n = tok.shape[0]
    valid = valid_rows(nv_ref, n)
    feat, slope = features(dot(tok[...], wk[...]))
    fk = (feat * valid).astype(BF)
    fv = dot(tok[...], wv[...]).astype(BF)
    fk_o[...] = fk
    fv_o[...] = fv
    sk_o[...] = slope * valid
    st_o[...] = pack_state(dot(fk, fv, TN))


def turn_kernel(core_ref, tok, own_o, par_o):
    n = own_o.shape[0]
    for which, out in ((core_ref[0], own_o), (1 - core_ref[0], par_o)):
        r = rows((n, 1))
        col = (r // 32) * 64 + which * 32 + r % 32
        one_hot = (lanes((n, tok.shape[1])) == col).astype(BF)
        out[...] = dot(one_hot, tok[...], NT).astype(out.dtype)


def q_kernel(tok, wq, dm, wo, fk, fv, fq_o, fqt_o, sq_o, do_o, nl_o):
    n = tok.shape[0]
    feat, slope = features(dot(tok[...], wq[...]))
    fq = feat.astype(BF)
    fq_o[...] = fq
    sq_o[...] = slope
    eye = (rows((GL, GL)) == lanes((GL, GL))).astype(BF)
    fqt_o[...] = dot(eye, fq, NT).astype(BF)
    do_o[...] = dot(dm[...], wo[...], NT)
    causal = rows((n, n)) >= lanes((n, n))
    total = jnp.zeros((n, GL), F32)
    for m in head_masks((n, GL)):
        hi, lo = split(pick(causal, dot(pick(m, fq), fk[...], NT)))
        vm = pick(m, fv[...])
        total = total + dot(hi, vm) + dot(lo, vm)
    nl_o[...] = total


def norm_kernel(nv_ref, nl, st, fq, fqt, do, gain, at_o, dn_o, rs_o, gp_o):
    n = nl.shape[0]
    valid = valid_rows(nv_ref, n)
    s_hi, s_lo = split(unpack_state(st[...]))
    numer = nl[...] + dot(fq[...], s_hi) + dot(fq[...], s_lo)
    inv = lax.rsqrt(head_mean(numer * numer) + EPS)
    normed = numer * inv
    at_o[...] = (normed * gain[...] * valid).astype(BF)
    dov = do[...] * valid
    gp_o[...] = jnp.sum((dov * normed).reshape(n // 8, 8, GL), axis=0)
    g = dov * gain[...]
    dn = inv * (g - normed * head_mean(g * normed))
    dn_o[...] = dn
    d_hi, d_lo = split(dn)
    rs_o[...] = pack_state(dot(fqt[...], d_hi) + dot(fqt[...], d_lo))


def dq_kernel(dn, st, fk, fv, sq, gp, dq_o, send_o):
    n = dn.shape[0]
    s_hi, s_lo = split(unpack_state(st[...]))
    d_hi, d_lo = split(dn[...])
    total = dot(d_hi, s_hi, NT) + dot(d_lo, s_hi, NT) + dot(d_hi, s_lo, NT)
    causal = rows((n, n)) >= lanes((n, n))
    for m in head_masks((n, GL)):
        vm = pick(m, fv[...])
        hi, lo = split(pick(causal, dot(d_hi, vm, NT) + dot(d_lo, vm, NT)))
        km = pick(m, fk[...])
        total = total + dot(hi, km) + dot(lo, km)
    dq = (total * sq[...]).astype(BF)
    dq_o[...] = dq
    send_o[0:n, :] = dq.astype(F32)
    send_o[n:n + 8, :] = gp[...]


def local_kernel(at, wo, dn, fq, fk, fv, mo_o, lk_o, lv_o):
    n = dn.shape[0]
    mo_o[...] = dot(at[...], wo[...]).astype(BF)
    d_hi, d_lo = split(dn[...])
    later = lanes((n, n)) >= rows((n, n))
    tk = jnp.zeros((n, GL), F32)
    tv = jnp.zeros((n, GL), F32)
    for m in head_masks((n, GL)):
        vm = pick(m, fv[...])
        hi, lo = split(pick(later, dot(vm, d_hi, NT) + dot(vm, d_lo, NT)))
        qm = pick(m, fq[...])
        tk = tk + dot(hi, qm) + dot(lo, qm)
        hi, lo = split(pick(later, dot(pick(m, fk[...]), fq[...], NT)))
        dm = pick(m, d_hi)
        tv = tv + dot(hi, dm) + dot(lo, dm) + dot(hi, pick(m, d_lo))
    lk_o[...] = tk
    lv_o[...] = tv


def dk_kernel(lk, fv, st, sk, dk_o, send_o):
    r_hi, r_lo = split(unpack_state(st[...]))
    total = lk[...] + dot(fv[...], r_hi, NT) + dot(fv[...], r_lo, NT)
    dk = (total * sk[...]).astype(BF)
    dk_o[...] = dk
    send_o[...] = dk.astype(F32)


def dtok_kernel(lv, fk, st, dq, dk, wq, wk, wv, dt_o, acc):
    r_hi, r_lo = split(unpack_state(st[...]))
    dv = (lv[...] + dot(fk[...], r_hi) + dot(fk[...], r_lo)).astype(BF)
    term = dot(dq[...], wq[...], NT) + dot(dk[...], wk[...], NT) + dot(dv, wv[...], NT)

    @pl.when(pl.program_id(0) == 0)
    def _():
        acc[...] = term

    @pl.when(pl.program_id(0) > 0)
    def _():
        acc[...] += term

    @pl.when(pl.program_id(0) == pl.num_programs(0) - 1)
    def _():
        dt_o[...] = acc[...].astype(BF)


def wgrad_kernel(own_t, par_t, own, par, out):
    n = own.shape[0]
    k, m = out.shape[0], out.shape[1]
    res = dot(own_t[...], own[...]) + dot(par_t[...].astype(BF), par[0:n, :].astype(BF))
    out[...] = res.reshape(k, m, res.shape[1])


def wgrad_gain_kernel(own_t, par_t, own, par, gp, out):
    n, width = own.shape
    k, m = out.shape[0], out.shape[1]
    res = dot(own_t[...], own[...]) + dot(par_t[...].astype(BF), par[0:n, :].astype(BF))
    out[:, :, 0:width] = res.reshape(k, m, width)
    g = jnp.sum(gp[...] + par[n:n + 8, :], axis=0, keepdims=True)
    tile = jnp.concatenate([g[:, 128 * i:128 * i + 128] for i in range(width // 128)], axis=0)
    tile = jnp.concatenate([tile, jnp.zeros((m - width // 128, 128), F32)], axis=0)
    for i in range(k):
        out[i, :, width:width + 128] = tile


def prefix_kernel(backward, v, out):
    count = v.shape[0]
    order = range(count - 1, -1, -1) if backward else range(count)
    total = jnp.zeros(v.shape[1:], F32)
    for i in order:
        out[i] = total
        total = total + v[i]


def sum_kernel(v, out):
    total = v[0]
    for i in range(1, v.shape[0]):
        total = total + v[i]
    out[...] = total


def join_kernel(q, k, out):
    ksum = k[0]
    for i in range(1, k.shape[0]):
        ksum = ksum + k[i]
    width = k.shape[2]
    each = k.shape[1] // out.shape[0]
    for u in range(out.shape[0]):
        out[u, 0:each, 0:width] = q[each * u:each * u + each, 0:width]
        out[u, each:2 * each, 0:width] = ksum[each * u:each * u + each]
        out[u, :, width:width + 128] = q[0:8, width:width + 128]


def final_kernel(v, dw_o, dg_o):
    total = v[0]
    for i in range(1, v.shape[0]):
        total = total + v[i]
    width = v.shape[2] - 128
    each = v.shape[1] // 2
    for which in range(2):
        for i in range(each):
            r = which * each + i
            dw_o[which:which + 1, width * i:width * i + width] = total[r:r + 1, 0:width]
    dg_o[...] = total[:, width:width + 128]


def call(kernel, grid, in_specs, outs, name, flops, scratch=()):
    out_shape = [jax.ShapeDtypeStruct(s, d) for s, d, _ in outs]
    return pl.pallas_call(
        kernel,
        grid=grid,
        in_specs=in_specs,
        out_specs=[spec for _, _, spec in outs],
        out_shape=out_shape,
        scratch_shapes=list(scratch),
        name=name,
        cost_estimate=pl.CostEstimate(flops=flops, bytes_accessed=4 << 20, transcendentals=0),
        compiler_params=pltpu.CompilerParams(vmem_limit_bytes=VMEM_LIMIT),
    )


SMEM = pl.BlockSpec(memory_space=pltpu.SMEM)


def whole(shape):
    return pl.BlockSpec(shape, lambda *_: (0,) * len(shape))


def col(r, w=GL):
    return pl.BlockSpec((r, w), lambda g: (0, g))


def row(r, w):
    return pl.BlockSpec((r, w), lambda g: (g, 0))


def on_device(tokens, w_query, w_key, w_value, w_out, norm_gain, lengths, d_mixed):
    _, n, d = tokens.shape
    tok = tokens.reshape(n, d)
    dm = d_mixed.reshape(n, d)
    groups = d // GL
    nseq = lax.axis_size(SEQ)
    nxy = lax.axis_size(("x", "y"))
    nu = lax.axis_size("u")
    nv = lengths - lax.axis_index(SEQ) * n
    core = jnp.full((1,), lax.axis_index("c"), jnp.int32)
    gain = norm_gain.reshape(1, d)
    act = lambda dt: ((n, d), dt, col(n))
    st_rows = d // 2
    state = ((st_rows, 128), F32, row(128, 128))
    big = 2 * n * d * d

    fk, fv, sk, st1 = call(
        kv_kernel, (groups,), [SMEM, whole((n, d)), col(d), col(d)],
        [act(BF), act(BF), act(F32), state], "kv", 2 * big,
    )(nv, tok, w_key, w_value)

    def scan(st, backward, name):
        parts = lax.all_to_all(st.reshape(nseq, st_rows // nseq, 128), SEQ, 0, 0, tiled=True)
        shape = parts.shape
        (mine,) = call(
            functools.partial(prefix_kernel, backward), (), [whole(shape)],
            [(shape, F32, whole(shape))], name, 1 << 20,
        )(parts)
        back = lax.all_to_all(mine, SEQ, 0, 0, tiled=True)
        return back.reshape(st_rows, 128)

    st_in = scan(st1, False, "prefix")

    half = d // 2
    own_t, par_send = call(
        turn_kernel, (), [SMEM, whole((n, d))],
        [((half, n), BF, whole((half, n))), ((half, n), F32, whole((half, n)))],
        "turn", big,
    )(core, tok)
    swap = [(0, 1), (1, 0)]
    par_t = lax.ppermute(par_send, "c", swap)

    fq, fqt, sq, do, nl = call(
        q_kernel, (groups,),
        [whole((n, d)), col(d), whole((n, d)), row(GL, d), col(n), col(n)],
        [act(BF), ((d, n), BF, row(GL, n)), act(F32), act(F32), act(F32)],
        "query", 4 * big,
    )(tok, w_query, dm, w_out, fk, fv)

    at, dn, rs, gp = call(
        norm_kernel, (groups,),
        [SMEM, col(n), row(128, 128), col(n), row(GL, n), col(n), col(1)],
        [act(BF), act(F32), state, ((8, d), F32, col(8))], "norm", big,
    )(nv, nl, st_in, fq, fqt, do, gain)

    r_in = scan(rs, True, "suffix")

    dq, dq_send = call(
        dq_kernel, (groups,),
        [col(n), row(128, 128), col(n), col(n), col(n), col(8)],
        [act(BF), ((n + 8, d), F32, col(n + 8))], "dquery", 2 * big,
    )(dn, st_in, fk, fv, sq, gp)
    dq_par = lax.ppermute(dq_send, "c", swap)

    steps = 4
    gshape = (nxy, half // nxy, d + 128)
    (gq,) = call(
        wgrad_gain_kernel, (steps,),
        [row(half // steps, n), row(half // steps, n), whole((n, d)), whole((n + 8, d)), whole((8, d))],
        [(gshape, F32, pl.BlockSpec((nxy // steps,) + gshape[1:], lambda g: (g, 0, 0)))],
        "wgradq", 2 * big,
    )(own_t, par_t, dq, dq_par, gp)
    gq = lax.all_to_all(gq, ("x", "y"), 0, 0, tiled=True)
    (gq,) = call(
        sum_kernel, (), [whole(gshape)], [(gshape[1:], F32, whole(gshape[1:]))], "sumq", 1 << 22
    )(gq)

    mo, lk, lv = call(
        local_kernel, (groups,),
        [whole((n, d)), col(d), col(n), col(n), col(n), col(n)],
        [act(BF), act(F32), act(F32)], "local", 4 * big,
    )(at, w_out, dn, fq, fk, fv)

    dk, dk_send = call(
        dk_kernel, (groups,), [col(n), col(n), row(128, 128), col(n)],
        [act(BF), act(F32)], "dkey", big // 2,
    )(lk, fv, r_in, sk)
    dk_par = lax.ppermute(dk_send, "c", swap)

    kshape = (nxy, half // nxy, d)
    (gk,) = call(
        wgrad_kernel, (steps,),
        [row(half // steps, n), row(half // steps, n), whole((n, d)), whole((n, d))],
        [(kshape, F32, pl.BlockSpec((nxy // steps,) + kshape[1:], lambda g: (g, 0, 0)))],
        "wgradk", 2 * big,
    )(own_t, par_t, dk, dk_par)
    gk = lax.all_to_all(gk, ("x", "y"), 0, 0, tiled=True)

    (dt,) = call(
        dtok_kernel, (groups,),
        [col(n), col(n), row(128, 128), col(n), col(n), col(d), col(d), col(d)],
        [((n, d), BF, whole((n, d)))], "dtok", 4 * big,
        scratch=[pltpu.VMEM((n, d), F32)],
    )(lv, fk, r_in, dq, dk, w_query, w_key, w_value)

    each = half // nxy // nu
    jshape = (nu, 2 * each, d + 128)
    (both,) = call(
        join_kernel, (), [whole(gshape[1:]), whole(kshape)], [(jshape, F32, whole(jshape))],
        "join", 1 << 22,
    )(gq, gk)
    both = lax.all_to_all(both, "u", 0, 0, tiled=True)
    dw, dg = call(
        final_kernel, (), [whole(jshape)],
        [((2, each * d), F32, whole((2, each * d))), ((8, 128), F32, whole((8, 128)))],
        "final", 1 << 20,
    )(both)
    return mo.reshape(1, n, d), dt.reshape(1, n, d), dw, dg.reshape(d)


def solution(mesh):
    fine = Mesh(mesh.devices.reshape(4, 4, 2, 8), ("x", "y", "c", "u"))
    acts = P("u", SEQ, None)
    placed = (acts, P(), P(), P(), P(), P(), P("u"), acts)
    return jax.shard_map(
        on_device,
        mesh=fine,
        in_specs=placed,
        out_specs=(acts, acts, P(None, ("x", "y", "c", "u")), P()),
        check_vma=False,
    )
```

time: 635 us -> 182 us (0.29)
  the two profiles are of different devices: /device:TPU:1 before, /device:TPU:8 now
where the time goes in v1:
time: 182 us; the launch traced here: 181 us
  Pallas kernels  47.6 us (26%)
  waiting for transfers between devices  45.7 us (25%)
  starting transfers between devices  32.9 us (18%)
  blocking collectives  29.3 us (16%)
  local copies, waits for them, and re-layouts  23.8 us (13%)
    all_to_all x2, blocking collectives, scan(): lax.all_to_all(st.reshape(nseq, st_rows // nseq, 128), SEQ, 0, 0, tiled=T...  29.3 us
    all_to_all x1, waiting for transfers between devices, on_device(): gk = lax.all_to_all(gk, ('x', 'y'), 0, 0, tiled=True)  28.3 us
    unnamed x72, local copies, waits for them, and re-layouts  23.8 us
    all_to_all x2, starting transfers between devices, scan(): back = lax.all_to_all(mine, SEQ, 0, 0, tiled=True)  10.7 us
    pallas_call x1, Pallas kernels, on_device(): call(local_kernel, (groups,), [whole((n, d)), col(d), col(n), col(n), col...  9.93 us
    all_to_all x1, waiting for transfers between devices, on_device(): gq = lax.all_to_all(gq, ('x', 'y'), 0, 0, tiled=True)  8.54 us
    all_to_all x1, starting transfers between devices, on_device(): both = lax.all_to_all(both, 'u', 0, 0, tiled=True)  8.47 us
    all_to_all x1, starting transfers between devices, on_device(): gk = lax.all_to_all(gk, ('x', 'y'), 0, 0, tiled=True)  7.69 us
  transfers between devices with their start and end apart: 8, of which 5 were waited for; matrix products, arithmetic and copies ran while one was open for 0% of the time, Pallas kernels for 17%

profile of v1, /device:TPU:8, one launch (start us, length us, event | category | flops | bytes accessed | tf_op | source)
XLA Modules:
  0.0 180.8 jit_solution(4000314781300893124)
XLA Ops:
  1.3 1.6 copy-done.1
  3.9 4.5 %kv.1 = (bf16[256,1024]{1,0:T(8,128)(2,1)S(1)}, bf16[256,1024]{1,0:T(8,128)(2,1)S(1)}, f32[256,1024]{1,0:T(8,128)S(1)}, f32[512,128]{1,0:T(8,128)S(1)}) custom-call(s32[1]{0:T(128)S(6)} %sub.7.nv_ref, bf16[256,1024]{1,0:T(8,128)(2,1)S(1)} %bitcast.16, bf16[1024,1024]{1,0:T(8,128)(2,1)S(1)} %copy-done.1, bf16[1024,1024]{1,0:T(8,128)(2,1)} %wv.3), custom_call_target="tpu_custom_call" | custom-call | flops 1073741824 | bytes 4194304 | tf_op jit(solution)/shard_map/kv/pallas_call | solution.py:312
  9.4 14.7 %all_to_all.35.v = f32[32,16,128]{2,1,0:T(8,128)S(1)} all-to-all(f32[32,16,128]{2,1,0:T(8,128)S(1)} %bitcast.20), channel_id=1, replica_groups=mesh['x'=4,'y'=4,'c'=2,'u'=8] {'x','y','c'}, dimensions={0} | all-to-all | bytes 524288 | tf_op jit(solution)/shard_map/all_to_all | solution.py:318
  24.8 5.4 %all-to-all-start.1 = ((f32[32,16,128]{2,1,0:T(8,128)}), f32[32,16,128]{2,1,0:T(8,128)S(1)}, u32[]{:S(2)}, u32[]{:S(2)}) async-start(f32[32,16,128]{2,1,0:T(8,128)} %prefix.1), calls=%async_computation.1 | async-start | bytes 524288 | tf_op jit(solution)/shard_map/all_to_all | solution.py:324
  31.3 7.4 %query.1 = (bf16[256,1024]{1,0:T(8,128)(2,1)S(1)}, bf16[1024,256]{1,0:T(8,128)(2,1)S(1)}, f32[256,1024]{1,0:T(8,128)S(1)}, f32[256,1024]{1,0:T(8,128)S(1)}, f32[256,1024]{1,0:T(8,128)}) custom-call(bf16[256,1024]{1,0:T(8,128)(2,1)S(1)} %bitcast.17, bf16[1024,1024]{1,0:T(8,128)(2,1)} %wq.3, bf16[256,1024]{1,0:T(8,128)(2,1)S(1)} %bitcast.22, ...), custom_call_target="tpu_custom_call" | custom-call | flops 2147483648 | bytes 4194304 | tf_op jit(solution)/shard_map/query/pallas_call | solution.py:338
  44.6 4.3 %norm.1 = (bf16[256,1024]{1,0:T(8,128)(2,1)S(1)}, f32[256,1024]{1,0:T(8,128)S(1)}, f32[512,128]{1,0:T(8,128)S(1)}, f32[8,1024]{1,0:T(8,128)S(1)}) custom-call(s32[1]{0:T(128)S(6)} %sub.7.nv_ref, f32[256,1024]{1,0:T(8,128)S(1)} %copy-done.10, f32[512,128]{1,0:T(8,128)S(1)} %bitcast.14, bf16[256,1024]{1,0:T(8,128)(2,1)S(1)} %copy-done.24, ...), custom_call_target="tpu_custom_call" | custom-call | flops 536870912 | bytes 4194304 | tf_op jit(solution)/shard_map/norm/pallas_call | solution.py:345
  49.0 5.1 %dquery.1 = (bf16[256,1024]{1,0:T(8,128)(2,1)S(1)}, f32[264,1024]{1,0:T(8,128)}) custom-call(f32[256,1024]{1,0:T(8,128)S(1)} %get-tuple-element.36.dn, f32[512,128]{1,0:T(8,128)S(1)} %bitcast.15, bf16[256,1024]{1,0:T(8,128)(2,1)S(1)} %copy-done.16, bf16[256,1024]{1,0:T(8,128)(2,1)S(1)} %copy-done.20, f32[256,1024]{1,0:T(8,128)S(1)} %copy-done.35, ...), custom_call_target="tpu_custom_call" | custom-call | flops 1073741824 | bytes 4194304 | tf_op jit(solution)/shard_map/dquery/pallas_call | solution.py:353
  54.2 1.6 turn.1
  56.2 14.6 %all_to_all.36.v = f32[32,16,128]{2,1,0:T(8,128)S(1)} all-to-all(f32[32,16,128]{2,1,0:T(8,128)S(1)} %bitcast.19), channel_id=1, replica_groups=mesh['x'=4,'y'=4,'c'=2,'u'=8] {'x','y','c'}, dimensions={0} | all-to-all | bytes 524288 | tf_op jit(solution)/shard_map/all_to_all | solution.py:318
  71.5 5.4 %all-to-all-start.3 = ((f32[32,16,128]{2,1,0:T(8,128)}), f32[32,16,128]{2,1,0:T(8,128)S(1)}, u32[]{:S(2)}, u32[]{:S(2)}) async-start(f32[32,16,128]{2,1,0:T(8,128)} %suffix.1), calls=%async_computation.3 | async-start | bytes 524288 | tf_op jit(solution)/shard_map/all_to_all | solution.py:324
  78.2 1.4 copy-done
  79.6 4.7 %all-to-all-done.3 = f32[32,16,128]{2,1,0:T(8,128)S(1)} async-done(((f32[32,16,128]{2,1,0:T(8,128)}), f32[32,16,128]{2,1,0:T(8,128)S(1)}, u32[]{:S(2)}, u32[]{:S(2)}) %all-to-all-start.3) | async-done | bytes 262176 | tf_op jit(solution)/shard_map/all_to_all | solution.py:324
  84.4 5.3 %all-to-all-start.4 = ((f32[16,32,1152]{2,1,0:T(8,128)}), f32[16,32,1152]{2,1,0:T(8,128)S(1)}, u32[]{:S(2)}, u32[]{:S(2)}) async-start(f32[16,32,1152]{2,1,0:T(8,128)} %copy-done), calls=%async_computation.4 | async-start | bytes 4718592 | tf_op jit(solution)/shard_map/all_to_all | solution.py:368
  95.1 9.9 %local.1 = (bf16[256,1024]{1,0:T(8,128)(2,1)}, f32[256,1024]{1,0:T(8,128)S(1)}, f32[256,1024]{1,0:T(8,128)S(1)}) custom-call(bf16[256,1024]{1,0:T(8,128)(2,1)S(1)} %copy-done.33, bf16[1024,1024]{1,0:T(8,128)(2,1)} %wo.3, f32[256,1024]{1,0:T(8,128)S(1)} %copy-done.30, bf16[256,1024]{1,0:T(8,128)(2,1)S(1)} %copy-done.25, bf16[256,1024]{1,0:T(8,128)(2,1)S(1)} %copy-done.17, ...), custom_call_target="tpu_custom_call" | custom-call | flops 2147483648 | bytes 4194304 | tf_op jit(solution)/shard_map/local/pallas_call | solution.py:373
  106.1 1.5 dkey.1
  107.7 2.6 %collective-permute-done.2.par = f32[256,1024]{1,0:T(8,128)S(1)} collective-permute-done((f32[256,1024]{1,0:T(8,128)S(1)}, f32[256,1024]{1,0:T(8,128)S(1)}, u32[]{:S(2)}, u32[]{:S(2)}) %collective-permute-start.2) | collective-permute-done | bytes 1048608 | tf_op jit(solution)/shard_map/ppermute | solution.py:383
  111.6 1.3 copy-done.2
  113.7 8.5 %all-to-all-done.4.v = f32[16,32,1152]{2,1,0:T(8,128)S(1)} async-done(((f32[16,32,1152]{2,1,0:T(8,128)}), f32[16,32,1152]{2,1,0:T(8,128)S(1)}, u32[]{:S(2)}, u32[]{:S(2)}) %all-to-all-start.4) | async-done | bytes 2359328 | tf_op jit(solution)/shard_map/all_to_all | solution.py:368
  122.3 7.7 %all-to-all-start.5 = ((f32[16,32,1024]{2,1,0:T(8,128)}), f32[16,32,1024]{2,1,0:T(8,128)}, u32[]{:S(2)}, u32[]{:S(2)}) async-start(f32[16,32,1024]{2,1,0:T(8,128)} %copy-done.2), calls=%async_computation.5 | async-start | bytes 4194304 | tf_op jit(solution)/shard_map/all_to_all | solution.py:392
  130.1 28.3 %all-to-all-done.5.k = f32[16,32,1024]{2,1,0:T(8,128)} async-done(((f32[16,32,1024]{2,1,0:T(8,128)}), f32[16,32,1024]{2,1,0:T(8,128)}, u32[]{:S(2)}, u32[]{:S(2)}) %all-to-all-start.5) | async-done | bytes 2097184 | tf_op jit(solution)/shard_map/all_to_all | solution.py:392
  158.4 2.4 %join.1 = f32[8,8,1152]{2,1,0:T(8,128)} custom-call(f32[32,1152]{1,0:T(8,128)S(1)} %sumq.1.q, f32[16,32,1024]{2,1,0:T(8,128)} %all-to-all-done.5.k), custom_call_target="tpu_custom_call" | custom-call | flops 4194304 | bytes 4194304 | tf_op jit(solution)/shard_map/join/pallas_call | solution.py:403
  160.8 8.5 %all-to-all-start.6 = ((f32[8,8,1152]{2,1,0:T(8,128)}), f32[8,8,1152]{2,1,0:T(8,128)S(1)}, u32[]{:S(2)}, u32[]{:S(2)}) async-start(f32[8,8,1152]{2,1,0:T(8,128)} %join.1), calls=%async_computation.6 | async-start | bytes 589824 | tf_op jit(solution)/shard_map/all_to_all | solution.py:407
  172.6 6.0 %dtok.1 = bf16[256,1024]{1,0:T(8,128)(2,1)} custom-call(f32[256,1024]{1,0:T(8,128)S(1)} %copy-done.9, bf16[256,1024]{1,0:T(8,128)(2,1)S(1)} %copy-done.18, f32[512,128]{1,0:T(8,128)S(1)} %bitcast.13, bf16[256,1024]{1,0:T(8,128)(2,1)S(1)} %get-tuple-element.42.dq.own, bf16[256,1024]{1,0:T(8,128)(2,1)S(1)} %copy-done.7, bf16[1024,1024]{1,0:T(8,128)(2,1)S(1)} %copy-done.3, ...), custom_call_target="tpu_custom_call" | custom-call | flops 2147483648 | bytes 4194304 | tf_op jit(solution)/shard_map/dtok/pallas_call | solution.py:394
  178.7 1.5 all-to-all-done.6.v
  (81 shorter events, 24.9 us)
Async XLA Ops:
  1.3 1.6 copy-start.1
  3.9 26.3 %copy-start.14 = (bf16[1,256,1024]{2,1,0:T(8,128)(2,1)S(1)}, bf16[1,256,1024]{2,1,0:T(8,128)(2,1)}, u32[]{:S(2)}) copy-start(bf16[1,256,1024]{2,1,0:T(8,128)(2,1)} %param.8) | copy-start | bytes 1572868
  9.4 29.3 %copy-start.15 = (bf16[256,1024]{1,0:T(8,128)(2,1)}, bf16[256,1024]{1,0:T(8,128)(2,1)S(1)}, u32[]{:S(2)}) copy-start(bf16[256,1024]{1,0:T(8,128)(2,1)S(1)} %get-tuple-element.28.fk) | copy-start | bytes 1572868
  9.4 29.3 %copy-start.19 = (bf16[256,1024]{1,0:T(8,128)(2,1)}, bf16[256,1024]{1,0:T(8,128)(2,1)S(1)}, u32[]{:S(2)}) copy-start(bf16[256,1024]{1,0:T(8,128)(2,1)S(1)} %get-tuple-element.29.fv) | copy-start | bytes 1572868
  24.8 16.5 %all-to-all-start.1 = ((f32[32,16,128]{2,1,0:T(8,128)}), f32[32,16,128]{2,1,0:T(8,128)S(1)}, u32[]{:S(2)}, u32[]{:S(2)}) async-start(f32[32,16,128]{2,1,0:T(8,128)} %prefix.1), calls=%async_computation.1 | async-start | bytes 524288 | tf_op jit(solution)/shard_map/all_to_all | solution.py:324
  31.3 10.0 %copy-start.28 = (f32[1024]{0:T(1024)S(1)}, f32[1024]{0:T(1024)}, u32[]{:S(2)}) copy-start(f32[1024]{0:T(1024)} %param.13) | copy-start | bytes 12292
  44.6 4.3 %copy-start.16 = (bf16[256,1024]{1,0:T(8,128)(2,1)S(1)}, bf16[256,1024]{1,0:T(8,128)(2,1)}, u32[]{:S(2)}) copy-start(bf16[256,1024]{1,0:T(8,128)(2,1)} %copy-done.15) | copy-start | bytes 1572868
  44.6 4.3 %copy-start.20 = (bf16[256,1024]{1,0:T(8,128)(2,1)S(1)}, bf16[256,1024]{1,0:T(8,128)(2,1)}, u32[]{:S(2)}) copy-start(bf16[256,1024]{1,0:T(8,128)(2,1)} %copy-done.19) | copy-start | bytes 1572868
  44.6 4.3 %copy-start.35 = (f32[256,1024]{1,0:T(8,128)S(1)}, f32[256,1024]{1,0:T(8,128)}, u32[]{:S(2)}) copy-start(f32[256,1024]{1,0:T(8,128)} %copy-done.34) | copy-start | bytes 3145732
  48.9 6.9 %copy-start.29 = (f32[256,1024]{1,0:T(8,128)}, f32[256,1024]{1,0:T(8,128)S(1)}, u32[]{:S(2)}) copy-start(f32[256,1024]{1,0:T(8,128)S(1)} %get-tuple-element.36.dn) | copy-start | bytes 3145732
  48.9 6.9 %copy-start.32 = (bf16[256,1024]{1,0:T(8,128)(2,1)}, bf16[256,1024]{1,0:T(8,128)(2,1)S(1)}, u32[]{:S(2)}) copy-start(bf16[256,1024]{1,0:T(8,128)(2,1)S(1)} %get-tuple-element.35.at) | copy-start | bytes 1572868
  54.1 22.8 %collective-permute-start.1 = (f32[264,1024]{1,0:T(8,128)}, f32[264,1024]{1,0:T(8,128)S(1)}, u32[]{:S(2)}, u32[]{:S(2)}) collective-permute-start(f32[264,1024]{1,0:T(8,128)} %get-tuple-element.48), channel_id=1, source_target_pairs={{0,8},{8,0},{1,9},{9,1},{2,10},{10,2},{3,11},{11,3},{4,12},{12,4},... | collective-permute-start | bytes 3244040 | tf_op jit(solution)/shard_map/ppermute | solution.py:358
  55.8 21.1 %collective-permute-start = (f32[512,256]{1,0:T(8,128)}, f32[512,256]{1,0:T(8,128)S(1)}, u32[]{:S(2)}, u32[]{:S(2)}) collective-permute-start(f32[512,256]{1,0:T(8,128)} %get-tuple-element.47), channel_id=1, source_target_pairs={{0,8},{8,0},{1,9},{9,1},{2,10},{10,2},{3,11},{11,3},{4,12},{12,4},... | collective-permute-start | bytes 1572872 | tf_op jit(solution)/shard_map/ppermute | solution.py:336
  71.5 12.8 %all-to-all-start.3 = ((f32[32,16,128]{2,1,0:T(8,128)}), f32[32,16,128]{2,1,0:T(8,128)S(1)}, u32[]{:S(2)}, u32[]{:S(2)}) async-start(f32[32,16,128]{2,1,0:T(8,128)} %suffix.1), calls=%async_computation.3 | async-start | bytes 524288 | tf_op jit(solution)/shard_map/all_to_all | solution.py:324
  78.2 1.4 copy-start
  84.4 37.9 %all-to-all-start.4 = ((f32[16,32,1152]{2,1,0:T(8,128)}), f32[16,32,1152]{2,1,0:T(8,128)S(1)}, u32[]{:S(2)}, u32[]{:S(2)}) async-start(f32[16,32,1152]{2,1,0:T(8,128)} %copy-done), calls=%async_computation.4 | async-start | bytes 4718592 | tf_op jit(solution)/shard_map/all_to_all | solution.py:368
  95.1 11.0 %copy-start.12 = (f32[256,1024]{1,0:T(8,128)S(1)}, f32[256,1024]{1,0:T(8,128)}, u32[]{:S(2)}) copy-start(f32[256,1024]{1,0:T(8,128)} %copy-done.11) | copy-start | bytes 3145732
  95.1 11.0 %copy-start.22 = (bf16[256,1024]{1,0:T(8,128)(2,1)S(1)}, bf16[256,1024]{1,0:T(8,128)(2,1)}, u32[]{:S(2)}) copy-start(bf16[256,1024]{1,0:T(8,128)(2,1)} %copy-done.19) | copy-start | bytes 1572868
  106.0 4.3 %copy-start.5 = (f32[512,256]{1,0:T(8,128)S(1)}, f32[512,256]{1,0:T(8,128)}, u32[]{:S(2)}) copy-start(f32[512,256]{1,0:T(8,128)} %copy-done.4) | copy-start | bytes 1572868
  107.6 2.7 %collective-permute-start.2 = (f32[256,1024]{1,0:T(8,128)S(1)}, f32[256,1024]{1,0:T(8,128)S(1)}, u32[]{:S(2)}, u32[]{:S(2)}) collective-permute-start(f32[256,1024]{1,0:T(8,128)S(1)} %get-tuple-element.49), channel_id=1, source_target_pairs={{0,8},{8,0},{1,9},{9,1},{2,10},{10,2},{3,11},{11,3},{4,12},{12,4},... | collective-permute-start | bytes 3145736 | tf_op jit(solution)/shard_map/ppermute | solution.py:383
  111.6 1.3 copy-start.2
  122.3 36.2 %all-to-all-start.5 = ((f32[16,32,1024]{2,1,0:T(8,128)}), f32[16,32,1024]{2,1,0:T(8,128)}, u32[]{:S(2)}, u32[]{:S(2)}) async-start(f32[16,32,1024]{2,1,0:T(8,128)} %copy-done.2), calls=%async_computation.5 | async-start | bytes 4194304 | tf_op jit(solution)/shard_map/all_to_all | solution.py:392
  130.1 39.3 %copy-start.3 = (bf16[1024,1024]{1,0:T(8,128)(2,1)S(1)}, bf16[1024,1024]{1,0:T(8,128)(2,1)}, u32[]{:S(2)}) copy-start(bf16[1024,1024]{1,0:T(8,128)(2,1)} %wq.3) | copy-start | bytes 6291460
  160.8 19.3 %all-to-all-start.6 = ((f32[8,8,1152]{2,1,0:T(8,128)}), f32[8,8,1152]{2,1,0:T(8,128)S(1)}, u32[]{:S(2)}, u32[]{:S(2)}) async-start(f32[8,8,1152]{2,1,0:T(8,128)} %join.1), calls=%async_computation.6 | async-start | bytes 589824 | tf_op jit(solution)/shard_map/all_to_all | solution.py:407
  (20 other events, 20.8 us)

commit v2 on v1

--- a/solution.py
+++ b/solution.py
@@ -16,7 +16,7 @@
 NT = (((1,), (1,)), ((), ()))
 TN = (((0,), (0,)), ((), ()))
 SEQ = ("x", "y", "c")
-VMEM_LIMIT = 48 * 1024 * 1024
+VMEM_LIMIT = 64 * 1024 * 1024
 
 
 def dot(a, b, dims=NN):
@@ -106,8 +106,7 @@
         out[...] = dot(one_hot, tok[...], NT).astype(out.dtype)
 
 
-def q_kernel(tok, wq, dm, wo, fk, fv, fq_o, fqt_o, sq_o, do_o, nl_o):
-    n = tok.shape[0]
+def q_kernel(tok, wq, dm, wo, fq_o, fqt_o, sq_o, do_o):
     feat, slope = features(dot(tok[...], wq[...]))
     fq = feat.astype(BF)
     fq_o[...] = fq
@@ -115,10 +114,14 @@
     eye = (rows((GL, GL)) == lanes((GL, GL))).astype(BF)
     fqt_o[...] = dot(eye, fq, NT).astype(BF)
     do_o[...] = dot(dm[...], wo[...], NT)
+
+
+def numer_kernel(fq, fk, fv, nl_o):
+    n = fq.shape[0]
     causal = rows((n, n)) >= lanes((n, n))
     total = jnp.zeros((n, GL), F32)
     for m in head_masks((n, GL)):
-        hi, lo = split(pick(causal, dot(pick(m, fq), fk[...], NT)))
+        hi, lo = split(pick(causal, dot(pick(m, fq[...]), fk[...], NT)))
         vm = pick(m, fv[...])
         total = total + dot(hi, vm) + dot(lo, vm)
     nl_o[...] = total
@@ -158,22 +161,29 @@
     send_o[n:n + 8, :] = gp[...]
 
 
-def local_kernel(at, wo, dn, fq, fk, fv, mo_o, lk_o, lv_o):
+def local_k_kernel(dn, fq, fv, lk_o):
     n = dn.shape[0]
-    mo_o[...] = dot(at[...], wo[...]).astype(BF)
     d_hi, d_lo = split(dn[...])
     later = lanes((n, n)) >= rows((n, n))
     tk = jnp.zeros((n, GL), F32)
-    tv = jnp.zeros((n, GL), F32)
     for m in head_masks((n, GL)):
         vm = pick(m, fv[...])
         hi, lo = split(pick(later, dot(vm, d_hi, NT) + dot(vm, d_lo, NT)))
         qm = pick(m, fq[...])
         tk = tk + dot(hi, qm) + dot(lo, qm)
+    lk_o[...] = tk
+
+
+def local_v_kernel(at, wo, dn, fq, fk, mo_o, lv_o):
+    n = dn.shape[0]
+    mo_o[...] = dot(at[...], wo[...]).astype(BF)
+    d_hi, d_lo = split(dn[...])
+    later = lanes((n, n)) >= rows((n, n))
+    tv = jnp.zeros((n, GL), F32)
+    for m in head_masks((n, GL)):
         hi, lo = split(pick(later, dot(pick(m, fk[...]), fq[...], NT)))
         dm = pick(m, d_hi)
         tv = tv + dot(hi, dm) + dot(lo, dm) + dot(hi, pick(m, d_lo))
-    lk_o[...] = tk
     lv_o[...] = tv
 
 
@@ -229,13 +239,6 @@
     for i in order:
         out[i] = total
         total = total + v[i]
-
-
-def sum_kernel(v, out):
-    total = v[0]
-    for i in range(1, v.shape[0]):
-        total = total + v[i]
-    out[...] = total
 
 
 def join_kernel(q, k, out):
@@ -314,33 +317,44 @@
         [act(BF), act(BF), act(F32), state], "kv", 2 * big,
     )(nv, tok, w_key, w_value)
 
-    def scan(st, backward, name):
-        parts = lax.all_to_all(st.reshape(nseq, st_rows // nseq, 128), SEQ, 0, 0, tiled=True)
+    tie = lax.optimization_barrier
+
+    def to_parts(st):
+        return lax.all_to_all(st.reshape(nseq, st_rows // nseq, 128), SEQ, 0, 0, tiled=True)
+
+    def run(parts, backward, name):
         shape = parts.shape
         (mine,) = call(
             functools.partial(prefix_kernel, backward), (), [whole(shape)],
             [(shape, F32, whole(shape))], name, 1 << 20,
         )(parts)
-        back = lax.all_to_all(mine, SEQ, 0, 0, tiled=True)
-        return back.reshape(st_rows, 128)
-
-    st_in = scan(st1, False, "prefix")
-
+        return mine
+
+    def from_parts(mine):
+        return lax.all_to_all(mine, SEQ, 0, 0, tiled=True).reshape(st_rows, 128)
+
+    parts = to_parts(st1)
+    tok_1, _ = tie((tok, st1))
     half = d // 2
     own_t, par_send = call(
         turn_kernel, (), [SMEM, whole((n, d))],
         [((half, n), BF, whole((half, n))), ((half, n), F32, whole((half, n)))],
         "turn", big,
-    )(core, tok)
+    )(core, tok_1)
     swap = [(0, 1), (1, 0)]
     par_t = lax.ppermute(par_send, "c", swap)
-
-    fq, fqt, sq, do, nl = call(
-        q_kernel, (groups,),
-        [whole((n, d)), col(d), whole((n, d)), row(GL, d), col(n), col(n)],
-        [act(BF), ((d, n), BF, row(GL, n)), act(F32), act(F32), act(F32)],
-        "query", 4 * big,
-    )(tok, w_query, dm, w_out, fk, fv)
+    fq, fqt, sq, do = call(
+        q_kernel, (groups,), [whole((n, d)), col(d), whole((n, d)), row(GL, d)],
+        [act(BF), ((d, n), BF, row(GL, n)), act(F32), act(F32)], "query", 2 * big,
+    )(tok_1, w_query, dm, w_out)
+    parts, fq, own_t = tie((parts, fq, own_t))
+    mine = run(parts, False, "prefix")
+
+    st_in = from_parts(mine)
+    fq_2, _ = tie((fq, mine))
+    (nl,) = call(
+        numer_kernel, (groups,), [col(n), col(n), col(n)], [act(F32)], "numer", 2 * big,
+    )(fq_2, fk, fv)
 
     at, dn, rs, gp = call(
         norm_kernel, (groups,),
@@ -348,39 +362,39 @@
         [act(BF), act(F32), state, ((8, d), F32, col(8))], "norm", big,
     )(nv, nl, st_in, fq, fqt, do, gain)
 
-    r_in = scan(rs, True, "suffix")
-
+    parts = to_parts(rs)
+    dn_3, _ = tie((dn, rs))
     dq, dq_send = call(
         dq_kernel, (groups,),
         [col(n), row(128, 128), col(n), col(n), col(n), col(8)],
         [act(BF), ((n + 8, d), F32, col(n + 8))], "dquery", 2 * big,
-    )(dn, st_in, fk, fv, sq, gp)
+    )(dn_3, st_in, fk, fv, sq, gp)
+    parts, dq, dq_send = tie((parts, dq, dq_send))
+    mine = run(parts, True, "suffix")
+
+    r_in = from_parts(mine)
+    dq_send, dn_4, _ = tie((dq_send, dn, mine))
     dq_par = lax.ppermute(dq_send, "c", swap)
-
+    (lk,) = call(
+        local_k_kernel, (groups,), [col(n), col(n), col(n)], [act(F32)], "localk", 2 * big,
+    )(dn_4, fq, fv)
+    dk, dk_send = call(
+        dk_kernel, (groups,), [col(n), col(n), row(128, 128), col(n)],
+        [act(BF), act(F32)], "dkey", big // 2,
+    )(lk, fv, r_in, sk)
+
+    dk_par = lax.ppermute(dk_send, "c", swap)
     steps = 4
     gshape = (nxy, half // nxy, d + 128)
+    dq_5, _ = tie((dq, dk))
     (gq,) = call(
         wgrad_gain_kernel, (steps,),
         [row(half // steps, n), row(half // steps, n), whole((n, d)), whole((n + 8, d)), whole((8, d))],
         [(gshape, F32, pl.BlockSpec((nxy // steps,) + gshape[1:], lambda g: (g, 0, 0)))],
         "wgradq", 2 * big,
-    )(own_t, par_t, dq, dq_par, gp)
-    gq = lax.all_to_all(gq, ("x", "y"), 0, 0, tiled=True)
-    (gq,) = call(
-        sum_kernel, (), [whole(gshape)], [(gshape[1:], F32, whole(gshape[1:]))], "sumq", 1 << 22
-    )(gq)
-
-    mo, lk, lv = call(
-        local_kernel, (groups,),
-        [whole((n, d)), col(d), col(n), col(n), col(n), col(n)],
-        [act(BF), act(F32), act(F32)], "local", 4 * big,
-    )(at, w_out, dn, fq, fk, fv)
-
-    dk, dk_send = call(
-        dk_kernel, (groups,), [col(n), col(n), row(128, 128), col(n)],
-        [act(BF), act(F32)], "dkey", big // 2,
-    )(lk, fv, r_in, sk)
-    dk_par = lax.ppermute(dk_send, "c", swap)
+    )(own_t, par_t, dq_5, dq_par, gp)
+    gq_sum = lax.psum_scatter(gq, ("x", "y"), scatter_dimension=0, tiled=True)
+    gq_sum = gq_sum.reshape(gshape[1:])
 
     kshape = (nxy, half // nxy, d)
     (gk,) = call(
@@ -389,21 +403,27 @@
         [(kshape, F32, pl.BlockSpec((nxy // steps,) + kshape[1:], lambda g: (g, 0, 0)))],
         "wgradk", 2 * big,
     )(own_t, par_t, dk, dk_par)
-    gk = lax.all_to_all(gk, ("x", "y"), 0, 0, tiled=True)
-
+    gk_parts = lax.all_to_all(gk, ("x", "y"), 0, 0, tiled=True)
+
+    dn_5, dk_5, _ = tie((dn, dk, gk))
+    mo, lv = call(
+        local_v_kernel, (groups,),
+        [whole((n, d)), col(d), col(n), col(n), col(n)], [act(BF), act(F32)], "localv", 4 * big,
+    )(at, w_out, dn_5, fq, fk)
     (dt,) = call(
         dtok_kernel, (groups,),
         [col(n), col(n), row(128, 128), col(n), col(n), col(d), col(d), col(d)],
         [((n, d), BF, whole((n, d)))], "dtok", 4 * big,
         scratch=[pltpu.VMEM((n, d), F32)],
-    )(lv, fk, r_in, dq, dk, w_query, w_key, w_value)
+    )(lv, fk, r_in, dq, dk_5, w_query, w_key, w_value)
+    gk_parts, mo, dt = tie((gk_parts, mo, dt))
 
     each = half // nxy // nu
     jshape = (nu, 2 * each, d + 128)
     (both,) = call(
         join_kernel, (), [whole(gshape[1:]), whole(kshape)], [(jshape, F32, whole(jshape))],
         "join", 1 << 22,
-    )(gq, gk)
+    )(gq_sum, gk_parts)
     both = lax.all_to_all(both, "u", 0, 0, tiled=True)
     dw, dg = call(
         final_kernel, (), [whole(jshape)],

time: 182 us -> 222 us (1.22)
  the two profiles are of different devices: /device:TPU:8 before, /device:TPU:1 now
where the time goes in v2:
time: 222 us; the launch traced here: 218 us
  waiting for transfers between devices  80.7 us (36%)
  Pallas kernels  74.9 us (34%)
  starting transfers between devices  30.4 us (14%)
  blocking collectives  16.6 us (7%)
  between operations  14.7 us (7%)
    unnamed x2, waiting for transfers between devices  52.5 us
    all_to_all x1, blocking collectives, on_device(): both = lax.all_to_all(both, 'u', 0, 0, tiled=True)  16.6 us
    all_to_all x1, waiting for transfers between devices, on_device(): gk_parts = lax.all_to_all(gk, ('x', 'y'), 0, 0, tiled=True)  16.4 us
    all_to_all x2, starting transfers between devices, to_parts(): lax.all_to_all(st.reshape(nseq, st_rows // nseq, 128), SEQ, 0, 0, tiled=T...  13 us
    all_to_all x2, starting transfers between devices, from_parts(): return lax.all_to_all(mine, SEQ, 0, 0, tiled=True).reshape(st_rows, 128)  12.1 us
    pallas_call x1, Pallas kernels, on_device(): call(local_v_kernel, (groups,), [whole((n, d)), col(d), col(n), col(n), c...  8.33 us
    pallas_call x1, Pallas kernels, on_device(): call(dtok_kernel, (groups,), [col(n), col(n), row(128, 128), col(n), col(...  6.61 us
    pallas_call x1, Pallas kernels, on_device(): call(dq_kernel, (groups,), [col(n), row(128, 128), col(n), col(n), col(n)...  6.4 us
  transfers between devices with their start and end apart: 9, of which 7 were waited for; matrix products, arithmetic and copies ran while one was open for 0% of the time, Pallas kernels for 23%

profile of v2, /device:TPU:1, one launch (start us, length us, event | category | flops | bytes accessed | tf_op | source)
XLA Modules:
  0.0 218.5 jit_solution(10844568454021604375)
XLA Ops:
  7.8 5.5 %kv.1 = (bf16[256,1024]{1,0:T(8,128)(2,1)}, bf16[256,1024]{1,0:T(8,128)(2,1)}, f32[256,1024]{1,0:T(8,128)}, f32[512,128]{1,0:T(8,128)}) custom-call(s32[1]{0:T(128)S(6)} %sub.7.nv_ref, bf16[256,1024]{1,0:T(8,128)(2,1)} %bitcast.14, bf16[1024,1024]{1,0:T(8,128)(2,1)} %wk.3, bf16[1024,1024]{1,0:T(8,128)(2,1)} %wv.3), custom_call_target="tpu_custom_call" | custom-call | flops 1073741824 | bytes 4194304 | tf_op jit(solution)/shard_map/kv/pallas_call | solution.py:315
  13.3 8.6 %all-to-all-start = ((f32[32,16,128]{2,1,0:T(8,128)}), f32[32,16,128]{2,1,0:T(8,128)}, u32[]{:S(2)}, u32[]{:S(2)}) async-start(f32[32,16,128]{2,1,0:T(8,128)} %bitcast.20), calls=%async_computation | async-start | bytes 524288 | tf_op jit(solution)/shard_map/all_to_all | solution.py:323
  22.0 2.7 %turn.1 = (bf16[512,256]{1,0:T(8,128)(2,1)}, f32[512,256]{1,0:T(8,128)}) custom-call(s32[1]{0:T(128)} %bitcast.4.core_ref, bf16[256,1024]{1,0:T(8,128)(2,1)} %bitcast.15), custom_call_target="tpu_custom_call" | custom-call | flops 536870912 | bytes 4194304 | tf_op jit(solution)/shard_map/turn/pallas_call | solution.py:339
  24.7 6.2 %query.1 = (bf16[256,1024]{1,0:T(8,128)(2,1)}, bf16[1024,256]{1,0:T(8,128)(2,1)}, f32[256,1024]{1,0:T(8,128)}, f32[256,1024]{1,0:T(8,128)}) custom-call(bf16[256,1024]{1,0:T(8,128)(2,1)} %bitcast.16, bf16[1024,1024]{1,0:T(8,128)(2,1)} %wq.3, bf16[256,1024]{1,0:T(8,128)(2,1)} %bitcast.17, bf16[1024,1024]{1,0:T(8,128)(2,1)} %wo.3), custom_call_target="tpu_custom_call" | custom-call | flops 1073741824 | bytes 4194304 | tf_op jit(solution)/shard_map/query/pallas_call | solution.py:346
  32.7 7.3 %all-to-all-start.1 = ((f32[32,16,128]{2,1,0:T(8,128)}), f32[32,16,128]{2,1,0:T(8,128)}, u32[]{:S(2)}, u32[]{:S(2)}) async-start(f32[32,16,128]{2,1,0:T(8,128)} %prefix.1), calls=%async_computation.1 | async-start | bytes 524288 | tf_op jit(solution)/shard_map/all_to_all | solution.py:334
  40.1 5.6 %numer.1.nl = f32[256,1024]{1,0:T(8,128)} custom-call(bf16[256,1024]{1,0:T(8,128)(2,1)} %get-tuple-element.51.fq, bf16[256,1024]{1,0:T(8,128)(2,1)} %get-tuple-element.52.fk, bf16[256,1024]{1,0:T(8,128)(2,1)} %get-tuple-element.53.fv), custom_call_target="tpu_custom_call" | custom-call | flops 1073741824 | bytes 4194304 | tf_op jit(solution)/shard_map/numer/pallas_call | solution.py:355
  45.7 3.4 %all-to-all-done.1 = f32[32,16,128]{2,1,0:T(8,128)} async-done(((f32[32,16,128]{2,1,0:T(8,128)}), f32[32,16,128]{2,1,0:T(8,128)}, u32[]{:S(2)}, u32[]{:S(2)}) %all-to-all-start.1) | async-done | bytes 262176 | tf_op jit(solution)/shard_map/all_to_all | solution.py:334
  49.1 6.1 %norm.1 = (bf16[256,1024]{1,0:T(8,128)(2,1)}, f32[256,1024]{1,0:T(8,128)}, f32[512,128]{1,0:T(8,128)}, f32[8,1024]{1,0:T(8,128)}) custom-call(s32[1]{0:T(128)S(6)} %sub.7.nv_ref, f32[256,1024]{1,0:T(8,128)} %numer.1.nl, f32[512,128]{1,0:T(8,128)} %bitcast.5.st, bf16[256,1024]{1,0:T(8,128)(2,1)} %get-tuple-element.51.fq, ...), custom_call_target="tpu_custom_call" | custom-call | flops 536870912 | bytes 4194304 | tf_op jit(solution)/shard_map/norm/pallas_call | solution.py:359
  55.2 4.4 %all-to-all-start.2 = ((f32[32,16,128]{2,1,0:T(8,128)}), f32[32,16,128]{2,1,0:T(8,128)}, u32[]{:S(2)}, u32[]{:S(2)}) async-start(f32[32,16,128]{2,1,0:T(8,128)} %bitcast.19), calls=%async_computation.2 | async-start | bytes 524288 | tf_op jit(solution)/shard_map/all_to_all | solution.py:323
  59.6 6.4 %dquery.1 = (bf16[256,1024]{1,0:T(8,128)(2,1)}, f32[264,1024]{1,0:T(8,128)}) custom-call(f32[256,1024]{1,0:T(8,128)} %get-tuple-element.70.dn, f32[512,128]{1,0:T(8,128)} %bitcast.5.st, bf16[256,1024]{1,0:T(8,128)(2,1)} %get-tuple-element.52.fk, bf16[256,1024]{1,0:T(8,128)(2,1)} %get-tuple-element.53.fv, f32[256,1024]{1,0:T(8,128)} %get-tuple-element.59.sq, ...), custom_call_target="tpu_custom_call" | custom-call | flops 1073741824 | bytes 4194304 | tf_op jit(solution)/shard_map/dquery/pallas_call | solution.py:367
  66.0 2.7 %all-to-all-done.2.v = f32[32,16,128]{2,1,0:T(8,128)} async-done(((f32[32,16,128]{2,1,0:T(8,128)}), f32[32,16,128]{2,1,0:T(8,128)}, u32[]{:S(2)}, u32[]{:S(2)}) %all-to-all-start.2) | async-done | bytes 262176 | tf_op jit(solution)/shard_map/all_to_all | solution.py:323
  70.9 4.8 %all-to-all-start.3 = ((f32[32,16,128]{2,1,0:T(8,128)}), f32[32,16,128]{2,1,0:T(8,128)}, u32[]{:S(2)}, u32[]{:S(2)}) async-start(f32[32,16,128]{2,1,0:T(8,128)} %suffix.1), calls=%async_computation.3 | async-start | bytes 524288 | tf_op jit(solution)/shard_map/all_to_all | solution.py:334
  75.8 6.1 %localk.1.lk = f32[256,1024]{1,0:T(8,128)} custom-call(f32[256,1024]{1,0:T(8,128)} %get-tuple-element.70.dn, bf16[256,1024]{1,0:T(8,128)(2,1)} %get-tuple-element.51.fq, bf16[256,1024]{1,0:T(8,128)(2,1)} %get-tuple-element.53.fv), custom_call_target="tpu_custom_call" | custom-call | flops 1073741824 | bytes 4194304 | tf_op jit(solution)/shard_map/localk/pallas_call | solution.py:378
  81.8 2.9 %all-to-all-done.3 = f32[32,16,128]{2,1,0:T(8,128)} async-done(((f32[32,16,128]{2,1,0:T(8,128)}), f32[32,16,128]{2,1,0:T(8,128)}, u32[]{:S(2)}, u32[]{:S(2)}) %all-to-all-start.3) | async-done | bytes 262176 | tf_op jit(solution)/shard_map/all_to_all | solution.py:334
  84.7 4.4 %dkey.1 = (bf16[256,1024]{1,0:T(8,128)(2,1)}, f32[256,1024]{1,0:T(8,128)}) custom-call(f32[256,1024]{1,0:T(8,128)} %localk.1.lk, bf16[256,1024]{1,0:T(8,128)(2,1)} %get-tuple-element.53.fv, f32[512,128]{1,0:T(8,128)} %bitcast.8.st, f32[256,1024]{1,0:T(8,128)} %get-tuple-element.66.sk), custom_call_target="tpu_custom_call" | custom-call | flops 268435456 | bytes 4194304 | tf_op jit(solution)/shard_map/dkey/pallas_call | solution.py:381
  89.2 4.8 %wgradq.1 = f32[16,32,1152]{2,1,0:T(8,128)} custom-call(bf16[512,256]{1,0:T(8,128)(2,1)} %get-tuple-element.47.own_t, f32[512,256]{1,0:T(8,128)} %collective-permute-done.par_t, bf16[256,1024]{1,0:T(8,128)(2,1)} %get-tuple-element.77.dq.own, f32[264,1024]{1,0:T(8,128)} %collective-permute-done.2.par, f32[8,1024]{1,0:T(8,128)} %get-tuple-element.60.gp), custom_call_target="tpu_custom_call" | custom-call | flops 1073741824 | bytes 4194304 | tf_op jit(solution)/shard_map/wgradq/pallas_call | solution.py:390
  95.3 2.6 %collective-permute-done.1.par = f32[256,1024]{1,0:T(8,128)} collective-permute-done((f32[256,1024]{1,0:T(8,128)S(1)}, f32[256,1024]{1,0:T(8,128)}, u32[]{:S(2)}, u32[]{:S(2)}) %collective-permute-start.1) | collective-permute-done | bytes 1048608 | tf_op jit(solution)/shard_map/ppermute | solution.py:386
  97.9 4.7 %wgradk.1 = f32[16,32,1024]{2,1,0:T(8,128)} custom-call(bf16[512,256]{1,0:T(8,128)(2,1)} %get-tuple-element.47.own_t, f32[512,256]{1,0:T(8,128)} %collective-permute-done.par_t, bf16[256,1024]{1,0:T(8,128)(2,1)} %get-tuple-element.74.own.dk, f32[256,1024]{1,0:T(8,128)} %collective-permute-done.1.par), custom_call_target="tpu_custom_call" | custom-call | flops 1073741824 | bytes 4194304 | tf_op jit(solution)/shard_map/wgradk/pallas_call | solution.py:400
  102.6 4.4 %all-to-all-start.4 = ((f32[16,32,1024]{2,1,0:T(8,128)}), f32[16,32,1024]{2,1,0:T(8,128)}, u32[]{:S(2)}, u32[]{:S(2)}) async-start(f32[16,32,1024]{2,1,0:T(8,128)} %wgradk.1), calls=%async_computation.4 | async-start | bytes 4194304 | tf_op jit(solution)/shard_map/all_to_all | solution.py:406
  107.1 8.3 %localv.1 = (bf16[256,1024]{1,0:T(8,128)(2,1)}, f32[256,1024]{1,0:T(8,128)}) custom-call(bf16[256,1024]{1,0:T(8,128)(2,1)} %get-tuple-element.69.at, bf16[1024,1024]{1,0:T(8,128)(2,1)} %wo.3, f32[256,1024]{1,0:T(8,128)} %get-tuple-element.70.dn, bf16[256,1024]{1,0:T(8,128)(2,1)} %get-tuple-element.51.fq, bf16[256,1024]{1,0:T(8,128)(2,1)} %get-tuple-element.52.fk), custom_call_target="tpu_custom_call" | custom-call | flops 2147483648 | bytes 4194304 | tf_op jit(solution)/shard_map/localv/pallas_call | solution.py:409
  115.4 6.6 %dtok.1 = bf16[256,1024]{1,0:T(8,128)(2,1)} custom-call(f32[256,1024]{1,0:T(8,128)} %get-tuple-element.72.lv, bf16[256,1024]{1,0:T(8,128)(2,1)} %get-tuple-element.52.fk, f32[512,128]{1,0:T(8,128)} %bitcast.8.st, bf16[256,1024]{1,0:T(8,128)(2,1)} %get-tuple-element.77.dq.own, bf16[256,1024]{1,0:T(8,128)(2,1)} %get-tuple-element.74.own.dk, ...), custom_call_target="tpu_custom_call" | custom-call | flops 2147483648 | bytes 4194304 | tf_op jit(solution)/shard_map/dtok/pallas_call | solution.py:413
  122.0 16.4 %all-to-all-done.4.k = f32[16,32,1024]{2,1,0:T(8,128)} async-done(((f32[16,32,1024]{2,1,0:T(8,128)}), f32[16,32,1024]{2,1,0:T(8,128)}, u32[]{:S(2)}, u32[]{:S(2)}) %all-to-all-start.4) | async-done | bytes 2097184 | tf_op jit(solution)/shard_map/all_to_all | solution.py:406
  138.4 52.5 %reduce-scatter.4.cloned.1.call-done = f32[1,32,1152]{2,1,0:T(8,128)} async-done(((f32[16,32,1152]{2,1,0:T(8,128)}), f32[1,32,1152]{2,1,0:T(8,128)}) %reduce-scatter.4.cloned.1.call-update) | async-done | bytes 147472
  193.4 16.6 %all_to_all.30.v = f32[8,8,1152]{2,1,0:T(8,128)} all-to-all(f32[8,8,1152]{2,1,0:T(8,128)} %join.1), channel_id=1, replica_groups=mesh['x'=4,'y'=4,'c'=2,'u'=8] {'u'}, dimensions={0} | all-to-all | bytes 589824 | tf_op jit(solution)/shard_map/all_to_all | solution.py:427
  (14 shorter events, 9.6 us)
Async XLA Ops:
  13.3 17.7 %all-to-all-start = ((f32[32,16,128]{2,1,0:T(8,128)}), f32[32,16,128]{2,1,0:T(8,128)}, u32[]{:S(2)}, u32[]{:S(2)}) async-start(f32[32,16,128]{2,1,0:T(8,128)} %bitcast.20), calls=%async_computation | async-start | bytes 524288 | tf_op jit(solution)/shard_map/all_to_all | solution.py:323
  32.7 16.4 %all-to-all-start.1 = ((f32[32,16,128]{2,1,0:T(8,128)}), f32[32,16,128]{2,1,0:T(8,128)}, u32[]{:S(2)}, u32[]{:S(2)}) async-start(f32[32,16,128]{2,1,0:T(8,128)} %prefix.1), calls=%async_computation.1 | async-start | bytes 524288 | tf_op jit(solution)/shard_map/all_to_all | solution.py:334
  55.2 13.5 %all-to-all-start.2 = ((f32[32,16,128]{2,1,0:T(8,128)}), f32[32,16,128]{2,1,0:T(8,128)}, u32[]{:S(2)}, u32[]{:S(2)}) async-start(f32[32,16,128]{2,1,0:T(8,128)} %bitcast.19), calls=%async_computation.2 | async-start | bytes 524288 | tf_op jit(solution)/shard_map/all_to_all | solution.py:323
  70.4 18.8 %collective-permute-start.2 = (f32[264,1024]{1,0:T(8,128)}, f32[264,1024]{1,0:T(8,128)}, u32[]{:S(2)}, u32[]{:S(2)}) collective-permute-start(f32[264,1024]{1,0:T(8,128)} %get-tuple-element.78), channel_id=1, source_target_pairs={{0,8},{8,0},{1,9},{9,1},{2,10},{10,2},{3,11},{11,3},{4,12},{12,4},... | collective-permute-start | bytes 3244040 | tf_op jit(solution)/shard_map/ppermute | solution.py:377
  70.6 18.6 %collective-permute-start = (f32[512,256]{1,0:T(8,128)}, f32[512,256]{1,0:T(8,128)}, u32[]{:S(2)}, u32[]{:S(2)}) collective-permute-start(f32[512,256]{1,0:T(8,128)} %get-tuple-element.48), channel_id=1, source_target_pairs={{0,8},{8,0},{1,9},{9,1},{2,10},{10,2},{3,11},{11,3},{4,12},{12,4},... | collective-permute-start | bytes 1572872 | tf_op jit(solution)/shard_map/ppermute | solution.py:345
  70.9 13.9 %all-to-all-start.3 = ((f32[32,16,128]{2,1,0:T(8,128)}), f32[32,16,128]{2,1,0:T(8,128)}, u32[]{:S(2)}, u32[]{:S(2)}) async-start(f32[32,16,128]{2,1,0:T(8,128)} %suffix.1), calls=%async_computation.3 | async-start | bytes 524288 | tf_op jit(solution)/shard_map/all_to_all | solution.py:334
  75.7 115.2 %reduce-scatter.4.cloned.1.call-start = ((), (), s32[]{:S(2)}) async-start(), calls=%async_computation.7 | async-start | bytes 2506752
  93.9 1.2 copy-start
  95.2 2.8 %collective-permute-start.1 = (f32[256,1024]{1,0:T(8,128)S(1)}, f32[256,1024]{1,0:T(8,128)}, u32[]{:S(2)}, u32[]{:S(2)}) collective-permute-start(f32[256,1024]{1,0:T(8,128)S(1)} %copy-done), channel_id=1, source_target_pairs={{0,8},{8,0},{1,9},{9,1},{2,10},{10,2},{3,11},{11,3},{4,12},{12,4},... | collective-permute-start | bytes 3145736 | tf_op jit(solution)/shard_map/ppermute | solution.py:386
  102.6 35.8 %all-to-all-start.4 = ((f32[16,32,1024]{2,1,0:T(8,128)}), f32[16,32,1024]{2,1,0:T(8,128)}, u32[]{:S(2)}, u32[]{:S(2)}) async-start(f32[16,32,1024]{2,1,0:T(8,128)} %wgradk.1), calls=%async_computation.4 | async-start | bytes 4194304 | tf_op jit(solution)/shard_map/all_to_all | solution.py:406
Sparse Core Ops, SparseCore 0:
  94.1 96.8 reduce-scatter.3

commit v3 on v2

--- a/solution.py
+++ b/solution.py
@@ -16,6 +16,7 @@
 NT = (((1,), (1,)), ((), ()))
 TN = (((0,), (0,)), ((), ()))
 SEQ = ("x", "y", "c")
+GROUP = ("c", "b")
 VMEM_LIMIT = 64 * 1024 * 1024
 
 
@@ -97,13 +98,12 @@
     st_o[...] = pack_state(dot(fk, fv, TN))
 
 
-def turn_kernel(core_ref, tok, own_o, par_o):
-    n = own_o.shape[0]
-    for which, out in ((core_ref[0], own_o), (1 - core_ref[0], par_o)):
-        r = rows((n, 1))
-        col = (r // 32) * 64 + which * 32 + r % 32
-        one_hot = (lanes((n, tok.shape[1])) == col).astype(BF)
-        out[...] = dot(one_hot, tok[...], NT).astype(out.dtype)
+def turn_kernel(tok, t16_o, t32_o):
+    n = tok.shape[0]
+    eye = (rows((n, n)) == lanes((n, n))).astype(BF)
+    res = dot(tok[...], eye, TN)
+    t16_o[...] = res.astype(BF)
+    t32_o[...] = res
 
 
 def q_kernel(tok, wq, dm, wo, fq_o, fqt_o, sq_o, do_o):
@@ -144,7 +144,7 @@
     rs_o[...] = pack_state(dot(fqt[...], d_hi) + dot(fqt[...], d_lo))
 
 
-def dq_kernel(dn, st, fk, fv, sq, gp, dq_o, send_o):
+def dq_kernel(me_ref, dn, st, fk, fv, sq, gp, dq_o, *send):
     n = dn.shape[0]
     s_hi, s_lo = split(unpack_state(st[...]))
     d_hi, d_lo = split(dn[...])
@@ -157,8 +157,11 @@
         total = total + dot(hi, km) + dot(lo, km)
     dq = (total * sq[...]).astype(BF)
     dq_o[...] = dq
-    send_o[0:n, :] = dq.astype(F32)
-    send_o[n:n + 8, :] = gp[...]
+    for k, out in enumerate(send):
+        @pl.when(pl.program_id(0) == k)
+        def _():
+            out[0:n, :] = dq.astype(F32)
+            out[n:n + 8, :] = gp[...]
 
 
 def local_k_kernel(dn, fq, fv, lk_o):
@@ -187,12 +190,15 @@
     lv_o[...] = tv
 
 
-def dk_kernel(lk, fv, st, sk, dk_o, send_o):
+def dk_kernel(me_ref, lk, fv, st, sk, dk_o, *send):
     r_hi, r_lo = split(unpack_state(st[...]))
     total = lk[...] + dot(fv[...], r_hi, NT) + dot(fv[...], r_lo, NT)
     dk = (total * sk[...]).astype(BF)
     dk_o[...] = dk
-    send_o[...] = dk.astype(F32)
+    for k, out in enumerate(send):
+        @pl.when(pl.program_id(0) == k)
+        def _():
+            out[...] = dk.astype(F32)
 
 
 def dtok_kernel(lv, fk, st, dq, dk, wq, wk, wv, dt_o, acc):
@@ -213,23 +219,25 @@
         dt_o[...] = acc[...].astype(BF)
 
 
-def wgrad_kernel(own_t, par_t, own, par, out):
-    n = own.shape[0]
-    k, m = out.shape[0], out.shape[1]
-    res = dot(own_t[...], own[...]) + dot(par_t[...].astype(BF), par[0:n, :].astype(BF))
-    out[...] = res.reshape(k, m, res.shape[1])
-
-
-def wgrad_gain_kernel(own_t, par_t, own, par, gp, out):
-    n, width = own.shape
-    k, m = out.shape[0], out.shape[1]
-    res = dot(own_t[...], own[...]) + dot(par_t[...].astype(BF), par[0:n, :].astype(BF))
-    out[:, :, 0:width] = res.reshape(k, m, width)
-    g = jnp.sum(gp[...] + par[n:n + 8, :], axis=0, keepdims=True)
-    tile = jnp.concatenate([g[:, 128 * i:128 * i + 128] for i in range(width // 128)], axis=0)
-    tile = jnp.concatenate([tile, jnp.zeros((m - width // 128, 128), F32)], axis=0)
+def wgrad_q_kernel(t0, t1, t2, t3, d0, d1, d2, d3, out, all_o):
+    n = t0.shape[1]
+    k, m = out.shape[0], out.shape[1] - 8
+    res = jnp.zeros((t0.shape[0], out.shape[2]), F32)
+    gain = jnp.zeros((8, out.shape[2]), F32)
+    for i, (t, d) in enumerate(zip((t0, t1, t2, t3), (d0, d1, d2, d3))):
+        turned = t[...].astype(BF)
+        all_o[:, n * i:n * i + n] = turned
+        res = res + dot(turned, d[0:n, :].astype(BF))
+        gain = gain + d[n:n + 8, :]
+    out[:, 0:m, :] = res.reshape(k, m, res.shape[1])
     for i in range(k):
-        out[i, :, width:width + 128] = tile
+        out[i, m:m + 8, :] = gain
+
+
+def wgrad_k_kernel(t, d0, d1, d2, d3, out):
+    k, m, w = out.shape
+    d = jnp.concatenate([v[...].astype(BF) for v in (d0, d1, d2, d3)], axis=0)
+    out[...] = dot(t[...], d).reshape(k, m, w)
 
 
 def prefix_kernel(backward, v, out):
@@ -241,29 +249,44 @@
         total = total + v[i]
 
 
+def sum_kernel(v, out):
+    total = v[0]
+    for i in range(1, v.shape[0]):
+        total = total + v[i]
+    out[...] = total
+
+
 def join_kernel(q, k, out):
     ksum = k[0]
     for i in range(1, k.shape[0]):
         ksum = ksum + k[i]
-    width = k.shape[2]
-    each = k.shape[1] // out.shape[0]
-    for u in range(out.shape[0]):
-        out[u, 0:each, 0:width] = q[each * u:each * u + each, 0:width]
-        out[u, each:2 * each, 0:width] = ksum[each * u:each * u + each]
-        out[u, :, width:width + 128] = q[0:8, width:width + 128]
+    height, width = ksum.shape
+    gain = jnp.sum(q[height:height + 8, :], axis=0, keepdims=True)
+    parts = [gain[:, 128 * i:128 * i + 128] for i in range(width // 128)]
+    each = height // out.shape[0]
+    parts.append(jnp.zeros((2 * each - len(parts), 128), F32))
+    tile = jnp.concatenate(parts, axis=0)
+    for j in range(out.shape[0]):
+        out[j, 0:each, 0:width] = q[each * j:each * j + each, :]
+        out[j, each:2 * each, 0:width] = ksum[each * j:each * j + each]
+        out[j, :, width:width + 128] = tile
 
 
 def final_kernel(v, dw_o, dg_o):
-    total = v[0]
-    for i in range(1, v.shape[0]):
-        total = total + v[i]
     width = v.shape[2] - 128
     each = v.shape[1] // 2
-    for which in range(2):
-        for i in range(each):
-            r = which * each + i
-            dw_o[which:which + 1, width * i:width * i + width] = total[r:r + 1, 0:width]
-    dg_o[...] = total[:, width:width + 128]
+    for c in range(2):
+        for b in range(2):
+            g = 2 * c + b
+            total = v[8 * c + b]
+            for w in range(1, 4):
+                total = total + v[8 * c + 2 * w + b]
+            for which in range(2):
+                for i in range(each):
+                    r = which * each + i
+                    at = 4 * width * i + width * g
+                    dw_o[which:which + 1, at:at + width] = total[r:r + 1, 0:width]
+            dg_o[2 * g:2 * g + 2, :] = total[0:2, width:width + 128]
 
 
 def call(kernel, grid, in_specs, outs, name, flops, scratch=()):
@@ -281,6 +304,22 @@
     )
 
 
+def call_at(kernel, steps, in_specs, outs, name, flops):
+    return pl.pallas_call(
+        kernel,
+        grid_spec=pltpu.PrefetchScalarGridSpec(
+            num_scalar_prefetch=1,
+            grid=(steps,),
+            in_specs=in_specs,
+            out_specs=[spec for _, _, spec in outs],
+        ),
+        out_shape=[jax.ShapeDtypeStruct(s, d) for s, d, _ in outs],
+        name=name,
+        cost_estimate=pl.CostEstimate(flops=flops, bytes_accessed=4 << 20, transcendentals=0),
+        compiler_params=pltpu.CompilerParams(vmem_limit_bytes=VMEM_LIMIT),
+    )
+
+
 SMEM = pl.BlockSpec(memory_space=pltpu.SMEM)
 
 
@@ -294,6 +333,14 @@
 
 def row(r, w):
     return pl.BlockSpec((r, w), lambda g: (g, 0))
+
+
+def col_at(r):
+    return pl.BlockSpec((r, GL), lambda k, me: (0, jnp.bitwise_xor(me[0], k)))
+
+
+def row_at(r, w):
+    return pl.BlockSpec((r, w), lambda k, me: (jnp.bitwise_xor(me[0], k), 0))
 
 
 def on_device(tokens, w_query, w_key, w_value, w_out, norm_gain, lengths, d_mixed):
@@ -303,9 +350,9 @@
     groups = d // GL
     nseq = lax.axis_size(SEQ)
     nxy = lax.axis_size(("x", "y"))
-    nu = lax.axis_size("u")
+    ngroup = lax.axis_size(GROUP)
     nv = lengths - lax.axis_index(SEQ) * n
-    core = jnp.full((1,), lax.axis_index("c"), jnp.int32)
+    me = jnp.full((1,), lax.axis_index(GROUP), jnp.int32)
     gain = norm_gain.reshape(1, d)
     act = lambda dt: ((n, d), dt, col(n))
     st_rows = d // 2
@@ -333,22 +380,24 @@
     def from_parts(mine):
         return lax.all_to_all(mine, SEQ, 0, 0, tiled=True).reshape(st_rows, 128)
 
+    def swap(v, k):
+        return lax.ppermute(v, GROUP, [(i, i ^ k) for i in range(ngroup)])
+
     parts = to_parts(st1)
     tok_1, _ = tie((tok, st1))
-    half = d // 2
-    own_t, par_send = call(
-        turn_kernel, (), [SMEM, whole((n, d))],
-        [((half, n), BF, whole((half, n))), ((half, n), F32, whole((half, n)))],
-        "turn", big,
-    )(core, tok_1)
-    swap = [(0, 1), (1, 0)]
-    par_t = lax.ppermute(par_send, "c", swap)
+    t0, t32 = call(
+        turn_kernel, (groups,), [col(n)],
+        [((d, n), BF, row(GL, n)), ((d, n), F32, row(GL, n))], "turn", big // 4,
+    )(tok_1)
     fq, fqt, sq, do = call(
         q_kernel, (groups,), [whole((n, d)), col(d), whole((n, d)), row(GL, d)],
         [act(BF), ((d, n), BF, row(GL, n)), act(F32), act(F32)], "query", 2 * big,
     )(tok_1, w_query, dm, w_out)
-    parts, fq, own_t = tie((parts, fq, own_t))
+    parts, fq, t0 = tie((parts, fq, t0))
     mine = run(parts, False, "prefix")
+    t32, _ = tie((t32, mine))
+    t1 = swap(t32, 1)
+    t2 = swap(t32, 2)
 
     st_in = from_parts(mine)
     fq_2, _ = tie((fq, mine))
@@ -364,45 +413,53 @@
 
     parts = to_parts(rs)
     dn_3, _ = tie((dn, rs))
-    dq, dq_send = call(
-        dq_kernel, (groups,),
-        [col(n), row(128, 128), col(n), col(n), col(n), col(8)],
-        [act(BF), ((n + 8, d), F32, col(n + 8))], "dquery", 2 * big,
-    )(dn_3, st_in, fk, fv, sq, gp)
-    parts, dq, dq_send = tie((parts, dq, dq_send))
+    dq, *dq_send = call_at(
+        dq_kernel, ngroup,
+        [col_at(n), row_at(128, 128), col_at(n), col_at(n), col_at(n), col_at(8)],
+        [((n, d), BF, col_at(n))] + [((n + 8, GL), F32, whole((n + 8, GL)))] * ngroup,
+        "dquery", 2 * big,
+    )(me, dn_3, st_in, fk, fv, sq, gp)
+    parts, dq = tie((parts, dq))
+    dq_got = [dq_send[0]] + [swap(dq_send[k], k) for k in range(1, ngroup)]
     mine = run(parts, True, "suffix")
 
     r_in = from_parts(mine)
-    dq_send, dn_4, _ = tie((dq_send, dn, mine))
-    dq_par = lax.ppermute(dq_send, "c", swap)
+    dn_4, t1, _ = tie((dn, t1, mine))
+    t3 = swap(t1, 2)
     (lk,) = call(
         local_k_kernel, (groups,), [col(n), col(n), col(n)], [act(F32)], "localk", 2 * big,
     )(dn_4, fq, fv)
-    dk, dk_send = call(
-        dk_kernel, (groups,), [col(n), col(n), row(128, 128), col(n)],
-        [act(BF), act(F32)], "dkey", big // 2,
-    )(lk, fv, r_in, sk)
-
-    dk_par = lax.ppermute(dk_send, "c", swap)
     steps = 4
-    gshape = (nxy, half // nxy, d + 128)
-    dq_5, _ = tie((dq, dk))
-    (gq,) = call(
-        wgrad_gain_kernel, (steps,),
-        [row(half // steps, n), row(half // steps, n), whole((n, d)), whole((n + 8, d)), whole((8, d))],
-        [(gshape, F32, pl.BlockSpec((nxy // steps,) + gshape[1:], lambda g: (g, 0, 0)))],
+    per = d // nxy
+    gshape = (nxy, per + 8, GL)
+    t0, _ = tie((t0, mine))
+    gq, tall = call(
+        wgrad_q_kernel, (steps,),
+        [row(d // steps, n)] * 4 + [whole((n + 8, GL))] * 4,
+        [
+            (gshape, F32, pl.BlockSpec((nxy // steps,) + gshape[1:], lambda g: (g, 0, 0))),
+            ((d, 4 * n), BF, row(d // steps, 4 * n)),
+        ],
         "wgradq", 2 * big,
-    )(own_t, par_t, dq_5, dq_par, gp)
-    gq_sum = lax.psum_scatter(gq, ("x", "y"), scatter_dimension=0, tiled=True)
-    gq_sum = gq_sum.reshape(gshape[1:])
-
-    kshape = (nxy, half // nxy, d)
+    )(t0, t1, t2, t3, *dq_got)
+    lk, gq = tie((lk, gq))
+
+    dk, *dk_send = call_at(
+        dk_kernel, ngroup, [col_at(n), col_at(n), row_at(128, 128), col_at(n)],
+        [((n, d), BF, col_at(n))] + [((n, GL), F32, whole((n, GL)))] * ngroup,
+        "dkey", big // 2,
+    )(me, lk, fv, r_in, sk)
+
+    dk_got = [dk_send[0]] + [swap(dk_send[k], k) for k in range(1, ngroup)]
+    gq, dk = tie((gq, dk))
+    gq = lax.all_to_all(gq, ("x", "y"), 0, 0, tiled=True)
+
+    kshape = (nxy, per, GL)
     (gk,) = call(
-        wgrad_kernel, (steps,),
-        [row(half // steps, n), row(half // steps, n), whole((n, d)), whole((n, d))],
+        wgrad_k_kernel, (steps,), [row(d // steps, 4 * n)] + [whole((n, GL))] * 4,
         [(kshape, F32, pl.BlockSpec((nxy // steps,) + kshape[1:], lambda g: (g, 0, 0)))],
         "wgradk", 2 * big,
-    )(own_t, par_t, dk, dk_par)
+    )(tall, *dk_got)
     gk_parts = lax.all_to_all(gk, ("x", "y"), 0, 0, tiled=True)
 
     dn_5, dk_5, _ = tie((dn, dk, gk))
@@ -416,15 +473,20 @@
         [((n, d), BF, whole((n, d)))], "dtok", 4 * big,
         scratch=[pltpu.VMEM((n, d), F32)],
     )(lv, fk, r_in, dq, dk_5, w_query, w_key, w_value)
-    gk_parts, mo, dt = tie((gk_parts, mo, dt))
-
-    each = half // nxy // nu
-    jshape = (nu, 2 * each, d + 128)
+    (gq_sum,) = call(
+        sum_kernel, (), [whole(gshape)], [(gshape[1:], F32, whole(gshape[1:]))], "sumq", 1 << 22
+    )(gq)
+    gk_parts, mo, dt, gq_sum = tie((gk_parts, mo, dt, gq_sum))
+
+    last = ("c", "w", "b")
+    nlast = lax.axis_size(last)
+    each = per // nlast
+    jshape = (nlast, 2 * each, GL + 128)
     (both,) = call(
         join_kernel, (), [whole(gshape[1:]), whole(kshape)], [(jshape, F32, whole(jshape))],
         "join", 1 << 22,
     )(gq_sum, gk_parts)
-    both = lax.all_to_all(both, "u", 0, 0, tiled=True)
+    both = lax.all_to_all(both, last, 0, 0, tiled=True)
     dw, dg = call(
         final_kernel, (), [whole(jshape)],
         [((2, each * d), F32, whole((2, each * d))), ((8, 128), F32, whole((8, 128)))],
@@ -434,13 +496,13 @@
 
 
 def solution(mesh):
-    fine = Mesh(mesh.devices.reshape(4, 4, 2, 8), ("x", "y", "c", "u"))
-    acts = P("u", SEQ, None)
-    placed = (acts, P(), P(), P(), P(), P(), P("u"), acts)
+    fine = Mesh(mesh.devices.reshape(4, 4, 2, 4, 2), ("x", "y", "c", "w", "b"))
+    acts = P(("w", "b"), SEQ, None)
+    placed = (acts, P(), P(), P(), P(), P(), P(("w", "b")), acts)
     return jax.shard_map(
         on_device,
         mesh=fine,
         in_specs=placed,
-        out_specs=(acts, acts, P(None, ("x", "y", "c", "u")), P()),
+        out_specs=(acts, acts, P(None, ("x", "y", "c", "w", "b")), P()),
         check_vma=False,
     )

time: 222 us -> 162 us (0.73); the launches traced: 218 us -> 161 us
  waiting for transfers between devices: 80.7 us -> 19.1 us
  starting transfers between devices: 30.4 us -> 46.1 us
  between operations: 14.7 us -> 1.42 us
  Pallas kernels: 74.9 us -> 77.7 us
    unnamed x2 -> x0, waiting for transfers between devices: 52.5 us -> none
    all_to_all x1, waiting for transfers between devices: 16.4 us -> 1.47 us  [on_device(): gk_parts = lax.all_to_all(gk, ('x', 'y'), 0, 0, tiled=True)]
    ppermute x3 -> x9, waiting for transfers between devices: 2.61 us -> 12.2 us  [swap(): return lax.ppermute(v, GROUP, [(i, i ^ k) for i in range(ngroup)])]
    ppermute x3 -> x9, starting transfers between devices: 0.7 us -> 6.89 us  [swap(): return lax.ppermute(v, GROUP, [(i, i ^ k) for i in range(ngroup)])]
    all_to_all x0 -> x1, starting transfers between devices: none -> 6.01 us  [on_device(): gq = lax.all_to_all(gq, ('x', 'y'), 0, 0, tiled=True)]
    pallas_call x5 -> x6, Pallas kernels: 23 us -> 26.4 us  [the longest x1 6.64 us: on_device(): call_at(dq_kernel, ngroup, [col_at(n), row_at(128, 128), col_at(n), col_a...]
    all_to_all x2, waiting for transfers between devices: 6.34 us -> 3.42 us  [from_parts(): return lax.all_to_all(mine, SEQ, 0, 0, tiled=True).reshape(st_rows, 128)]
    all_to_all x1, starting transfers between devices: 4.45 us -> 6.83 us  [on_device(): gk_parts = lax.all_to_all(gk, ('x', 'y'), 0, 0, tiled=True)]
  transfers between devices with their start and end apart: 9 -> 15, of which waited for: 7 -> 6; matrix products, arithmetic and copies ran while one was open for 0% -> 0% of each run, Pallas kernels for 23% -> 39%
where the time goes in v3:
time: 162 us; the launch traced here: 161 us
  Pallas kernels  77.7 us (48%)
  starting transfers between devices  46.1 us (28%)
  waiting for transfers between devices  19.1 us (12%)
  blocking collectives  16.4 us (10%)
    all_to_all x1, blocking collectives, on_device(): both = lax.all_to_all(both, last, 0, 0, tiled=True)  16.4 us
    all_to_all x2, starting transfers between devices, from_parts(): return lax.all_to_all(mine, SEQ, 0, 0, tiled=True).reshape(st_rows, 128)  13.4 us
    all_to_all x2, starting transfers between devices, to_parts(): lax.all_to_all(st.reshape(nseq, st_rows // nseq, 128), SEQ, 0, 0, tiled=T...  13 us
    ppermute x9, waiting for transfers between devices, swap(): return lax.ppermute(v, GROUP, [(i, i ^ k) for i in range(ngroup)])  12.2 us
    pallas_call x1, Pallas kernels, on_device(): call(local_v_kernel, (groups,), [whole((n, d)), col(d), col(n), col(n), c...  8.28 us
    ppermute x9, starting transfers between devices, swap(): return lax.ppermute(v, GROUP, [(i, i ^ k) for i in range(ngroup)])  6.89 us
    all_to_all x1, starting transfers between devices, on_device(): gk_parts = lax.all_to_all(gk, ('x', 'y'), 0, 0, tiled=True)  6.83 us
    pallas_call x1, Pallas kernels, on_device(): call_at(dq_kernel, ngroup, [col_at(n), row_at(128, 128), col_at(n), col_a...  6.64 us
  transfers between devices with their start and end apart: 15, of which 6 were waited for; matrix products, arithmetic and copies ran while one was open for 0% of the time, Pallas kernels for 39%

profile of v3, /device:TPU:1, one launch (start us, length us, event | category | flops | bytes accessed | tf_op | source)
XLA Modules:
  0.0 160.8 jit_solution(15346309905386144984)
XLA Ops:
  1.3 5.4 %kv.1 = (bf16[256,1024]{1,0:T(8,128)(2,1)}, bf16[256,1024]{1,0:T(8,128)(2,1)}, f32[256,1024]{1,0:T(8,128)}, f32[512,128]{1,0:T(8,128)}) custom-call(s32[1]{0:T(128)S(6)} %sub.7.nv_ref, bf16[256,1024]{1,0:T(8,128)(2,1)} %bitcast.12, bf16[1024,1024]{1,0:T(8,128)(2,1)} %wk.3, bf16[1024,1024]{1,0:T(8,128)(2,1)} %wv.3), custom_call_target="tpu_custom_call" | custom-call | flops 1073741824 | bytes 4194304 | tf_op jit(solution)/shard_map/kv/pallas_call | solution.py:362
  6.7 8.6 %all-to-all-start = ((f32[32,16,128]{2,1,0:T(8,128)}), f32[32,16,128]{2,1,0:T(8,128)}, u32[]{:S(2)}, u32[]{:S(2)}) async-start(f32[32,16,128]{2,1,0:T(8,128)} %bitcast.18), calls=%async_computation | async-start | bytes 524288 | tf_op jit(solution)/shard_map/all_to_all | solution.py:370
  15.3 3.8 %turn.1 = (bf16[1024,256]{1,0:T(8,128)(2,1)}, f32[1024,256]{1,0:T(8,128)}) custom-call(bf16[256,1024]{1,0:T(8,128)(2,1)} %bitcast.13), custom_call_target="tpu_custom_call" | custom-call | flops 134217728 | bytes 4194304 | tf_op jit(solution)/shard_map/turn/pallas_call | solution.py:388
  19.2 6.2 %query.1 = (bf16[256,1024]{1,0:T(8,128)(2,1)}, bf16[1024,256]{1,0:T(8,128)(2,1)}, f32[256,1024]{1,0:T(8,128)}, f32[256,1024]{1,0:T(8,128)}) custom-call(bf16[256,1024]{1,0:T(8,128)(2,1)} %bitcast.14, bf16[1024,1024]{1,0:T(8,128)(2,1)} %wq.3, bf16[256,1024]{1,0:T(8,128)(2,1)} %bitcast.15, bf16[1024,1024]{1,0:T(8,128)(2,1)} %wo.3), custom_call_target="tpu_custom_call" | custom-call | flops 1073741824 | bytes 4194304 | tf_op jit(solution)/shard_map/query/pallas_call | solution.py:392
  28.7 7.7 %all-to-all-start.1 = ((f32[32,16,128]{2,1,0:T(8,128)}), f32[32,16,128]{2,1,0:T(8,128)}, u32[]{:S(2)}, u32[]{:S(2)}) async-start(f32[32,16,128]{2,1,0:T(8,128)} %prefix.1), calls=%async_computation.1 | async-start | bytes 524288 | tf_op jit(solution)/shard_map/all_to_all | solution.py:381
  36.5 5.6 %numer.1.nl = f32[256,1024]{1,0:T(8,128)} custom-call(bf16[256,1024]{1,0:T(8,128)(2,1)} %get-tuple-element.63.fq, bf16[256,1024]{1,0:T(8,128)(2,1)} %get-tuple-element.64.fk, bf16[256,1024]{1,0:T(8,128)(2,1)} %get-tuple-element.65.fv), custom_call_target="tpu_custom_call" | custom-call | flops 1073741824 | bytes 4194304 | tf_op jit(solution)/shard_map/numer/pallas_call | solution.py:404
  42.1 3.4 %all-to-all-done.1 = f32[32,16,128]{2,1,0:T(8,128)} async-done(((f32[32,16,128]{2,1,0:T(8,128)}), f32[32,16,128]{2,1,0:T(8,128)}, u32[]{:S(2)}, u32[]{:S(2)}) %all-to-all-start.1) | async-done | bytes 262176 | tf_op jit(solution)/shard_map/all_to_all | solution.py:381
  45.5 6.1 %norm.1 = (bf16[256,1024]{1,0:T(8,128)(2,1)}, f32[256,1024]{1,0:T(8,128)}, f32[512,128]{1,0:T(8,128)}, f32[8,1024]{1,0:T(8,128)}) custom-call(s32[1]{0:T(128)S(6)} %sub.7.nv_ref, f32[256,1024]{1,0:T(8,128)} %numer.1.nl, f32[512,128]{1,0:T(8,128)} %bitcast.4.st, bf16[256,1024]{1,0:T(8,128)(2,1)} %get-tuple-element.63.fq, ...), custom_call_target="tpu_custom_call" | custom-call | flops 536870912 | bytes 4194304 | tf_op jit(solution)/shard_map/norm/pallas_call | solution.py:408
  51.6 4.4 %all-to-all-start.2 = ((f32[32,16,128]{2,1,0:T(8,128)}), f32[32,16,128]{2,1,0:T(8,128)}, u32[]{:S(2)}, u32[]{:S(2)}) async-start(f32[32,16,128]{2,1,0:T(8,128)} %bitcast.17), calls=%async_computation.2 | async-start | bytes 524288 | tf_op jit(solution)/shard_map/all_to_all | solution.py:370
  56.5 6.6 %dquery.1 = (bf16[256,1024]{1,0:T(8,128)(2,1)}, f32[264,256]{1,0:T(8,128)}, f32[264,256]{1,0:T(8,128)}, f32[264,256]{1,0:T(8,128)}, f32[264,256]{1,0:T(8,128)}) custom-call(s32[1]{0:T(128)} %bitcast.7.me_ref, f32[256,1024]{1,0:T(8,128)} %get-tuple-element.96.dn, f32[512,128]{1,0:T(8,128)} %bitcast.4.st, bf16[256,1024]{1,0:T(8,128)(2,1)} %get-tuple-element.64.fk, ...), custom_call_target="tpu_custom_call" | custom-call | flops 1073741824 | bytes 4194304 | tf_op jit(solution)/shard_map/dquery/pallas_call | solution.py:416
  63.1 2.0 %all-to-all-done.2.v = f32[32,16,128]{2,1,0:T(8,128)} async-done(((f32[32,16,128]{2,1,0:T(8,128)}), f32[32,16,128]{2,1,0:T(8,128)}, u32[]{:S(2)}, u32[]{:S(2)}) %all-to-all-start.2) | async-done | bytes 262176 | tf_op jit(solution)/shard_map/all_to_all | solution.py:370
  68.9 5.7 %all-to-all-start.3 = ((f32[32,16,128]{2,1,0:T(8,128)}), f32[32,16,128]{2,1,0:T(8,128)}, u32[]{:S(2)}, u32[]{:S(2)}) async-start(f32[32,16,128]{2,1,0:T(8,128)} %suffix.1), calls=%async_computation.3 | async-start | bytes 524288 | tf_op jit(solution)/shard_map/all_to_all | solution.py:381
  74.6 6.1 %localk.1.lk = f32[256,1024]{1,0:T(8,128)} custom-call(f32[256,1024]{1,0:T(8,128)} %get-tuple-element.96.dn, bf16[256,1024]{1,0:T(8,128)(2,1)} %get-tuple-element.63.fq, bf16[256,1024]{1,0:T(8,128)(2,1)} %get-tuple-element.65.fv), custom_call_target="tpu_custom_call" | custom-call | flops 1073741824 | bytes 4194304 | tf_op jit(solution)/shard_map/localk/pallas_call | solution.py:429
  81.6 5.0 %wgradq.1 = (f32[16,72,256]{2,1,0:T(8,128)}, bf16[1024,1024]{1,0:T(8,128)(2,1)}) custom-call(bf16[1024,256]{1,0:T(8,128)(2,1)} %get-tuple-element.75.t0, f32[1024,256]{1,0:T(8,128)} %collective-permute-done.t1, f32[1024,256]{1,0:T(8,128)} %collective-permute-done.1.t2, f32[1024,256]{1,0:T(8,128)} %collective-permute-done.2.t3, ...), custom_call_target="tpu_custom_call" | custom-call | flops 1073741824 | bytes 4194304 | tf_op jit(solution)/shard_map/wgradq/pallas_call | solution.py:436
  86.5 4.6 %dkey.1 = (bf16[256,1024]{1,0:T(8,128)(2,1)}, f32[256,256]{1,0:T(8,128)}, f32[256,256]{1,0:T(8,128)}, f32[256,256]{1,0:T(8,128)}, f32[256,256]{1,0:T(8,128)}) custom-call(s32[1]{0:T(128)} %bitcast.7.me_ref, f32[256,1024]{1,0:T(8,128)} %localk.1.lk, bf16[256,1024]{1,0:T(8,128)(2,1)} %get-tuple-element.65.fv, f32[512,128]{1,0:T(8,128)} %bitcast.8.st, ...), custom_call_target="tpu_custom_call" | custom-call | flops 268435456 | bytes 4194304 | tf_op jit(solution)/shard_map/dkey/pallas_call | solution.py:447
  91.1 6.0 %all-to-all-start.5 = ((f32[16,72,256]{2,1,0:T(8,128)}), f32[16,72,256]{2,1,0:T(8,128)}, u32[]{:S(2)}, u32[]{:S(2)}) async-start(f32[16,72,256]{2,1,0:T(8,128)} %get-tuple-element.101), calls=%async_computation.5 | async-start | bytes 2359296 | tf_op jit(solution)/shard_map/all_to_all | solution.py:455
  99.8 4.7 %collective-permute-done.6.d1 = f32[256,256]{1,0:T(8,128)} collective-permute-done((f32[256,256]{1,0:T(8,128)S(1)}, f32[256,256]{1,0:T(8,128)}, u32[]{:S(2)}, u32[]{:S(2)}) %collective-permute-start.6) | collective-permute-done | bytes 262176 | tf_op jit(solution)/shard_map/ppermute | solution.py:384
  104.6 6.6 %collective-permute-done.8.d3 = f32[256,256]{1,0:T(8,128)} collective-permute-done((f32[256,256]{1,0:T(8,128)S(1)}, f32[256,256]{1,0:T(8,128)}, u32[]{:S(2)}, u32[]{:S(2)}) %collective-permute-start.8) | collective-permute-done | bytes 262176 | tf_op jit(solution)/shard_map/ppermute | solution.py:384
  111.1 4.5 %wgradk.1 = f32[16,64,256]{2,1,0:T(8,128)} custom-call(bf16[1024,1024]{1,0:T(8,128)(2,1)} %get-tuple-element.83.t, f32[256,256]{1,0:T(8,128)} %get-tuple-element.88.d0, f32[256,256]{1,0:T(8,128)} %collective-permute-done.6.d1, f32[256,256]{1,0:T(8,128)} %collective-permute-done.7.d2, f32[256,256]{1,0:T(8,128)} %collective-permute-done.8.d3), custom_call_target="tpu_custom_call" | custom-call | flops 1073741824 | bytes 4194304 | tf_op jit(solution)/shard_map/wgradk/pallas_call | solution.py:458
  115.6 6.8 %all-to-all-start.4 = ((f32[16,64,256]{2,1,0:T(8,128)}), f32[16,64,256]{2,1,0:T(8,128)}, u32[]{:S(2)}, u32[]{:S(2)}) async-start(f32[16,64,256]{2,1,0:T(8,128)} %wgradk.1), calls=%async_computation.4 | async-start | bytes 2097152 | tf_op jit(solution)/shard_map/all_to_all | solution.py:463
  122.5 8.3 %localv.1 = (bf16[256,1024]{1,0:T(8,128)(2,1)}, f32[256,1024]{1,0:T(8,128)}) custom-call(bf16[256,1024]{1,0:T(8,128)(2,1)} %get-tuple-element.92.at, bf16[1024,1024]{1,0:T(8,128)(2,1)} %wo.3, f32[256,1024]{1,0:T(8,128)} %get-tuple-element.96.dn, bf16[256,1024]{1,0:T(8,128)(2,1)} %get-tuple-element.63.fq, bf16[256,1024]{1,0:T(8,128)(2,1)} %get-tuple-element.64.fk), custom_call_target="tpu_custom_call" | custom-call | flops 2147483648 | bytes 4194304 | tf_op jit(solution)/shard_map/localv/pallas_call | solution.py:466
  130.7 6.6 %dtok.1 = bf16[256,1024]{1,0:T(8,128)(2,1)} custom-call(f32[256,1024]{1,0:T(8,128)} %get-tuple-element.98.lv, bf16[256,1024]{1,0:T(8,128)(2,1)} %get-tuple-element.64.fk, f32[512,128]{1,0:T(8,128)} %bitcast.8.st, bf16[256,1024]{1,0:T(8,128)(2,1)} %get-tuple-element.99.dq, bf16[256,1024]{1,0:T(8,128)(2,1)} %get-tuple-element.100.dk, bf16[1024,1024]{1,0:T(8,128)(2,1)} %wq.3, ...), custom_call_target="tpu_custom_call" | custom-call | flops 2147483648 | bytes 4194304 | tf_op jit(solution)/shard_map/dtok/pallas_call | solution.py:470
  140.8 2.0 %join.1 = f32[16,8,384]{2,1,0:T(8,128)} custom-call(f32[72,256]{1,0:T(8,128)} %sumq.1.q, f32[16,64,256]{2,1,0:T(8,128)} %all-to-all-done.4.k), custom_call_target="tpu_custom_call" | custom-call | flops 4194304 | bytes 4194304 | tf_op jit(solution)/shard_map/join/pallas_call | solution.py:485
  142.8 16.4 %all_to_all.35.v = f32[16,8,384]{2,1,0:T(8,128)} all-to-all(f32[16,8,384]{2,1,0:T(8,128)} %join.1), channel_id=1, replica_groups=mesh['x'=4,'y'=4,'c'=2,'w'=4,'b'=2] {'c','w','b'}, dimensions={0} | all-to-all | bytes 393216 | tf_op jit(solution)/shard_map/all_to_all | solution.py:489
  (30 shorter events, 16.2 us)
Async XLA Ops:
  6.7 18.7 %all-to-all-start = ((f32[32,16,128]{2,1,0:T(8,128)}), f32[32,16,128]{2,1,0:T(8,128)}, u32[]{:S(2)}, u32[]{:S(2)}) async-start(f32[32,16,128]{2,1,0:T(8,128)} %bitcast.18), calls=%async_computation | async-start | bytes 524288 | tf_op jit(solution)/shard_map/all_to_all | solution.py:370
  27.1 39.7 %collective-permute-start = (f32[1024,256]{1,0:T(8,128)}, f32[1024,256]{1,0:T(8,128)}, u32[]{:S(2)}, u32[]{:S(2)}) collective-permute-start(f32[1024,256]{1,0:T(8,128)} %get-tuple-element.77), channel_id=1, source_target_pairs={{0,1},{1,0},{8,9},{9,8},{2,3},{3,2},{10,11},{11,10},{4,5},{5,4},{1... | collective-permute-start | bytes 3145736 | tf_op jit(solution)/shard_map/ppermute | solution.py:384
  28.7 16.8 %all-to-all-start.1 = ((f32[32,16,128]{2,1,0:T(8,128)}), f32[32,16,128]{2,1,0:T(8,128)}, u32[]{:S(2)}, u32[]{:S(2)}) async-start(f32[32,16,128]{2,1,0:T(8,128)} %prefix.1), calls=%async_computation.1 | async-start | bytes 524288 | tf_op jit(solution)/shard_map/all_to_all | solution.py:381
  51.6 13.5 %all-to-all-start.2 = ((f32[32,16,128]{2,1,0:T(8,128)}), f32[32,16,128]{2,1,0:T(8,128)}, u32[]{:S(2)}, u32[]{:S(2)}) async-start(f32[32,16,128]{2,1,0:T(8,128)} %bitcast.17), calls=%async_computation.2 | async-start | bytes 524288 | tf_op jit(solution)/shard_map/all_to_all | solution.py:370
  56.0 25.6 %collective-permute-start.1 = (f32[1024,256]{1,0:T(8,128)}, f32[1024,256]{1,0:T(8,128)}, u32[]{:S(2)}, u32[]{:S(2)}) collective-permute-start(f32[1024,256]{1,0:T(8,128)} %get-tuple-element.77), channel_id=1, source_target_pairs={{0,8},{1,9},{8,0},{9,1},{2,10},{3,11},{10,2},{11,3},{4,12},{5,13},... | collective-permute-start | bytes 3145736 | tf_op jit(solution)/shard_map/ppermute | solution.py:384
  66.8 14.8 %collective-permute-start.2 = (f32[1024,256]{1,0:T(8,128)}, f32[1024,256]{1,0:T(8,128)}, u32[]{:S(2)}, u32[]{:S(2)}) collective-permute-start(f32[1024,256]{1,0:T(8,128)} %collective-permute-done.t1), channel_id=1, source_target_pairs={{0,8},{1,9},{8,0},{9,1},{2,10},{3,11},{10,2},{11,3},{4,12},{5,13},... | collective-permute-start | bytes 3145736 | tf_op jit(solution)/shard_map/ppermute | solution.py:384
  67.0 13.7 %collective-permute-start.3 = (f32[264,256]{1,0:T(8,128)}, f32[264,256]{1,0:T(8,128)}, u32[]{:S(2)}, u32[]{:S(2)}) collective-permute-start(f32[264,256]{1,0:T(8,128)} %get-tuple-element.80), channel_id=1, source_target_pairs={{0,1},{1,0},{8,9},{9,8},{2,3},{3,2},{10,11},{11,10},{4,5},{5,4},{1... | collective-permute-start | bytes 811016 | tf_op jit(solution)/shard_map/ppermute | solution.py:384
  67.0 13.7 %collective-permute-start.4 = (f32[264,256]{1,0:T(8,128)}, f32[264,256]{1,0:T(8,128)}, u32[]{:S(2)}, u32[]{:S(2)}) collective-permute-start(f32[264,256]{1,0:T(8,128)} %get-tuple-element.81), channel_id=1, source_target_pairs={{0,8},{1,9},{8,0},{9,1},{2,10},{3,11},{10,2},{11,3},{4,12},{5,13},... | collective-permute-start | bytes 811016 | tf_op jit(solution)/shard_map/ppermute | solution.py:384
  67.4 14.2 %collective-permute-start.5 = (f32[264,256]{1,0:T(8,128)}, f32[264,256]{1,0:T(8,128)}, u32[]{:S(2)}, u32[]{:S(2)}) collective-permute-start(f32[264,256]{1,0:T(8,128)} %get-tuple-element.82), channel_id=1, source_target_pairs={{0,9},{1,8},{8,1},{9,0},{2,11},{3,10},{10,3},{11,2},{4,13},{5,12},... | collective-permute-start | bytes 811016 | tf_op jit(solution)/shard_map/ppermute | solution.py:384
  68.9 17.6 %all-to-all-start.3 = ((f32[32,16,128]{2,1,0:T(8,128)}), f32[32,16,128]{2,1,0:T(8,128)}, u32[]{:S(2)}, u32[]{:S(2)}) async-start(f32[32,16,128]{2,1,0:T(8,128)} %suffix.1), calls=%async_computation.3 | async-start | bytes 524288 | tf_op jit(solution)/shard_map/all_to_all | solution.py:381
  91.1 6.1 %copy-start.2 = (f32[256,256]{1,0:T(8,128)S(1)}, f32[256,256]{1,0:T(8,128)}, u32[]{:S(2)}) copy-start(f32[256,256]{1,0:T(8,128)} %get-tuple-element.89) | copy-start | bytes 786436
  91.1 6.2 %copy-start.1 = (f32[256,256]{1,0:T(8,128)S(1)}, f32[256,256]{1,0:T(8,128)}, u32[]{:S(2)}) copy-start(f32[256,256]{1,0:T(8,128)} %get-tuple-element.90) | copy-start | bytes 786436
  91.1 6.9 %copy-start = (f32[256,256]{1,0:T(8,128)S(1)}, f32[256,256]{1,0:T(8,128)}, u32[]{:S(2)}) copy-start(f32[256,256]{1,0:T(8,128)} %get-tuple-element.91) | copy-start | bytes 786436
  91.1 24.5 %all-to-all-start.5 = ((f32[16,72,256]{2,1,0:T(8,128)}), f32[16,72,256]{2,1,0:T(8,128)}, u32[]{:S(2)}, u32[]{:S(2)}) async-start(f32[16,72,256]{2,1,0:T(8,128)} %get-tuple-element.101), calls=%async_computation.5 | async-start | bytes 2359296 | tf_op jit(solution)/shard_map/all_to_all | solution.py:455
  97.2 7.4 %collective-permute-start.6 = (f32[256,256]{1,0:T(8,128)S(1)}, f32[256,256]{1,0:T(8,128)}, u32[]{:S(2)}, u32[]{:S(2)}) collective-permute-start(f32[256,256]{1,0:T(8,128)S(1)} %copy-done.2), channel_id=1, source_target_pairs={{0,1},{1,0},{8,9},{9,8},{2,3},{3,2},{10,11},{11,10},{4,5},{5,4},{1... | collective-permute-start | bytes 786440 | tf_op jit(solution)/shard_map/ppermute | solution.py:384
  97.3 7.3 %collective-permute-start.7 = (f32[256,256]{1,0:T(8,128)S(1)}, f32[256,256]{1,0:T(8,128)}, u32[]{:S(2)}, u32[]{:S(2)}) collective-permute-start(f32[256,256]{1,0:T(8,128)S(1)} %copy-done.1), channel_id=1, source_target_pairs={{0,8},{1,9},{8,0},{9,1},{2,10},{3,11},{10,2},{11,3},{4,12},{5,13},... | collective-permute-start | bytes 786440 | tf_op jit(solution)/shard_map/ppermute | solution.py:384
  98.0 13.1 %collective-permute-start.8 = (f32[256,256]{1,0:T(8,128)S(1)}, f32[256,256]{1,0:T(8,128)}, u32[]{:S(2)}, u32[]{:S(2)}) collective-permute-start(f32[256,256]{1,0:T(8,128)S(1)} %copy-done), channel_id=1, source_target_pairs={{0,9},{1,8},{8,1},{9,0},{2,11},{3,10},{10,3},{11,2},{4,13},{5,12},... | collective-permute-start | bytes 786440 | tf_op jit(solution)/shard_map/ppermute | solution.py:384
  115.6 25.1 %all-to-all-start.4 = ((f32[16,64,256]{2,1,0:T(8,128)}), f32[16,64,256]{2,1,0:T(8,128)}, u32[]{:S(2)}, u32[]{:S(2)}) async-start(f32[16,64,256]{2,1,0:T(8,128)} %wgradk.1), calls=%async_computation.4 | async-start | bytes 2097152 | tf_op jit(solution)/shard_map/all_to_all | solution.py:463

commit v4 on v3

--- a/solution.py
+++ b/solution.py
@@ -80,10 +80,20 @@
     return jnp.where(up, raw + 1.0, ex), jnp.where(up, 1.0, ex)
 
 
-def head_mean(v):
+def head_mean(*parts):
     same = (rows((GL, GL)) // HD == lanes((GL, GL)) // HD).astype(BF)
-    hi, lo = split(v)
-    return (dot(hi, same) + dot(lo, same)) * (1.0 / HD)
+    total = dot(parts[0], same)
+    for p in parts[1:]:
+        total = total + dot(p, same)
+    return total * (1.0 / HD)
+
+
+def groups_of(ref):
+    return [(j, slice(GL * j, GL * j + GL)) for j in range(ref.shape[-1] // GL)]
+
+
+def group_at(j, ref):
+    return pl.program_id(0) * (ref.shape[-1] // GL) + j
 
 
 def kv_kernel(nv_ref, tok, wk, wv, fk_o, fv_o, sk_o, st_o):
@@ -95,7 +105,8 @@
     fk_o[...] = fk
     fv_o[...] = fv
     sk_o[...] = slope * valid
-    st_o[...] = pack_state(dot(fk, fv, TN))
+    for j, c in groups_of(fk):
+        st_o[128 * j:128 * j + 128, :] = pack_state(dot(fk[:, c], fv[:, c], TN))
 
 
 def turn_kernel(tok, t16_o, t32_o):
@@ -106,105 +117,110 @@
     t32_o[...] = res
 
 
-def q_kernel(tok, wq, dm, wo, fq_o, fqt_o, sq_o, do_o):
+def q_kernel(tok, wq, fq_o, fqt_o, sq_o):
     feat, slope = features(dot(tok[...], wq[...]))
     fq = feat.astype(BF)
     fq_o[...] = fq
     sq_o[...] = slope
     eye = (rows((GL, GL)) == lanes((GL, GL))).astype(BF)
-    fqt_o[...] = dot(eye, fq, NT).astype(BF)
+    for _, c in groups_of(fq):
+        fqt_o[c, :] = dot(eye, fq[:, c], NT).astype(BF)
+
+
+def numer_kernel(fq, fk, fv, dm, wo, nl_o, do_o):
+    n = fq.shape[0]
     do_o[...] = dot(dm[...], wo[...], NT)
-
-
-def numer_kernel(fq, fk, fv, nl_o):
-    n = fq.shape[0]
     causal = rows((n, n)) >= lanes((n, n))
-    total = jnp.zeros((n, GL), F32)
-    for m in head_masks((n, GL)):
-        hi, lo = split(pick(causal, dot(pick(m, fq[...]), fk[...], NT)))
-        vm = pick(m, fv[...])
-        total = total + dot(hi, vm) + dot(lo, vm)
-    nl_o[...] = total
+    for _, c in groups_of(fq):
+        total = jnp.zeros((n, GL), F32)
+        for m in head_masks((n, GL)):
+            s = pick(causal, dot(pick(m, fq[:, c]), fk[:, c], NT)).astype(BF)
+            total = total + dot(s, pick(m, fv[:, c]))
+        nl_o[:, c] = total
 
 
 def norm_kernel(nv_ref, nl, st, fq, fqt, do, gain, at_o, dn_o, rs_o, gp_o):
     n = nl.shape[0]
     valid = valid_rows(nv_ref, n)
-    s_hi, s_lo = split(unpack_state(st[...]))
-    numer = nl[...] + dot(fq[...], s_hi) + dot(fq[...], s_lo)
-    inv = lax.rsqrt(head_mean(numer * numer) + EPS)
-    normed = numer * inv
-    at_o[...] = (normed * gain[...] * valid).astype(BF)
-    dov = do[...] * valid
-    gp_o[...] = jnp.sum((dov * normed).reshape(n // 8, 8, GL), axis=0)
-    g = dov * gain[...]
-    dn = inv * (g - normed * head_mean(g * normed))
-    dn_o[...] = dn
-    d_hi, d_lo = split(dn)
-    rs_o[...] = pack_state(dot(fqt[...], d_hi) + dot(fqt[...], d_lo))
+    for j, c in groups_of(nl):
+        r = slice(128 * j, 128 * j + 128)
+        numer = nl[:, c] + dot(fq[:, c], unpack_state(st[r, :].astype(BF)))
+        inv = lax.rsqrt(head_mean((numer * numer).astype(BF)) + EPS)
+        normed = numer * inv
+        scale = gain[:, c]
+        at_o[:, c] = (normed * scale * valid).astype(BF)
+        dov = do[:, c] * valid
+        gp_o[:, c] = jnp.sum((dov * normed).reshape(n // 8, 8, GL), axis=0)
+        g = dov * scale
+        dn = inv * (g - normed * head_mean(*split(g * normed)))
+        dn_o[:, c] = dn
+        rs_o[r, :] = pack_state(dot(fqt[c, :], dn.astype(BF)))
 
 
 def dq_kernel(me_ref, dn, st, fk, fv, sq, gp, dq_o, *send):
     n = dn.shape[0]
-    s_hi, s_lo = split(unpack_state(st[...]))
-    d_hi, d_lo = split(dn[...])
-    total = dot(d_hi, s_hi, NT) + dot(d_lo, s_hi, NT) + dot(d_hi, s_lo, NT)
     causal = rows((n, n)) >= lanes((n, n))
-    for m in head_masks((n, GL)):
-        vm = pick(m, fv[...])
-        hi, lo = split(pick(causal, dot(d_hi, vm, NT) + dot(d_lo, vm, NT)))
-        km = pick(m, fk[...])
-        total = total + dot(hi, km) + dot(lo, km)
-    dq = (total * sq[...]).astype(BF)
-    dq_o[...] = dq
-    for k, out in enumerate(send):
-        @pl.when(pl.program_id(0) == k)
-        def _():
-            out[0:n, :] = dq.astype(F32)
-            out[n:n + 8, :] = gp[...]
+    for j, c in groups_of(dn):
+        s_hi, s_lo = split(unpack_state(st[128 * j:128 * j + 128, :]))
+        d_hi, d_lo = split(dn[:, c])
+        total = dot(d_hi, s_hi, NT) + dot(d_lo, s_hi, NT) + dot(d_hi, s_lo, NT)
+        for m in head_masks((n, GL)):
+            vm = pick(m, fv[:, c])
+            w = pick(causal, dot(d_hi, vm, NT) + dot(d_lo, vm, NT)).astype(BF)
+            total = total + dot(w, pick(m, fk[:, c]))
+        dq = (total * sq[:, c]).astype(BF)
+        dq_o[:, c] = dq
+        for k, out in enumerate(send):
+            @pl.when(group_at(j, dn) == jnp.bitwise_xor(me_ref[0], k))
+            def _():
+                out[0:n, :] = dq.astype(F32)
+                out[n:n + 8, :] = gp[:, c]
 
 
 def local_k_kernel(dn, fq, fv, lk_o):
     n = dn.shape[0]
-    d_hi, d_lo = split(dn[...])
     later = lanes((n, n)) >= rows((n, n))
-    tk = jnp.zeros((n, GL), F32)
-    for m in head_masks((n, GL)):
-        vm = pick(m, fv[...])
-        hi, lo = split(pick(later, dot(vm, d_hi, NT) + dot(vm, d_lo, NT)))
-        qm = pick(m, fq[...])
-        tk = tk + dot(hi, qm) + dot(lo, qm)
-    lk_o[...] = tk
+    for _, c in groups_of(dn):
+        d_hi, d_lo = split(dn[:, c])
+        total = jnp.zeros((n, GL), F32)
+        for m in head_masks((n, GL)):
+            vm = pick(m, fv[:, c])
+            w = pick(later, dot(vm, d_hi, NT) + dot(vm, d_lo, NT)).astype(BF)
+            total = total + dot(w, pick(m, fq[:, c]))
+        lk_o[:, c] = total
 
 
 def local_v_kernel(at, wo, dn, fq, fk, mo_o, lv_o):
     n = dn.shape[0]
     mo_o[...] = dot(at[...], wo[...]).astype(BF)
-    d_hi, d_lo = split(dn[...])
     later = lanes((n, n)) >= rows((n, n))
-    tv = jnp.zeros((n, GL), F32)
-    for m in head_masks((n, GL)):
-        hi, lo = split(pick(later, dot(pick(m, fk[...]), fq[...], NT)))
-        dm = pick(m, d_hi)
-        tv = tv + dot(hi, dm) + dot(lo, dm) + dot(hi, pick(m, d_lo))
-    lv_o[...] = tv
+    for _, c in groups_of(dn):
+        d_hi = dn[:, c].astype(BF)
+        total = jnp.zeros((n, GL), F32)
+        for m in head_masks((n, GL)):
+            s = pick(later, dot(pick(m, fk[:, c]), fq[:, c], NT)).astype(BF)
+            total = total + dot(s, pick(m, d_hi))
+        lv_o[:, c] = total
 
 
 def dk_kernel(me_ref, lk, fv, st, sk, dk_o, *send):
-    r_hi, r_lo = split(unpack_state(st[...]))
-    total = lk[...] + dot(fv[...], r_hi, NT) + dot(fv[...], r_lo, NT)
-    dk = (total * sk[...]).astype(BF)
-    dk_o[...] = dk
-    for k, out in enumerate(send):
-        @pl.when(pl.program_id(0) == k)
-        def _():
-            out[...] = dk.astype(F32)
+    for j, c in groups_of(lk):
+        state = unpack_state(st[128 * j:128 * j + 128, :].astype(BF))
+        dk = ((lk[:, c] + dot(fv[:, c], state, NT)) * sk[:, c]).astype(BF)
+        dk_o[:, c] = dk
+        for k, out in enumerate(send):
+            @pl.when(group_at(j, lk) == jnp.bitwise_xor(me_ref[0], k))
+            def _():
+                out[...] = dk.astype(F32)
 
 
 def dtok_kernel(lv, fk, st, dq, dk, wq, wk, wv, dt_o, acc):
-    r_hi, r_lo = split(unpack_state(st[...]))
-    dv = (lv[...] + dot(fk[...], r_hi) + dot(fk[...], r_lo)).astype(BF)
-    term = dot(dq[...], wq[...], NT) + dot(dk[...], wk[...], NT) + dot(dv, wv[...], NT)
+    term = dot(dq[...], wq[...], NT) + dot(dk[...], wk[...], NT)
+    dv = []
+    for j, c in groups_of(lv):
+        state = unpack_state(st[128 * j:128 * j + 128, :].astype(BF))
+        dv.append((lv[:, c] + dot(fk[:, c], state)).astype(BF))
+    term = term + dot(jnp.concatenate(dv, axis=1), wv[...], NT)
 
     @pl.when(pl.program_id(0) == 0)
     def _():
@@ -304,22 +320,6 @@
     )
 
 
-def call_at(kernel, steps, in_specs, outs, name, flops):
-    return pl.pallas_call(
-        kernel,
-        grid_spec=pltpu.PrefetchScalarGridSpec(
-            num_scalar_prefetch=1,
-            grid=(steps,),
-            in_specs=in_specs,
-            out_specs=[spec for _, _, spec in outs],
-        ),
-        out_shape=[jax.ShapeDtypeStruct(s, d) for s, d, _ in outs],
-        name=name,
-        cost_estimate=pl.CostEstimate(flops=flops, bytes_accessed=4 << 20, transcendentals=0),
-        compiler_params=pltpu.CompilerParams(vmem_limit_bytes=VMEM_LIMIT),
-    )
-
-
 SMEM = pl.BlockSpec(memory_space=pltpu.SMEM)
 
 
@@ -333,34 +333,28 @@
 
 def row(r, w):
     return pl.BlockSpec((r, w), lambda g: (g, 0))
-
-
-def col_at(r):
-    return pl.BlockSpec((r, GL), lambda k, me: (0, jnp.bitwise_xor(me[0], k)))
-
-
-def row_at(r, w):
-    return pl.BlockSpec((r, w), lambda k, me: (jnp.bitwise_xor(me[0], k), 0))
 
 
 def on_device(tokens, w_query, w_key, w_value, w_out, norm_gain, lengths, d_mixed):
     _, n, d = tokens.shape
     tok = tokens.reshape(n, d)
     dm = d_mixed.reshape(n, d)
-    groups = d // GL
+    w = 2 * GL
+    halves = d // w
     nseq = lax.axis_size(SEQ)
     nxy = lax.axis_size(("x", "y"))
     ngroup = lax.axis_size(GROUP)
     nv = lengths - lax.axis_index(SEQ) * n
     me = jnp.full((1,), lax.axis_index(GROUP), jnp.int32)
     gain = norm_gain.reshape(1, d)
-    act = lambda dt: ((n, d), dt, col(n))
+    act = lambda dt: ((n, d), dt, col(n, w))
     st_rows = d // 2
-    state = ((st_rows, 128), F32, row(128, 128))
+    st_spec = row(w // 2, 128)
+    state = ((st_rows, 128), F32, st_spec)
     big = 2 * n * d * d
 
     fk, fv, sk, st1 = call(
-        kv_kernel, (groups,), [SMEM, whole((n, d)), col(d), col(d)],
+        kv_kernel, (halves,), [SMEM, whole((n, d)), col(d, w), col(d, w)],
         [act(BF), act(BF), act(F32), state], "kv", 2 * big,
     )(nv, tok, w_key, w_value)
 
@@ -386,13 +380,13 @@
     parts = to_parts(st1)
     tok_1, _ = tie((tok, st1))
     t0, t32 = call(
-        turn_kernel, (groups,), [col(n)],
-        [((d, n), BF, row(GL, n)), ((d, n), F32, row(GL, n))], "turn", big // 4,
+        turn_kernel, (halves,), [col(n, w)],
+        [((d, n), BF, row(w, n)), ((d, n), F32, row(w, n))], "turn", big // 4,
     )(tok_1)
-    fq, fqt, sq, do = call(
-        q_kernel, (groups,), [whole((n, d)), col(d), whole((n, d)), row(GL, d)],
-        [act(BF), ((d, n), BF, row(GL, n)), act(F32), act(F32)], "query", 2 * big,
-    )(tok_1, w_query, dm, w_out)
+    fq, fqt, sq = call(
+        q_kernel, (halves,), [whole((n, d)), col(d, w)],
+        [act(BF), ((d, n), BF, row(w, n)), act(F32)], "query", big,
+    )(tok_1, w_query)
     parts, fq, t0 = tie((parts, fq, t0))
     mine = run(parts, False, "prefix")
     t32, _ = tie((t32, mine))
@@ -401,22 +395,24 @@
 
     st_in = from_parts(mine)
     fq_2, _ = tie((fq, mine))
-    (nl,) = call(
-        numer_kernel, (groups,), [col(n), col(n), col(n)], [act(F32)], "numer", 2 * big,
-    )(fq_2, fk, fv)
+    nl, do = call(
+        numer_kernel, (halves,),
+        [col(n, w), col(n, w), col(n, w), whole((n, d)), row(w, d)],
+        [act(F32), act(F32)], "numer", 2 * big,
+    )(fq_2, fk, fv, dm, w_out)
 
     at, dn, rs, gp = call(
-        norm_kernel, (groups,),
-        [SMEM, col(n), row(128, 128), col(n), row(GL, n), col(n), col(1)],
-        [act(BF), act(F32), state, ((8, d), F32, col(8))], "norm", big,
+        norm_kernel, (halves,),
+        [SMEM, col(n, w), st_spec, col(n, w), row(w, n), col(n, w), col(1, w)],
+        [act(BF), act(F32), state, ((8, d), F32, col(8, w))], "norm", big,
     )(nv, nl, st_in, fq, fqt, do, gain)
 
     parts = to_parts(rs)
     dn_3, _ = tie((dn, rs))
-    dq, *dq_send = call_at(
-        dq_kernel, ngroup,
-        [col_at(n), row_at(128, 128), col_at(n), col_at(n), col_at(n), col_at(8)],
-        [((n, d), BF, col_at(n))] + [((n + 8, GL), F32, whole((n + 8, GL)))] * ngroup,
+    dq, *dq_send = call(
+        dq_kernel, (halves,),
+        [SMEM, col(n, w), st_spec, col(n, w), col(n, w), col(n, w), col(8, w)],
+        [act(BF)] + [((n + 8, GL), F32, whole((n + 8, GL)))] * ngroup,
         "dquery", 2 * big,
     )(me, dn_3, st_in, fk, fv, sq, gp)
     parts, dq = tie((parts, dq))
@@ -427,9 +423,9 @@
     dn_4, t1, _ = tie((dn, t1, mine))
     t3 = swap(t1, 2)
     (lk,) = call(
-        local_k_kernel, (groups,), [col(n), col(n), col(n)], [act(F32)], "localk", 2 * big,
+        local_k_kernel, (halves,), [col(n, w), col(n, w), col(n, w)], [act(F32)], "localk", 2 * big,
     )(dn_4, fq, fv)
-    steps = 4
+    steps = 2
     per = d // nxy
     gshape = (nxy, per + 8, GL)
     t0, _ = tie((t0, mine))
@@ -444,9 +440,9 @@
     )(t0, t1, t2, t3, *dq_got)
     lk, gq = tie((lk, gq))
 
-    dk, *dk_send = call_at(
-        dk_kernel, ngroup, [col_at(n), col_at(n), row_at(128, 128), col_at(n)],
-        [((n, d), BF, col_at(n))] + [((n, GL), F32, whole((n, GL)))] * ngroup,
+    dk, *dk_send = call(
+        dk_kernel, (halves,), [SMEM, col(n, w), col(n, w), st_spec, col(n, w)],
+        [act(BF)] + [((n, GL), F32, whole((n, GL)))] * ngroup,
         "dkey", big // 2,
     )(me, lk, fv, r_in, sk)
 
@@ -464,12 +460,12 @@
 
     dn_5, dk_5, _ = tie((dn, dk, gk))
     mo, lv = call(
-        local_v_kernel, (groups,),
-        [whole((n, d)), col(d), col(n), col(n), col(n)], [act(BF), act(F32)], "localv", 4 * big,
+        local_v_kernel, (halves,),
+        [whole((n, d)), col(d, w), col(n, w), col(n, w), col(n, w)], [act(BF), act(F32)], "localv", 4 * big,
     )(at, w_out, dn_5, fq, fk)
     (dt,) = call(
-        dtok_kernel, (groups,),
-        [col(n), col(n), row(128, 128), col(n), col(n), col(d), col(d), col(d)],
+        dtok_kernel, (halves,),
+        [col(n, w), col(n, w), st_spec, col(n, w), col(n, w), col(d, w), col(d, w), col(d, w)],
         [((n, d), BF, whole((n, d)))], "dtok", 4 * big,
         scratch=[pltpu.VMEM((n, d), F32)],
     )(lv, fk, r_in, dq, dk_5, w_query, w_key, w_value)

time: 162 us -> 152 us (0.938)
  Pallas kernels: 77.7 us -> 62.4 us
  waiting for transfers between devices: 19.1 us -> 28.3 us
  starting transfers between devices: 46.1 us -> 39 us
  blocking collectives: 16.4 us -> 19.5 us
    pallas_call x10, Pallas kernels: 59.3 us -> 46.4 us  [the longest x1 6.46 us: on_device(): call(dq_kernel, (halves,), [SMEM, col(n, w), st_spec, col(n, w), col(n, w...]
    all_to_all x2, waiting for transfers between devices: 1.99 us -> 5.05 us  [to_parts(): lax.all_to_all(st.reshape(nseq, st_rows // nseq, 128), SEQ, 0, 0, tiled=T...]
    all_to_all x2, starting transfers between devices: 13.4 us -> 10.3 us  [from_parts(): return lax.all_to_all(mine, SEQ, 0, 0, tiled=True).reshape(st_rows, 128)]
    all_to_all x1, blocking collectives: 16.4 us -> 19.5 us  [on_device(): both = lax.all_to_all(both, last, 0, 0, tiled=True)]
    ppermute x9, waiting for transfers between devices: 12.2 us -> 14.9 us  [swap(): return lax.ppermute(v, GROUP, [(i, i ^ k) for i in range(ngroup)])]
    all_to_all x1, starting transfers between devices: 6.83 us -> 4.71 us  [on_device(): gk_parts = lax.all_to_all(gk, ('x', 'y'), 0, 0, tiled=True)]
    all_to_all x1, waiting for transfers between devices: 0.01 us -> 1.96 us  [on_device(): gq = lax.all_to_all(gq, ('x', 'y'), 0, 0, tiled=True)]
  transfers between devices with their start and end apart: 15 -> 15, of which waited for: 6 -> 8; matrix products, arithmetic and copies ran while one was open for 0% -> 0% of each run, Pallas kernels for 39% -> 32%
where the time goes in v4:
time: 152 us; the launch traced here: 151 us
  Pallas kernels  62.4 us (41%)
  starting transfers between devices  39 us (26%)
  waiting for transfers between devices  28.3 us (19%)
  blocking collectives  19.5 us (13%)
    all_to_all x1, blocking collectives, on_device(): both = lax.all_to_all(both, last, 0, 0, tiled=True)  19.5 us
    ppermute x9, waiting for transfers between devices, swap(): return lax.ppermute(v, GROUP, [(i, i ^ k) for i in range(ngroup)])  14.9 us
    all_to_all x2, starting transfers between devices, to_parts(): lax.all_to_all(st.reshape(nseq, st_rows // nseq, 128), SEQ, 0, 0, tiled=T...  13 us
    all_to_all x2, starting transfers between devices, from_parts(): return lax.all_to_all(mine, SEQ, 0, 0, tiled=True).reshape(st_rows, 128)  10.3 us
    pallas_call x1, Pallas kernels, on_device(): call(dq_kernel, (halves,), [SMEM, col(n, w), st_spec, col(n, w), col(n, w...  6.46 us
    ppermute x9, starting transfers between devices, swap(): return lax.ppermute(v, GROUP, [(i, i ^ k) for i in range(ngroup)])  6.21 us
    pallas_call x1, Pallas kernels, on_device(): call(dtok_kernel, (halves,), [col(n, w), col(n, w), st_spec, col(n, w), c...  5.77 us
    pallas_call x1, Pallas kernels, on_device(): call(local_v_kernel, (halves,), [whole((n, d)), col(d, w), col(n, w), col...  5.09 us
  transfers between devices with their start and end apart: 15, of which 8 were waited for; matrix products, arithmetic and copies ran while one was open for 0% of the time, Pallas kernels for 32%

profile of v4, /device:TPU:1, one launch (start us, length us, event | category | flops | bytes accessed | tf_op | source)
XLA Modules:
  0.0 150.6 jit_solution(14614279968233380104)
XLA Ops:
  1.3 4.8 %kv.1 = (bf16[256,1024]{1,0:T(8,128)(2,1)}, bf16[256,1024]{1,0:T(8,128)(2,1)}, f32[256,1024]{1,0:T(8,128)}, f32[512,128]{1,0:T(8,128)}) custom-call(s32[1]{0:T(128)S(6)} %sub.7.nv_ref, bf16[256,1024]{1,0:T(8,128)(2,1)} %bitcast.12, bf16[1024,1024]{1,0:T(8,128)(2,1)} %wk.3, bf16[1024,1024]{1,0:T(8,128)(2,1)} %wv.3), custom_call_target="tpu_custom_call" | custom-call | flops 1073741824 | bytes 4194304 | tf_op jit(solution)/shard_map/kv/pallas_call | solution.py:356
  6.0 8.6 %all-to-all-start = ((f32[32,16,128]{2,1,0:T(8,128)}), f32[32,16,128]{2,1,0:T(8,128)}, u32[]{:S(2)}, u32[]{:S(2)}) async-start(f32[32,16,128]{2,1,0:T(8,128)} %bitcast.18), calls=%async_computation | async-start | bytes 524288 | tf_op jit(solution)/shard_map/all_to_all | solution.py:364
  17.1 3.7 %query.1 = (bf16[256,1024]{1,0:T(8,128)(2,1)}, bf16[1024,256]{1,0:T(8,128)(2,1)}, f32[256,1024]{1,0:T(8,128)}) custom-call(bf16[256,1024]{1,0:T(8,128)(2,1)} %bitcast.14, bf16[1024,1024]{1,0:T(8,128)(2,1)} %wq.3), custom_call_target="tpu_custom_call" | custom-call | flops 536870912 | bytes 4194304 | tf_op jit(solution)/shard_map/query/pallas_call | solution.py:386
  20.8 2.9 %all-to-all-done.v = f32[32,16,128]{2,1,0:T(8,128)} async-done(((f32[32,16,128]{2,1,0:T(8,128)}), f32[32,16,128]{2,1,0:T(8,128)}, u32[]{:S(2)}, u32[]{:S(2)}) %all-to-all-start) | async-done | bytes 262176 | tf_op jit(solution)/shard_map/all_to_all | solution.py:364
  27.1 4.8 %all-to-all-start.1 = ((f32[32,16,128]{2,1,0:T(8,128)}), f32[32,16,128]{2,1,0:T(8,128)}, u32[]{:S(2)}, u32[]{:S(2)}) async-start(f32[32,16,128]{2,1,0:T(8,128)} %prefix.1), calls=%async_computation.1 | async-start | bytes 524288 | tf_op jit(solution)/shard_map/all_to_all | solution.py:375
  31.9 5.1 %numer.1 = (f32[256,1024]{1,0:T(8,128)}, f32[256,1024]{1,0:T(8,128)}) custom-call(bf16[256,1024]{1,0:T(8,128)(2,1)} %get-tuple-element.64.fq, bf16[256,1024]{1,0:T(8,128)(2,1)} %get-tuple-element.65.fk, bf16[256,1024]{1,0:T(8,128)(2,1)} %get-tuple-element.66.fv, bf16[256,1024]{1,0:T(8,128)(2,1)} %bitcast.16, bf16[1024,1024]{1,0:T(8,128)(2,1)} %wo.3), custom_call_target="tpu_custom_call" | custom-call | flops 1073741824 | bytes 4194304 | tf_op jit(solution)/shard_map/numer/pallas_call | solution.py:398
  37.0 4.0 %all-to-all-done.1 = f32[32,16,128]{2,1,0:T(8,128)} async-done(((f32[32,16,128]{2,1,0:T(8,128)}), f32[32,16,128]{2,1,0:T(8,128)}, u32[]{:S(2)}, u32[]{:S(2)}) %all-to-all-start.1) | async-done | bytes 262176 | tf_op jit(solution)/shard_map/all_to_all | solution.py:375
  40.9 5.0 %norm.1 = (bf16[256,1024]{1,0:T(8,128)(2,1)}, f32[256,1024]{1,0:T(8,128)}, f32[512,128]{1,0:T(8,128)}, f32[8,1024]{1,0:T(8,128)}) custom-call(s32[1]{0:T(128)S(6)} %sub.7.nv_ref, f32[256,1024]{1,0:T(8,128)} %get-tuple-element.67.nl, f32[512,128]{1,0:T(8,128)} %bitcast.4.st, bf16[256,1024]{1,0:T(8,128)(2,1)} %get-tuple-element.64.fq, ...), custom_call_target="tpu_custom_call" | custom-call | flops 536870912 | bytes 4194304 | tf_op jit(solution)/shard_map/norm/pallas_call | solution.py:404
  46.0 4.4 %all-to-all-start.2 = ((f32[32,16,128]{2,1,0:T(8,128)}), f32[32,16,128]{2,1,0:T(8,128)}, u32[]{:S(2)}, u32[]{:S(2)}) async-start(f32[32,16,128]{2,1,0:T(8,128)} %bitcast.17), calls=%async_computation.2 | async-start | bytes 524288 | tf_op jit(solution)/shard_map/all_to_all | solution.py:364
  50.9 6.5 %dquery.1 = (bf16[256,1024]{1,0:T(8,128)(2,1)}, f32[264,256]{1,0:T(8,128)}, f32[264,256]{1,0:T(8,128)}, f32[264,256]{1,0:T(8,128)}, f32[264,256]{1,0:T(8,128)}) custom-call(s32[1]{0:T(128)} %bitcast.7.me_ref, f32[256,1024]{1,0:T(8,128)} %get-tuple-element.98.dn, f32[512,128]{1,0:T(8,128)} %bitcast.4.st, bf16[256,1024]{1,0:T(8,128)(2,1)} %get-tuple-element.65.fk, ...), custom_call_target="tpu_custom_call" | custom-call | flops 1073741824 | bytes 4194304 | tf_op jit(solution)/shard_map/dquery/pallas_call | solution.py:412
  63.3 5.5 %all-to-all-start.3 = ((f32[32,16,128]{2,1,0:T(8,128)}), f32[32,16,128]{2,1,0:T(8,128)}, u32[]{:S(2)}, u32[]{:S(2)}) async-start(f32[32,16,128]{2,1,0:T(8,128)} %suffix.1), calls=%async_computation.3 | async-start | bytes 524288 | tf_op jit(solution)/shard_map/all_to_all | solution.py:375
  68.8 4.4 %localk.1.lk = f32[256,1024]{1,0:T(8,128)} custom-call(f32[256,1024]{1,0:T(8,128)} %get-tuple-element.98.dn, bf16[256,1024]{1,0:T(8,128)(2,1)} %get-tuple-element.64.fq, bf16[256,1024]{1,0:T(8,128)(2,1)} %get-tuple-element.66.fv), custom_call_target="tpu_custom_call" | custom-call | flops 1073741824 | bytes 4194304 | tf_op jit(solution)/shard_map/localk/pallas_call | solution.py:425
  73.3 2.7 %collective-permute-done.5.d3 = f32[264,256]{1,0:T(8,128)} collective-permute-done((f32[264,256]{1,0:T(8,128)}, f32[264,256]{1,0:T(8,128)}, u32[]{:S(2)}, u32[]{:S(2)}) %collective-permute-start.5) | collective-permute-done | bytes 270368 | tf_op jit(solution)/shard_map/ppermute | solution.py:378
  76.0 3.9 %wgradq.1 = (f32[16,72,256]{2,1,0:T(8,128)}, bf16[1024,1024]{1,0:T(8,128)(2,1)}) custom-call(bf16[1024,256]{1,0:T(8,128)(2,1)} %get-tuple-element.77.t0, f32[1024,256]{1,0:T(8,128)} %collective-permute-done.t1, f32[1024,256]{1,0:T(8,128)} %collective-permute-done.1.t2, f32[1024,256]{1,0:T(8,128)} %collective-permute-done.2.t3, ...), custom_call_target="tpu_custom_call" | custom-call | flops 1073741824 | bytes 4194304 | tf_op jit(solution)/shard_map/wgradq/pallas_call | solution.py:432
  79.9 3.6 %dkey.1 = (bf16[256,1024]{1,0:T(8,128)(2,1)}, f32[256,256]{1,0:T(8,128)}, f32[256,256]{1,0:T(8,128)}, f32[256,256]{1,0:T(8,128)}, f32[256,256]{1,0:T(8,128)}) custom-call(s32[1]{0:T(128)} %bitcast.7.me_ref, f32[256,1024]{1,0:T(8,128)} %localk.1.lk, bf16[256,1024]{1,0:T(8,128)(2,1)} %get-tuple-element.66.fv, f32[512,128]{1,0:T(8,128)} %bitcast.8.st, ...), custom_call_target="tpu_custom_call" | custom-call | flops 268435456 | bytes 4194304 | tf_op jit(solution)/shard_map/dkey/pallas_call | solution.py:443
  83.5 4.7 %all-to-all-start.5 = ((f32[16,72,256]{2,1,0:T(8,128)}), f32[16,72,256]{2,1,0:T(8,128)}, u32[]{:S(2)}, u32[]{:S(2)}) async-start(f32[16,72,256]{2,1,0:T(8,128)} %get-tuple-element.103), calls=%async_computation.5 | async-start | bytes 2359296 | tf_op jit(solution)/shard_map/all_to_all | solution.py:451
  90.2 6.0 %collective-permute-done.6.d1 = f32[256,256]{1,0:T(8,128)} collective-permute-done((f32[256,256]{1,0:T(8,128)S(1)}, f32[256,256]{1,0:T(8,128)}, u32[]{:S(2)}, u32[]{:S(2)}) %collective-permute-start.6) | collective-permute-done | bytes 262176 | tf_op jit(solution)/shard_map/ppermute | solution.py:378
  96.2 6.2 %collective-permute-done.8.d3 = f32[256,256]{1,0:T(8,128)} collective-permute-done((f32[256,256]{1,0:T(8,128)S(1)}, f32[256,256]{1,0:T(8,128)}, u32[]{:S(2)}, u32[]{:S(2)}) %collective-permute-start.8) | collective-permute-done | bytes 262176 | tf_op jit(solution)/shard_map/ppermute | solution.py:378
  102.4 3.2 %wgradk.1 = f32[16,64,256]{2,1,0:T(8,128)} custom-call(bf16[1024,1024]{1,0:T(8,128)(2,1)} %get-tuple-element.85.t, f32[256,256]{1,0:T(8,128)} %get-tuple-element.90.d0, f32[256,256]{1,0:T(8,128)} %collective-permute-done.6.d1, f32[256,256]{1,0:T(8,128)} %collective-permute-done.7.d2, f32[256,256]{1,0:T(8,128)} %collective-permute-done.8.d3), custom_call_target="tpu_custom_call" | custom-call | flops 1073741824 | bytes 4194304 | tf_op jit(solution)/shard_map/wgradk/pallas_call | solution.py:454
  107.5 4.7 %all-to-all-start.4 = ((f32[16,64,256]{2,1,0:T(8,128)}), f32[16,64,256]{2,1,0:T(8,128)}, u32[]{:S(2)}, u32[]{:S(2)}) async-start(f32[16,64,256]{2,1,0:T(8,128)} %wgradk.1), calls=%async_computation.4 | async-start | bytes 2097152 | tf_op jit(solution)/shard_map/all_to_all | solution.py:459
  112.3 5.1 %localv.1 = (bf16[256,1024]{1,0:T(8,128)(2,1)}, f32[256,1024]{1,0:T(8,128)}) custom-call(bf16[256,1024]{1,0:T(8,128)(2,1)} %get-tuple-element.94.at, bf16[1024,1024]{1,0:T(8,128)(2,1)} %wo.3, f32[256,1024]{1,0:T(8,128)} %get-tuple-element.98.dn, bf16[256,1024]{1,0:T(8,128)(2,1)} %get-tuple-element.64.fq, bf16[256,1024]{1,0:T(8,128)(2,1)} %get-tuple-element.65.fk), custom_call_target="tpu_custom_call" | custom-call | flops 2147483648 | bytes 4194304 | tf_op jit(solution)/shard_map/localv/pallas_call | solution.py:462
  117.3 5.8 %dtok.1 = bf16[256,1024]{1,0:T(8,128)(2,1)} custom-call(f32[256,1024]{1,0:T(8,128)} %get-tuple-element.100.lv, bf16[256,1024]{1,0:T(8,128)(2,1)} %get-tuple-element.65.fk, f32[512,128]{1,0:T(8,128)} %bitcast.8.st, bf16[256,1024]{1,0:T(8,128)(2,1)} %get-tuple-element.101.dq, bf16[256,1024]{1,0:T(8,128)(2,1)} %get-tuple-element.102.dk, bf16[1024,1024]{1,0:T(8,128)(2,1)} %wq.3, ...), custom_call_target="tpu_custom_call" | custom-call | flops 2147483648 | bytes 4194304 | tf_op jit(solution)/shard_map/dtok/pallas_call | solution.py:466
  125.1 2.5 %all-to-all-done.4.k = f32[16,64,256]{2,1,0:T(8,128)} async-done(((f32[16,64,256]{2,1,0:T(8,128)}), f32[16,64,256]{2,1,0:T(8,128)}, u32[]{:S(2)}, u32[]{:S(2)}) %all-to-all-start.4) | async-done | bytes 1048608 | tf_op jit(solution)/shard_map/all_to_all | solution.py:459
  129.6 19.5 %all_to_all.35.v = f32[16,8,384]{2,1,0:T(8,128)} all-to-all(f32[16,8,384]{2,1,0:T(8,128)} %join.1), channel_id=1, replica_groups=mesh['x'=4,'y'=4,'c'=2,'w'=4,'b'=2] {'c','w','b'}, dimensions={0} | all-to-all | bytes 393216 | tf_op jit(solution)/shard_map/all_to_all | solution.py:485
  (30 shorter events, 21.7 us)
Async XLA Ops:
  6.0 17.7 %all-to-all-start = ((f32[32,16,128]{2,1,0:T(8,128)}), f32[32,16,128]{2,1,0:T(8,128)}, u32[]{:S(2)}, u32[]{:S(2)}) async-start(f32[32,16,128]{2,1,0:T(8,128)} %bitcast.18), calls=%async_computation | async-start | bytes 524288 | tf_op jit(solution)/shard_map/all_to_all | solution.py:364
  25.4 35.8 %collective-permute-start = (f32[1024,256]{1,0:T(8,128)}, f32[1024,256]{1,0:T(8,128)}, u32[]{:S(2)}, u32[]{:S(2)}) collective-permute-start(f32[1024,256]{1,0:T(8,128)} %get-tuple-element.79), channel_id=1, source_target_pairs={{0,1},{1,0},{8,9},{9,8},{2,3},{3,2},{10,11},{11,10},{4,5},{5,4},{1... | collective-permute-start | bytes 3145736 | tf_op jit(solution)/shard_map/ppermute | solution.py:378
  27.1 13.9 %all-to-all-start.1 = ((f32[32,16,128]{2,1,0:T(8,128)}), f32[32,16,128]{2,1,0:T(8,128)}, u32[]{:S(2)}, u32[]{:S(2)}) async-start(f32[32,16,128]{2,1,0:T(8,128)} %prefix.1), calls=%async_computation.1 | async-start | bytes 524288 | tf_op jit(solution)/shard_map/all_to_all | solution.py:375
  46.0 13.5 %all-to-all-start.2 = ((f32[32,16,128]{2,1,0:T(8,128)}), f32[32,16,128]{2,1,0:T(8,128)}, u32[]{:S(2)}, u32[]{:S(2)}) async-start(f32[32,16,128]{2,1,0:T(8,128)} %bitcast.17), calls=%async_computation.2 | async-start | bytes 524288 | tf_op jit(solution)/shard_map/all_to_all | solution.py:364
  50.4 25.6 %collective-permute-start.1 = (f32[1024,256]{1,0:T(8,128)}, f32[1024,256]{1,0:T(8,128)}, u32[]{:S(2)}, u32[]{:S(2)}) collective-permute-start(f32[1024,256]{1,0:T(8,128)} %get-tuple-element.79), channel_id=1, source_target_pairs={{0,8},{1,9},{8,0},{9,1},{2,10},{3,11},{10,2},{11,3},{4,12},{5,13},... | collective-permute-start | bytes 3145736 | tf_op jit(solution)/shard_map/ppermute | solution.py:378
  61.2 14.8 %collective-permute-start.2 = (f32[1024,256]{1,0:T(8,128)}, f32[1024,256]{1,0:T(8,128)}, u32[]{:S(2)}, u32[]{:S(2)}) collective-permute-start(f32[1024,256]{1,0:T(8,128)} %collective-permute-done.t1), channel_id=1, source_target_pairs={{0,8},{1,9},{8,0},{9,1},{2,10},{3,11},{10,2},{11,3},{4,12},{5,13},... | collective-permute-start | bytes 3145736 | tf_op jit(solution)/shard_map/ppermute | solution.py:378
  61.4 11.9 %collective-permute-start.3 = (f32[264,256]{1,0:T(8,128)}, f32[264,256]{1,0:T(8,128)}, u32[]{:S(2)}, u32[]{:S(2)}) collective-permute-start(f32[264,256]{1,0:T(8,128)} %get-tuple-element.82), channel_id=1, source_target_pairs={{0,1},{1,0},{8,9},{9,8},{2,3},{3,2},{10,11},{11,10},{4,5},{5,4},{1... | collective-permute-start | bytes 811016 | tf_op jit(solution)/shard_map/ppermute | solution.py:378
  61.4 11.9 %collective-permute-start.4 = (f32[264,256]{1,0:T(8,128)}, f32[264,256]{1,0:T(8,128)}, u32[]{:S(2)}, u32[]{:S(2)}) collective-permute-start(f32[264,256]{1,0:T(8,128)} %get-tuple-element.83), channel_id=1, source_target_pairs={{0,8},{1,9},{8,0},{9,1},{2,10},{3,11},{10,2},{11,3},{4,12},{5,13},... | collective-permute-start | bytes 811016 | tf_op jit(solution)/shard_map/ppermute | solution.py:378
  61.8 14.2 %collective-permute-start.5 = (f32[264,256]{1,0:T(8,128)}, f32[264,256]{1,0:T(8,128)}, u32[]{:S(2)}, u32[]{:S(2)}) collective-permute-start(f32[264,256]{1,0:T(8,128)} %get-tuple-element.84), channel_id=1, source_target_pairs={{0,9},{1,8},{8,1},{9,0},{2,11},{3,10},{10,3},{11,2},{4,13},{5,12},... | collective-permute-start | bytes 811016 | tf_op jit(solution)/shard_map/ppermute | solution.py:378
  63.3 16.5 %all-to-all-start.3 = ((f32[32,16,128]{2,1,0:T(8,128)}), f32[32,16,128]{2,1,0:T(8,128)}, u32[]{:S(2)}, u32[]{:S(2)}) async-start(f32[32,16,128]{2,1,0:T(8,128)} %suffix.1), calls=%async_computation.3 | async-start | bytes 524288 | tf_op jit(solution)/shard_map/all_to_all | solution.py:375
  83.5 4.8 %copy-start.2 = (f32[256,256]{1,0:T(8,128)S(1)}, f32[256,256]{1,0:T(8,128)}, u32[]{:S(2)}) copy-start(f32[256,256]{1,0:T(8,128)} %get-tuple-element.91) | copy-start | bytes 786436
  83.5 4.9 %copy-start.1 = (f32[256,256]{1,0:T(8,128)S(1)}, f32[256,256]{1,0:T(8,128)}, u32[]{:S(2)}) copy-start(f32[256,256]{1,0:T(8,128)} %get-tuple-element.92) | copy-start | bytes 786436
  83.5 5.2 %copy-start = (f32[256,256]{1,0:T(8,128)S(1)}, f32[256,256]{1,0:T(8,128)}, u32[]{:S(2)}) copy-start(f32[256,256]{1,0:T(8,128)} %get-tuple-element.93) | copy-start | bytes 786436
  83.5 24.1 %all-to-all-start.5 = ((f32[16,72,256]{2,1,0:T(8,128)}), f32[16,72,256]{2,1,0:T(8,128)}, u32[]{:S(2)}, u32[]{:S(2)}) async-start(f32[16,72,256]{2,1,0:T(8,128)} %get-tuple-element.103), calls=%async_computation.5 | async-start | bytes 2359296 | tf_op jit(solution)/shard_map/all_to_all | solution.py:451
  88.2 8.0 %collective-permute-start.6 = (f32[256,256]{1,0:T(8,128)S(1)}, f32[256,256]{1,0:T(8,128)}, u32[]{:S(2)}, u32[]{:S(2)}) collective-permute-start(f32[256,256]{1,0:T(8,128)S(1)} %copy-done.2), channel_id=1, source_target_pairs={{0,1},{1,0},{8,9},{9,8},{2,3},{3,2},{10,11},{11,10},{4,5},{5,4},{1... | collective-permute-start | bytes 786440 | tf_op jit(solution)/shard_map/ppermute | solution.py:378
  88.3 7.9 %collective-permute-start.7 = (f32[256,256]{1,0:T(8,128)S(1)}, f32[256,256]{1,0:T(8,128)}, u32[]{:S(2)}, u32[]{:S(2)}) collective-permute-start(f32[256,256]{1,0:T(8,128)S(1)} %copy-done.1), channel_id=1, source_target_pairs={{0,8},{1,9},{8,0},{9,1},{2,10},{3,11},{10,2},{11,3},{4,12},{5,13},... | collective-permute-start | bytes 786440 | tf_op jit(solution)/shard_map/ppermute | solution.py:378
  88.7 13.7 %collective-permute-start.8 = (f32[256,256]{1,0:T(8,128)S(1)}, f32[256,256]{1,0:T(8,128)}, u32[]{:S(2)}, u32[]{:S(2)}) collective-permute-start(f32[256,256]{1,0:T(8,128)S(1)} %copy-done), channel_id=1, source_target_pairs={{0,9},{1,8},{8,1},{9,0},{2,11},{3,10},{10,3},{11,2},{4,13},{5,12},... | collective-permute-start | bytes 786440 | tf_op jit(solution)/shard_map/ppermute | solution.py:378
  107.5 20.0 %all-to-all-start.4 = ((f32[16,64,256]{2,1,0:T(8,128)}), f32[16,64,256]{2,1,0:T(8,128)}, u32[]{:S(2)}, u32[]{:S(2)}) async-start(f32[16,64,256]{2,1,0:T(8,128)} %wgradk.1), calls=%async_computation.4 | async-start | bytes 2097152 | tf_op jit(solution)/shard_map/all_to_all | solution.py:459

commit v5 on v4

--- a/solution.py
+++ b/solution.py
@@ -144,7 +144,8 @@
     valid = valid_rows(nv_ref, n)
     for j, c in groups_of(nl):
         r = slice(128 * j, 128 * j + 128)
-        numer = nl[:, c] + dot(fq[:, c], unpack_state(st[r, :].astype(BF)))
+        s_hi, s_lo = split(unpack_state(st[r, :]))
+        numer = nl[:, c] + dot(fq[:, c], s_hi) + dot(fq[:, c], s_lo)
         inv = lax.rsqrt(head_mean((numer * numer).astype(BF)) + EPS)
         normed = numer * inv
         scale = gain[:, c]
@@ -154,7 +155,8 @@
         g = dov * scale
         dn = inv * (g - normed * head_mean(*split(g * normed)))
         dn_o[:, c] = dn
-        rs_o[r, :] = pack_state(dot(fqt[c, :], dn.astype(BF)))
+        d_hi, d_lo = split(dn)
+        rs_o[r, :] = pack_state(dot(fqt[c, :], d_hi) + dot(fqt[c, :], d_lo))
 
 
 def dq_kernel(me_ref, dn, st, fk, fv, sq, gp, dq_o, *send):
@@ -205,8 +207,9 @@
 
 def dk_kernel(me_ref, lk, fv, st, sk, dk_o, *send):
     for j, c in groups_of(lk):
-        state = unpack_state(st[128 * j:128 * j + 128, :].astype(BF))
-        dk = ((lk[:, c] + dot(fv[:, c], state, NT)) * sk[:, c]).astype(BF)
+        r_hi, r_lo = split(unpack_state(st[128 * j:128 * j + 128, :]))
+        total = lk[:, c] + dot(fv[:, c], r_hi, NT) + dot(fv[:, c], r_lo, NT)
+        dk = (total * sk[:, c]).astype(BF)
         dk_o[:, c] = dk
         for k, out in enumerate(send):
             @pl.when(group_at(j, lk) == jnp.bitwise_xor(me_ref[0], k))
@@ -218,8 +221,8 @@
     term = dot(dq[...], wq[...], NT) + dot(dk[...], wk[...], NT)
     dv = []
     for j, c in groups_of(lv):
-        state = unpack_state(st[128 * j:128 * j + 128, :].astype(BF))
-        dv.append((lv[:, c] + dot(fk[:, c], state)).astype(BF))
+        r_hi, r_lo = split(unpack_state(st[128 * j:128 * j + 128, :]))
+        dv.append((lv[:, c] + dot(fk[:, c], r_hi) + dot(fk[:, c], r_lo)).astype(BF))
     term = term + dot(jnp.concatenate(dv, axis=1), wv[...], NT)
 
     @pl.when(pl.program_id(0) == 0)
@@ -454,7 +457,7 @@
     (gk,) = call(
         wgrad_k_kernel, (steps,), [row(d // steps, 4 * n)] + [whole((n, GL))] * 4,
         [(kshape, F32, pl.BlockSpec((nxy // steps,) + kshape[1:], lambda g: (g, 0, 0)))],
-        "wgradk", 2 * big,
+        "wgradk", 400 * big,
     )(tall, *dk_got)
     gk_parts = lax.all_to_all(gk, ("x", "y"), 0, 0, tiled=True)
 

time: 152 us -> 152 us (level)
    all_to_all x1, waiting for transfers between devices: 1.96 us -> 7.57 us  [on_device(): gq = lax.all_to_all(gq, ('x', 'y'), 0, 0, tiled=True)]
    ppermute x9, waiting for transfers between devices: 14.9 us -> 10.6 us  [swap(): return lax.ppermute(v, GROUP, [(i, i ^ k) for i in range(ngroup)])]
where the time goes in v5:
time: 152 us; the launch traced here: 151 us
  Pallas kernels  62.7 us (41%)
  starting transfers between devices  38.4 us (25%)
  waiting for transfers between devices  29.4 us (19%)
  blocking collectives  19 us (12%)
    all_to_all x1, blocking collectives, on_device(): both = lax.all_to_all(both, last, 0, 0, tiled=True)  19 us
    all_to_all x2, starting transfers between devices, to_parts(): lax.all_to_all(st.reshape(nseq, st_rows // nseq, 128), SEQ, 0, 0, tiled=T...  13 us
    ppermute x9, waiting for transfers between devices, swap(): return lax.ppermute(v, GROUP, [(i, i ^ k) for i in range(ngroup)])  10.6 us
    all_to_all x2, starting transfers between devices, from_parts(): return lax.all_to_all(mine, SEQ, 0, 0, tiled=True).reshape(st_rows, 128)  10.3 us
    all_to_all x1, waiting for transfers between devices, on_device(): gq = lax.all_to_all(gq, ('x', 'y'), 0, 0, tiled=True)  7.57 us
    pallas_call x1, Pallas kernels, on_device(): call(dq_kernel, (halves,), [SMEM, col(n, w), st_spec, col(n, w), col(n, w...  6.47 us
    ppermute x9, starting transfers between devices, swap(): return lax.ppermute(v, GROUP, [(i, i ^ k) for i in range(ngroup)])  6.18 us
    pallas_call x1, Pallas kernels, on_device(): call(dtok_kernel, (halves,), [col(n, w), col(n, w), st_spec, col(n, w), c...  5.83 us
  transfers between devices with their start and end apart: 15, of which 8 were waited for; matrix products, arithmetic and copies ran while one was open for 0% of the time, Pallas kernels for 32%

profile of v5, /device:TPU:1, one launch (start us, length us, event | category | flops | bytes accessed | tf_op | source)
XLA Modules:
  0.0 151.0 jit_solution(4395217210052525080)
XLA Ops:
  1.3 4.7 %kv.1 = (bf16[256,1024]{1,0:T(8,128)(2,1)}, bf16[256,1024]{1,0:T(8,128)(2,1)}, f32[256,1024]{1,0:T(8,128)}, f32[512,128]{1,0:T(8,128)}) custom-call(s32[1]{0:T(128)S(6)} %sub.7.nv_ref, bf16[256,1024]{1,0:T(8,128)(2,1)} %bitcast.12, bf16[1024,1024]{1,0:T(8,128)(2,1)} %wk.3, bf16[1024,1024]{1,0:T(8,128)(2,1)} %wv.3), custom_call_target="tpu_custom_call" | custom-call | flops 1073741824 | bytes 4194304 | tf_op jit(solution)/shard_map/kv/pallas_call | solution.py:359
  6.0 8.6 %all-to-all-start = ((f32[32,16,128]{2,1,0:T(8,128)}), f32[32,16,128]{2,1,0:T(8,128)}, u32[]{:S(2)}, u32[]{:S(2)}) async-start(f32[32,16,128]{2,1,0:T(8,128)} %bitcast.18), calls=%async_computation | async-start | bytes 524288 | tf_op jit(solution)/shard_map/all_to_all | solution.py:367
  14.7 2.4 %turn.1 = (bf16[1024,256]{1,0:T(8,128)(2,1)}, f32[1024,256]{1,0:T(8,128)}) custom-call(bf16[256,1024]{1,0:T(8,128)(2,1)} %bitcast.13), custom_call_target="tpu_custom_call" | custom-call | flops 134217728 | bytes 4194304 | tf_op jit(solution)/shard_map/turn/pallas_call | solution.py:385
  17.1 3.7 %query.1 = (bf16[256,1024]{1,0:T(8,128)(2,1)}, bf16[1024,256]{1,0:T(8,128)(2,1)}, f32[256,1024]{1,0:T(8,128)}) custom-call(bf16[256,1024]{1,0:T(8,128)(2,1)} %bitcast.14, bf16[1024,1024]{1,0:T(8,128)(2,1)} %wq.3), custom_call_target="tpu_custom_call" | custom-call | flops 536870912 | bytes 4194304 | tf_op jit(solution)/shard_map/query/pallas_call | solution.py:389
  20.8 2.9 %all-to-all-done.v = f32[32,16,128]{2,1,0:T(8,128)} async-done(((f32[32,16,128]{2,1,0:T(8,128)}), f32[32,16,128]{2,1,0:T(8,128)}, u32[]{:S(2)}, u32[]{:S(2)}) %all-to-all-start) | async-done | bytes 262176 | tf_op jit(solution)/shard_map/all_to_all | solution.py:367
  27.1 4.8 %all-to-all-start.1 = ((f32[32,16,128]{2,1,0:T(8,128)}), f32[32,16,128]{2,1,0:T(8,128)}, u32[]{:S(2)}, u32[]{:S(2)}) async-start(f32[32,16,128]{2,1,0:T(8,128)} %prefix.1), calls=%async_computation.1 | async-start | bytes 524288 | tf_op jit(solution)/shard_map/all_to_all | solution.py:378
  31.9 5.1 %numer.1 = (f32[256,1024]{1,0:T(8,128)}, f32[256,1024]{1,0:T(8,128)}) custom-call(bf16[256,1024]{1,0:T(8,128)(2,1)} %get-tuple-element.64.fq, bf16[256,1024]{1,0:T(8,128)(2,1)} %get-tuple-element.65.fk, bf16[256,1024]{1,0:T(8,128)(2,1)} %get-tuple-element.66.fv, bf16[256,1024]{1,0:T(8,128)(2,1)} %bitcast.16, bf16[1024,1024]{1,0:T(8,128)(2,1)} %wo.3), custom_call_target="tpu_custom_call" | custom-call | flops 1073741824 | bytes 4194304 | tf_op jit(solution)/shard_map/numer/pallas_call | solution.py:401
  36.9 4.0 %all-to-all-done.1 = f32[32,16,128]{2,1,0:T(8,128)} async-done(((f32[32,16,128]{2,1,0:T(8,128)}), f32[32,16,128]{2,1,0:T(8,128)}, u32[]{:S(2)}, u32[]{:S(2)}) %all-to-all-start.1) | async-done | bytes 262176 | tf_op jit(solution)/shard_map/all_to_all | solution.py:378
  40.9 5.2 %norm.1 = (bf16[256,1024]{1,0:T(8,128)(2,1)}, f32[256,1024]{1,0:T(8,128)}, f32[512,128]{1,0:T(8,128)}, f32[8,1024]{1,0:T(8,128)}) custom-call(s32[1]{0:T(128)S(6)} %sub.7.nv_ref, f32[256,1024]{1,0:T(8,128)} %get-tuple-element.67.nl, f32[512,128]{1,0:T(8,128)} %bitcast.4.st, bf16[256,1024]{1,0:T(8,128)(2,1)} %get-tuple-element.64.fq, ...), custom_call_target="tpu_custom_call" | custom-call | flops 536870912 | bytes 4194304 | tf_op jit(solution)/shard_map/norm/pallas_call | solution.py:407
  46.1 4.4 %all-to-all-start.2 = ((f32[32,16,128]{2,1,0:T(8,128)}), f32[32,16,128]{2,1,0:T(8,128)}, u32[]{:S(2)}, u32[]{:S(2)}) async-start(f32[32,16,128]{2,1,0:T(8,128)} %bitcast.17), calls=%async_computation.2 | async-start | bytes 524288 | tf_op jit(solution)/shard_map/all_to_all | solution.py:367
  51.0 6.5 %dquery.1 = (bf16[256,1024]{1,0:T(8,128)(2,1)}, f32[264,256]{1,0:T(8,128)}, f32[264,256]{1,0:T(8,128)}, f32[264,256]{1,0:T(8,128)}, f32[264,256]{1,0:T(8,128)}) custom-call(s32[1]{0:T(128)} %bitcast.7.me_ref, f32[256,1024]{1,0:T(8,128)} %get-tuple-element.98.dn, f32[512,128]{1,0:T(8,128)} %bitcast.4.st, bf16[256,1024]{1,0:T(8,128)(2,1)} %get-tuple-element.65.fk, ...), custom_call_target="tpu_custom_call" | custom-call | flops 1073741824 | bytes 4194304 | tf_op jit(solution)/shard_map/dquery/pallas_call | solution.py:415
  63.4 5.5 %all-to-all-start.3 = ((f32[32,16,128]{2,1,0:T(8,128)}), f32[32,16,128]{2,1,0:T(8,128)}, u32[]{:S(2)}, u32[]{:S(2)}) async-start(f32[32,16,128]{2,1,0:T(8,128)} %suffix.1), calls=%async_computation.3 | async-start | bytes 524288 | tf_op jit(solution)/shard_map/all_to_all | solution.py:378
  68.9 4.4 %localk.1.lk = f32[256,1024]{1,0:T(8,128)} custom-call(f32[256,1024]{1,0:T(8,128)} %get-tuple-element.98.dn, bf16[256,1024]{1,0:T(8,128)(2,1)} %get-tuple-element.64.fq, bf16[256,1024]{1,0:T(8,128)(2,1)} %get-tuple-element.66.fv), custom_call_target="tpu_custom_call" | custom-call | flops 1073741824 | bytes 4194304 | tf_op jit(solution)/shard_map/localk/pallas_call | solution.py:428
  73.3 2.8 %collective-permute-done.5.d3 = f32[264,256]{1,0:T(8,128)} collective-permute-done((f32[264,256]{1,0:T(8,128)}, f32[264,256]{1,0:T(8,128)}, u32[]{:S(2)}, u32[]{:S(2)}) %collective-permute-start.5) | collective-permute-done | bytes 270368 | tf_op jit(solution)/shard_map/ppermute | solution.py:381
  76.1 3.9 %wgradq.1 = (f32[16,72,256]{2,1,0:T(8,128)}, bf16[1024,1024]{1,0:T(8,128)(2,1)}) custom-call(bf16[1024,256]{1,0:T(8,128)(2,1)} %get-tuple-element.77.t0, f32[1024,256]{1,0:T(8,128)} %collective-permute-done.t1, f32[1024,256]{1,0:T(8,128)} %collective-permute-done.1.t2, f32[1024,256]{1,0:T(8,128)} %collective-permute-done.2.t3, ...), custom_call_target="tpu_custom_call" | custom-call | flops 1073741824 | bytes 4194304 | tf_op jit(solution)/shard_map/wgradq/pallas_call | solution.py:435
  80.0 3.9 %dkey.1 = (bf16[256,1024]{1,0:T(8,128)(2,1)}, f32[256,256]{1,0:T(8,128)}, f32[256,256]{1,0:T(8,128)}, f32[256,256]{1,0:T(8,128)}, f32[256,256]{1,0:T(8,128)}) custom-call(s32[1]{0:T(128)} %bitcast.7.me_ref, f32[256,1024]{1,0:T(8,128)} %localk.1.lk, bf16[256,1024]{1,0:T(8,128)(2,1)} %get-tuple-element.66.fv, f32[512,128]{1,0:T(8,128)} %bitcast.8.st, ...), custom_call_target="tpu_custom_call" | custom-call | flops 268435456 | bytes 4194304 | tf_op jit(solution)/shard_map/dkey/pallas_call | solution.py:446
  85.8 4.6 %all-to-all-start.5 = ((f32[16,72,256]{2,1,0:T(8,128)}), f32[16,72,256]{2,1,0:T(8,128)}, u32[]{:S(2)}, u32[]{:S(2)}) async-start(f32[16,72,256]{2,1,0:T(8,128)} %get-tuple-element.103), calls=%async_computation.5 | async-start | bytes 2359296 | tf_op jit(solution)/shard_map/all_to_all | solution.py:454
  92.4 5.7 %collective-permute-done.8.d3 = f32[256,256]{1,0:T(8,128)} collective-permute-done((f32[256,256]{1,0:T(8,128)}, f32[256,256]{1,0:T(8,128)}, u32[]{:S(2)}, u32[]{:S(2)}) %collective-permute-start.8) | collective-permute-done | bytes 262176 | tf_op jit(solution)/shard_map/ppermute | solution.py:381
  98.2 3.2 %wgradk.1 = f32[16,64,256]{2,1,0:T(8,128)} custom-call(bf16[1024,1024]{1,0:T(8,128)(2,1)} %get-tuple-element.85.t, f32[256,256]{1,0:T(8,128)} %get-tuple-element.90.d0, f32[256,256]{1,0:T(8,128)} %collective-permute-done.6.d1, f32[256,256]{1,0:T(8,128)} %collective-permute-done.7.d2, f32[256,256]{1,0:T(8,128)} %collective-permute-done.8.d3), custom_call_target="tpu_custom_call" | custom-call | flops 214748364800 | bytes 4194304 | tf_op jit(solution)/shard_map/wgradk/pallas_call | solution.py:457
  101.4 7.6 %all-to-all-done.5.v = f32[16,72,256]{2,1,0:T(8,128)} async-done(((f32[16,72,256]{2,1,0:T(8,128)}), f32[16,72,256]{2,1,0:T(8,128)}, u32[]{:S(2)}, u32[]{:S(2)}) %all-to-all-start.5) | async-done | bytes 1179680 | tf_op jit(solution)/shard_map/all_to_all | solution.py:454
  109.0 4.3 %all-to-all-start.4 = ((f32[16,64,256]{2,1,0:T(8,128)}), f32[16,64,256]{2,1,0:T(8,128)}, u32[]{:S(2)}, u32[]{:S(2)}) async-start(f32[16,64,256]{2,1,0:T(8,128)} %wgradk.1), calls=%async_computation.4 | async-start | bytes 2097152 | tf_op jit(solution)/shard_map/all_to_all | solution.py:462
  113.3 5.1 %localv.1 = (bf16[256,1024]{1,0:T(8,128)(2,1)}, f32[256,1024]{1,0:T(8,128)}) custom-call(bf16[256,1024]{1,0:T(8,128)(2,1)} %get-tuple-element.94.at, bf16[1024,1024]{1,0:T(8,128)(2,1)} %wo.3, f32[256,1024]{1,0:T(8,128)} %get-tuple-element.98.dn, bf16[256,1024]{1,0:T(8,128)(2,1)} %get-tuple-element.64.fq, bf16[256,1024]{1,0:T(8,128)(2,1)} %get-tuple-element.65.fk), custom_call_target="tpu_custom_call" | custom-call | flops 2147483648 | bytes 4194304 | tf_op jit(solution)/shard_map/localv/pallas_call | solution.py:465
  118.4 5.8 %dtok.1 = bf16[256,1024]{1,0:T(8,128)(2,1)} custom-call(f32[256,1024]{1,0:T(8,128)} %get-tuple-element.100.lv, bf16[256,1024]{1,0:T(8,128)(2,1)} %get-tuple-element.65.fk, f32[512,128]{1,0:T(8,128)} %bitcast.8.st, bf16[256,1024]{1,0:T(8,128)(2,1)} %get-tuple-element.101.dq, bf16[256,1024]{1,0:T(8,128)(2,1)} %get-tuple-element.102.dk, bf16[1024,1024]{1,0:T(8,128)(2,1)} %wq.3, ...), custom_call_target="tpu_custom_call" | custom-call | flops 2147483648 | bytes 4194304 | tf_op jit(solution)/shard_map/dtok/pallas_call | solution.py:469
  130.4 19.0 %all_to_all.35.v = f32[16,8,384]{2,1,0:T(8,128)} all-to-all(f32[16,8,384]{2,1,0:T(8,128)} %join.1), channel_id=1, replica_groups=mesh['x'=4,'y'=4,'c'=2,'w'=4,'b'=2] {'c','w','b'}, dimensions={0} | all-to-all | bytes 393216 | tf_op jit(solution)/shard_map/all_to_all | solution.py:488
  (24 shorter events, 21.5 us)
Async XLA Ops:
  6.0 17.7 %all-to-all-start = ((f32[32,16,128]{2,1,0:T(8,128)}), f32[32,16,128]{2,1,0:T(8,128)}, u32[]{:S(2)}, u32[]{:S(2)}) async-start(f32[32,16,128]{2,1,0:T(8,128)} %bitcast.18), calls=%async_computation | async-start | bytes 524288 | tf_op jit(solution)/shard_map/all_to_all | solution.py:367
  25.4 35.9 %collective-permute-start = (f32[1024,256]{1,0:T(8,128)}, f32[1024,256]{1,0:T(8,128)}, u32[]{:S(2)}, u32[]{:S(2)}) collective-permute-start(f32[1024,256]{1,0:T(8,128)} %get-tuple-element.79), channel_id=1, source_target_pairs={{0,1},{1,0},{8,9},{9,8},{2,3},{3,2},{10,11},{11,10},{4,5},{5,4},{1... | collective-permute-start | bytes 3145736 | tf_op jit(solution)/shard_map/ppermute | solution.py:381
  27.1 13.9 %all-to-all-start.1 = ((f32[32,16,128]{2,1,0:T(8,128)}), f32[32,16,128]{2,1,0:T(8,128)}, u32[]{:S(2)}, u32[]{:S(2)}) async-start(f32[32,16,128]{2,1,0:T(8,128)} %prefix.1), calls=%async_computation.1 | async-start | bytes 524288 | tf_op jit(solution)/shard_map/all_to_all | solution.py:378
  46.1 13.5 %all-to-all-start.2 = ((f32[32,16,128]{2,1,0:T(8,128)}), f32[32,16,128]{2,1,0:T(8,128)}, u32[]{:S(2)}, u32[]{:S(2)}) async-start(f32[32,16,128]{2,1,0:T(8,128)} %bitcast.17), calls=%async_computation.2 | async-start | bytes 524288 | tf_op jit(solution)/shard_map/all_to_all | solution.py:367
  50.5 25.6 %collective-permute-start.1 = (f32[1024,256]{1,0:T(8,128)}, f32[1024,256]{1,0:T(8,128)}, u32[]{:S(2)}, u32[]{:S(2)}) collective-permute-start(f32[1024,256]{1,0:T(8,128)} %get-tuple-element.79), channel_id=1, source_target_pairs={{0,8},{1,9},{8,0},{9,1},{2,10},{3,11},{10,2},{11,3},{4,12},{5,13},... | collective-permute-start | bytes 3145736 | tf_op jit(solution)/shard_map/ppermute | solution.py:381
  61.3 14.8 %collective-permute-start.2 = (f32[1024,256]{1,0:T(8,128)}, f32[1024,256]{1,0:T(8,128)}, u32[]{:S(2)}, u32[]{:S(2)}) collective-permute-start(f32[1024,256]{1,0:T(8,128)} %collective-permute-done.t1), channel_id=1, source_target_pairs={{0,8},{1,9},{8,0},{9,1},{2,10},{3,11},{10,2},{11,3},{4,12},{5,13},... | collective-permute-start | bytes 3145736 | tf_op jit(solution)/shard_map/ppermute | solution.py:381
  61.5 11.9 %collective-permute-start.3 = (f32[264,256]{1,0:T(8,128)}, f32[264,256]{1,0:T(8,128)}, u32[]{:S(2)}, u32[]{:S(2)}) collective-permute-start(f32[264,256]{1,0:T(8,128)} %get-tuple-element.82), channel_id=1, source_target_pairs={{0,1},{1,0},{8,9},{9,8},{2,3},{3,2},{10,11},{11,10},{4,5},{5,4},{1... | collective-permute-start | bytes 811016 | tf_op jit(solution)/shard_map/ppermute | solution.py:381
  61.5 11.9 %collective-permute-start.4 = (f32[264,256]{1,0:T(8,128)}, f32[264,256]{1,0:T(8,128)}, u32[]{:S(2)}, u32[]{:S(2)}) collective-permute-start(f32[264,256]{1,0:T(8,128)} %get-tuple-element.83), channel_id=1, source_target_pairs={{0,8},{1,9},{8,0},{9,1},{2,10},{3,11},{10,2},{11,3},{4,12},{5,13},... | collective-permute-start | bytes 811016 | tf_op jit(solution)/shard_map/ppermute | solution.py:381
  61.9 14.2 %collective-permute-start.5 = (f32[264,256]{1,0:T(8,128)}, f32[264,256]{1,0:T(8,128)}, u32[]{:S(2)}, u32[]{:S(2)}) collective-permute-start(f32[264,256]{1,0:T(8,128)} %get-tuple-element.84), channel_id=1, source_target_pairs={{0,9},{1,8},{8,1},{9,0},{2,11},{3,10},{10,3},{11,2},{4,13},{5,12},... | collective-permute-start | bytes 811016 | tf_op jit(solution)/shard_map/ppermute | solution.py:381
  63.4 16.5 %all-to-all-start.3 = ((f32[32,16,128]{2,1,0:T(8,128)}), f32[32,16,128]{2,1,0:T(8,128)}, u32[]{:S(2)}, u32[]{:S(2)}) async-start(f32[32,16,128]{2,1,0:T(8,128)} %suffix.1), calls=%async_computation.3 | async-start | bytes 524288 | tf_op jit(solution)/shard_map/all_to_all | solution.py:378
  83.8 8.6 %collective-permute-start.6 = (f32[256,256]{1,0:T(8,128)}, f32[256,256]{1,0:T(8,128)}, u32[]{:S(2)}, u32[]{:S(2)}) collective-permute-start(f32[256,256]{1,0:T(8,128)} %get-tuple-element.91), channel_id=1, source_target_pairs={{0,1},{1,0},{8,9},{9,8},{2,3},{3,2},{10,11},{11,10},{4,5},{5,4},{1... | collective-permute-start | bytes 786440 | tf_op jit(solution)/shard_map/ppermute | solution.py:381
  83.9 8.5 %collective-permute-start.7 = (f32[256,256]{1,0:T(8,128)}, f32[256,256]{1,0:T(8,128)}, u32[]{:S(2)}, u32[]{:S(2)}) collective-permute-start(f32[256,256]{1,0:T(8,128)} %get-tuple-element.92), channel_id=1, source_target_pairs={{0,8},{1,9},{8,0},{9,1},{2,10},{3,11},{10,2},{11,3},{4,12},{5,13},... | collective-permute-start | bytes 786440 | tf_op jit(solution)/shard_map/ppermute | solution.py:381
  84.0 14.1 %collective-permute-start.8 = (f32[256,256]{1,0:T(8,128)}, f32[256,256]{1,0:T(8,128)}, u32[]{:S(2)}, u32[]{:S(2)}) collective-permute-start(f32[256,256]{1,0:T(8,128)} %get-tuple-element.93), channel_id=1, source_target_pairs={{0,9},{1,8},{8,1},{9,0},{2,11},{3,10},{10,3},{11,2},{4,13},{5,12},... | collective-permute-start | bytes 786440 | tf_op jit(solution)/shard_map/ppermute | solution.py:381
  85.8 23.2 %all-to-all-start.5 = ((f32[16,72,256]{2,1,0:T(8,128)}), f32[16,72,256]{2,1,0:T(8,128)}, u32[]{:S(2)}, u32[]{:S(2)}) async-start(f32[16,72,256]{2,1,0:T(8,128)} %get-tuple-element.103), calls=%async_computation.5 | async-start | bytes 2359296 | tf_op jit(solution)/shard_map/all_to_all | solution.py:454
  109.0 19.4 %all-to-all-start.4 = ((f32[16,64,256]{2,1,0:T(8,128)}), f32[16,64,256]{2,1,0:T(8,128)}, u32[]{:S(2)}, u32[]{:S(2)}) async-start(f32[16,64,256]{2,1,0:T(8,128)} %wgradk.1), calls=%async_computation.4 | async-start | bytes 2097152 | tf_op jit(solution)/shard_map/all_to_all | solution.py:462

commit v6 on v5

--- a/solution.py
+++ b/solution.py
@@ -18,6 +18,8 @@
 SEQ = ("x", "y", "c")
 GROUP = ("c", "b")
 VMEM_LIMIT = 64 * 1024 * 1024
+GRANT = {name: 58 << 20 for name in ("turn", "query", "dquery")}
+GRANT.update({name: 4 << 20 for name in ("prefix", "suffix", "final")})
 
 
 def dot(a, b, dims=NN):
@@ -92,8 +94,19 @@
     return [(j, slice(GL * j, GL * j + GL)) for j in range(ref.shape[-1] // GL)]
 
 
-def group_at(j, ref):
-    return pl.program_id(0) * (ref.shape[-1] // GL) + j
+def my_groups(me_ref, step):
+    for i in range(2):
+        at = jnp.bitwise_xor(jnp.bitwise_and(me_ref[0], 1), i)
+        yield (
+            2 * step + i,
+            pl.ds(pl.multiple_of(at * GL, GL), GL),
+            pl.ds(pl.multiple_of(at * 128, 128), 128),
+        )
+
+
+def each_step(body):
+    for step in range(2):
+        pl.when(pl.program_id(0) == step)(functools.partial(body, step))
 
 
 def kv_kernel(nv_ref, tok, wk, wv, fk_o, fv_o, sk_o, st_o):
@@ -161,22 +174,24 @@
 
 def dq_kernel(me_ref, dn, st, fk, fv, sq, gp, dq_o, *send):
     n = dn.shape[0]
-    causal = rows((n, n)) >= lanes((n, n))
-    for j, c in groups_of(dn):
-        s_hi, s_lo = split(unpack_state(st[128 * j:128 * j + 128, :]))
-        d_hi, d_lo = split(dn[:, c])
-        total = dot(d_hi, s_hi, NT) + dot(d_lo, s_hi, NT) + dot(d_hi, s_lo, NT)
-        for m in head_masks((n, GL)):
-            vm = pick(m, fv[:, c])
-            w = pick(causal, dot(d_hi, vm, NT) + dot(d_lo, vm, NT)).astype(BF)
-            total = total + dot(w, pick(m, fk[:, c]))
-        dq = (total * sq[:, c]).astype(BF)
-        dq_o[:, c] = dq
-        for k, out in enumerate(send):
-            @pl.when(group_at(j, dn) == jnp.bitwise_xor(me_ref[0], k))
-            def _():
-                out[0:n, :] = dq.astype(F32)
-                out[n:n + 8, :] = gp[:, c]
+
+    def body(step):
+        causal = rows((n, n)) >= lanes((n, n))
+        for k, c, r in my_groups(me_ref, step):
+            s_hi, s_lo = split(unpack_state(st[r, :]))
+            d_hi, d_lo = split(dn[:, c])
+            total = dot(d_hi, s_hi, NT) + dot(d_lo, s_hi, NT) + dot(d_hi, s_lo, NT)
+            keys, values = fk[:, c], fv[:, c]
+            for m in head_masks((n, GL)):
+                vm = pick(m, values)
+                w = pick(causal, dot(d_hi, vm, NT) + dot(d_lo, vm, NT)).astype(BF)
+                total = total + dot(w, pick(m, keys))
+            dq = (total * sq[:, c]).astype(BF)
+            dq_o[:, c] = dq
+            send[k][0:n, :] = dq.astype(F32)
+            send[k][n:n + 8, :] = gp[:, c]
+
+    each_step(body)
 
 
 def local_k_kernel(dn, fq, fv, lk_o):
@@ -206,15 +221,15 @@
 
 
 def dk_kernel(me_ref, lk, fv, st, sk, dk_o, *send):
-    for j, c in groups_of(lk):
-        r_hi, r_lo = split(unpack_state(st[128 * j:128 * j + 128, :]))
-        total = lk[:, c] + dot(fv[:, c], r_hi, NT) + dot(fv[:, c], r_lo, NT)
-        dk = (total * sk[:, c]).astype(BF)
-        dk_o[:, c] = dk
-        for k, out in enumerate(send):
-            @pl.when(group_at(j, lk) == jnp.bitwise_xor(me_ref[0], k))
-            def _():
-                out[...] = dk.astype(F32)
+    def body(step):
+        for k, c, r in my_groups(me_ref, step):
+            r_hi, r_lo = split(unpack_state(st[r, :]))
+            total = lk[:, c] + dot(fv[:, c], r_hi, NT) + dot(fv[:, c], r_lo, NT)
+            dk = (total * sk[:, c]).astype(BF)
+            dk_o[:, c] = dk
+            send[k][...] = dk.astype(F32)
+
+    each_step(body)
 
 
 def dtok_kernel(lv, fk, st, dq, dk, wq, wk, wv, dt_o, acc):
@@ -238,25 +253,30 @@
         dt_o[...] = acc[...].astype(BF)
 
 
-def wgrad_q_kernel(t0, t1, t2, t3, d0, d1, d2, d3, out, all_o):
+def wgrad_q_kernel(t0, t1, t2, t3, d0, d1, d2, d3, first, rest, all_o):
     n = t0.shape[1]
-    k, m = out.shape[0], out.shape[1] - 8
-    res = jnp.zeros((t0.shape[0], out.shape[2]), F32)
-    gain = jnp.zeros((8, out.shape[2]), F32)
+    k, m = first.shape[0], first.shape[1]
+    left = rest.shape[1] - 8
+    res = jnp.zeros((t0.shape[0], first.shape[2]), F32)
+    gain = jnp.zeros((8, first.shape[2]), F32)
     for i, (t, d) in enumerate(zip((t0, t1, t2, t3), (d0, d1, d2, d3))):
         turned = t[...].astype(BF)
         all_o[:, n * i:n * i + n] = turned
         res = res + dot(turned, d[0:n, :].astype(BF))
         gain = gain + d[n:n + 8, :]
-    out[:, 0:m, :] = res.reshape(k, m, res.shape[1])
+    res = res.reshape(k, m + left, res.shape[1])
+    first[...] = res[:, 0:m, :]
+    rest[:, 0:left, :] = res[:, m:m + left, :]
     for i in range(k):
-        out[i, m:m + 8, :] = gain
-
-
-def wgrad_k_kernel(t, d0, d1, d2, d3, out):
+        rest[i, left:left + 8, :] = gain
+
+
+def wgrad_k_kernel(t, d0, d1, d2, d3, rest, out):
     k, m, w = out.shape
+    left = rest.shape[1]
     d = jnp.concatenate([v[...].astype(BF) for v in (d0, d1, d2, d3)], axis=0)
-    out[...] = dot(t[...], d).reshape(k, m, w)
+    out[:, 0:m - left, :] = dot(t[...], d).reshape(k, m - left, w)
+    out[:, m - left:m, :] = rest[...]
 
 
 def prefix_kernel(backward, v, out):
@@ -276,18 +296,20 @@
 
 
 def join_kernel(q, k, out):
-    ksum = k[0]
+    total = k[0]
     for i in range(1, k.shape[0]):
-        ksum = ksum + k[i]
-    height, width = ksum.shape
-    gain = jnp.sum(q[height:height + 8, :], axis=0, keepdims=True)
+        total = total + k[i]
+    first, width = q.shape
+    each = out.shape[1] // 2
+    height = each * out.shape[0]
+    qsum = jnp.concatenate([q[...], total[height:2 * height - first]], axis=0)
+    gain = jnp.sum(total[2 * height - first:], axis=0, keepdims=True)
     parts = [gain[:, 128 * i:128 * i + 128] for i in range(width // 128)]
-    each = height // out.shape[0]
     parts.append(jnp.zeros((2 * each - len(parts), 128), F32))
     tile = jnp.concatenate(parts, axis=0)
     for j in range(out.shape[0]):
-        out[j, 0:each, 0:width] = q[each * j:each * j + each, :]
-        out[j, each:2 * each, 0:width] = ksum[each * j:each * j + each]
+        out[j, 0:each, 0:width] = qsum[each * j:each * j + each]
+        out[j, each:2 * each, 0:width] = total[each * j:each * j + each]
         out[j, :, width:width + 128] = tile
 
 
@@ -319,7 +341,23 @@
         scratch_shapes=list(scratch),
         name=name,
         cost_estimate=pl.CostEstimate(flops=flops, bytes_accessed=4 << 20, transcendentals=0),
-        compiler_params=pltpu.CompilerParams(vmem_limit_bytes=VMEM_LIMIT),
+        compiler_params=pltpu.CompilerParams(vmem_limit_bytes=GRANT.get(name, VMEM_LIMIT)),
+    )
+
+
+def call_mine(kernel, in_specs, outs, name, flops):
+    return pl.pallas_call(
+        kernel,
+        grid_spec=pltpu.PrefetchScalarGridSpec(
+            num_scalar_prefetch=1,
+            grid=(2,),
+            in_specs=in_specs,
+            out_specs=[spec for _, _, spec in outs],
+        ),
+        out_shape=[jax.ShapeDtypeStruct(s, d) for s, d, _ in outs],
+        name=name,
+        cost_estimate=pl.CostEstimate(flops=flops, bytes_accessed=4 << 20, transcendentals=0),
+        compiler_params=pltpu.CompilerParams(vmem_limit_bytes=GRANT.get(name, VMEM_LIMIT)),
     )
 
 
@@ -336,6 +374,18 @@
 
 def row(r, w):
     return pl.BlockSpec((r, w), lambda g: (g, 0))
+
+
+def pair_at(step, me):
+    return jnp.bitwise_xor(jnp.right_shift(me[0], 1), step)
+
+
+def col_mine(r, w):
+    return pl.BlockSpec((r, w), lambda step, me: (0, pair_at(step, me)))
+
+
+def row_mine(r, w):
+    return pl.BlockSpec((r, w), lambda step, me: (pair_at(step, me), 0))
 
 
 def on_device(tokens, w_query, w_key, w_value, w_out, norm_gain, lengths, d_mixed):
@@ -412,10 +462,11 @@
 
     parts = to_parts(rs)
     dn_3, _ = tie((dn, rs))
-    dq, *dq_send = call(
-        dq_kernel, (halves,),
-        [SMEM, col(n, w), st_spec, col(n, w), col(n, w), col(n, w), col(8, w)],
-        [act(BF)] + [((n + 8, GL), F32, whole((n + 8, GL)))] * ngroup,
+    mine_act = ((n, d), BF, col_mine(n, w))
+    dq, *dq_send = call_mine(
+        dq_kernel,
+        [col_mine(n, w), row_mine(w // 2, 128)] + [col_mine(n, w)] * 3 + [col_mine(8, w)],
+        [mine_act] + [((n + 8, GL), F32, whole((n + 8, GL)))] * ngroup,
         "dquery", 2 * big,
     )(me, dn_3, st_in, fk, fv, sq, gp)
     parts, dq = tie((parts, dq))
@@ -430,22 +481,27 @@
     )(dn_4, fq, fv)
     steps = 2
     per = d // nxy
-    gshape = (nxy, per + 8, GL)
+    first = per // 2
+    gshape = (nxy, first, GL)
+    rshape = (nxy, per - first + 8, GL)
+    in_steps = lambda shape: pl.BlockSpec((nxy // steps,) + shape[1:], lambda g: (g, 0, 0))
     t0, _ = tie((t0, mine))
-    gq, tall = call(
+    gq, rest, tall = call(
         wgrad_q_kernel, (steps,),
         [row(d // steps, n)] * 4 + [whole((n + 8, GL))] * 4,
         [
-            (gshape, F32, pl.BlockSpec((nxy // steps,) + gshape[1:], lambda g: (g, 0, 0))),
+            (gshape, F32, in_steps(gshape)),
+            (rshape, F32, in_steps(rshape)),
             ((d, 4 * n), BF, row(d // steps, 4 * n)),
         ],
         "wgradq", 2 * big,
     )(t0, t1, t2, t3, *dq_got)
     lk, gq = tie((lk, gq))
 
-    dk, *dk_send = call(
-        dk_kernel, (halves,), [SMEM, col(n, w), col(n, w), st_spec, col(n, w)],
-        [act(BF)] + [((n, GL), F32, whole((n, GL)))] * ngroup,
+    dk, *dk_send = call_mine(
+        dk_kernel,
+        [col_mine(n, w), col_mine(n, w), row_mine(w // 2, 128), col_mine(n, w)],
+        [mine_act] + [((n, GL), F32, whole((n, GL)))] * ngroup,
         "dkey", big // 2,
     )(me, lk, fv, r_in, sk)
 
@@ -453,12 +509,12 @@
     gq, dk = tie((gq, dk))
     gq = lax.all_to_all(gq, ("x", "y"), 0, 0, tiled=True)
 
-    kshape = (nxy, per, GL)
+    kshape = (nxy, per + rshape[1], GL)
     (gk,) = call(
-        wgrad_k_kernel, (steps,), [row(d // steps, 4 * n)] + [whole((n, GL))] * 4,
-        [(kshape, F32, pl.BlockSpec((nxy // steps,) + kshape[1:], lambda g: (g, 0, 0)))],
+        wgrad_k_kernel, (steps,), [row(d // steps, 4 * n)] + [whole((n, GL))] * 4 + [in_steps(rshape)],
+        [(kshape, F32, in_steps(kshape))],
         "wgradk", 400 * big,
-    )(tall, *dk_got)
+    )(tall, *dk_got, rest)
     gk_parts = lax.all_to_all(gk, ("x", "y"), 0, 0, tiled=True)
 
     dn_5, dk_5, _ = tie((dn, dk, gk))

time: 152 us -> 149 us (0.980)
  Pallas kernels: 62.7 us -> 59.2 us
    all_to_all x1, waiting for transfers between devices: 2.23 us -> 9.97 us  [on_device(): gk_parts = lax.all_to_all(gk, ('x', 'y'), 0, 0, tiled=True)]
    all_to_all x1, waiting for transfers between devices: 7.57 us -> 0.01 us  [on_device(): gq = lax.all_to_all(gq, ('x', 'y'), 0, 0, tiled=True)]
    pallas_call x2, Pallas kernels: 3.38 us -> 1.49 us  [run(): call(functools.partial(prefix_kernel, backward), (), [whole(shape)], [(sh...]
  transfers between devices with their start and end apart: 15 -> 15, of which waited for: 8 -> 7; matrix products, arithmetic and copies ran while one was open for 0% -> 0% of each run, Pallas kernels for 32% -> 32%
where the time goes in v6:
time: 149 us; the launch traced here: 148 us
  Pallas kernels  59.2 us (40%)
  starting transfers between devices  37.1 us (25%)
  waiting for transfers between devices  30.8 us (21%)
  blocking collectives  19.7 us (13%)
    all_to_all x1, blocking collectives, on_device(): both = lax.all_to_all(both, last, 0, 0, tiled=True)  19.7 us
    all_to_all x2, starting transfers between devices, to_parts(): lax.all_to_all(st.reshape(nseq, st_rows // nseq, 128), SEQ, 0, 0, tiled=T...  12.3 us
    ppermute x9, waiting for transfers between devices, swap(): return lax.ppermute(v, GROUP, [(i, i ^ k) for i in range(ngroup)])  11.3 us
    all_to_all x1, waiting for transfers between devices, on_device(): gk_parts = lax.all_to_all(gk, ('x', 'y'), 0, 0, tiled=True)  9.97 us
    all_to_all x2, starting transfers between devices, from_parts(): return lax.all_to_all(mine, SEQ, 0, 0, tiled=True).reshape(st_rows, 128)  9.93 us
    ppermute x9, starting transfers between devices, swap(): return lax.ppermute(v, GROUP, [(i, i ^ k) for i in range(ngroup)])  6.14 us
    pallas_call x1, Pallas kernels, on_device(): call_mine(dq_kernel, [col_mine(n, w), row_mine(w // 2, 128)] + [col_mine(...  5.98 us
    pallas_call x1, Pallas kernels, on_device(): call(dtok_kernel, (halves,), [col(n, w), col(n, w), st_spec, col(n, w), c...  5.83 us
  transfers between devices with their start and end apart: 15, of which 7 were waited for; matrix products, arithmetic and copies ran while one was open for 0% of the time, Pallas kernels for 32%

profile of v6, /device:TPU:1, one launch (start us, length us, event | category | flops | bytes accessed | tf_op | source)
XLA Modules:
  0.0 148.1 jit_solution(16780288817875004361)
XLA Ops:
  1.3 4.7 %kv.1 = (bf16[256,1024]{1,0:T(8,128)(2,1)}, bf16[256,1024]{1,0:T(8,128)(2,1)}, f32[256,1024]{1,0:T(8,128)}, f32[512,128]{1,0:T(8,128)}) custom-call(s32[1]{0:T(128)S(6)} %sub.7.nv_ref, bf16[256,1024]{1,0:T(8,128)(2,1)} %bitcast.12, bf16[1024,1024]{1,0:T(8,128)(2,1)} %wk.3, bf16[1024,1024]{1,0:T(8,128)(2,1)} %wv.3), custom_call_target="tpu_custom_call" | custom-call | flops 1073741824 | bytes 4194304 | tf_op jit(solution)/shard_map/kv/pallas_call | solution.py:409
  6.0 8.6 %all-to-all-start = ((f32[32,16,128]{2,1,0:T(8,128)}), f32[32,16,128]{2,1,0:T(8,128)S(1)}, u32[]{:S(2)}, u32[]{:S(2)}) async-start(f32[32,16,128]{2,1,0:T(8,128)} %bitcast.18), calls=%async_computation | async-start | bytes 524288 | tf_op jit(solution)/shard_map/all_to_all | solution.py:417
  17.1 3.7 %query.1 = (bf16[256,1024]{1,0:T(8,128)(2,1)}, bf16[1024,256]{1,0:T(8,128)(2,1)}, f32[256,1024]{1,0:T(8,128)}) custom-call(bf16[256,1024]{1,0:T(8,128)(2,1)} %bitcast.14, bf16[1024,1024]{1,0:T(8,128)(2,1)} %wq.3), custom_call_target="tpu_custom_call" | custom-call | flops 536870912 | bytes 4194304 | tf_op jit(solution)/shard_map/query/pallas_call | solution.py:439
  20.8 2.8 %all-to-all-done.v = f32[32,16,128]{2,1,0:T(8,128)S(1)} async-done(((f32[32,16,128]{2,1,0:T(8,128)}), f32[32,16,128]{2,1,0:T(8,128)S(1)}, u32[]{:S(2)}, u32[]{:S(2)}) %all-to-all-start) | async-done | bytes 262176 | tf_op jit(solution)/shard_map/all_to_all | solution.py:417
  26.0 4.9 %all-to-all-start.1 = ((f32[32,16,128]{2,1,0:T(8,128)}), f32[32,16,128]{2,1,0:T(8,128)}, u32[]{:S(2)}, u32[]{:S(2)}) async-start(f32[32,16,128]{2,1,0:T(8,128)} %prefix.1), calls=%async_computation.1 | async-start | bytes 524288 | tf_op jit(solution)/shard_map/all_to_all | solution.py:428
  30.9 5.1 %numer.1 = (f32[256,1024]{1,0:T(8,128)}, f32[256,1024]{1,0:T(8,128)}) custom-call(bf16[256,1024]{1,0:T(8,128)(2,1)} %get-tuple-element.65.fq, bf16[256,1024]{1,0:T(8,128)(2,1)} %get-tuple-element.66.fk, bf16[256,1024]{1,0:T(8,128)(2,1)} %get-tuple-element.67.fv, bf16[256,1024]{1,0:T(8,128)(2,1)} %bitcast.16, bf16[1024,1024]{1,0:T(8,128)(2,1)} %wo.3), custom_call_target="tpu_custom_call" | custom-call | flops 1073741824 | bytes 4194304 | tf_op jit(solution)/shard_map/numer/pallas_call | solution.py:451
  36.0 3.9 %all-to-all-done.1 = f32[32,16,128]{2,1,0:T(8,128)} async-done(((f32[32,16,128]{2,1,0:T(8,128)}), f32[32,16,128]{2,1,0:T(8,128)}, u32[]{:S(2)}, u32[]{:S(2)}) %all-to-all-start.1) | async-done | bytes 262176 | tf_op jit(solution)/shard_map/all_to_all | solution.py:428
  39.9 5.1 %norm.1 = (bf16[256,1024]{1,0:T(8,128)(2,1)}, f32[256,1024]{1,0:T(8,128)}, f32[512,128]{1,0:T(8,128)}, f32[8,1024]{1,0:T(8,128)}) custom-call(s32[1]{0:T(128)S(6)} %sub.7.nv_ref, f32[256,1024]{1,0:T(8,128)} %get-tuple-element.68.nl, f32[512,128]{1,0:T(8,128)} %bitcast.4.st, bf16[256,1024]{1,0:T(8,128)(2,1)} %get-tuple-element.65.fq, ...), custom_call_target="tpu_custom_call" | custom-call | flops 536870912 | bytes 4194304 | tf_op jit(solution)/shard_map/norm/pallas_call | solution.py:457
  45.1 3.7 %all-to-all-start.2 = ((f32[32,16,128]{2,1,0:T(8,128)}), f32[32,16,128]{2,1,0:T(8,128)S(1)}, u32[]{:S(2)}, u32[]{:S(2)}) async-start(f32[32,16,128]{2,1,0:T(8,128)} %bitcast.17), calls=%async_computation.2 | async-start | bytes 524288 | tf_op jit(solution)/shard_map/all_to_all | solution.py:417
  49.2 6.0 %dquery.1 = (bf16[256,1024]{1,0:T(8,128)(2,1)}, f32[264,256]{1,0:T(8,128)}, f32[264,256]{1,0:T(8,128)}, f32[264,256]{1,0:T(8,128)}, f32[264,256]{1,0:T(8,128)}) custom-call(s32[1]{0:T(128)} %bitcast.7.me_ref, f32[256,1024]{1,0:T(8,128)} %get-tuple-element.100.dn, f32[512,128]{1,0:T(8,128)} %bitcast.4.st, bf16[256,1024]{1,0:T(8,128)(2,1)} %get-tuple-element.66.fk, ...), custom_call_target="tpu_custom_call" | custom-call | flops 1073741824 | bytes 4194304 | tf_op jit(solution)/shard_map/dquery/pallas_call | solution.py:466
  55.2 2.7 %all-to-all-done.2.v = f32[32,16,128]{2,1,0:T(8,128)S(1)} async-done(((f32[32,16,128]{2,1,0:T(8,128)}), f32[32,16,128]{2,1,0:T(8,128)S(1)}, u32[]{:S(2)}, u32[]{:S(2)}) %all-to-all-start.2) | async-done | bytes 262176 | tf_op jit(solution)/shard_map/all_to_all | solution.py:417
  60.8 5.1 %all-to-all-start.3 = ((f32[32,16,128]{2,1,0:T(8,128)}), f32[32,16,128]{2,1,0:T(8,128)}, u32[]{:S(2)}, u32[]{:S(2)}) async-start(f32[32,16,128]{2,1,0:T(8,128)} %suffix.1), calls=%async_computation.3 | async-start | bytes 524288 | tf_op jit(solution)/shard_map/all_to_all | solution.py:428
  65.8 4.4 %localk.1.lk = f32[256,1024]{1,0:T(8,128)} custom-call(f32[256,1024]{1,0:T(8,128)} %get-tuple-element.100.dn, bf16[256,1024]{1,0:T(8,128)(2,1)} %get-tuple-element.65.fq, bf16[256,1024]{1,0:T(8,128)(2,1)} %get-tuple-element.67.fv), custom_call_target="tpu_custom_call" | custom-call | flops 1073741824 | bytes 4194304 | tf_op jit(solution)/shard_map/localk/pallas_call | solution.py:479
  70.2 3.2 %collective-permute-done.5.d3 = f32[264,256]{1,0:T(8,128)} collective-permute-done((f32[264,256]{1,0:T(8,128)}, f32[264,256]{1,0:T(8,128)}, u32[]{:S(2)}, u32[]{:S(2)}) %collective-permute-start.5) | collective-permute-done | bytes 270368 | tf_op jit(solution)/shard_map/ppermute | solution.py:431
  73.4 4.1 %wgradq.1 = (f32[16,32,256]{2,1,0:T(8,128)}, f32[16,40,256]{2,1,0:T(8,128)}, bf16[1024,1024]{1,0:T(8,128)(2,1)}) custom-call(bf16[1024,256]{1,0:T(8,128)(2,1)} %get-tuple-element.78.t0, f32[1024,256]{1,0:T(8,128)} %collective-permute-done.t1, f32[1024,256]{1,0:T(8,128)} %collective-permute-done.1.t2, f32[1024,256]{1,0:T(8,128)} %collective-permute-done.2.t3, ...), custom_call_target="tpu_custom_call" | custom-call | flops 1073741824 | bytes 4194304 | tf_op jit(solution)/shard_map/wgradq/pallas_call | solution.py:489
  77.5 3.2 %dkey.1 = (bf16[256,1024]{1,0:T(8,128)(2,1)}, f32[256,256]{1,0:T(8,128)}, f32[256,256]{1,0:T(8,128)}, f32[256,256]{1,0:T(8,128)}, f32[256,256]{1,0:T(8,128)}) custom-call(s32[1]{0:T(128)} %bitcast.7.me_ref, f32[256,1024]{1,0:T(8,128)} %localk.1.lk, bf16[256,1024]{1,0:T(8,128)(2,1)} %get-tuple-element.67.fv, f32[512,128]{1,0:T(8,128)} %bitcast.8.st, ...), custom_call_target="tpu_custom_call" | custom-call | flops 268435456 | bytes 4194304 | tf_op jit(solution)/shard_map/dkey/pallas_call | solution.py:501
  82.7 4.3 %all-to-all-start.5 = ((f32[16,32,256]{2,1,0:T(8,128)}), f32[16,32,256]{2,1,0:T(8,128)}, u32[]{:S(2)}, u32[]{:S(2)}) async-start(f32[16,32,256]{2,1,0:T(8,128)} %get-tuple-element.105), calls=%async_computation.5 | async-start | bytes 1048576 | tf_op jit(solution)/shard_map/all_to_all | solution.py:510
  89.4 5.7 %collective-permute-done.8.d3 = f32[256,256]{1,0:T(8,128)} collective-permute-done((f32[256,256]{1,0:T(8,128)}, f32[256,256]{1,0:T(8,128)}, u32[]{:S(2)}, u32[]{:S(2)}) %collective-permute-start.8) | collective-permute-done | bytes 262176 | tf_op jit(solution)/shard_map/ppermute | solution.py:431
  95.1 3.4 %wgradk.1 = f32[16,104,256]{2,1,0:T(8,128)} custom-call(bf16[1024,1024]{1,0:T(8,128)(2,1)} %get-tuple-element.86.t, f32[256,256]{1,0:T(8,128)} %get-tuple-element.91.d0, f32[256,256]{1,0:T(8,128)} %collective-permute-done.6.d1, f32[256,256]{1,0:T(8,128)} %collective-permute-done.7.d2, f32[256,256]{1,0:T(8,128)} %collective-permute-done.8.d3, ...), custom_call_target="tpu_custom_call" | custom-call | flops 214748364800 | bytes 4194304 | tf_op jit(solution)/shard_map/wgradk/pallas_call | solution.py:513
  98.5 4.4 %all-to-all-start.4 = ((f32[16,104,256]{2,1,0:T(8,128)}), f32[16,104,256]{2,1,0:T(8,128)}, u32[]{:S(2)}, u32[]{:S(2)}) async-start(f32[16,104,256]{2,1,0:T(8,128)} %wgradk.1), calls=%async_computation.4 | async-start | bytes 3407872 | tf_op jit(solution)/shard_map/all_to_all | solution.py:518
  103.0 5.1 %localv.1 = (bf16[256,1024]{1,0:T(8,128)(2,1)}, f32[256,1024]{1,0:T(8,128)}) custom-call(bf16[256,1024]{1,0:T(8,128)(2,1)} %get-tuple-element.96.at, bf16[1024,1024]{1,0:T(8,128)(2,1)} %wo.3, f32[256,1024]{1,0:T(8,128)} %get-tuple-element.100.dn, bf16[256,1024]{1,0:T(8,128)(2,1)} %get-tuple-element.65.fq, bf16[256,1024]{1,0:T(8,128)(2,1)} %get-tuple-element.66.fk), custom_call_target="tpu_custom_call" | custom-call | flops 2147483648 | bytes 4194304 | tf_op jit(solution)/shard_map/localv/pallas_call | solution.py:521
  108.1 5.8 %dtok.1 = bf16[256,1024]{1,0:T(8,128)(2,1)} custom-call(f32[256,1024]{1,0:T(8,128)} %get-tuple-element.102.lv, bf16[256,1024]{1,0:T(8,128)(2,1)} %get-tuple-element.66.fk, f32[512,128]{1,0:T(8,128)} %bitcast.8.st, bf16[256,1024]{1,0:T(8,128)(2,1)} %get-tuple-element.103.dq, bf16[256,1024]{1,0:T(8,128)(2,1)} %get-tuple-element.104.dk, bf16[1024,1024]{1,0:T(8,128)(2,1)} %wq.3, ...), custom_call_target="tpu_custom_call" | custom-call | flops 2147483648 | bytes 4194304 | tf_op jit(solution)/shard_map/dtok/pallas_call | solution.py:525
  115.6 10.0 %all-to-all-done.4.k = f32[16,104,256]{2,1,0:T(8,128)} async-done(((f32[16,104,256]{2,1,0:T(8,128)}), f32[16,104,256]{2,1,0:T(8,128)}, u32[]{:S(2)}, u32[]{:S(2)}) %all-to-all-start.4) | async-done | bytes 1703968 | tf_op jit(solution)/shard_map/all_to_all | solution.py:518
  127.8 19.7 %all_to_all.35.v = f32[16,8,384]{2,1,0:T(8,128)S(1)} all-to-all(f32[16,8,384]{2,1,0:T(8,128)} %join.1), channel_id=1, replica_groups=mesh['x'=4,'y'=4,'c'=2,'w'=4,'b'=2] {'c','w','b'}, dimensions={0} | all-to-all | bytes 393216 | tf_op jit(solution)/shard_map/all_to_all | solution.py:544
  (24 shorter events, 17.0 us)
Async XLA Ops:
  6.0 17.6 %all-to-all-start = ((f32[32,16,128]{2,1,0:T(8,128)}), f32[32,16,128]{2,1,0:T(8,128)S(1)}, u32[]{:S(2)}, u32[]{:S(2)}) async-start(f32[32,16,128]{2,1,0:T(8,128)} %bitcast.18), calls=%async_computation | async-start | bytes 524288 | tf_op jit(solution)/shard_map/all_to_all | solution.py:417
  24.4 34.3 %collective-permute-start = (f32[1024,256]{1,0:T(8,128)}, f32[1024,256]{1,0:T(8,128)}, u32[]{:S(2)}, u32[]{:S(2)}) collective-permute-start(f32[1024,256]{1,0:T(8,128)} %get-tuple-element.80), channel_id=1, source_target_pairs={{0,1},{1,0},{8,9},{9,8},{2,3},{3,2},{10,11},{11,10},{4,5},{5,4},{1... | collective-permute-start | bytes 3145736 | tf_op jit(solution)/shard_map/ppermute | solution.py:431
  26.0 13.9 %all-to-all-start.1 = ((f32[32,16,128]{2,1,0:T(8,128)}), f32[32,16,128]{2,1,0:T(8,128)}, u32[]{:S(2)}, u32[]{:S(2)}) async-start(f32[32,16,128]{2,1,0:T(8,128)} %prefix.1), calls=%async_computation.1 | async-start | bytes 524288 | tf_op jit(solution)/shard_map/all_to_all | solution.py:428
  45.1 12.8 %all-to-all-start.2 = ((f32[32,16,128]{2,1,0:T(8,128)}), f32[32,16,128]{2,1,0:T(8,128)S(1)}, u32[]{:S(2)}, u32[]{:S(2)}) async-start(f32[32,16,128]{2,1,0:T(8,128)} %bitcast.17), calls=%async_computation.2 | async-start | bytes 524288 | tf_op jit(solution)/shard_map/all_to_all | solution.py:417
  48.8 24.6 %collective-permute-start.1 = (f32[1024,256]{1,0:T(8,128)}, f32[1024,256]{1,0:T(8,128)}, u32[]{:S(2)}, u32[]{:S(2)}) collective-permute-start(f32[1024,256]{1,0:T(8,128)} %get-tuple-element.80), channel_id=1, source_target_pairs={{0,8},{1,9},{8,0},{9,1},{2,10},{3,11},{10,2},{11,3},{4,12},{5,13},... | collective-permute-start | bytes 3145736 | tf_op jit(solution)/shard_map/ppermute | solution.py:431
  58.6 14.8 %collective-permute-start.2 = (f32[1024,256]{1,0:T(8,128)}, f32[1024,256]{1,0:T(8,128)}, u32[]{:S(2)}, u32[]{:S(2)}) collective-permute-start(f32[1024,256]{1,0:T(8,128)} %collective-permute-done.t1), channel_id=1, source_target_pairs={{0,8},{1,9},{8,0},{9,1},{2,10},{3,11},{10,2},{11,3},{4,12},{5,13},... | collective-permute-start | bytes 3145736 | tf_op jit(solution)/shard_map/ppermute | solution.py:431
  58.8 11.4 %collective-permute-start.3 = (f32[264,256]{1,0:T(8,128)}, f32[264,256]{1,0:T(8,128)}, u32[]{:S(2)}, u32[]{:S(2)}) collective-permute-start(f32[264,256]{1,0:T(8,128)} %get-tuple-element.83), channel_id=1, source_target_pairs={{0,1},{1,0},{8,9},{9,8},{2,3},{3,2},{10,11},{11,10},{4,5},{5,4},{1... | collective-permute-start | bytes 811016 | tf_op jit(solution)/shard_map/ppermute | solution.py:431
  58.8 11.4 %collective-permute-start.4 = (f32[264,256]{1,0:T(8,128)}, f32[264,256]{1,0:T(8,128)}, u32[]{:S(2)}, u32[]{:S(2)}) collective-permute-start(f32[264,256]{1,0:T(8,128)} %get-tuple-element.84), channel_id=1, source_target_pairs={{0,8},{1,9},{8,0},{9,1},{2,10},{3,11},{10,2},{11,3},{4,12},{5,13},... | collective-permute-start | bytes 811016 | tf_op jit(solution)/shard_map/ppermute | solution.py:431
  59.3 14.2 %collective-permute-start.5 = (f32[264,256]{1,0:T(8,128)}, f32[264,256]{1,0:T(8,128)}, u32[]{:S(2)}, u32[]{:S(2)}) collective-permute-start(f32[264,256]{1,0:T(8,128)} %get-tuple-element.85), channel_id=1, source_target_pairs={{0,9},{1,8},{8,1},{9,0},{2,11},{3,10},{10,3},{11,2},{4,13},{5,12},... | collective-permute-start | bytes 811016 | tf_op jit(solution)/shard_map/ppermute | solution.py:431
  60.8 16.7 %all-to-all-start.3 = ((f32[32,16,128]{2,1,0:T(8,128)}), f32[32,16,128]{2,1,0:T(8,128)}, u32[]{:S(2)}, u32[]{:S(2)}) async-start(f32[32,16,128]{2,1,0:T(8,128)} %suffix.1), calls=%async_computation.3 | async-start | bytes 524288 | tf_op jit(solution)/shard_map/all_to_all | solution.py:428
  80.8 8.6 %collective-permute-start.6 = (f32[256,256]{1,0:T(8,128)}, f32[256,256]{1,0:T(8,128)}, u32[]{:S(2)}, u32[]{:S(2)}) collective-permute-start(f32[256,256]{1,0:T(8,128)} %get-tuple-element.92), channel_id=1, source_target_pairs={{0,1},{1,0},{8,9},{9,8},{2,3},{3,2},{10,11},{11,10},{4,5},{5,4},{1... | collective-permute-start | bytes 786440 | tf_op jit(solution)/shard_map/ppermute | solution.py:431
  80.8 8.5 %collective-permute-start.7 = (f32[256,256]{1,0:T(8,128)}, f32[256,256]{1,0:T(8,128)}, u32[]{:S(2)}, u32[]{:S(2)}) collective-permute-start(f32[256,256]{1,0:T(8,128)} %get-tuple-element.93), channel_id=1, source_target_pairs={{0,8},{1,9},{8,0},{9,1},{2,10},{3,11},{10,2},{11,3},{4,12},{5,13},... | collective-permute-start | bytes 786440 | tf_op jit(solution)/shard_map/ppermute | solution.py:431
  80.9 14.1 %collective-permute-start.8 = (f32[256,256]{1,0:T(8,128)}, f32[256,256]{1,0:T(8,128)}, u32[]{:S(2)}, u32[]{:S(2)}) collective-permute-start(f32[256,256]{1,0:T(8,128)} %get-tuple-element.94), channel_id=1, source_target_pairs={{0,9},{1,8},{8,1},{9,0},{2,11},{3,10},{10,3},{11,2},{4,13},{5,12},... | collective-permute-start | bytes 786440 | tf_op jit(solution)/shard_map/ppermute | solution.py:431
  82.7 15.8 %all-to-all-start.5 = ((f32[16,32,256]{2,1,0:T(8,128)}), f32[16,32,256]{2,1,0:T(8,128)}, u32[]{:S(2)}, u32[]{:S(2)}) async-start(f32[16,32,256]{2,1,0:T(8,128)} %get-tuple-element.105), calls=%async_computation.5 | async-start | bytes 1048576 | tf_op jit(solution)/shard_map/all_to_all | solution.py:510
  98.5 27.0 %all-to-all-start.4 = ((f32[16,104,256]{2,1,0:T(8,128)}), f32[16,104,256]{2,1,0:T(8,128)}, u32[]{:S(2)}, u32[]{:S(2)}) async-start(f32[16,104,256]{2,1,0:T(8,128)} %wgradk.1), calls=%async_computation.4 | async-start | bytes 3407872 | tf_op jit(solution)/shard_map/all_to_all | solution.py:518

commit v7 on v6

--- a/solution.py
+++ b/solution.py
@@ -253,30 +253,34 @@
         dt_o[...] = acc[...].astype(BF)
 
 
-def wgrad_q_kernel(t0, t1, t2, t3, d0, d1, d2, d3, first, rest, all_o):
-    n = t0.shape[1]
-    k, m = first.shape[0], first.shape[1]
-    left = rest.shape[1] - 8
-    res = jnp.zeros((t0.shape[0], first.shape[2]), F32)
-    gain = jnp.zeros((8, first.shape[2]), F32)
+def wgrad_q_kernel(y_ref, t0, t1, t2, t3, d0, d1, d2, d3, all_o, *send):
+    n = t0.shape[3]
+    blocks, m = t0.shape[0], t0.shape[2]
+    res = jnp.zeros((blocks * m, d0.shape[1]), F32)
+    gain = jnp.zeros((8, d0.shape[1]), F32)
     for i, (t, d) in enumerate(zip((t0, t1, t2, t3), (d0, d1, d2, d3))):
-        turned = t[...].astype(BF)
-        all_o[:, n * i:n * i + n] = turned
+        turned = t[...].reshape(blocks * m, n).astype(BF)
+        all_o[:, :, :, n * i:n * i + n] = turned.reshape(blocks, 1, m, n)
         res = res + dot(turned, d[0:n, :].astype(BF))
         gain = gain + d[n:n + 8, :]
-    res = res.reshape(k, m + left, res.shape[1])
-    first[...] = res[:, 0:m, :]
-    rest[:, 0:left, :] = res[:, m:m + left, :]
-    for i in range(k):
-        rest[i, left:left + 8, :] = gain
-
-
-def wgrad_k_kernel(t, d0, d1, d2, d3, rest, out):
+    for k, out in enumerate(send):
+        @pl.when(pl.program_id(0) == k)
+        def _():
+            out[:, 0:m, :] = res.reshape(blocks, m, res.shape[1])
+            for i in range(blocks):
+                out[i, m:m + 8, :] = gain
+
+
+def sum_y_kernel(x_ref, v0, v1, v2, v3, *send):
+    for k, out in enumerate(send):
+        at = jnp.bitwise_xor(x_ref[0], k)
+        out[...] = v0[at] + v1[at] + v2[at] + v3[at]
+
+
+def wgrad_k_kernel(t, d0, d1, d2, d3, out):
     k, m, w = out.shape
-    left = rest.shape[1]
     d = jnp.concatenate([v[...].astype(BF) for v in (d0, d1, d2, d3)], axis=0)
-    out[:, 0:m - left, :] = dot(t[...], d).reshape(k, m - left, w)
-    out[:, m - left:m, :] = rest[...]
+    out[...] = dot(t[...], d).reshape(k, m, w)
 
 
 def prefix_kernel(backward, v, out):
@@ -288,27 +292,19 @@
         total = total + v[i]
 
 
-def sum_kernel(v, out):
-    total = v[0]
-    for i in range(1, v.shape[0]):
-        total = total + v[i]
-    out[...] = total
-
-
-def join_kernel(q, k, out):
+def join_kernel(q0, q1, q2, q3, k, out):
     total = k[0]
     for i in range(1, k.shape[0]):
         total = total + k[i]
-    first, width = q.shape
+    height, width = total.shape
     each = out.shape[1] // 2
-    height = each * out.shape[0]
-    qsum = jnp.concatenate([q[...], total[height:2 * height - first]], axis=0)
-    gain = jnp.sum(total[2 * height - first:], axis=0, keepdims=True)
+    q = q0[...] + q1[...] + q2[...] + q3[...]
+    gain = jnp.sum(q[height:height + 8], axis=0, keepdims=True)
     parts = [gain[:, 128 * i:128 * i + 128] for i in range(width // 128)]
     parts.append(jnp.zeros((2 * each - len(parts), 128), F32))
     tile = jnp.concatenate(parts, axis=0)
     for j in range(out.shape[0]):
-        out[j, 0:each, 0:width] = qsum[each * j:each * j + each]
+        out[j, 0:each, 0:width] = q[each * j:each * j + each]
         out[j, each:2 * each, 0:width] = total[each * j:each * j + each]
         out[j, :, width:width + 128] = tile
 
@@ -345,12 +341,12 @@
     )
 
 
-def call_mine(kernel, in_specs, outs, name, flops):
+def call_mine(kernel, in_specs, outs, name, flops, steps=2):
     return pl.pallas_call(
         kernel,
         grid_spec=pltpu.PrefetchScalarGridSpec(
             num_scalar_prefetch=1,
-            grid=(2,),
+            grid=(steps,),
             in_specs=in_specs,
             out_specs=[spec for _, _, spec in outs],
         ),
@@ -398,7 +394,8 @@
     nxy = lax.axis_size(("x", "y"))
     ngroup = lax.axis_size(GROUP)
     nv = lengths - lax.axis_index(SEQ) * n
-    me = jnp.full((1,), lax.axis_index(GROUP), jnp.int32)
+    own = lambda axes: jnp.full((1,), lax.axis_index(axes), jnp.int32)
+    me = own(GROUP)
     gain = norm_gain.reshape(1, d)
     act = lambda dt: ((n, d), dt, col(n, w))
     st_rows = d // 2
@@ -429,6 +426,9 @@
 
     def swap(v, k):
         return lax.ppermute(v, GROUP, [(i, i ^ k) for i in range(ngroup)])
+
+    def turn_about(axis, v, k):
+        return lax.ppermute(v, axis, [(i, i ^ k) for i in range(lax.axis_size(axis))])
 
     parts = to_parts(st1)
     tok_1, _ = tie((tok, st1))
@@ -477,70 +477,68 @@
     dn_4, t1, _ = tie((dn, t1, mine))
     t3 = swap(t1, 2)
     (lk,) = call(
-        local_k_kernel, (halves,), [col(n, w), col(n, w), col(n, w)], [act(F32)], "localk", 2 * big,
+        local_k_kernel, (halves,), [col(n, w), col(n, w), col(n, w)], [act(F32)], "localk", 1,
     )(dn_4, fq, fv)
-    steps = 2
-    per = d // nxy
-    first = per // 2
-    gshape = (nxy, first, GL)
-    rshape = (nxy, per - first + 8, GL)
-    in_steps = lambda shape: pl.BlockSpec((nxy // steps,) + shape[1:], lambda g: (g, 0, 0))
-    t0, _ = tie((t0, mine))
-    gq, rest, tall = call(
-        wgrad_q_kernel, (steps,),
-        [row(d // steps, n)] * 4 + [whole((n + 8, GL))] * 4,
-        [
-            (gshape, F32, in_steps(gshape)),
-            (rshape, F32, in_steps(rshape)),
-            ((d, 4 * n), BF, row(d // steps, 4 * n)),
-        ],
-        "wgradq", 2 * big,
-    )(t0, t1, t2, t3, *dq_got)
-    lk, gq = tie((lk, gq))
-
     dk, *dk_send = call_mine(
         dk_kernel,
         [col_mine(n, w), col_mine(n, w), row_mine(w // 2, 128), col_mine(n, w)],
         [mine_act] + [((n, GL), F32, whole((n, GL)))] * ngroup,
-        "dkey", big // 2,
+        "dkey", 1,
     )(me, lk, fv, r_in, sk)
 
     dk_got = [dk_send[0]] + [swap(dk_send[k], k) for k in range(1, ngroup)]
-    gq, dk = tie((gq, dk))
-    gq = lax.all_to_all(gq, ("x", "y"), 0, 0, tiled=True)
-
-    kshape = (nxy, per + rshape[1], GL)
+    side = lax.axis_size("x")
+    per = d // nxy
+    dq_got, _ = tie((dq_got, dk))
+    at_y = lambda depth: pl.BlockSpec(
+        (side, 1, per, depth), lambda k, y: (0, jnp.bitwise_xor(y[0], k), 0, 0)
+    )
+    by_xy = lambda v: v.reshape(side, side, per, v.shape[-1])
+    qshape = (side, per + 8, GL)
+    tall, *gq_send = call_mine(
+        wgrad_q_kernel,
+        [at_y(n)] * 4 + [whole((n + 8, GL))] * 4,
+        [((side, side, per, 4 * n), BF, at_y(4 * n))] + [(qshape, F32, whole(qshape))] * side,
+        "wgradq", 2 * big, side,
+    )(own("y"), by_xy(t0), by_xy(t1), by_xy(t2), by_xy(t3), *dq_got)
+    gq_got = [gq_send[0]] + [turn_about("y", gq_send[k], k) for k in range(1, side)]
+
+    steps = 2
+    kshape = (nxy, per, GL)
     (gk,) = call(
-        wgrad_k_kernel, (steps,), [row(d // steps, 4 * n)] + [whole((n, GL))] * 4 + [in_steps(rshape)],
-        [(kshape, F32, in_steps(kshape))],
+        wgrad_k_kernel, (steps,), [row(d // steps, 4 * n)] + [whole((n, GL))] * 4,
+        [(kshape, F32, pl.BlockSpec((nxy // steps,) + kshape[1:], lambda g: (g, 0, 0)))],
         "wgradk", 400 * big,
-    )(tall, *dk_got, rest)
+    )(tall.reshape(d, 4 * n), *dk_got)
     gk_parts = lax.all_to_all(gk, ("x", "y"), 0, 0, tiled=True)
 
     dn_5, dk_5, _ = tie((dn, dk, gk))
     mo, lv = call(
         local_v_kernel, (halves,),
-        [whole((n, d)), col(d, w), col(n, w), col(n, w), col(n, w)], [act(BF), act(F32)], "localv", 4 * big,
+        [whole((n, d)), col(d, w), col(n, w), col(n, w), col(n, w)], [act(BF), act(F32)], "localv", 400 * big,
     )(at, w_out, dn_5, fq, fk)
     (dt,) = call(
         dtok_kernel, (halves,),
         [col(n, w), col(n, w), st_spec, col(n, w), col(n, w), col(d, w), col(d, w), col(d, w)],
-        [((n, d), BF, whole((n, d)))], "dtok", 4 * big,
+        [((n, d), BF, whole((n, d)))], "dtok", 1,
         scratch=[pltpu.VMEM((n, d), F32)],
     )(lv, fk, r_in, dq, dk_5, w_query, w_key, w_value)
-    (gq_sum,) = call(
-        sum_kernel, (), [whole(gshape)], [(gshape[1:], F32, whole(gshape[1:]))], "sumq", 1 << 22
-    )(gq)
-    gk_parts, mo, dt, gq_sum = tie((gk_parts, mo, dt, gq_sum))
+    gq_got, _ = tie((gq_got, gk))
+    gq_send = call(
+        sum_y_kernel, (), [SMEM] + [whole(qshape)] * side,
+        [(qshape[1:], F32, whole(qshape[1:]))] * side, "sumy", 1 << 22,
+    )(own("x"), *gq_got)
+    gq_got = [gq_send[0]] + [turn_about("x", gq_send[k], k) for k in range(1, side)]
+    gk_parts, mo, dt, gq_got = tie((gk_parts, mo, dt, gq_got))
 
     last = ("c", "w", "b")
     nlast = lax.axis_size(last)
     each = per // nlast
     jshape = (nlast, 2 * each, GL + 128)
     (both,) = call(
-        join_kernel, (), [whole(gshape[1:]), whole(kshape)], [(jshape, F32, whole(jshape))],
-        "join", 1 << 22,
-    )(gq_sum, gk_parts)
+        join_kernel, (), [whole(qshape[1:])] * side + [whole(kshape)],
+        [(jshape, F32, whole(jshape))], "join", 1 << 22,
+    )(*gq_got, gk_parts)
     both = lax.all_to_all(both, last, 0, 0, tiled=True)
     dw, dg = call(
         final_kernel, (), [whole(jshape)],

time: 149 us -> 144 us (0.966)
  waiting for transfers between devices: 30.8 us -> 20.3 us
  starting transfers between devices: 37.1 us -> 40.6 us
    all_to_all x1, waiting for transfers between devices: 9.97 us -> 0.01 us  [on_device(): gk_parts = lax.all_to_all(gk, ('x', 'y'), 0, 0, tiled=True)]
    ppermute x9, waiting for transfers between devices: 11.3 us -> 2.94 us  [swap(): return lax.ppermute(v, GROUP, [(i, i ^ k) for i in range(ngroup)])]
    ppermute x0 -> x6, starting transfers between devices: none -> 7.8 us  [turn_about(): lax.ppermute(v, axis, [(i, i ^ k) for i in range(lax.axis_size(axis))])]
    all_to_all x2, waiting for transfers between devices: 3.93 us -> 8.64 us  [from_parts(): return lax.all_to_all(mine, SEQ, 0, 0, tiled=True).reshape(st_rows, 128)]
    all_to_all x1 -> x0, starting transfers between devices: 4.26 us -> none  [on_device(): gq = lax.all_to_all(gq, ('x', 'y'), 0, 0, tiled=True)]
    ppermute x0 -> x6, waiting for transfers between devices: none -> 3.23 us  [turn_about(): lax.ppermute(v, axis, [(i, i ^ k) for i in range(lax.axis_size(axis))])]
    pallas_call x3, Pallas kernels: 7.99 us -> 9.61 us  [the longest x1 5.45 us: on_device(): call_mine(wgrad_q_kernel, [at_y(n)] * 4 + [whole((n + 8, GL))] * 4, [((si...]
  transfers between devices with their start and end apart: 15 -> 20, of which waited for: 7 -> 7; matrix products, arithmetic and copies ran while one was open for 0% -> 0% of each run, Pallas kernels for 32% -> 37%
where the time goes in v7:
time: 144 us; the launch traced here: 143 us
  Pallas kernels  60.6 us (42%)
  starting transfers between devices  40.6 us (28%)
  blocking collectives  20.4 us (14%)
  waiting for transfers between devices  20.3 us (14%)
    all_to_all x1, blocking collectives, on_device(): both = lax.all_to_all(both, last, 0, 0, tiled=True)  20.4 us
    all_to_all x2, starting transfers between devices, to_parts(): lax.all_to_all(st.reshape(nseq, st_rows // nseq, 128), SEQ, 0, 0, tiled=T...  12.3 us
    all_to_all x2, starting transfers between devices, from_parts(): return lax.all_to_all(mine, SEQ, 0, 0, tiled=True).reshape(st_rows, 128)  9.94 us
    all_to_all x2, waiting for transfers between devices, from_parts(): return lax.all_to_all(mine, SEQ, 0, 0, tiled=True).reshape(st_rows, 128)  8.64 us
    ppermute x6, starting transfers between devices, turn_about(): lax.ppermute(v, axis, [(i, i ^ k) for i in range(lax.axis_size(axis))])  7.8 us
    ppermute x9, starting transfers between devices, swap(): return lax.ppermute(v, GROUP, [(i, i ^ k) for i in range(ngroup)])  6.21 us
    pallas_call x1, Pallas kernels, on_device(): call_mine(dq_kernel, [col_mine(n, w), row_mine(w // 2, 128)] + [col_mine(...  5.96 us
    pallas_call x1, Pallas kernels, on_device(): call(dtok_kernel, (halves,), [col(n, w), col(n, w), st_spec, col(n, w), c...  5.88 us
  transfers between devices with their start and end apart: 20, of which 7 were waited for; matrix products, arithmetic and copies ran while one was open for 0% of the time, Pallas kernels for 37%

profile of v7, /device:TPU:1, one launch (start us, length us, event | category | flops | bytes accessed | tf_op | source)
XLA Modules:
  0.0 143.4 jit_solution(2067983399476441928)
XLA Ops:
  1.3 4.8 %kv.1 = (bf16[256,1024]{1,0:T(8,128)(2,1)}, bf16[256,1024]{1,0:T(8,128)(2,1)}, f32[256,1024]{1,0:T(8,128)}, f32[512,128]{1,0:T(8,128)}) custom-call(s32[1]{0:T(128)S(6)} %sub.7.nv_ref, bf16[256,1024]{1,0:T(8,128)(2,1)} %bitcast.19, bf16[1024,1024]{1,0:T(8,128)(2,1)} %wk.3, bf16[1024,1024]{1,0:T(8,128)(2,1)} %wv.3), custom_call_target="tpu_custom_call" | custom-call | flops 1073741824 | bytes 4194304 | tf_op jit(solution)/shard_map/kv/pallas_call | solution.py:406
  6.0 8.6 %all-to-all-start = ((f32[32,16,128]{2,1,0:T(8,128)}), f32[32,16,128]{2,1,0:T(8,128)S(1)}, u32[]{:S(2)}, u32[]{:S(2)}) async-start(f32[32,16,128]{2,1,0:T(8,128)} %bitcast.26), calls=%async_computation | async-start | bytes 524288 | tf_op jit(solution)/shard_map/all_to_all | solution.py:414
  14.6 2.5 %turn.1 = (bf16[1024,256]{1,0:T(8,128)(2,1)}, f32[1024,256]{1,0:T(8,128)}) custom-call(bf16[256,1024]{1,0:T(8,128)(2,1)} %bitcast.20), custom_call_target="tpu_custom_call" | custom-call | flops 134217728 | bytes 4194304 | tf_op jit(solution)/shard_map/turn/pallas_call | solution.py:435
  17.1 3.7 %query.1 = (bf16[256,1024]{1,0:T(8,128)(2,1)}, bf16[1024,256]{1,0:T(8,128)(2,1)}, f32[256,1024]{1,0:T(8,128)}) custom-call(bf16[256,1024]{1,0:T(8,128)(2,1)} %bitcast.21, bf16[1024,1024]{1,0:T(8,128)(2,1)} %wq.3), custom_call_target="tpu_custom_call" | custom-call | flops 536870912 | bytes 4194304 | tf_op jit(solution)/shard_map/query/pallas_call | solution.py:439
  20.8 2.8 %all-to-all-done.v = f32[32,16,128]{2,1,0:T(8,128)S(1)} async-done(((f32[32,16,128]{2,1,0:T(8,128)}), f32[32,16,128]{2,1,0:T(8,128)S(1)}, u32[]{:S(2)}, u32[]{:S(2)}) %all-to-all-start) | async-done | bytes 262176 | tf_op jit(solution)/shard_map/all_to_all | solution.py:414
  26.0 4.9 %all-to-all-start.1 = ((f32[32,16,128]{2,1,0:T(8,128)}), f32[32,16,128]{2,1,0:T(8,128)}, u32[]{:S(2)}, u32[]{:S(2)}) async-start(f32[32,16,128]{2,1,0:T(8,128)} %prefix.1), calls=%async_computation.1 | async-start | bytes 524288 | tf_op jit(solution)/shard_map/all_to_all | solution.py:425
  30.9 5.1 %numer.1 = (f32[256,1024]{1,0:T(8,128)}, f32[256,1024]{1,0:T(8,128)}) custom-call(bf16[256,1024]{1,0:T(8,128)(2,1)} %get-tuple-element.77.fq, bf16[256,1024]{1,0:T(8,128)(2,1)} %get-tuple-element.78.fk, bf16[256,1024]{1,0:T(8,128)(2,1)} %get-tuple-element.79.fv, bf16[256,1024]{1,0:T(8,128)(2,1)} %bitcast.24, bf16[1024,1024]{1,0:T(8,128)(2,1)} %wo.3), custom_call_target="tpu_custom_call" | custom-call | flops 1073741824 | bytes 4194304 | tf_op jit(solution)/shard_map/numer/pallas_call | solution.py:451
  36.0 4.0 %all-to-all-done.1 = f32[32,16,128]{2,1,0:T(8,128)} async-done(((f32[32,16,128]{2,1,0:T(8,128)}), f32[32,16,128]{2,1,0:T(8,128)}, u32[]{:S(2)}, u32[]{:S(2)}) %all-to-all-start.1) | async-done | bytes 262176 | tf_op jit(solution)/shard_map/all_to_all | solution.py:425
  40.0 5.2 %norm.1 = (bf16[256,1024]{1,0:T(8,128)(2,1)}, f32[256,1024]{1,0:T(8,128)}, f32[512,128]{1,0:T(8,128)}, f32[8,1024]{1,0:T(8,128)}) custom-call(s32[1]{0:T(128)S(6)} %sub.7.nv_ref, f32[256,1024]{1,0:T(8,128)} %get-tuple-element.80.nl, f32[512,128]{1,0:T(8,128)} %bitcast.6.st, bf16[256,1024]{1,0:T(8,128)(2,1)} %get-tuple-element.77.fq, ...), custom_call_target="tpu_custom_call" | custom-call | flops 536870912 | bytes 4194304 | tf_op jit(solution)/shard_map/norm/pallas_call | solution.py:457
  45.1 3.7 %all-to-all-start.2 = ((f32[32,16,128]{2,1,0:T(8,128)}), f32[32,16,128]{2,1,0:T(8,128)S(1)}, u32[]{:S(2)}, u32[]{:S(2)}) async-start(f32[32,16,128]{2,1,0:T(8,128)} %bitcast.25), calls=%async_computation.2 | async-start | bytes 524288 | tf_op jit(solution)/shard_map/all_to_all | solution.py:414
  49.3 6.0 %dquery.1 = (bf16[256,1024]{1,0:T(8,128)(2,1)}, f32[264,256]{1,0:T(8,128)}, f32[264,256]{1,0:T(8,128)}, f32[264,256]{1,0:T(8,128)}, f32[264,256]{1,0:T(8,128)}) custom-call(s32[1]{0:T(128)} %bitcast.9.me_ref, f32[256,1024]{1,0:T(8,128)} %get-tuple-element.110.dn, f32[512,128]{1,0:T(8,128)} %bitcast.6.st, bf16[256,1024]{1,0:T(8,128)(2,1)} %get-tuple-element.78.fk, ...), custom_call_target="tpu_custom_call" | custom-call | flops 1073741824 | bytes 4194304 | tf_op jit(solution)/shard_map/dquery/pallas_call | solution.py:466
  55.3 2.7 %all-to-all-done.2.v = f32[32,16,128]{2,1,0:T(8,128)S(1)} async-done(((f32[32,16,128]{2,1,0:T(8,128)}), f32[32,16,128]{2,1,0:T(8,128)S(1)}, u32[]{:S(2)}, u32[]{:S(2)}) %all-to-all-start.2) | async-done | bytes 262176 | tf_op jit(solution)/shard_map/all_to_all | solution.py:414
  60.8 5.0 %all-to-all-start.3 = ((f32[32,16,128]{2,1,0:T(8,128)}), f32[32,16,128]{2,1,0:T(8,128)}, u32[]{:S(2)}, u32[]{:S(2)}) async-start(f32[32,16,128]{2,1,0:T(8,128)} %suffix.1), calls=%async_computation.3 | async-start | bytes 524288 | tf_op jit(solution)/shard_map/all_to_all | solution.py:425
  65.9 4.4 %localk.1.lk = f32[256,1024]{1,0:T(8,128)} custom-call(f32[256,1024]{1,0:T(8,128)} %get-tuple-element.110.dn, bf16[256,1024]{1,0:T(8,128)(2,1)} %get-tuple-element.77.fq, bf16[256,1024]{1,0:T(8,128)(2,1)} %get-tuple-element.79.fv), custom_call_target="tpu_custom_call" | custom-call | flops 1 | bytes 4194304 | tf_op jit(solution)/shard_map/localk/pallas_call | solution.py:479
  70.2 4.7 %all-to-all-done.3 = f32[32,16,128]{2,1,0:T(8,128)} async-done(((f32[32,16,128]{2,1,0:T(8,128)}), f32[32,16,128]{2,1,0:T(8,128)}, u32[]{:S(2)}, u32[]{:S(2)}) %all-to-all-start.3) | async-done | bytes 262176 | tf_op jit(solution)/shard_map/all_to_all | solution.py:425
  74.9 3.3 %dkey.1 = (bf16[256,1024]{1,0:T(8,128)(2,1)}, f32[256,256]{1,0:T(8,128)}, f32[256,256]{1,0:T(8,128)}, f32[256,256]{1,0:T(8,128)}, f32[256,256]{1,0:T(8,128)}) custom-call(s32[1]{0:T(128)} %bitcast.9.me_ref, f32[256,1024]{1,0:T(8,128)} %localk.1.lk, bf16[256,1024]{1,0:T(8,128)(2,1)} %get-tuple-element.79.fv, f32[512,128]{1,0:T(8,128)} %bitcast.13.st, ...), custom_call_target="tpu_custom_call" | custom-call | flops 1 | bytes 4194304 | tf_op jit(solution)/shard_map/dkey/pallas_call | solution.py:482
  80.2 5.4 %wgradq.1 = (bf16[4,4,64,1024]{3,2,1,0:T(8,128)(2,1)}, f32[4,72,256]{2,1,0:T(8,128)}, f32[4,72,256]{2,1,0:T(8,128)}, f32[4,72,256]{2,1,0:T(8,128)}, f32[4,72,256]{2,1,0:T(8,128)}) custom-call(s32[1]{0:T(128)} %bitcast.y_ref, bf16[4,4,64,256]{3,2,1,0:T(8,128)(2,1)} %bitcast.22, f32[4,4,64,256]{3,2,1,0:T(8,128)} %bitcast.10.t1, f32[4,4,64,256]{3,2,1,0:T(8,128)} %bitcast.11.t2, ...), custom_call_target="tpu_custom_call" | custom-call | flops 1073741824 | bytes 4194304 | tf_op jit(solution)/shard_map/wgradq/pallas_call | solution.py:498
  89.6 2.9 %collective-permute-done.8.d3 = f32[256,256]{1,0:T(8,128)} collective-permute-done((f32[256,256]{1,0:T(8,128)}, f32[256,256]{1,0:T(8,128)}, u32[]{:S(2)}, u32[]{:S(2)}) %collective-permute-start.8) | collective-permute-done | bytes 262176 | tf_op jit(solution)/shard_map/ppermute | solution.py:428
  92.5 3.2 %wgradk.1 = f32[16,64,256]{2,1,0:T(8,128)} custom-call(bf16[1024,1024]{1,0:T(8,128)(2,1)} %bitcast.28, f32[256,256]{1,0:T(8,128)} %get-tuple-element.105.d0, f32[256,256]{1,0:T(8,128)} %collective-permute-done.6.d1, f32[256,256]{1,0:T(8,128)} %collective-permute-done.7.d2, f32[256,256]{1,0:T(8,128)} %collective-permute-done.8.d3), custom_call_target="tpu_custom_call" | custom-call | flops 214748364800 | bytes 4194304 | tf_op jit(solution)/shard_map/wgradk/pallas_call | solution.py:508
  95.7 4.3 %all-to-all-start.4 = ((f32[16,64,256]{2,1,0:T(8,128)}), f32[16,64,256]{2,1,0:T(8,128)}, u32[]{:S(2)}, u32[]{:S(2)}) async-start(f32[16,64,256]{2,1,0:T(8,128)} %wgradk.1), calls=%async_computation.4 | async-start | bytes 2097152 | tf_op jit(solution)/shard_map/all_to_all | solution.py:513
  109.2 5.1 %localv.1 = (bf16[256,1024]{1,0:T(8,128)(2,1)}, f32[256,1024]{1,0:T(8,128)}) custom-call(bf16[256,1024]{1,0:T(8,128)(2,1)} %get-tuple-element.109.at, bf16[1024,1024]{1,0:T(8,128)(2,1)} %wo.3, f32[256,1024]{1,0:T(8,128)} %get-tuple-element.110.dn, bf16[256,1024]{1,0:T(8,128)(2,1)} %get-tuple-element.77.fq, bf16[256,1024]{1,0:T(8,128)(2,1)} %get-tuple-element.78.fk), custom_call_target="tpu_custom_call" | custom-call | flops 214748364800 | bytes 4194304 | tf_op jit(solution)/shard_map/localv/pallas_call | solution.py:516
  114.3 5.9 %dtok.1 = bf16[256,1024]{1,0:T(8,128)(2,1)} custom-call(f32[256,1024]{1,0:T(8,128)} %get-tuple-element.112.lv, bf16[256,1024]{1,0:T(8,128)(2,1)} %get-tuple-element.78.fk, f32[512,128]{1,0:T(8,128)} %bitcast.13.st, bf16[256,1024]{1,0:T(8,128)(2,1)} %get-tuple-element.113.dq, bf16[256,1024]{1,0:T(8,128)(2,1)} %get-tuple-element.114.dk, ...), custom_call_target="tpu_custom_call" | custom-call | flops 1 | bytes 4194304 | tf_op jit(solution)/shard_map/dtok/pallas_call | solution.py:520
  120.2 2.1 %join.1 = f32[16,8,384]{2,1,0:T(8,128)} custom-call(f32[72,256]{1,0:T(8,128)} %get-tuple-element.129.q0, f32[72,256]{1,0:T(8,128)} %collective-permute-done.12.q1, f32[72,256]{1,0:T(8,128)} %collective-permute-done.13.q2, f32[72,256]{1,0:T(8,128)} %collective-permute-done.14.q3, f32[16,64,256]{2,1,0:T(8,128)} %all-to-all-done.4.k), custom_call_target="tpu_custom_call" | custom-call | flops 4194304 | bytes 4194304 | tf_op jit(solution)/shard_map/join/pallas_call | solution.py:538
  122.3 20.4 %all_to_all.30.v = f32[16,8,384]{2,1,0:T(8,128)S(1)} all-to-all(f32[16,8,384]{2,1,0:T(8,128)} %join.1), channel_id=1, replica_groups=mesh['x'=4,'y'=4,'c'=2,'w'=4,'b'=2] {'c','w','b'}, dimensions={0} | all-to-all | bytes 393216 | tf_op jit(solution)/shard_map/all_to_all | solution.py:542
  (34 shorter events, 21.4 us)
Async XLA Ops:
  6.0 17.6 %all-to-all-start = ((f32[32,16,128]{2,1,0:T(8,128)}), f32[32,16,128]{2,1,0:T(8,128)S(1)}, u32[]{:S(2)}, u32[]{:S(2)}) async-start(f32[32,16,128]{2,1,0:T(8,128)} %bitcast.26), calls=%async_computation | async-start | bytes 524288 | tf_op jit(solution)/shard_map/all_to_all | solution.py:414
  24.4 34.3 %collective-permute-start = (f32[1024,256]{1,0:T(8,128)}, f32[1024,256]{1,0:T(8,128)}, u32[]{:S(2)}, u32[]{:S(2)}) collective-permute-start(f32[1024,256]{1,0:T(8,128)} %get-tuple-element.85), channel_id=1, source_target_pairs={{0,1},{1,0},{8,9},{9,8},{2,3},{3,2},{10,11},{11,10},{4,5},{5,4},{1... | collective-permute-start | bytes 3145736 | tf_op jit(solution)/shard_map/ppermute | solution.py:428
  26.0 14.0 %all-to-all-start.1 = ((f32[32,16,128]{2,1,0:T(8,128)}), f32[32,16,128]{2,1,0:T(8,128)}, u32[]{:S(2)}, u32[]{:S(2)}) async-start(f32[32,16,128]{2,1,0:T(8,128)} %prefix.1), calls=%async_computation.1 | async-start | bytes 524288 | tf_op jit(solution)/shard_map/all_to_all | solution.py:425
  45.1 12.8 %all-to-all-start.2 = ((f32[32,16,128]{2,1,0:T(8,128)}), f32[32,16,128]{2,1,0:T(8,128)S(1)}, u32[]{:S(2)}, u32[]{:S(2)}) async-start(f32[32,16,128]{2,1,0:T(8,128)} %bitcast.25), calls=%async_computation.2 | async-start | bytes 524288 | tf_op jit(solution)/shard_map/all_to_all | solution.py:414
  48.9 31.3 %collective-permute-start.1 = (f32[1024,256]{1,0:T(8,128)}, f32[1024,256]{1,0:T(8,128)}, u32[]{:S(2)}, u32[]{:S(2)}) collective-permute-start(f32[1024,256]{1,0:T(8,128)} %get-tuple-element.85), channel_id=1, source_target_pairs={{0,8},{1,9},{8,0},{9,1},{2,10},{3,11},{10,2},{11,3},{4,12},{5,13},... | collective-permute-start | bytes 3145736 | tf_op jit(solution)/shard_map/ppermute | solution.py:428
  58.7 21.5 %collective-permute-start.2 = (f32[1024,256]{1,0:T(8,128)}, f32[1024,256]{1,0:T(8,128)}, u32[]{:S(2)}, u32[]{:S(2)}) collective-permute-start(f32[1024,256]{1,0:T(8,128)} %collective-permute-done), channel_id=1, source_target_pairs={{0,8},{1,9},{8,0},{9,1},{2,10},{3,11},{10,2},{11,3},{4,12},{5,13},... | collective-permute-start | bytes 3145736 | tf_op jit(solution)/shard_map/ppermute | solution.py:428
  58.9 19.3 %collective-permute-start.3 = (f32[264,256]{1,0:T(8,128)}, f32[264,256]{1,0:T(8,128)}, u32[]{:S(2)}, u32[]{:S(2)}) collective-permute-start(f32[264,256]{1,0:T(8,128)} %get-tuple-element.94), channel_id=1, source_target_pairs={{0,1},{1,0},{8,9},{9,8},{2,3},{3,2},{10,11},{11,10},{4,5},{5,4},{1... | collective-permute-start | bytes 811016 | tf_op jit(solution)/shard_map/ppermute | solution.py:428
  58.9 19.4 %collective-permute-start.4 = (f32[264,256]{1,0:T(8,128)}, f32[264,256]{1,0:T(8,128)}, u32[]{:S(2)}, u32[]{:S(2)}) collective-permute-start(f32[264,256]{1,0:T(8,128)} %get-tuple-element.95), channel_id=1, source_target_pairs={{0,8},{1,9},{8,0},{9,1},{2,10},{3,11},{10,2},{11,3},{4,12},{5,13},... | collective-permute-start | bytes 811016 | tf_op jit(solution)/shard_map/ppermute | solution.py:428
  59.3 19.3 %collective-permute-start.5 = (f32[264,256]{1,0:T(8,128)}, f32[264,256]{1,0:T(8,128)}, u32[]{:S(2)}, u32[]{:S(2)}) collective-permute-start(f32[264,256]{1,0:T(8,128)} %get-tuple-element.96), channel_id=1, source_target_pairs={{0,9},{1,8},{8,1},{9,0},{2,11},{3,10},{10,3},{11,2},{4,13},{5,12},... | collective-permute-start | bytes 811016 | tf_op jit(solution)/shard_map/ppermute | solution.py:428
  60.8 14.1 %all-to-all-start.3 = ((f32[32,16,128]{2,1,0:T(8,128)}), f32[32,16,128]{2,1,0:T(8,128)}, u32[]{:S(2)}, u32[]{:S(2)}) async-start(f32[32,16,128]{2,1,0:T(8,128)} %suffix.1), calls=%async_computation.3 | async-start | bytes 524288 | tf_op jit(solution)/shard_map/all_to_all | solution.py:425
  78.2 9.6 %collective-permute-start.6 = (f32[256,256]{1,0:T(8,128)}, f32[256,256]{1,0:T(8,128)}, u32[]{:S(2)}, u32[]{:S(2)}) collective-permute-start(f32[256,256]{1,0:T(8,128)} %get-tuple-element.106), channel_id=1, source_target_pairs={{0,1},{1,0},{8,9},{9,8},{2,3},{3,2},{10,11},{11,10},{4,5},{5,4},{1... | collective-permute-start | bytes 786440 | tf_op jit(solution)/shard_map/ppermute | solution.py:428
  78.3 11.3 %collective-permute-start.7 = (f32[256,256]{1,0:T(8,128)}, f32[256,256]{1,0:T(8,128)}, u32[]{:S(2)}, u32[]{:S(2)}) collective-permute-start(f32[256,256]{1,0:T(8,128)} %get-tuple-element.107), channel_id=1, source_target_pairs={{0,8},{1,9},{8,0},{9,1},{2,10},{3,11},{10,2},{11,3},{4,12},{5,13},... | collective-permute-start | bytes 786440 | tf_op jit(solution)/shard_map/ppermute | solution.py:428
  78.6 13.9 %collective-permute-start.8 = (f32[256,256]{1,0:T(8,128)}, f32[256,256]{1,0:T(8,128)}, u32[]{:S(2)}, u32[]{:S(2)}) collective-permute-start(f32[256,256]{1,0:T(8,128)} %get-tuple-element.108), channel_id=1, source_target_pairs={{0,9},{1,8},{8,1},{9,0},{2,11},{3,10},{10,3},{11,2},{4,13},{5,12},... | collective-permute-start | bytes 786440 | tf_op jit(solution)/shard_map/ppermute | solution.py:428
  85.6 14.4 %collective-permute-start.9 = (f32[4,72,256]{2,1,0:T(8,128)}, f32[4,72,256]{2,1,0:T(8,128)}, u32[]{:S(2)}, u32[]{:S(2)}) collective-permute-start(f32[4,72,256]{2,1,0:T(8,128)} %get-tuple-element.116), channel_id=1, source_target_pairs={{0,16},{16,0},{32,48},{48,32},{1,17},{17,1},{33,49},{49,33},{2,18}... | collective-permute-start | bytes 884744 | tf_op jit(solution)/shard_map/ppermute | solution.py:431
  85.9 15.4 %collective-permute-start.10 = (f32[4,72,256]{2,1,0:T(8,128)}, f32[4,72,256]{2,1,0:T(8,128)}, u32[]{:S(2)}, u32[]{:S(2)}) collective-permute-start(f32[4,72,256]{2,1,0:T(8,128)} %get-tuple-element.117), channel_id=1, source_target_pairs={{0,32},{16,48},{32,0},{48,16},{1,33},{17,49},{33,1},{49,17},{2,34}... | collective-permute-start | bytes 884744 | tf_op jit(solution)/shard_map/ppermute | solution.py:431
  87.8 15.5 %collective-permute-start.11 = (f32[4,72,256]{2,1,0:T(8,128)}, f32[4,72,256]{2,1,0:T(8,128)}, u32[]{:S(2)}, u32[]{:S(2)}) collective-permute-start(f32[4,72,256]{2,1,0:T(8,128)} %get-tuple-element.118), channel_id=1, source_target_pairs={{0,48},{16,32},{32,16},{48,0},{1,49},{17,33},{33,17},{49,1},{2,50}... | collective-permute-start | bytes 884744 | tf_op jit(solution)/shard_map/ppermute | solution.py:431
  95.7 24.5 %all-to-all-start.4 = ((f32[16,64,256]{2,1,0:T(8,128)}), f32[16,64,256]{2,1,0:T(8,128)}, u32[]{:S(2)}, u32[]{:S(2)}) async-start(f32[16,64,256]{2,1,0:T(8,128)} %wgradk.1), calls=%async_computation.4 | async-start | bytes 2097152 | tf_op jit(solution)/shard_map/all_to_all | solution.py:513
  105.3 14.8 %collective-permute-start.12 = (f32[72,256]{1,0:T(8,128)}, f32[72,256]{1,0:T(8,128)}, u32[]{:S(2)}, u32[]{:S(2)}) collective-permute-start(f32[72,256]{1,0:T(8,128)} %get-tuple-element.124), channel_id=1, source_target_pairs={{0,64},{64,0},{128,192},{192,128},{1,65},{65,1},{129,193},{193,129... | collective-permute-start | bytes 221192 | tf_op jit(solution)/shard_map/ppermute | solution.py:431
  105.7 14.5 %collective-permute-start.13 = (f32[72,256]{1,0:T(8,128)}, f32[72,256]{1,0:T(8,128)}, u32[]{:S(2)}, u32[]{:S(2)}) collective-permute-start(f32[72,256]{1,0:T(8,128)} %get-tuple-element.125), channel_id=1, source_target_pairs={{0,128},{64,192},{128,0},{192,64},{1,129},{65,193},{129,1},{193,65... | collective-permute-start | bytes 221192 | tf_op jit(solution)/shard_map/ppermute | solution.py:431
  107.4 12.8 %collective-permute-start.14 = (f32[72,256]{1,0:T(8,128)}, f32[72,256]{1,0:T(8,128)}, u32[]{:S(2)}, u32[]{:S(2)}) collective-permute-start(f32[72,256]{1,0:T(8,128)} %get-tuple-element.126), channel_id=1, source_target_pairs={{0,192},{64,128},{128,64},{192,0},{1,193},{65,129},{129,65},{193,1... | collective-permute-start | bytes 221192 | tf_op jit(solution)/shard_map/ppermute | solution.py:431

commit v8 on v7

--- a/solution.py
+++ b/solution.py
@@ -442,6 +442,7 @@
     )(tok_1, w_query)
     parts, fq, t0 = tie((parts, fq, t0))
     mine = run(parts, False, "prefix")
+
     t32, _ = tie((t32, mine))
     t1 = swap(t32, 1)
     t2 = swap(t32, 2)
@@ -512,24 +513,18 @@
     )(tall.reshape(d, 4 * n), *dk_got)
     gk_parts = lax.all_to_all(gk, ("x", "y"), 0, 0, tiled=True)
 
-    dn_5, dk_5, _ = tie((dn, dk, gk))
+    dn_5, _ = tie((dn, gk))
     mo, lv = call(
         local_v_kernel, (halves,),
         [whole((n, d)), col(d, w), col(n, w), col(n, w), col(n, w)], [act(BF), act(F32)], "localv", 400 * big,
     )(at, w_out, dn_5, fq, fk)
-    (dt,) = call(
-        dtok_kernel, (halves,),
-        [col(n, w), col(n, w), st_spec, col(n, w), col(n, w), col(d, w), col(d, w), col(d, w)],
-        [((n, d), BF, whole((n, d)))], "dtok", 1,
-        scratch=[pltpu.VMEM((n, d), F32)],
-    )(lv, fk, r_in, dq, dk_5, w_query, w_key, w_value)
     gq_got, _ = tie((gq_got, gk))
     gq_send = call(
         sum_y_kernel, (), [SMEM] + [whole(qshape)] * side,
         [(qshape[1:], F32, whole(qshape[1:]))] * side, "sumy", 1 << 22,
     )(own("x"), *gq_got)
     gq_got = [gq_send[0]] + [turn_about("x", gq_send[k], k) for k in range(1, side)]
-    gk_parts, mo, dt, gq_got = tie((gk_parts, mo, dt, gq_got))
+    gk_parts, mo, lv, gq_got = tie((gk_parts, mo, lv, gq_got))
 
     last = ("c", "w", "b")
     nlast = lax.axis_size(last)
@@ -539,7 +534,15 @@
         join_kernel, (), [whole(qshape[1:])] * side + [whole(kshape)],
         [(jshape, F32, whole(jshape))], "join", 1 << 22,
     )(*gq_got, gk_parts)
+    dk_6, _ = tie((dk, both))
     both = lax.all_to_all(both, last, 0, 0, tiled=True)
+
+    (dt,) = call(
+        dtok_kernel, (halves,),
+        [col(n, w), col(n, w), st_spec, col(n, w), col(n, w), col(d, w), col(d, w), col(d, w)],
+        [((n, d), BF, whole((n, d)))], "dtok", 1,
+        scratch=[pltpu.VMEM((n, d), F32)],
+    )(lv, fk, r_in, dq, dk_6, w_query, w_key, w_value)
     dw, dg = call(
         final_kernel, (), [whole(jshape)],
         [((2, each * d), F32, whole((2, each * d))), ((8, 128), F32, whole((8, 128)))],

time: 144 us -> 140 us (0.972)
  blocking collectives: 20.4 us -> 0 us
  starting transfers between devices: 40.6 us -> 48.8 us
  waiting for transfers between devices: 20.3 us -> 27.3 us
    all_to_all x1 -> x0, blocking collectives: 20.4 us -> none  [on_device(): both = lax.all_to_all(both, last, 0, 0, tiled=True)]
    all_to_all x0 -> x1, starting transfers between devices: none -> 8.23 us  [on_device(): both = lax.all_to_all(both, last, 0, 0, tiled=True)]
    ppermute x6, waiting for transfers between devices: 3.23 us -> 7.77 us  [turn_about(): lax.ppermute(v, axis, [(i, i ^ k) for i in range(lax.axis_size(axis))])]
    all_to_all x0 -> x1, waiting for transfers between devices: none -> 2.43 us  [on_device(): both = lax.all_to_all(both, last, 0, 0, tiled=True)]
  transfers between devices with their start and end apart: 20 -> 21, of which waited for: 7 -> 10; matrix products, arithmetic and copies ran while one was open for 0% -> 0% of each run, Pallas kernels for 37% -> 38%
where the time goes in v8:
time: 140 us; the launch traced here: 139 us
  Pallas kernels  61.6 us (44%)
  starting transfers between devices  48.8 us (35%)
  waiting for transfers between devices  27.3 us (20%)
  between operations  1.41 us (1%)
    all_to_all x2, starting transfers between devices, to_parts(): lax.all_to_all(st.reshape(nseq, st_rows // nseq, 128), SEQ, 0, 0, tiled=T...  12.3 us
    all_to_all x2, starting transfers between devices, from_parts(): return lax.all_to_all(mine, SEQ, 0, 0, tiled=True).reshape(st_rows, 128)  9.93 us
    all_to_all x2, waiting for transfers between devices, from_parts(): return lax.all_to_all(mine, SEQ, 0, 0, tiled=True).reshape(st_rows, 128)  8.64 us
    all_to_all x1, starting transfers between devices, on_device(): both = lax.all_to_all(both, last, 0, 0, tiled=True)  8.23 us
    ppermute x6, starting transfers between devices, turn_about(): lax.ppermute(v, axis, [(i, i ^ k) for i in range(lax.axis_size(axis))])  7.8 us
    ppermute x6, waiting for transfers between devices, turn_about(): lax.ppermute(v, axis, [(i, i ^ k) for i in range(lax.axis_size(axis))])  7.77 us
    ppermute x9, starting transfers between devices, swap(): return lax.ppermute(v, GROUP, [(i, i ^ k) for i in range(ngroup)])  6.21 us
    pallas_call x1, Pallas kernels, on_device(): call_mine(dq_kernel, [col_mine(n, w), row_mine(w // 2, 128)] + [col_mine(...  5.99 us
  transfers between devices with their start and end apart: 21, of which 10 were waited for; matrix products, arithmetic and copies ran while one was open for 0% of the time, Pallas kernels for 38%

profile of v8, /device:TPU:1, one launch (start us, length us, event | category | flops | bytes accessed | tf_op | source)
XLA Modules:
  0.0 139.1 jit_solution(7011537601716818122)
XLA Ops:
  1.3 4.7 %kv.1 = (bf16[256,1024]{1,0:T(8,128)(2,1)}, bf16[256,1024]{1,0:T(8,128)(2,1)}, f32[256,1024]{1,0:T(8,128)}, f32[512,128]{1,0:T(8,128)}) custom-call(s32[1]{0:T(128)S(6)} %sub.7.nv_ref, bf16[256,1024]{1,0:T(8,128)(2,1)} %bitcast.19, bf16[1024,1024]{1,0:T(8,128)(2,1)} %wk.3, bf16[1024,1024]{1,0:T(8,128)(2,1)} %wv.3), custom_call_target="tpu_custom_call" | custom-call | flops 1073741824 | bytes 4194304 | tf_op jit(solution)/shard_map/kv/pallas_call | solution.py:406
  6.0 8.6 %all-to-all-start = ((f32[32,16,128]{2,1,0:T(8,128)}), f32[32,16,128]{2,1,0:T(8,128)S(1)}, u32[]{:S(2)}, u32[]{:S(2)}) async-start(f32[32,16,128]{2,1,0:T(8,128)} %bitcast.26), calls=%async_computation | async-start | bytes 524288 | tf_op jit(solution)/shard_map/all_to_all | solution.py:414
  17.0 3.7 %query.1 = (bf16[256,1024]{1,0:T(8,128)(2,1)}, bf16[1024,256]{1,0:T(8,128)(2,1)}, f32[256,1024]{1,0:T(8,128)}) custom-call(bf16[256,1024]{1,0:T(8,128)(2,1)} %bitcast.21, bf16[1024,1024]{1,0:T(8,128)(2,1)} %wq.3), custom_call_target="tpu_custom_call" | custom-call | flops 536870912 | bytes 4194304 | tf_op jit(solution)/shard_map/query/pallas_call | solution.py:439
  20.7 2.8 %all-to-all-done.v = f32[32,16,128]{2,1,0:T(8,128)S(1)} async-done(((f32[32,16,128]{2,1,0:T(8,128)}), f32[32,16,128]{2,1,0:T(8,128)S(1)}, u32[]{:S(2)}, u32[]{:S(2)}) %all-to-all-start) | async-done | bytes 262176 | tf_op jit(solution)/shard_map/all_to_all | solution.py:414
  26.0 4.9 %all-to-all-start.1 = ((f32[32,16,128]{2,1,0:T(8,128)}), f32[32,16,128]{2,1,0:T(8,128)}, u32[]{:S(2)}, u32[]{:S(2)}) async-start(f32[32,16,128]{2,1,0:T(8,128)} %prefix.1), calls=%async_computation.1 | async-start | bytes 524288 | tf_op jit(solution)/shard_map/all_to_all | solution.py:425
  30.8 5.1 %numer.1 = (f32[256,1024]{1,0:T(8,128)}, f32[256,1024]{1,0:T(8,128)}) custom-call(bf16[256,1024]{1,0:T(8,128)(2,1)} %get-tuple-element.77.fq, bf16[256,1024]{1,0:T(8,128)(2,1)} %get-tuple-element.78.fk, bf16[256,1024]{1,0:T(8,128)(2,1)} %get-tuple-element.79.fv, bf16[256,1024]{1,0:T(8,128)(2,1)} %bitcast.24, bf16[1024,1024]{1,0:T(8,128)(2,1)} %wo.3), custom_call_target="tpu_custom_call" | custom-call | flops 1073741824 | bytes 4194304 | tf_op jit(solution)/shard_map/numer/pallas_call | solution.py:452
  35.9 4.0 %all-to-all-done.1 = f32[32,16,128]{2,1,0:T(8,128)} async-done(((f32[32,16,128]{2,1,0:T(8,128)}), f32[32,16,128]{2,1,0:T(8,128)}, u32[]{:S(2)}, u32[]{:S(2)}) %all-to-all-start.1) | async-done | bytes 262176 | tf_op jit(solution)/shard_map/all_to_all | solution.py:425
  39.9 5.2 %norm.1 = (bf16[256,1024]{1,0:T(8,128)(2,1)}, f32[256,1024]{1,0:T(8,128)}, f32[512,128]{1,0:T(8,128)}, f32[8,1024]{1,0:T(8,128)}) custom-call(s32[1]{0:T(128)S(6)} %sub.7.nv_ref, f32[256,1024]{1,0:T(8,128)} %get-tuple-element.80.nl, f32[512,128]{1,0:T(8,128)} %bitcast.6.st, bf16[256,1024]{1,0:T(8,128)(2,1)} %get-tuple-element.77.fq, ...), custom_call_target="tpu_custom_call" | custom-call | flops 536870912 | bytes 4194304 | tf_op jit(solution)/shard_map/norm/pallas_call | solution.py:458
  45.0 3.7 %all-to-all-start.2 = ((f32[32,16,128]{2,1,0:T(8,128)}), f32[32,16,128]{2,1,0:T(8,128)S(1)}, u32[]{:S(2)}, u32[]{:S(2)}) async-start(f32[32,16,128]{2,1,0:T(8,128)} %bitcast.25), calls=%async_computation.2 | async-start | bytes 524288 | tf_op jit(solution)/shard_map/all_to_all | solution.py:414
  49.2 6.0 %dquery.1 = (bf16[256,1024]{1,0:T(8,128)(2,1)}, f32[264,256]{1,0:T(8,128)}, f32[264,256]{1,0:T(8,128)}, f32[264,256]{1,0:T(8,128)}, f32[264,256]{1,0:T(8,128)}) custom-call(s32[1]{0:T(128)} %bitcast.9.me_ref, f32[256,1024]{1,0:T(8,128)} %get-tuple-element.110.dn, f32[512,128]{1,0:T(8,128)} %bitcast.6.st, bf16[256,1024]{1,0:T(8,128)(2,1)} %get-tuple-element.78.fk, ...), custom_call_target="tpu_custom_call" | custom-call | flops 1073741824 | bytes 4194304 | tf_op jit(solution)/shard_map/dquery/pallas_call | solution.py:467
  55.2 2.7 %all-to-all-done.2.v = f32[32,16,128]{2,1,0:T(8,128)S(1)} async-done(((f32[32,16,128]{2,1,0:T(8,128)}), f32[32,16,128]{2,1,0:T(8,128)S(1)}, u32[]{:S(2)}, u32[]{:S(2)}) %all-to-all-start.2) | async-done | bytes 262176 | tf_op jit(solution)/shard_map/all_to_all | solution.py:414
  60.7 5.1 %all-to-all-start.3 = ((f32[32,16,128]{2,1,0:T(8,128)}), f32[32,16,128]{2,1,0:T(8,128)}, u32[]{:S(2)}, u32[]{:S(2)}) async-start(f32[32,16,128]{2,1,0:T(8,128)} %suffix.1), calls=%async_computation.3 | async-start | bytes 524288 | tf_op jit(solution)/shard_map/all_to_all | solution.py:425
  65.8 4.4 %localk.1.lk = f32[256,1024]{1,0:T(8,128)} custom-call(f32[256,1024]{1,0:T(8,128)} %get-tuple-element.110.dn, bf16[256,1024]{1,0:T(8,128)(2,1)} %get-tuple-element.77.fq, bf16[256,1024]{1,0:T(8,128)(2,1)} %get-tuple-element.79.fv), custom_call_target="tpu_custom_call" | custom-call | flops 1 | bytes 4194304 | tf_op jit(solution)/shard_map/localk/pallas_call | solution.py:480
  70.2 4.7 %all-to-all-done.3 = f32[32,16,128]{2,1,0:T(8,128)} async-done(((f32[32,16,128]{2,1,0:T(8,128)}), f32[32,16,128]{2,1,0:T(8,128)}, u32[]{:S(2)}, u32[]{:S(2)}) %all-to-all-start.3) | async-done | bytes 262176 | tf_op jit(solution)/shard_map/all_to_all | solution.py:425
  74.8 3.3 %dkey.1 = (bf16[256,1024]{1,0:T(8,128)(2,1)}, f32[256,256]{1,0:T(8,128)}, f32[256,256]{1,0:T(8,128)}, f32[256,256]{1,0:T(8,128)}, f32[256,256]{1,0:T(8,128)}) custom-call(s32[1]{0:T(128)} %bitcast.9.me_ref, f32[256,1024]{1,0:T(8,128)} %localk.1.lk, bf16[256,1024]{1,0:T(8,128)(2,1)} %get-tuple-element.79.fv, f32[512,128]{1,0:T(8,128)} %bitcast.13.st, ...), custom_call_target="tpu_custom_call" | custom-call | flops 1 | bytes 4194304 | tf_op jit(solution)/shard_map/dkey/pallas_call | solution.py:483
  80.1 5.5 %wgradq.1 = (bf16[4,4,64,1024]{3,2,1,0:T(8,128)(2,1)}, f32[4,72,256]{2,1,0:T(8,128)}, f32[4,72,256]{2,1,0:T(8,128)}, f32[4,72,256]{2,1,0:T(8,128)}, f32[4,72,256]{2,1,0:T(8,128)}) custom-call(s32[1]{0:T(128)} %bitcast.y_ref, bf16[4,4,64,256]{3,2,1,0:T(8,128)(2,1)} %bitcast.22, f32[4,4,64,256]{3,2,1,0:T(8,128)} %bitcast.10.t1, f32[4,4,64,256]{3,2,1,0:T(8,128)} %bitcast.11.t2, ...), custom_call_target="tpu_custom_call" | custom-call | flops 1073741824 | bytes 4194304 | tf_op jit(solution)/shard_map/wgradq/pallas_call | solution.py:499
  89.5 2.9 %collective-permute-done.8.d3 = f32[256,256]{1,0:T(8,128)} collective-permute-done((f32[256,256]{1,0:T(8,128)}, f32[256,256]{1,0:T(8,128)}, u32[]{:S(2)}, u32[]{:S(2)}) %collective-permute-start.8) | collective-permute-done | bytes 262176 | tf_op jit(solution)/shard_map/ppermute | solution.py:428
  92.5 3.2 %wgradk.1 = f32[16,64,256]{2,1,0:T(8,128)} custom-call(bf16[1024,1024]{1,0:T(8,128)(2,1)} %bitcast.28, f32[256,256]{1,0:T(8,128)} %get-tuple-element.105.d0, f32[256,256]{1,0:T(8,128)} %collective-permute-done.6.d1, f32[256,256]{1,0:T(8,128)} %collective-permute-done.7.d2, f32[256,256]{1,0:T(8,128)} %collective-permute-done.8.d3), custom_call_target="tpu_custom_call" | custom-call | flops 214748364800 | bytes 4194304 | tf_op jit(solution)/shard_map/wgradk/pallas_call | solution.py:509
  95.7 4.3 %all-to-all-start.4 = ((f32[16,64,256]{2,1,0:T(8,128)}), f32[16,64,256]{2,1,0:T(8,128)}, u32[]{:S(2)}, u32[]{:S(2)}) async-start(f32[16,64,256]{2,1,0:T(8,128)} %wgradk.1), calls=%async_computation.4 | async-start | bytes 2097152 | tf_op jit(solution)/shard_map/all_to_all | solution.py:514
  109.1 5.1 %localv.1 = (bf16[256,1024]{1,0:T(8,128)(2,1)}, f32[256,1024]{1,0:T(8,128)}) custom-call(bf16[256,1024]{1,0:T(8,128)(2,1)} %get-tuple-element.109.at, bf16[1024,1024]{1,0:T(8,128)(2,1)} %wo.3, f32[256,1024]{1,0:T(8,128)} %get-tuple-element.110.dn, bf16[256,1024]{1,0:T(8,128)(2,1)} %get-tuple-element.77.fq, bf16[256,1024]{1,0:T(8,128)(2,1)} %get-tuple-element.78.fk), custom_call_target="tpu_custom_call" | custom-call | flops 214748364800 | bytes 4194304 | tf_op jit(solution)/shard_map/localv/pallas_call | solution.py:517
  115.4 3.4 %collective-permute-done.13.q2 = f32[72,256]{1,0:T(8,128)} collective-permute-done((f32[72,256]{1,0:T(8,128)}, f32[72,256]{1,0:T(8,128)}, u32[]{:S(2)}, u32[]{:S(2)}) %collective-permute-start.13) | collective-permute-done | bytes 73760 | tf_op jit(solution)/shard_map/ppermute | solution.py:431
  120.9 8.2 %all-to-all-start.5 = ((f32[16,8,384]{2,1,0:T(8,128)}), f32[16,8,384]{2,1,0:T(8,128)}, u32[]{:S(2)}, u32[]{:S(2)}) async-start(f32[16,8,384]{2,1,0:T(8,128)} %join.1), calls=%async_computation.5 | async-start | bytes 393216 | tf_op jit(solution)/shard_map/all_to_all | solution.py:538
  129.2 6.0 %dtok.1 = bf16[256,1024]{1,0:T(8,128)(2,1)} custom-call(f32[256,1024]{1,0:T(8,128)} %get-tuple-element.126.lv, bf16[256,1024]{1,0:T(8,128)(2,1)} %get-tuple-element.78.fk, f32[512,128]{1,0:T(8,128)} %bitcast.13.st, bf16[256,1024]{1,0:T(8,128)(2,1)} %get-tuple-element.127.dq, bf16[256,1024]{1,0:T(8,128)(2,1)} %get-tuple-element.133.dk, ...), custom_call_target="tpu_custom_call" | custom-call | flops 1 | bytes 4194304 | tf_op jit(solution)/shard_map/dtok/pallas_call | solution.py:540
  135.1 2.4 %all-to-all-done.5.v = f32[16,8,384]{2,1,0:T(8,128)} async-done(((f32[16,8,384]{2,1,0:T(8,128)}), f32[16,8,384]{2,1,0:T(8,128)}, u32[]{:S(2)}, u32[]{:S(2)}) %all-to-all-start.5) | async-done | bytes 196640 | tf_op jit(solution)/shard_map/all_to_all | solution.py:538
  (35 shorter events, 28.0 us)
Async XLA Ops:
  6.0 17.6 %all-to-all-start = ((f32[32,16,128]{2,1,0:T(8,128)}), f32[32,16,128]{2,1,0:T(8,128)S(1)}, u32[]{:S(2)}, u32[]{:S(2)}) async-start(f32[32,16,128]{2,1,0:T(8,128)} %bitcast.26), calls=%async_computation | async-start | bytes 524288 | tf_op jit(solution)/shard_map/all_to_all | solution.py:414
  24.3 34.3 %collective-permute-start = (f32[1024,256]{1,0:T(8,128)}, f32[1024,256]{1,0:T(8,128)}, u32[]{:S(2)}, u32[]{:S(2)}) collective-permute-start(f32[1024,256]{1,0:T(8,128)} %get-tuple-element.85), channel_id=1, source_target_pairs={{0,1},{1,0},{8,9},{9,8},{2,3},{3,2},{10,11},{11,10},{4,5},{5,4},{1... | collective-permute-start | bytes 3145736 | tf_op jit(solution)/shard_map/ppermute | solution.py:428
  26.0 13.9 %all-to-all-start.1 = ((f32[32,16,128]{2,1,0:T(8,128)}), f32[32,16,128]{2,1,0:T(8,128)}, u32[]{:S(2)}, u32[]{:S(2)}) async-start(f32[32,16,128]{2,1,0:T(8,128)} %prefix.1), calls=%async_computation.1 | async-start | bytes 524288 | tf_op jit(solution)/shard_map/all_to_all | solution.py:425
  45.0 12.8 %all-to-all-start.2 = ((f32[32,16,128]{2,1,0:T(8,128)}), f32[32,16,128]{2,1,0:T(8,128)S(1)}, u32[]{:S(2)}, u32[]{:S(2)}) async-start(f32[32,16,128]{2,1,0:T(8,128)} %bitcast.25), calls=%async_computation.2 | async-start | bytes 524288 | tf_op jit(solution)/shard_map/all_to_all | solution.py:414
  48.8 31.4 %collective-permute-start.1 = (f32[1024,256]{1,0:T(8,128)}, f32[1024,256]{1,0:T(8,128)}, u32[]{:S(2)}, u32[]{:S(2)}) collective-permute-start(f32[1024,256]{1,0:T(8,128)} %get-tuple-element.85), channel_id=1, source_target_pairs={{0,8},{1,9},{8,0},{9,1},{2,10},{3,11},{10,2},{11,3},{4,12},{5,13},... | collective-permute-start | bytes 3145736 | tf_op jit(solution)/shard_map/ppermute | solution.py:428
  58.6 21.5 %collective-permute-start.2 = (f32[1024,256]{1,0:T(8,128)}, f32[1024,256]{1,0:T(8,128)}, u32[]{:S(2)}, u32[]{:S(2)}) collective-permute-start(f32[1024,256]{1,0:T(8,128)} %collective-permute-done), channel_id=1, source_target_pairs={{0,8},{1,9},{8,0},{9,1},{2,10},{3,11},{10,2},{11,3},{4,12},{5,13},... | collective-permute-start | bytes 3145736 | tf_op jit(solution)/shard_map/ppermute | solution.py:428
  58.8 19.3 %collective-permute-start.3 = (f32[264,256]{1,0:T(8,128)}, f32[264,256]{1,0:T(8,128)}, u32[]{:S(2)}, u32[]{:S(2)}) collective-permute-start(f32[264,256]{1,0:T(8,128)} %get-tuple-element.94), channel_id=1, source_target_pairs={{0,1},{1,0},{8,9},{9,8},{2,3},{3,2},{10,11},{11,10},{4,5},{5,4},{1... | collective-permute-start | bytes 811016 | tf_op jit(solution)/shard_map/ppermute | solution.py:428
  58.8 19.4 %collective-permute-start.4 = (f32[264,256]{1,0:T(8,128)}, f32[264,256]{1,0:T(8,128)}, u32[]{:S(2)}, u32[]{:S(2)}) collective-permute-start(f32[264,256]{1,0:T(8,128)} %get-tuple-element.95), channel_id=1, source_target_pairs={{0,8},{1,9},{8,0},{9,1},{2,10},{3,11},{10,2},{11,3},{4,12},{5,13},... | collective-permute-start | bytes 811016 | tf_op jit(solution)/shard_map/ppermute | solution.py:428
  59.2 19.3 %collective-permute-start.5 = (f32[264,256]{1,0:T(8,128)}, f32[264,256]{1,0:T(8,128)}, u32[]{:S(2)}, u32[]{:S(2)}) collective-permute-start(f32[264,256]{1,0:T(8,128)} %get-tuple-element.96), channel_id=1, source_target_pairs={{0,9},{1,8},{8,1},{9,0},{2,11},{3,10},{10,3},{11,2},{4,13},{5,12},... | collective-permute-start | bytes 811016 | tf_op jit(solution)/shard_map/ppermute | solution.py:428
  60.7 14.1 %all-to-all-start.3 = ((f32[32,16,128]{2,1,0:T(8,128)}), f32[32,16,128]{2,1,0:T(8,128)}, u32[]{:S(2)}, u32[]{:S(2)}) async-start(f32[32,16,128]{2,1,0:T(8,128)} %suffix.1), calls=%async_computation.3 | async-start | bytes 524288 | tf_op jit(solution)/shard_map/all_to_all | solution.py:425
  78.1 9.6 %collective-permute-start.6 = (f32[256,256]{1,0:T(8,128)}, f32[256,256]{1,0:T(8,128)}, u32[]{:S(2)}, u32[]{:S(2)}) collective-permute-start(f32[256,256]{1,0:T(8,128)} %get-tuple-element.106), channel_id=1, source_target_pairs={{0,1},{1,0},{8,9},{9,8},{2,3},{3,2},{10,11},{11,10},{4,5},{5,4},{1... | collective-permute-start | bytes 786440 | tf_op jit(solution)/shard_map/ppermute | solution.py:428
  78.2 11.3 %collective-permute-start.7 = (f32[256,256]{1,0:T(8,128)}, f32[256,256]{1,0:T(8,128)}, u32[]{:S(2)}, u32[]{:S(2)}) collective-permute-start(f32[256,256]{1,0:T(8,128)} %get-tuple-element.107), channel_id=1, source_target_pairs={{0,8},{1,9},{8,0},{9,1},{2,10},{3,11},{10,2},{11,3},{4,12},{5,13},... | collective-permute-start | bytes 786440 | tf_op jit(solution)/shard_map/ppermute | solution.py:428
  78.5 13.9 %collective-permute-start.8 = (f32[256,256]{1,0:T(8,128)}, f32[256,256]{1,0:T(8,128)}, u32[]{:S(2)}, u32[]{:S(2)}) collective-permute-start(f32[256,256]{1,0:T(8,128)} %get-tuple-element.108), channel_id=1, source_target_pairs={{0,9},{1,8},{8,1},{9,0},{2,11},{3,10},{10,3},{11,2},{4,13},{5,12},... | collective-permute-start | bytes 786440 | tf_op jit(solution)/shard_map/ppermute | solution.py:428
  85.6 14.4 %collective-permute-start.9 = (f32[4,72,256]{2,1,0:T(8,128)}, f32[4,72,256]{2,1,0:T(8,128)}, u32[]{:S(2)}, u32[]{:S(2)}) collective-permute-start(f32[4,72,256]{2,1,0:T(8,128)} %get-tuple-element.114), channel_id=1, source_target_pairs={{0,16},{16,0},{32,48},{48,32},{1,17},{17,1},{33,49},{49,33},{2,18}... | collective-permute-start | bytes 884744 | tf_op jit(solution)/shard_map/ppermute | solution.py:431
  85.8 15.4 %collective-permute-start.10 = (f32[4,72,256]{2,1,0:T(8,128)}, f32[4,72,256]{2,1,0:T(8,128)}, u32[]{:S(2)}, u32[]{:S(2)}) collective-permute-start(f32[4,72,256]{2,1,0:T(8,128)} %get-tuple-element.115), channel_id=1, source_target_pairs={{0,32},{16,48},{32,0},{48,16},{1,33},{17,49},{33,1},{49,17},{2,34}... | collective-permute-start | bytes 884744 | tf_op jit(solution)/shard_map/ppermute | solution.py:431
  87.7 15.5 %collective-permute-start.11 = (f32[4,72,256]{2,1,0:T(8,128)}, f32[4,72,256]{2,1,0:T(8,128)}, u32[]{:S(2)}, u32[]{:S(2)}) collective-permute-start(f32[4,72,256]{2,1,0:T(8,128)} %get-tuple-element.116), channel_id=1, source_target_pairs={{0,48},{16,32},{32,16},{48,0},{1,49},{17,33},{33,17},{49,1},{2,50}... | collective-permute-start | bytes 884744 | tf_op jit(solution)/shard_map/ppermute | solution.py:431
  95.7 23.1 %all-to-all-start.4 = ((f32[16,64,256]{2,1,0:T(8,128)}), f32[16,64,256]{2,1,0:T(8,128)}, u32[]{:S(2)}, u32[]{:S(2)}) async-start(f32[16,64,256]{2,1,0:T(8,128)} %wgradk.1), calls=%async_computation.4 | async-start | bytes 2097152 | tf_op jit(solution)/shard_map/all_to_all | solution.py:514
  105.3 10.1 %collective-permute-start.12 = (f32[72,256]{1,0:T(8,128)}, f32[72,256]{1,0:T(8,128)}, u32[]{:S(2)}, u32[]{:S(2)}) collective-permute-start(f32[72,256]{1,0:T(8,128)} %get-tuple-element.122), channel_id=1, source_target_pairs={{0,64},{64,0},{128,192},{192,128},{1,65},{65,1},{129,193},{193,129... | collective-permute-start | bytes 221192 | tf_op jit(solution)/shard_map/ppermute | solution.py:431
  105.6 13.2 %collective-permute-start.13 = (f32[72,256]{1,0:T(8,128)}, f32[72,256]{1,0:T(8,128)}, u32[]{:S(2)}, u32[]{:S(2)}) collective-permute-start(f32[72,256]{1,0:T(8,128)} %get-tuple-element.123), channel_id=1, source_target_pairs={{0,128},{64,192},{128,0},{192,64},{1,129},{65,193},{129,1},{193,65... | collective-permute-start | bytes 221192 | tf_op jit(solution)/shard_map/ppermute | solution.py:431
  107.3 11.5 %collective-permute-start.14 = (f32[72,256]{1,0:T(8,128)}, f32[72,256]{1,0:T(8,128)}, u32[]{:S(2)}, u32[]{:S(2)}) collective-permute-start(f32[72,256]{1,0:T(8,128)} %get-tuple-element.124), channel_id=1, source_target_pairs={{0,192},{64,128},{128,64},{192,0},{1,193},{65,129},{129,65},{193,1... | collective-permute-start | bytes 221192 | tf_op jit(solution)/shard_map/ppermute | solution.py:431
  120.9 16.6 %all-to-all-start.5 = ((f32[16,8,384]{2,1,0:T(8,128)}), f32[16,8,384]{2,1,0:T(8,128)}, u32[]{:S(2)}, u32[]{:S(2)}) async-start(f32[16,8,384]{2,1,0:T(8,128)} %join.1), calls=%async_computation.5 | async-start | bytes 393216 | tf_op jit(solution)/shard_map/all_to_all | solution.py:538

commit v9 on v8

--- a/solution.py
+++ b/solution.py
@@ -220,20 +220,18 @@
         lv_o[:, c] = total
 
 
-def dk_kernel(me_ref, lk, fv, st, sk, dk_o, *send):
-    def body(step):
-        for k, c, r in my_groups(me_ref, step):
-            r_hi, r_lo = split(unpack_state(st[r, :]))
-            total = lk[:, c] + dot(fv[:, c], r_hi, NT) + dot(fv[:, c], r_lo, NT)
-            dk = (total * sk[:, c]).astype(BF)
-            dk_o[:, c] = dk
-            send[k][...] = dk.astype(F32)
-
-    each_step(body)
-
-
-def dtok_kernel(lv, fk, st, dq, dk, wq, wk, wv, dt_o, acc):
-    term = dot(dq[...], wq[...], NT) + dot(dk[...], wk[...], NT)
+def dk_kernel(first, me_ref, lk, fv, st, sk, dk_o, *send):
+    for k, c, r in my_groups(me_ref, first):
+        r_hi, r_lo = split(unpack_state(st[r, :]))
+        total = lk[:, c] + dot(fv[:, c], r_hi, NT) + dot(fv[:, c], r_lo, NT)
+        dk = (total * sk[:, c]).astype(BF)
+        dk_o[:, c] = dk
+        send[k - 2 * first][...] = dk.astype(F32)
+
+
+def dtok_kernel(me_ref, lv, fk, st, dq, near, far, wq, wk, wv, dt_o, acc):
+    dk = jnp.where(jnp.right_shift(me_ref[0], 1) == pl.program_id(0), near[...], far[...])
+    term = dot(dq[...], wq[...], NT) + dot(dk, wk[...], NT)
     dv = []
     for j, c in groups_of(lv):
         r_hi, r_lo = split(unpack_state(st[128 * j:128 * j + 128, :]))
@@ -256,19 +254,23 @@
 def wgrad_q_kernel(y_ref, t0, t1, t2, t3, d0, d1, d2, d3, all_o, *send):
     n = t0.shape[3]
     blocks, m = t0.shape[0], t0.shape[2]
-    res = jnp.zeros((blocks * m, d0.shape[1]), F32)
-    gain = jnp.zeros((8, d0.shape[1]), F32)
-    for i, (t, d) in enumerate(zip((t0, t1, t2, t3), (d0, d1, d2, d3))):
-        turned = t[...].reshape(blocks * m, n).astype(BF)
-        all_o[:, :, :, n * i:n * i + n] = turned.reshape(blocks, 1, m, n)
-        res = res + dot(turned, d[0:n, :].astype(BF))
-        gain = gain + d[n:n + 8, :]
-    for k, out in enumerate(send):
-        @pl.when(pl.program_id(0) == k)
-        def _():
+
+    def body(step):
+        parts = [d[0:n, :].astype(BF) for d in (d0, d1, d2, d3)]
+        gain = d0[n:n + 8, :] + d1[n:n + 8, :] + d2[n:n + 8, :] + d3[n:n + 8, :]
+        for i in range(2):
+            out = send[2 * step + i]
+            at = jnp.bitwise_xor(jnp.bitwise_and(y_ref[0], 1), i)
+            res = jnp.zeros((blocks * m, d0.shape[1]), F32)
+            for j, t in enumerate((t0, t1, t2, t3)):
+                turned = t[:, at].reshape(blocks * m, n).astype(BF)
+                all_o[:, at, :, n * j:n * j + n] = turned.reshape(blocks, m, n)
+                res = res + dot(turned, parts[j])
             out[:, 0:m, :] = res.reshape(blocks, m, res.shape[1])
-            for i in range(blocks):
-                out[i, m:m + 8, :] = gain
+            for block in range(blocks):
+                out[block, m:m + 8, :] = gain
+
+    each_step(body)
 
 
 def sum_y_kernel(x_ref, v0, v1, v2, v3, *send):
@@ -314,7 +316,7 @@
     each = v.shape[1] // 2
     for c in range(2):
         for b in range(2):
-            g = 2 * c + b
+            g = 2 * b + c
             total = v[8 * c + b]
             for w in range(1, 4):
                 total = total + v[8 * c + 2 * w + b]
@@ -395,7 +397,7 @@
     ngroup = lax.axis_size(GROUP)
     nv = lengths - lax.axis_index(SEQ) * n
     own = lambda axes: jnp.full((1,), lax.axis_index(axes), jnp.int32)
-    me = own(GROUP)
+    me = 2 * own("b") + own("c")
     gain = norm_gain.reshape(1, d)
     act = lambda dt: ((n, d), dt, col(n, w))
     st_rows = d // 2
@@ -425,6 +427,7 @@
         return lax.all_to_all(mine, SEQ, 0, 0, tiled=True).reshape(st_rows, 128)
 
     def swap(v, k):
+        k = (k & 1) * 2 + k // 2
         return lax.ppermute(v, GROUP, [(i, i ^ k) for i in range(ngroup)])
 
     def turn_about(axis, v, k):
@@ -475,24 +478,29 @@
     mine = run(parts, True, "suffix")
 
     r_in = from_parts(mine)
-    dn_4, t1, _ = tie((dn, t1, mine))
-    t3 = swap(t1, 2)
+    dn_4, t2, _ = tie((dn, t2, mine))
+    t3 = swap(t2, 1)
     (lk,) = call(
         local_k_kernel, (halves,), [col(n, w), col(n, w), col(n, w)], [act(F32)], "localk", 1,
     )(dn_4, fq, fv)
-    dk, *dk_send = call_mine(
-        dk_kernel,
-        [col_mine(n, w), col_mine(n, w), row_mine(w // 2, 128), col_mine(n, w)],
-        [mine_act] + [((n, GL), F32, whole((n, GL)))] * ngroup,
-        "dkey", 1,
-    )(me, lk, fv, r_in, sk)
-
-    dk_got = [dk_send[0]] + [swap(dk_send[k], k) for k in range(1, ngroup)]
+    def dkey(first, lk, name):
+        pair = lambda r: pl.BlockSpec((r, w), lambda _, me: (0, pair_at(first, me)))
+        wide = ((n, w), BF, whole((n, w)))
+        one = ((n, GL), F32, whole((n, GL)))
+        st_pair = pl.BlockSpec((w // 2, 128), lambda _, me: (pair_at(first, me), 0))
+        return call_mine(
+            functools.partial(dk_kernel, first), [pair(n), pair(n), st_pair, pair(n)],
+            [wide, one, one], name, 1, 1,
+        )(me, lk, fv, r_in, sk)
+
+    dk_far, *far = dkey(1, lk, "dkeyfar")
+
+    far_got = [swap(far[0], 2), swap(far[1], 3)]
     side = lax.axis_size("x")
     per = d // nxy
-    dq_got, _ = tie((dq_got, dk))
+    dq_got, _ = tie((dq_got, dk_far))
     at_y = lambda depth: pl.BlockSpec(
-        (side, 1, per, depth), lambda k, y: (0, jnp.bitwise_xor(y[0], k), 0, 0)
+        (side, 2, per, depth), lambda step, y: (0, pair_at(step, y), 0, 0)
     )
     by_xy = lambda v: v.reshape(side, side, per, v.shape[-1])
     qshape = (side, per + 8, GL)
@@ -500,9 +508,13 @@
         wgrad_q_kernel,
         [at_y(n)] * 4 + [whole((n + 8, GL))] * 4,
         [((side, side, per, 4 * n), BF, at_y(4 * n))] + [(qshape, F32, whole(qshape))] * side,
-        "wgradq", 2 * big, side,
+        "wgradq", 2 * big,
     )(own("y"), by_xy(t0), by_xy(t1), by_xy(t2), by_xy(t3), *dq_got)
     gq_got = [gq_send[0]] + [turn_about("y", gq_send[k], k) for k in range(1, side)]
+
+    lk_near, _ = tie((lk, gq_send[0]))
+    dk_near, *near = dkey(0, lk_near, "dkeynear")
+    dk_got = [near[0], swap(near[1], 1)] + far_got
 
     steps = 2
     kshape = (nxy, per, GL)
@@ -534,15 +546,16 @@
         join_kernel, (), [whole(qshape[1:])] * side + [whole(kshape)],
         [(jshape, F32, whole(jshape))], "join", 1 << 22,
     )(*gq_got, gk_parts)
-    dk_6, _ = tie((dk, both))
+    lv, _ = tie((lv, both))
     both = lax.all_to_all(both, last, 0, 0, tiled=True)
 
     (dt,) = call(
         dtok_kernel, (halves,),
-        [col(n, w), col(n, w), st_spec, col(n, w), col(n, w), col(d, w), col(d, w), col(d, w)],
+        [SMEM, col(n, w), col(n, w), st_spec, col(n, w), whole((n, w)), whole((n, w))]
+        + [col(d, w)] * 3,
         [((n, d), BF, whole((n, d)))], "dtok", 1,
         scratch=[pltpu.VMEM((n, d), F32)],
-    )(lv, fk, r_in, dq, dk_6, w_query, w_key, w_value)
+    )(me, lv, fk, r_in, dq, dk_near, dk_far, w_query, w_key, w_value)
     dw, dg = call(
         final_kernel, (), [whole(jshape)],
         [((2, each * d), F32, whole((2, each * d))), ((8, 128), F32, whole((8, 128)))],

time: 140 us -> 146 us (1.043)
  starting transfers between devices: 48.8 us -> 55.4 us
  waiting for transfers between devices: 27.3 us -> 25.1 us
    all_to_all x1, starting transfers between devices: 8.23 us -> 15.2 us  [on_device(): both = lax.all_to_all(both, last, 0, 0, tiled=True)]
    pallas_call x2 -> x3, Pallas kernels: 9.22 us -> 11.5 us  [the longest x1 6.29 us: on_device(): call(dtok_kernel, (halves,), [SMEM, col(n, w), col(n, w), st_spec, col(n,...]
  transfers between devices with their start and end apart: 21 -> 21, of which waited for: 10 -> 10; matrix products, arithmetic and copies ran while one was open for 0% -> 0% of each run, Pallas kernels for 38% -> 37%
where the time goes in v9:
time: 146 us; the launch traced here: 145 us
  Pallas kernels  62.8 us (43%)
  starting transfers between devices  55.4 us (38%)
  waiting for transfers between devices  25.1 us (17%)
    all_to_all x1, starting transfers between devices, on_device(): both = lax.all_to_all(both, last, 0, 0, tiled=True)  15.2 us
    all_to_all x2, starting transfers between devices, to_parts(): lax.all_to_all(st.reshape(nseq, st_rows // nseq, 128), SEQ, 0, 0, tiled=T...  12.3 us
    all_to_all x2, starting transfers between devices, from_parts(): return lax.all_to_all(mine, SEQ, 0, 0, tiled=True).reshape(st_rows, 128)  9.53 us
    all_to_all x2, waiting for transfers between devices, from_parts(): return lax.all_to_all(mine, SEQ, 0, 0, tiled=True).reshape(st_rows, 128)  8.64 us
    ppermute x6, starting transfers between devices, turn_about(): lax.ppermute(v, axis, [(i, i ^ k) for i in range(lax.axis_size(axis))])  7.72 us
    ppermute x6, waiting for transfers between devices, turn_about(): lax.ppermute(v, axis, [(i, i ^ k) for i in range(lax.axis_size(axis))])  6.43 us
    ppermute x9, starting transfers between devices, swap(): return lax.ppermute(v, GROUP, [(i, i ^ k) for i in range(ngroup)])  6.35 us
    pallas_call x1, Pallas kernels, on_device(): call(dtok_kernel, (halves,), [SMEM, col(n, w), col(n, w), st_spec, col(n,...  6.29 us
  transfers between devices with their start and end apart: 21, of which 10 were waited for; matrix products, arithmetic and copies ran while one was open for 0% of the time, Pallas kernels for 37%

profile of v9, /device:TPU:1, one launch (start us, length us, event | category | flops | bytes accessed | tf_op | source)
XLA Modules:
  0.0 144.7 jit_solution(283890941603161305)
XLA Ops:
  1.3 4.8 %kv.1 = (bf16[256,1024]{1,0:T(8,128)(2,1)}, bf16[256,1024]{1,0:T(8,128)(2,1)}, f32[256,1024]{1,0:T(8,128)}, f32[512,128]{1,0:T(8,128)}) custom-call(s32[1]{0:T(128)S(6)} %sub.7.nv_ref, bf16[256,1024]{1,0:T(8,128)(2,1)} %bitcast.19, bf16[1024,1024]{1,0:T(8,128)(2,1)} %wk.3, bf16[1024,1024]{1,0:T(8,128)(2,1)} %wv.3), custom_call_target="tpu_custom_call" | custom-call | flops 1073741824 | bytes 4194304 | tf_op jit(solution)/shard_map/kv/pallas_call | solution.py:408
  6.0 8.6 %all-to-all-start = ((f32[32,16,128]{2,1,0:T(8,128)}), f32[32,16,128]{2,1,0:T(8,128)S(1)}, u32[]{:S(2)}, u32[]{:S(2)}) async-start(f32[32,16,128]{2,1,0:T(8,128)} %bitcast.26), calls=%async_computation | async-start | bytes 524288 | tf_op jit(solution)/shard_map/all_to_all | solution.py:416
  17.1 3.7 %query.1 = (bf16[256,1024]{1,0:T(8,128)(2,1)}, bf16[1024,256]{1,0:T(8,128)(2,1)}, f32[256,1024]{1,0:T(8,128)}) custom-call(bf16[256,1024]{1,0:T(8,128)(2,1)} %bitcast.21, bf16[1024,1024]{1,0:T(8,128)(2,1)} %wq.3), custom_call_target="tpu_custom_call" | custom-call | flops 536870912 | bytes 4194304 | tf_op jit(solution)/shard_map/query/pallas_call | solution.py:442
  20.8 2.8 %all-to-all-done.v = f32[32,16,128]{2,1,0:T(8,128)S(1)} async-done(((f32[32,16,128]{2,1,0:T(8,128)}), f32[32,16,128]{2,1,0:T(8,128)S(1)}, u32[]{:S(2)}, u32[]{:S(2)}) %all-to-all-start) | async-done | bytes 262176 | tf_op jit(solution)/shard_map/all_to_all | solution.py:416
  26.0 4.9 %all-to-all-start.1 = ((f32[32,16,128]{2,1,0:T(8,128)}), f32[32,16,128]{2,1,0:T(8,128)}, u32[]{:S(2)}, u32[]{:S(2)}) async-start(f32[32,16,128]{2,1,0:T(8,128)} %prefix.1), calls=%async_computation.1 | async-start | bytes 524288 | tf_op jit(solution)/shard_map/all_to_all | solution.py:427
  30.9 5.1 %numer.1 = (f32[256,1024]{1,0:T(8,128)}, f32[256,1024]{1,0:T(8,128)}) custom-call(bf16[256,1024]{1,0:T(8,128)(2,1)} %get-tuple-element.81.fq, bf16[256,1024]{1,0:T(8,128)(2,1)} %get-tuple-element.82.fk, bf16[256,1024]{1,0:T(8,128)(2,1)} %get-tuple-element.83.fv, bf16[256,1024]{1,0:T(8,128)(2,1)} %bitcast.24, bf16[1024,1024]{1,0:T(8,128)(2,1)} %wo.3), custom_call_target="tpu_custom_call" | custom-call | flops 1073741824 | bytes 4194304 | tf_op jit(solution)/shard_map/numer/pallas_call | solution.py:455
  36.0 4.0 %all-to-all-done.1 = f32[32,16,128]{2,1,0:T(8,128)} async-done(((f32[32,16,128]{2,1,0:T(8,128)}), f32[32,16,128]{2,1,0:T(8,128)}, u32[]{:S(2)}, u32[]{:S(2)}) %all-to-all-start.1) | async-done | bytes 262176 | tf_op jit(solution)/shard_map/all_to_all | solution.py:427
  39.9 5.1 %norm.1 = (bf16[256,1024]{1,0:T(8,128)(2,1)}, f32[256,1024]{1,0:T(8,128)}, f32[512,128]{1,0:T(8,128)}, f32[8,1024]{1,0:T(8,128)}) custom-call(s32[1]{0:T(128)S(6)} %sub.7.nv_ref, f32[256,1024]{1,0:T(8,128)} %get-tuple-element.84.nl, f32[512,128]{1,0:T(8,128)} %bitcast.7.st, bf16[256,1024]{1,0:T(8,128)(2,1)} %get-tuple-element.81.fq, ...), custom_call_target="tpu_custom_call" | custom-call | flops 536870912 | bytes 4194304 | tf_op jit(solution)/shard_map/norm/pallas_call | solution.py:461
  45.1 3.7 %all-to-all-start.2 = ((f32[32,16,128]{2,1,0:T(8,128)}), f32[32,16,128]{2,1,0:T(8,128)S(1)}, u32[]{:S(2)}, u32[]{:S(2)}) async-start(f32[32,16,128]{2,1,0:T(8,128)} %bitcast.25), calls=%async_computation.2 | async-start | bytes 524288 | tf_op jit(solution)/shard_map/all_to_all | solution.py:416
  49.2 6.0 %dquery.1 = (bf16[256,1024]{1,0:T(8,128)(2,1)}, f32[264,256]{1,0:T(8,128)}, f32[264,256]{1,0:T(8,128)}, f32[264,256]{1,0:T(8,128)}, f32[264,256]{1,0:T(8,128)}) custom-call(s32[1]{0:T(128)} %bitcast.10.me_ref, f32[256,1024]{1,0:T(8,128)} %get-tuple-element.114.dn, f32[512,128]{1,0:T(8,128)} %bitcast.7.st, bf16[256,1024]{1,0:T(8,128)(2,1)} %get-tuple-element.82.fk, ...), custom_call_target="tpu_custom_call" | custom-call | flops 1073741824 | bytes 4194304 | tf_op jit(solution)/shard_map/dquery/pallas_call | solution.py:470
  55.2 2.7 %all-to-all-done.2.v = f32[32,16,128]{2,1,0:T(8,128)S(1)} async-done(((f32[32,16,128]{2,1,0:T(8,128)}), f32[32,16,128]{2,1,0:T(8,128)S(1)}, u32[]{:S(2)}, u32[]{:S(2)}) %all-to-all-start.2) | async-done | bytes 262176 | tf_op jit(solution)/shard_map/all_to_all | solution.py:416
  61.0 4.7 %all-to-all-start.3 = ((f32[32,16,128]{2,1,0:T(8,128)}), f32[32,16,128]{2,1,0:T(8,128)}, u32[]{:S(2)}, u32[]{:S(2)}) async-start(f32[32,16,128]{2,1,0:T(8,128)} %suffix.1), calls=%async_computation.3 | async-start | bytes 524288 | tf_op jit(solution)/shard_map/all_to_all | solution.py:427
  65.6 4.3 %localk.1.lk = f32[256,1024]{1,0:T(8,128)} custom-call(f32[256,1024]{1,0:T(8,128)} %get-tuple-element.114.dn, bf16[256,1024]{1,0:T(8,128)(2,1)} %get-tuple-element.81.fq, bf16[256,1024]{1,0:T(8,128)(2,1)} %get-tuple-element.83.fv), custom_call_target="tpu_custom_call" | custom-call | flops 1 | bytes 4194304 | tf_op jit(solution)/shard_map/localk/pallas_call | solution.py:483
  70.0 4.7 %all-to-all-done.3 = f32[32,16,128]{2,1,0:T(8,128)} async-done(((f32[32,16,128]{2,1,0:T(8,128)}), f32[32,16,128]{2,1,0:T(8,128)}, u32[]{:S(2)}, u32[]{:S(2)}) %all-to-all-start.3) | async-done | bytes 262176 | tf_op jit(solution)/shard_map/all_to_all | solution.py:427
  79.2 4.3 %wgradq.1 = (bf16[4,4,64,1024]{3,2,1,0:T(8,128)(2,1)}, f32[4,72,256]{2,1,0:T(8,128)}, f32[4,72,256]{2,1,0:T(8,128)}, f32[4,72,256]{2,1,0:T(8,128)}, f32[4,72,256]{2,1,0:T(8,128)}) custom-call(s32[1]{0:T(128)} %bitcast.y_ref, bf16[4,4,64,256]{3,2,1,0:T(8,128)(2,1)} %bitcast.22, f32[4,4,64,256]{3,2,1,0:T(8,128)} %bitcast.5.t1, f32[4,4,64,256]{3,2,1,0:T(8,128)} %bitcast.11.t2, ...), custom_call_target="tpu_custom_call" | custom-call | flops 1073741824 | bytes 4194304 | tf_op jit(solution)/shard_map/wgradq/pallas_call | solution.py:507
  83.5 2.6 %dkeynear.1 = (bf16[256,512]{1,0:T(8,128)(2,1)}, f32[256,256]{1,0:T(8,128)}, f32[256,256]{1,0:T(8,128)}) custom-call(s32[1]{0:T(128)} %bitcast.10.me_ref, f32[256,1024]{1,0:T(8,128)} %localk.1.lk, bf16[256,1024]{1,0:T(8,128)(2,1)} %get-tuple-element.83.fv, f32[512,128]{1,0:T(8,128)} %bitcast.13.st, f32[256,1024]{1,0:T(8,128)} %get-tuple-element.100.sk), custom_call_target="tpu_custom_call" | custom-call | flops 1 | bytes 4194304 | tf_op jit(solution)/shard_map/dkeynear/pallas_call | solution.py:491
  91.6 3.2 %wgradk.1 = f32[16,64,256]{2,1,0:T(8,128)} custom-call(bf16[1024,1024]{1,0:T(8,128)(2,1)} %bitcast.28, f32[256,256]{1,0:T(8,128)} %get-tuple-element.109.d0, f32[256,256]{1,0:T(8,128)} %collective-permute-done.6.d1, f32[256,256]{1,0:T(8,128)} %collective-permute-done.7.d2, f32[256,256]{1,0:T(8,128)} %collective-permute-done.8.d3), custom_call_target="tpu_custom_call" | custom-call | flops 214748364800 | bytes 4194304 | tf_op jit(solution)/shard_map/wgradk/pallas_call | solution.py:521
  94.8 4.3 %all-to-all-start.4 = ((f32[16,64,256]{2,1,0:T(8,128)}), f32[16,64,256]{2,1,0:T(8,128)}, u32[]{:S(2)}, u32[]{:S(2)}) async-start(f32[16,64,256]{2,1,0:T(8,128)} %wgradk.1), calls=%async_computation.4 | async-start | bytes 2097152 | tf_op jit(solution)/shard_map/all_to_all | solution.py:526
  99.2 2.7 %collective-permute-done.10.v2 = f32[4,72,256]{2,1,0:T(8,128)} collective-permute-done((f32[4,72,256]{2,1,0:T(8,128)}, f32[4,72,256]{2,1,0:T(8,128)}, u32[]{:S(2)}, u32[]{:S(2)}) %collective-permute-start.10) | collective-permute-done | bytes 294944 | tf_op jit(solution)/shard_map/ppermute | solution.py:434
  101.8 3.4 %collective-permute-done.11.v3 = f32[4,72,256]{2,1,0:T(8,128)} collective-permute-done((f32[4,72,256]{2,1,0:T(8,128)}, f32[4,72,256]{2,1,0:T(8,128)}, u32[]{:S(2)}, u32[]{:S(2)}) %collective-permute-start.11) | collective-permute-done | bytes 294944 | tf_op jit(solution)/shard_map/ppermute | solution.py:434
  107.9 3.2 %collective-permute-start.14 = (f32[72,256]{1,0:T(8,128)}, f32[72,256]{1,0:T(8,128)}, u32[]{:S(2)}, u32[]{:S(2)}) collective-permute-start(f32[72,256]{1,0:T(8,128)} %get-tuple-element.127), channel_id=1, source_target_pairs={{0,192},{64,128},{128,64},{192,0},{1,193},{65,129},{129,65},{193,1... | collective-permute-start | bytes 221192 | tf_op jit(solution)/shard_map/ppermute | solution.py:434
  111.1 5.1 %localv.1 = (bf16[256,1024]{1,0:T(8,128)(2,1)}, f32[256,1024]{1,0:T(8,128)}) custom-call(bf16[256,1024]{1,0:T(8,128)(2,1)} %get-tuple-element.113.at, bf16[1024,1024]{1,0:T(8,128)(2,1)} %wo.3, f32[256,1024]{1,0:T(8,128)} %get-tuple-element.114.dn, bf16[256,1024]{1,0:T(8,128)(2,1)} %get-tuple-element.81.fq, bf16[256,1024]{1,0:T(8,128)(2,1)} %get-tuple-element.82.fk), custom_call_target="tpu_custom_call" | custom-call | flops 214748364800 | bytes 4194304 | tf_op jit(solution)/shard_map/localv/pallas_call | solution.py:529
  119.6 15.2 %all-to-all-start.5 = ((f32[16,8,384]{2,1,0:T(8,128)}), f32[16,8,384]{2,1,0:T(8,128)}, u32[]{:S(2)}, u32[]{:S(2)}) async-start(f32[16,8,384]{2,1,0:T(8,128)} %join.1), calls=%async_computation.5 | async-start | bytes 393216 | tf_op jit(solution)/shard_map/all_to_all | solution.py:550
  134.8 6.3 %dtok.1 = bf16[256,1024]{1,0:T(8,128)(2,1)} custom-call(s32[1]{0:T(128)} %bitcast.10.me_ref, f32[256,1024]{1,0:T(8,128)} %get-tuple-element.135.lv, bf16[256,1024]{1,0:T(8,128)(2,1)} %get-tuple-element.82.fk, f32[512,128]{1,0:T(8,128)} %bitcast.13.st, bf16[256,1024]{1,0:T(8,128)(2,1)} %get-tuple-element.136.dq, bf16[256,512]{1,0:T(8,128)(2,1)} %get-tuple-element.137.near, ...), custom_call_target="tpu_custom_call" | custom-call | flops 1 | bytes 4194304 | tf_op jit(solution)/shard_map/dtok/pallas_call | solution.py:552
  (36 shorter events, 28.0 us)
Async XLA Ops:
  6.0 17.6 %all-to-all-start = ((f32[32,16,128]{2,1,0:T(8,128)}), f32[32,16,128]{2,1,0:T(8,128)S(1)}, u32[]{:S(2)}, u32[]{:S(2)}) async-start(f32[32,16,128]{2,1,0:T(8,128)} %bitcast.26), calls=%async_computation | async-start | bytes 524288 | tf_op jit(solution)/shard_map/all_to_all | solution.py:416
  24.4 34.2 %collective-permute-start.1 = (f32[1024,256]{1,0:T(8,128)}, f32[1024,256]{1,0:T(8,128)}, u32[]{:S(2)}, u32[]{:S(2)}) collective-permute-start(f32[1024,256]{1,0:T(8,128)} %get-tuple-element.79), channel_id=1, source_target_pairs={{0,1},{1,0},{8,9},{9,8},{2,3},{3,2},{10,11},{11,10},{4,5},{5,4},{1... | collective-permute-start | bytes 3145736 | tf_op jit(solution)/shard_map/ppermute | solution.py:431
  26.0 13.9 %all-to-all-start.1 = ((f32[32,16,128]{2,1,0:T(8,128)}), f32[32,16,128]{2,1,0:T(8,128)}, u32[]{:S(2)}, u32[]{:S(2)}) async-start(f32[32,16,128]{2,1,0:T(8,128)} %prefix.1), calls=%async_computation.1 | async-start | bytes 524288 | tf_op jit(solution)/shard_map/all_to_all | solution.py:427
  45.1 12.8 %all-to-all-start.2 = ((f32[32,16,128]{2,1,0:T(8,128)}), f32[32,16,128]{2,1,0:T(8,128)S(1)}, u32[]{:S(2)}, u32[]{:S(2)}) async-start(f32[32,16,128]{2,1,0:T(8,128)} %bitcast.25), calls=%async_computation.2 | async-start | bytes 524288 | tf_op jit(solution)/shard_map/all_to_all | solution.py:416
  48.8 30.3 %collective-permute-start = (f32[1024,256]{1,0:T(8,128)}, f32[1024,256]{1,0:T(8,128)}, u32[]{:S(2)}, u32[]{:S(2)}) collective-permute-start(f32[1024,256]{1,0:T(8,128)} %get-tuple-element.79), channel_id=1, source_target_pairs={{0,8},{1,9},{8,0},{9,1},{2,10},{3,11},{10,2},{11,3},{4,12},{5,13},... | collective-permute-start | bytes 3145736 | tf_op jit(solution)/shard_map/ppermute | solution.py:431
  58.6 20.5 %collective-permute-start.2 = (f32[1024,256]{1,0:T(8,128)}, f32[1024,256]{1,0:T(8,128)}, u32[]{:S(2)}, u32[]{:S(2)}) collective-permute-start(f32[1024,256]{1,0:T(8,128)} %collective-permute-done.1), channel_id=1, source_target_pairs={{0,8},{1,9},{8,0},{9,1},{2,10},{3,11},{10,2},{11,3},{4,12},{5,13},... | collective-permute-start | bytes 3145736 | tf_op jit(solution)/shard_map/ppermute | solution.py:431
  58.8 18.4 %collective-permute-start.3 = (f32[264,256]{1,0:T(8,128)}, f32[264,256]{1,0:T(8,128)}, u32[]{:S(2)}, u32[]{:S(2)}) collective-permute-start(f32[264,256]{1,0:T(8,128)} %get-tuple-element.96), channel_id=1, source_target_pairs={{0,8},{1,9},{8,0},{9,1},{2,10},{3,11},{10,2},{11,3},{4,12},{5,13},... | collective-permute-start | bytes 811016 | tf_op jit(solution)/shard_map/ppermute | solution.py:431
  59.1 18.1 %collective-permute-start.4 = (f32[264,256]{1,0:T(8,128)}, f32[264,256]{1,0:T(8,128)}, u32[]{:S(2)}, u32[]{:S(2)}) collective-permute-start(f32[264,256]{1,0:T(8,128)} %get-tuple-element.97), channel_id=1, source_target_pairs={{0,1},{1,0},{8,9},{9,8},{2,3},{3,2},{10,11},{11,10},{4,5},{5,4},{1... | collective-permute-start | bytes 811016 | tf_op jit(solution)/shard_map/ppermute | solution.py:431
  59.1 18.1 %collective-permute-start.5 = (f32[264,256]{1,0:T(8,128)}, f32[264,256]{1,0:T(8,128)}, u32[]{:S(2)}, u32[]{:S(2)}) collective-permute-start(f32[264,256]{1,0:T(8,128)} %get-tuple-element.98), channel_id=1, source_target_pairs={{0,9},{1,8},{8,1},{9,0},{2,11},{3,10},{10,3},{11,2},{4,13},{5,12},... | collective-permute-start | bytes 811016 | tf_op jit(solution)/shard_map/ppermute | solution.py:431
  61.0 13.7 %all-to-all-start.3 = ((f32[32,16,128]{2,1,0:T(8,128)}), f32[32,16,128]{2,1,0:T(8,128)}, u32[]{:S(2)}, u32[]{:S(2)}) async-start(f32[32,16,128]{2,1,0:T(8,128)} %suffix.1), calls=%async_computation.3 | async-start | bytes 524288 | tf_op jit(solution)/shard_map/all_to_all | solution.py:427
  77.2 11.1 %collective-permute-start.7 = (f32[256,256]{1,0:T(8,128)}, f32[256,256]{1,0:T(8,128)}, u32[]{:S(2)}, u32[]{:S(2)}) collective-permute-start(f32[256,256]{1,0:T(8,128)} %get-tuple-element.111), channel_id=1, source_target_pairs={{0,1},{1,0},{8,9},{9,8},{2,3},{3,2},{10,11},{11,10},{4,5},{5,4},{1... | collective-permute-start | bytes 786440 | tf_op jit(solution)/shard_map/ppermute | solution.py:431
  77.3 14.2 %collective-permute-start.8 = (f32[256,256]{1,0:T(8,128)}, f32[256,256]{1,0:T(8,128)}, u32[]{:S(2)}, u32[]{:S(2)}) collective-permute-start(f32[256,256]{1,0:T(8,128)} %get-tuple-element.112), channel_id=1, source_target_pairs={{0,9},{1,8},{8,1},{9,0},{2,11},{3,10},{10,3},{11,2},{4,13},{5,12},... | collective-permute-start | bytes 786440 | tf_op jit(solution)/shard_map/ppermute | solution.py:431
  86.1 5.5 %collective-permute-start.6 = (f32[256,256]{1,0:T(8,128)}, f32[256,256]{1,0:T(8,128)}, u32[]{:S(2)}, u32[]{:S(2)}) collective-permute-start(f32[256,256]{1,0:T(8,128)} %get-tuple-element.110), channel_id=1, source_target_pairs={{0,8},{1,9},{8,0},{9,1},{2,10},{3,11},{10,2},{11,3},{4,12},{5,13},... | collective-permute-start | bytes 786440 | tf_op jit(solution)/shard_map/ppermute | solution.py:431
  86.2 13.0 %collective-permute-start.9 = (f32[4,72,256]{2,1,0:T(8,128)}, f32[4,72,256]{2,1,0:T(8,128)}, u32[]{:S(2)}, u32[]{:S(2)}) collective-permute-start(f32[4,72,256]{2,1,0:T(8,128)} %get-tuple-element.117), channel_id=1, source_target_pairs={{0,16},{16,0},{32,48},{48,32},{1,17},{17,1},{33,49},{49,33},{2,18}... | collective-permute-start | bytes 884744 | tf_op jit(solution)/shard_map/ppermute | solution.py:434
  86.4 15.4 %collective-permute-start.10 = (f32[4,72,256]{2,1,0:T(8,128)}, f32[4,72,256]{2,1,0:T(8,128)}, u32[]{:S(2)}, u32[]{:S(2)}) collective-permute-start(f32[4,72,256]{2,1,0:T(8,128)} %get-tuple-element.118), channel_id=1, source_target_pairs={{0,32},{16,48},{32,0},{48,16},{1,33},{17,49},{33,1},{49,17},{2,34}... | collective-permute-start | bytes 884744 | tf_op jit(solution)/shard_map/ppermute | solution.py:434
  88.3 16.9 %collective-permute-start.11 = (f32[4,72,256]{2,1,0:T(8,128)}, f32[4,72,256]{2,1,0:T(8,128)}, u32[]{:S(2)}, u32[]{:S(2)}) collective-permute-start(f32[4,72,256]{2,1,0:T(8,128)} %get-tuple-element.119), channel_id=1, source_target_pairs={{0,48},{16,32},{32,16},{48,0},{1,49},{17,33},{33,17},{49,1},{2,50}... | collective-permute-start | bytes 884744 | tf_op jit(solution)/shard_map/ppermute | solution.py:434
  94.8 22.6 %all-to-all-start.4 = ((f32[16,64,256]{2,1,0:T(8,128)}), f32[16,64,256]{2,1,0:T(8,128)}, u32[]{:S(2)}, u32[]{:S(2)}) async-start(f32[16,64,256]{2,1,0:T(8,128)} %wgradk.1), calls=%async_computation.4 | async-start | bytes 2097152 | tf_op jit(solution)/shard_map/all_to_all | solution.py:526
  107.3 8.9 %collective-permute-start.12 = (f32[72,256]{1,0:T(8,128)}, f32[72,256]{1,0:T(8,128)}, u32[]{:S(2)}, u32[]{:S(2)}) collective-permute-start(f32[72,256]{1,0:T(8,128)} %get-tuple-element.125), channel_id=1, source_target_pairs={{0,64},{64,0},{128,192},{192,128},{1,65},{65,1},{129,193},{193,129... | collective-permute-start | bytes 221192 | tf_op jit(solution)/shard_map/ppermute | solution.py:434
  107.3 9.3 %collective-permute-start.13 = (f32[72,256]{1,0:T(8,128)}, f32[72,256]{1,0:T(8,128)}, u32[]{:S(2)}, u32[]{:S(2)}) collective-permute-start(f32[72,256]{1,0:T(8,128)} %get-tuple-element.126), channel_id=1, source_target_pairs={{0,128},{64,192},{128,0},{192,64},{1,129},{65,193},{129,1},{193,65... | collective-permute-start | bytes 221192 | tf_op jit(solution)/shard_map/ppermute | solution.py:434
  107.9 8.7 %collective-permute-start.14 = (f32[72,256]{1,0:T(8,128)}, f32[72,256]{1,0:T(8,128)}, u32[]{:S(2)}, u32[]{:S(2)}) collective-permute-start(f32[72,256]{1,0:T(8,128)} %get-tuple-element.127), channel_id=1, source_target_pairs={{0,192},{64,128},{128,64},{192,0},{1,193},{65,129},{129,65},{193,1... | collective-permute-start | bytes 221192 | tf_op jit(solution)/shard_map/ppermute | solution.py:434
  119.6 23.5 %all-to-all-start.5 = ((f32[16,8,384]{2,1,0:T(8,128)}), f32[16,8,384]{2,1,0:T(8,128)}, u32[]{:S(2)}, u32[]{:S(2)}) async-start(f32[16,8,384]{2,1,0:T(8,128)} %join.1), calls=%async_computation.5 | async-start | bytes 393216 | tf_op jit(solution)/shard_map/all_to_all | solution.py:550

commit v10 on v8

--- a/solution.py
+++ b/solution.py
@@ -256,19 +256,23 @@
 def wgrad_q_kernel(y_ref, t0, t1, t2, t3, d0, d1, d2, d3, all_o, *send):
     n = t0.shape[3]
     blocks, m = t0.shape[0], t0.shape[2]
-    res = jnp.zeros((blocks * m, d0.shape[1]), F32)
-    gain = jnp.zeros((8, d0.shape[1]), F32)
-    for i, (t, d) in enumerate(zip((t0, t1, t2, t3), (d0, d1, d2, d3))):
-        turned = t[...].reshape(blocks * m, n).astype(BF)
-        all_o[:, :, :, n * i:n * i + n] = turned.reshape(blocks, 1, m, n)
-        res = res + dot(turned, d[0:n, :].astype(BF))
-        gain = gain + d[n:n + 8, :]
-    for k, out in enumerate(send):
-        @pl.when(pl.program_id(0) == k)
-        def _():
+
+    def body(step):
+        parts = [d[0:n, :].astype(BF) for d in (d0, d1, d2, d3)]
+        gain = d0[n:n + 8, :] + d1[n:n + 8, :] + d2[n:n + 8, :] + d3[n:n + 8, :]
+        for i in range(2):
+            out = send[2 * step + i]
+            at = jnp.bitwise_xor(jnp.bitwise_and(y_ref[0], 1), i)
+            res = jnp.zeros((blocks * m, d0.shape[1]), F32)
+            for j, t in enumerate((t0, t1, t2, t3)):
+                turned = t[:, at].reshape(blocks * m, n).astype(BF)
+                all_o[:, at, :, n * j:n * j + n] = turned.reshape(blocks, m, n)
+                res = res + dot(turned, parts[j])
             out[:, 0:m, :] = res.reshape(blocks, m, res.shape[1])
-            for i in range(blocks):
-                out[i, m:m + 8, :] = gain
+            for block in range(blocks):
+                out[block, m:m + 8, :] = gain
+
+    each_step(body)
 
 
 def sum_y_kernel(x_ref, v0, v1, v2, v3, *send):
@@ -492,7 +496,7 @@
     per = d // nxy
     dq_got, _ = tie((dq_got, dk))
     at_y = lambda depth: pl.BlockSpec(
-        (side, 1, per, depth), lambda k, y: (0, jnp.bitwise_xor(y[0], k), 0, 0)
+        (side, 2, per, depth), lambda step, y: (0, pair_at(step, y), 0, 0)
     )
     by_xy = lambda v: v.reshape(side, side, per, v.shape[-1])
     qshape = (side, per + 8, GL)
@@ -500,7 +504,7 @@
         wgrad_q_kernel,
         [at_y(n)] * 4 + [whole((n + 8, GL))] * 4,
         [((side, side, per, 4 * n), BF, at_y(4 * n))] + [(qshape, F32, whole(qshape))] * side,
-        "wgradq", 2 * big, side,
+        "wgradq", 2 * big,
     )(own("y"), by_xy(t0), by_xy(t1), by_xy(t2), by_xy(t3), *dq_got)
     gq_got = [gq_send[0]] + [turn_about("y", gq_send[k], k) for k in range(1, side)]
 

time: 140 us -> 140 us (level)
  transfers between devices with their start and end apart: 21 -> 21, of which waited for: 10 -> 10; matrix products, arithmetic and copies ran while one was open for 0% -> 0% of each run, Pallas kernels for 38% -> 37%
where the time goes in v10:
time: 140 us; the launch traced here: 139 us
  Pallas kernels  60.4 us (43%)
  starting transfers between devices  48.8 us (35%)
  waiting for transfers between devices  28.4 us (20%)
  between operations  1.41 us (1%)
    all_to_all x2, starting transfers between devices, to_parts(): lax.all_to_all(st.reshape(nseq, st_rows // nseq, 128), SEQ, 0, 0, tiled=T...  12.3 us
    all_to_all x2, starting transfers between devices, from_parts(): return lax.all_to_all(mine, SEQ, 0, 0, tiled=True).reshape(st_rows, 128)  9.93 us
    all_to_all x2, waiting for transfers between devices, from_parts(): return lax.all_to_all(mine, SEQ, 0, 0, tiled=True).reshape(st_rows, 128)  8.64 us
    all_to_all x1, starting transfers between devices, on_device(): both = lax.all_to_all(both, last, 0, 0, tiled=True)  8.23 us
    ppermute x6, starting transfers between devices, turn_about(): lax.ppermute(v, axis, [(i, i ^ k) for i in range(lax.axis_size(axis))])  7.8 us
    ppermute x6, waiting for transfers between devices, turn_about(): lax.ppermute(v, axis, [(i, i ^ k) for i in range(lax.axis_size(axis))])  7.77 us
    ppermute x9, starting transfers between devices, swap(): return lax.ppermute(v, GROUP, [(i, i ^ k) for i in range(ngroup)])  6.21 us
    pallas_call x1, Pallas kernels, on_device(): call_mine(dq_kernel, [col_mine(n, w), row_mine(w // 2, 128)] + [col_mine(...  5.99 us
  transfers between devices with their start and end apart: 21, of which 10 were waited for; matrix products, arithmetic and copies ran while one was open for 0% of the time, Pallas kernels for 37%

profile of v10, /device:TPU:1, one launch (start us, length us, event | category | flops | bytes accessed | tf_op | source)
XLA Modules:
  0.0 139.1 jit_solution(6569665957225241690)
XLA Ops:
  1.3 4.7 %kv.1 = (bf16[256,1024]{1,0:T(8,128)(2,1)}, bf16[256,1024]{1,0:T(8,128)(2,1)}, f32[256,1024]{1,0:T(8,128)}, f32[512,128]{1,0:T(8,128)}) custom-call(s32[1]{0:T(128)S(6)} %sub.7.nv_ref, bf16[256,1024]{1,0:T(8,128)(2,1)} %bitcast.19, bf16[1024,1024]{1,0:T(8,128)(2,1)} %wk.3, bf16[1024,1024]{1,0:T(8,128)(2,1)} %wv.3), custom_call_target="tpu_custom_call" | custom-call | flops 1073741824 | bytes 4194304 | tf_op jit(solution)/shard_map/kv/pallas_call | solution.py:410
  6.0 8.6 %all-to-all-start = ((f32[32,16,128]{2,1,0:T(8,128)}), f32[32,16,128]{2,1,0:T(8,128)S(1)}, u32[]{:S(2)}, u32[]{:S(2)}) async-start(f32[32,16,128]{2,1,0:T(8,128)} %bitcast.26), calls=%async_computation | async-start | bytes 524288 | tf_op jit(solution)/shard_map/all_to_all | solution.py:418
  17.0 3.7 %query.1 = (bf16[256,1024]{1,0:T(8,128)(2,1)}, bf16[1024,256]{1,0:T(8,128)(2,1)}, f32[256,1024]{1,0:T(8,128)}) custom-call(bf16[256,1024]{1,0:T(8,128)(2,1)} %bitcast.21, bf16[1024,1024]{1,0:T(8,128)(2,1)} %wq.3), custom_call_target="tpu_custom_call" | custom-call | flops 536870912 | bytes 4194304 | tf_op jit(solution)/shard_map/query/pallas_call | solution.py:443
  20.7 2.8 %all-to-all-done.v = f32[32,16,128]{2,1,0:T(8,128)S(1)} async-done(((f32[32,16,128]{2,1,0:T(8,128)}), f32[32,16,128]{2,1,0:T(8,128)S(1)}, u32[]{:S(2)}, u32[]{:S(2)}) %all-to-all-start) | async-done | bytes 262176 | tf_op jit(solution)/shard_map/all_to_all | solution.py:418
  26.0 4.9 %all-to-all-start.1 = ((f32[32,16,128]{2,1,0:T(8,128)}), f32[32,16,128]{2,1,0:T(8,128)}, u32[]{:S(2)}, u32[]{:S(2)}) async-start(f32[32,16,128]{2,1,0:T(8,128)} %prefix.1), calls=%async_computation.1 | async-start | bytes 524288 | tf_op jit(solution)/shard_map/all_to_all | solution.py:429
  30.8 5.1 %numer.1 = (f32[256,1024]{1,0:T(8,128)}, f32[256,1024]{1,0:T(8,128)}) custom-call(bf16[256,1024]{1,0:T(8,128)(2,1)} %get-tuple-element.77.fq, bf16[256,1024]{1,0:T(8,128)(2,1)} %get-tuple-element.78.fk, bf16[256,1024]{1,0:T(8,128)(2,1)} %get-tuple-element.79.fv, bf16[256,1024]{1,0:T(8,128)(2,1)} %bitcast.24, bf16[1024,1024]{1,0:T(8,128)(2,1)} %wo.3), custom_call_target="tpu_custom_call" | custom-call | flops 1073741824 | bytes 4194304 | tf_op jit(solution)/shard_map/numer/pallas_call | solution.py:456
  35.9 4.0 %all-to-all-done.1 = f32[32,16,128]{2,1,0:T(8,128)} async-done(((f32[32,16,128]{2,1,0:T(8,128)}), f32[32,16,128]{2,1,0:T(8,128)}, u32[]{:S(2)}, u32[]{:S(2)}) %all-to-all-start.1) | async-done | bytes 262176 | tf_op jit(solution)/shard_map/all_to_all | solution.py:429
  39.9 5.2 %norm.1 = (bf16[256,1024]{1,0:T(8,128)(2,1)}, f32[256,1024]{1,0:T(8,128)}, f32[512,128]{1,0:T(8,128)}, f32[8,1024]{1,0:T(8,128)}) custom-call(s32[1]{0:T(128)S(6)} %sub.7.nv_ref, f32[256,1024]{1,0:T(8,128)} %get-tuple-element.80.nl, f32[512,128]{1,0:T(8,128)} %bitcast.6.st, bf16[256,1024]{1,0:T(8,128)(2,1)} %get-tuple-element.77.fq, ...), custom_call_target="tpu_custom_call" | custom-call | flops 536870912 | bytes 4194304 | tf_op jit(solution)/shard_map/norm/pallas_call | solution.py:462
  45.0 3.7 %all-to-all-start.2 = ((f32[32,16,128]{2,1,0:T(8,128)}), f32[32,16,128]{2,1,0:T(8,128)S(1)}, u32[]{:S(2)}, u32[]{:S(2)}) async-start(f32[32,16,128]{2,1,0:T(8,128)} %bitcast.25), calls=%async_computation.2 | async-start | bytes 524288 | tf_op jit(solution)/shard_map/all_to_all | solution.py:418
  49.2 6.0 %dquery.1 = (bf16[256,1024]{1,0:T(8,128)(2,1)}, f32[264,256]{1,0:T(8,128)}, f32[264,256]{1,0:T(8,128)}, f32[264,256]{1,0:T(8,128)}, f32[264,256]{1,0:T(8,128)}) custom-call(s32[1]{0:T(128)} %bitcast.9.me_ref, f32[256,1024]{1,0:T(8,128)} %get-tuple-element.110.dn, f32[512,128]{1,0:T(8,128)} %bitcast.6.st, bf16[256,1024]{1,0:T(8,128)(2,1)} %get-tuple-element.78.fk, ...), custom_call_target="tpu_custom_call" | custom-call | flops 1073741824 | bytes 4194304 | tf_op jit(solution)/shard_map/dquery/pallas_call | solution.py:471
  55.2 2.7 %all-to-all-done.2.v = f32[32,16,128]{2,1,0:T(8,128)S(1)} async-done(((f32[32,16,128]{2,1,0:T(8,128)}), f32[32,16,128]{2,1,0:T(8,128)S(1)}, u32[]{:S(2)}, u32[]{:S(2)}) %all-to-all-start.2) | async-done | bytes 262176 | tf_op jit(solution)/shard_map/all_to_all | solution.py:418
  60.7 5.1 %all-to-all-start.3 = ((f32[32,16,128]{2,1,0:T(8,128)}), f32[32,16,128]{2,1,0:T(8,128)}, u32[]{:S(2)}, u32[]{:S(2)}) async-start(f32[32,16,128]{2,1,0:T(8,128)} %suffix.1), calls=%async_computation.3 | async-start | bytes 524288 | tf_op jit(solution)/shard_map/all_to_all | solution.py:429
  65.8 4.4 %localk.1.lk = f32[256,1024]{1,0:T(8,128)} custom-call(f32[256,1024]{1,0:T(8,128)} %get-tuple-element.110.dn, bf16[256,1024]{1,0:T(8,128)(2,1)} %get-tuple-element.77.fq, bf16[256,1024]{1,0:T(8,128)(2,1)} %get-tuple-element.79.fv), custom_call_target="tpu_custom_call" | custom-call | flops 1 | bytes 4194304 | tf_op jit(solution)/shard_map/localk/pallas_call | solution.py:484
  70.2 4.7 %all-to-all-done.3 = f32[32,16,128]{2,1,0:T(8,128)} async-done(((f32[32,16,128]{2,1,0:T(8,128)}), f32[32,16,128]{2,1,0:T(8,128)}, u32[]{:S(2)}, u32[]{:S(2)}) %all-to-all-start.3) | async-done | bytes 262176 | tf_op jit(solution)/shard_map/all_to_all | solution.py:429
  74.8 3.3 %dkey.1 = (bf16[256,1024]{1,0:T(8,128)(2,1)}, f32[256,256]{1,0:T(8,128)}, f32[256,256]{1,0:T(8,128)}, f32[256,256]{1,0:T(8,128)}, f32[256,256]{1,0:T(8,128)}) custom-call(s32[1]{0:T(128)} %bitcast.9.me_ref, f32[256,1024]{1,0:T(8,128)} %localk.1.lk, bf16[256,1024]{1,0:T(8,128)(2,1)} %get-tuple-element.79.fv, f32[512,128]{1,0:T(8,128)} %bitcast.13.st, ...), custom_call_target="tpu_custom_call" | custom-call | flops 1 | bytes 4194304 | tf_op jit(solution)/shard_map/dkey/pallas_call | solution.py:487
  80.1 4.3 %wgradq.1 = (bf16[4,4,64,1024]{3,2,1,0:T(8,128)(2,1)}, f32[4,72,256]{2,1,0:T(8,128)}, f32[4,72,256]{2,1,0:T(8,128)}, f32[4,72,256]{2,1,0:T(8,128)}, f32[4,72,256]{2,1,0:T(8,128)}) custom-call(s32[1]{0:T(128)} %bitcast.y_ref, bf16[4,4,64,256]{3,2,1,0:T(8,128)(2,1)} %bitcast.22, f32[4,4,64,256]{3,2,1,0:T(8,128)} %bitcast.10.t1, f32[4,4,64,256]{3,2,1,0:T(8,128)} %bitcast.11.t2, ...), custom_call_target="tpu_custom_call" | custom-call | flops 1073741824 | bytes 4194304 | tf_op jit(solution)/shard_map/wgradq/pallas_call | solution.py:503
  88.4 4.1 %collective-permute-done.8.d3 = f32[256,256]{1,0:T(8,128)} collective-permute-done((f32[256,256]{1,0:T(8,128)}, f32[256,256]{1,0:T(8,128)}, u32[]{:S(2)}, u32[]{:S(2)}) %collective-permute-start.8) | collective-permute-done | bytes 262176 | tf_op jit(solution)/shard_map/ppermute | solution.py:432
  92.5 3.2 %wgradk.1 = f32[16,64,256]{2,1,0:T(8,128)} custom-call(bf16[1024,1024]{1,0:T(8,128)(2,1)} %bitcast.28, f32[256,256]{1,0:T(8,128)} %get-tuple-element.105.d0, f32[256,256]{1,0:T(8,128)} %collective-permute-done.6.d1, f32[256,256]{1,0:T(8,128)} %collective-permute-done.7.d2, f32[256,256]{1,0:T(8,128)} %collective-permute-done.8.d3), custom_call_target="tpu_custom_call" | custom-call | flops 214748364800 | bytes 4194304 | tf_op jit(solution)/shard_map/wgradk/pallas_call | solution.py:513
  95.7 4.3 %all-to-all-start.4 = ((f32[16,64,256]{2,1,0:T(8,128)}), f32[16,64,256]{2,1,0:T(8,128)}, u32[]{:S(2)}, u32[]{:S(2)}) async-start(f32[16,64,256]{2,1,0:T(8,128)} %wgradk.1), calls=%async_computation.4 | async-start | bytes 2097152 | tf_op jit(solution)/shard_map/all_to_all | solution.py:518
  107.7 5.1 %localv.1 = (bf16[256,1024]{1,0:T(8,128)(2,1)}, f32[256,1024]{1,0:T(8,128)}) custom-call(bf16[256,1024]{1,0:T(8,128)(2,1)} %get-tuple-element.109.at, bf16[1024,1024]{1,0:T(8,128)(2,1)} %wo.3, f32[256,1024]{1,0:T(8,128)} %get-tuple-element.110.dn, bf16[256,1024]{1,0:T(8,128)(2,1)} %get-tuple-element.77.fq, bf16[256,1024]{1,0:T(8,128)(2,1)} %get-tuple-element.78.fk), custom_call_target="tpu_custom_call" | custom-call | flops 214748364800 | bytes 4194304 | tf_op jit(solution)/shard_map/localv/pallas_call | solution.py:521
  112.8 2.6 %collective-permute-done.12.q1 = f32[72,256]{1,0:T(8,128)} collective-permute-done((f32[72,256]{1,0:T(8,128)}, f32[72,256]{1,0:T(8,128)}, u32[]{:S(2)}, u32[]{:S(2)}) %collective-permute-start.12) | collective-permute-done | bytes 73760 | tf_op jit(solution)/shard_map/ppermute | solution.py:435
  115.4 3.4 %collective-permute-done.13.q2 = f32[72,256]{1,0:T(8,128)} collective-permute-done((f32[72,256]{1,0:T(8,128)}, f32[72,256]{1,0:T(8,128)}, u32[]{:S(2)}, u32[]{:S(2)}) %collective-permute-start.13) | collective-permute-done | bytes 73760 | tf_op jit(solution)/shard_map/ppermute | solution.py:435
  120.9 8.2 %all-to-all-start.5 = ((f32[16,8,384]{2,1,0:T(8,128)}), f32[16,8,384]{2,1,0:T(8,128)}, u32[]{:S(2)}, u32[]{:S(2)}) async-start(f32[16,8,384]{2,1,0:T(8,128)} %join.1), calls=%async_computation.5 | async-start | bytes 393216 | tf_op jit(solution)/shard_map/all_to_all | solution.py:542
  129.2 6.0 %dtok.1 = bf16[256,1024]{1,0:T(8,128)(2,1)} custom-call(f32[256,1024]{1,0:T(8,128)} %get-tuple-element.126.lv, bf16[256,1024]{1,0:T(8,128)(2,1)} %get-tuple-element.78.fk, f32[512,128]{1,0:T(8,128)} %bitcast.13.st, bf16[256,1024]{1,0:T(8,128)(2,1)} %get-tuple-element.127.dq, bf16[256,1024]{1,0:T(8,128)(2,1)} %get-tuple-element.133.dk, ...), custom_call_target="tpu_custom_call" | custom-call | flops 1 | bytes 4194304 | tf_op jit(solution)/shard_map/dtok/pallas_call | solution.py:544
  (35 shorter events, 27.8 us)
Async XLA Ops:
  6.0 17.6 %all-to-all-start = ((f32[32,16,128]{2,1,0:T(8,128)}), f32[32,16,128]{2,1,0:T(8,128)S(1)}, u32[]{:S(2)}, u32[]{:S(2)}) async-start(f32[32,16,128]{2,1,0:T(8,128)} %bitcast.26), calls=%async_computation | async-start | bytes 524288 | tf_op jit(solution)/shard_map/all_to_all | solution.py:418
  24.3 34.3 %collective-permute-start = (f32[1024,256]{1,0:T(8,128)}, f32[1024,256]{1,0:T(8,128)}, u32[]{:S(2)}, u32[]{:S(2)}) collective-permute-start(f32[1024,256]{1,0:T(8,128)} %get-tuple-element.85), channel_id=1, source_target_pairs={{0,1},{1,0},{8,9},{9,8},{2,3},{3,2},{10,11},{11,10},{4,5},{5,4},{1... | collective-permute-start | bytes 3145736 | tf_op jit(solution)/shard_map/ppermute | solution.py:432
  26.0 13.9 %all-to-all-start.1 = ((f32[32,16,128]{2,1,0:T(8,128)}), f32[32,16,128]{2,1,0:T(8,128)}, u32[]{:S(2)}, u32[]{:S(2)}) async-start(f32[32,16,128]{2,1,0:T(8,128)} %prefix.1), calls=%async_computation.1 | async-start | bytes 524288 | tf_op jit(solution)/shard_map/all_to_all | solution.py:429
  45.0 12.8 %all-to-all-start.2 = ((f32[32,16,128]{2,1,0:T(8,128)}), f32[32,16,128]{2,1,0:T(8,128)S(1)}, u32[]{:S(2)}, u32[]{:S(2)}) async-start(f32[32,16,128]{2,1,0:T(8,128)} %bitcast.25), calls=%async_computation.2 | async-start | bytes 524288 | tf_op jit(solution)/shard_map/all_to_all | solution.py:418
  48.8 31.4 %collective-permute-start.1 = (f32[1024,256]{1,0:T(8,128)}, f32[1024,256]{1,0:T(8,128)}, u32[]{:S(2)}, u32[]{:S(2)}) collective-permute-start(f32[1024,256]{1,0:T(8,128)} %get-tuple-element.85), channel_id=1, source_target_pairs={{0,8},{1,9},{8,0},{9,1},{2,10},{3,11},{10,2},{11,3},{4,12},{5,13},... | collective-permute-start | bytes 3145736 | tf_op jit(solution)/shard_map/ppermute | solution.py:432
  58.6 21.5 %collective-permute-start.2 = (f32[1024,256]{1,0:T(8,128)}, f32[1024,256]{1,0:T(8,128)}, u32[]{:S(2)}, u32[]{:S(2)}) collective-permute-start(f32[1024,256]{1,0:T(8,128)} %collective-permute-done), channel_id=1, source_target_pairs={{0,8},{1,9},{8,0},{9,1},{2,10},{3,11},{10,2},{11,3},{4,12},{5,13},... | collective-permute-start | bytes 3145736 | tf_op jit(solution)/shard_map/ppermute | solution.py:432
  58.8 19.3 %collective-permute-start.3 = (f32[264,256]{1,0:T(8,128)}, f32[264,256]{1,0:T(8,128)}, u32[]{:S(2)}, u32[]{:S(2)}) collective-permute-start(f32[264,256]{1,0:T(8,128)} %get-tuple-element.94), channel_id=1, source_target_pairs={{0,1},{1,0},{8,9},{9,8},{2,3},{3,2},{10,11},{11,10},{4,5},{5,4},{1... | collective-permute-start | bytes 811016 | tf_op jit(solution)/shard_map/ppermute | solution.py:432
  58.8 19.4 %collective-permute-start.4 = (f32[264,256]{1,0:T(8,128)}, f32[264,256]{1,0:T(8,128)}, u32[]{:S(2)}, u32[]{:S(2)}) collective-permute-start(f32[264,256]{1,0:T(8,128)} %get-tuple-element.95), channel_id=1, source_target_pairs={{0,8},{1,9},{8,0},{9,1},{2,10},{3,11},{10,2},{11,3},{4,12},{5,13},... | collective-permute-start | bytes 811016 | tf_op jit(solution)/shard_map/ppermute | solution.py:432
  59.2 19.3 %collective-permute-start.5 = (f32[264,256]{1,0:T(8,128)}, f32[264,256]{1,0:T(8,128)}, u32[]{:S(2)}, u32[]{:S(2)}) collective-permute-start(f32[264,256]{1,0:T(8,128)} %get-tuple-element.96), channel_id=1, source_target_pairs={{0,9},{1,8},{8,1},{9,0},{2,11},{3,10},{10,3},{11,2},{4,13},{5,12},... | collective-permute-start | bytes 811016 | tf_op jit(solution)/shard_map/ppermute | solution.py:432
  60.7 14.1 %all-to-all-start.3 = ((f32[32,16,128]{2,1,0:T(8,128)}), f32[32,16,128]{2,1,0:T(8,128)}, u32[]{:S(2)}, u32[]{:S(2)}) async-start(f32[32,16,128]{2,1,0:T(8,128)} %suffix.1), calls=%async_computation.3 | async-start | bytes 524288 | tf_op jit(solution)/shard_map/all_to_all | solution.py:429
  78.1 8.5 %collective-permute-start.6 = (f32[256,256]{1,0:T(8,128)}, f32[256,256]{1,0:T(8,128)}, u32[]{:S(2)}, u32[]{:S(2)}) collective-permute-start(f32[256,256]{1,0:T(8,128)} %get-tuple-element.106), channel_id=1, source_target_pairs={{0,1},{1,0},{8,9},{9,8},{2,3},{3,2},{10,11},{11,10},{4,5},{5,4},{1... | collective-permute-start | bytes 786440 | tf_op jit(solution)/shard_map/ppermute | solution.py:432
  78.2 10.2 %collective-permute-start.7 = (f32[256,256]{1,0:T(8,128)}, f32[256,256]{1,0:T(8,128)}, u32[]{:S(2)}, u32[]{:S(2)}) collective-permute-start(f32[256,256]{1,0:T(8,128)} %get-tuple-element.107), channel_id=1, source_target_pairs={{0,8},{1,9},{8,0},{9,1},{2,10},{3,11},{10,2},{11,3},{4,12},{5,13},... | collective-permute-start | bytes 786440 | tf_op jit(solution)/shard_map/ppermute | solution.py:432
  78.5 13.9 %collective-permute-start.8 = (f32[256,256]{1,0:T(8,128)}, f32[256,256]{1,0:T(8,128)}, u32[]{:S(2)}, u32[]{:S(2)}) collective-permute-start(f32[256,256]{1,0:T(8,128)} %get-tuple-element.108), channel_id=1, source_target_pairs={{0,9},{1,8},{8,1},{9,0},{2,11},{3,10},{10,3},{11,2},{4,13},{5,12},... | collective-permute-start | bytes 786440 | tf_op jit(solution)/shard_map/ppermute | solution.py:432
  84.4 15.6 %collective-permute-start.9 = (f32[4,72,256]{2,1,0:T(8,128)}, f32[4,72,256]{2,1,0:T(8,128)}, u32[]{:S(2)}, u32[]{:S(2)}) collective-permute-start(f32[4,72,256]{2,1,0:T(8,128)} %get-tuple-element.114), channel_id=1, source_target_pairs={{0,16},{16,0},{32,48},{48,32},{1,17},{17,1},{33,49},{49,33},{2,18}... | collective-permute-start | bytes 884744 | tf_op jit(solution)/shard_map/ppermute | solution.py:435
  84.7 15.5 %collective-permute-start.10 = (f32[4,72,256]{2,1,0:T(8,128)}, f32[4,72,256]{2,1,0:T(8,128)}, u32[]{:S(2)}, u32[]{:S(2)}) collective-permute-start(f32[4,72,256]{2,1,0:T(8,128)} %get-tuple-element.115), channel_id=1, source_target_pairs={{0,32},{16,48},{32,0},{48,16},{1,33},{17,49},{33,1},{49,17},{2,34}... | collective-permute-start | bytes 884744 | tf_op jit(solution)/shard_map/ppermute | solution.py:435
  86.6 15.1 %collective-permute-start.11 = (f32[4,72,256]{2,1,0:T(8,128)}, f32[4,72,256]{2,1,0:T(8,128)}, u32[]{:S(2)}, u32[]{:S(2)}) collective-permute-start(f32[4,72,256]{2,1,0:T(8,128)} %get-tuple-element.116), channel_id=1, source_target_pairs={{0,48},{16,32},{32,16},{48,0},{1,49},{17,33},{33,17},{49,1},{2,50}... | collective-permute-start | bytes 884744 | tf_op jit(solution)/shard_map/ppermute | solution.py:435
  95.7 23.1 %all-to-all-start.4 = ((f32[16,64,256]{2,1,0:T(8,128)}), f32[16,64,256]{2,1,0:T(8,128)}, u32[]{:S(2)}, u32[]{:S(2)}) async-start(f32[16,64,256]{2,1,0:T(8,128)} %wgradk.1), calls=%async_computation.4 | async-start | bytes 2097152 | tf_op jit(solution)/shard_map/all_to_all | solution.py:518
  103.8 11.6 %collective-permute-start.12 = (f32[72,256]{1,0:T(8,128)}, f32[72,256]{1,0:T(8,128)}, u32[]{:S(2)}, u32[]{:S(2)}) collective-permute-start(f32[72,256]{1,0:T(8,128)} %get-tuple-element.122), channel_id=1, source_target_pairs={{0,64},{64,0},{128,192},{192,128},{1,65},{65,1},{129,193},{193,129... | collective-permute-start | bytes 221192 | tf_op jit(solution)/shard_map/ppermute | solution.py:435
  104.2 14.6 %collective-permute-start.13 = (f32[72,256]{1,0:T(8,128)}, f32[72,256]{1,0:T(8,128)}, u32[]{:S(2)}, u32[]{:S(2)}) collective-permute-start(f32[72,256]{1,0:T(8,128)} %get-tuple-element.123), channel_id=1, source_target_pairs={{0,128},{64,192},{128,0},{192,64},{1,129},{65,193},{129,1},{193,65... | collective-permute-start | bytes 221192 | tf_op jit(solution)/shard_map/ppermute | solution.py:435
  105.9 12.9 %collective-permute-start.14 = (f32[72,256]{1,0:T(8,128)}, f32[72,256]{1,0:T(8,128)}, u32[]{:S(2)}, u32[]{:S(2)}) collective-permute-start(f32[72,256]{1,0:T(8,128)} %get-tuple-element.124), channel_id=1, source_target_pairs={{0,192},{64,128},{128,64},{192,0},{1,193},{65,129},{129,65},{193,1... | collective-permute-start | bytes 221192 | tf_op jit(solution)/shard_map/ppermute | solution.py:435
  120.9 16.6 %all-to-all-start.5 = ((f32[16,8,384]{2,1,0:T(8,128)}), f32[16,8,384]{2,1,0:T(8,128)}, u32[]{:S(2)}, u32[]{:S(2)}) async-start(f32[16,8,384]{2,1,0:T(8,128)} %join.1), calls=%async_computation.5 | async-start | bytes 393216 | tf_op jit(solution)/shard_map/all_to_all | solution.py:542

commit v11 on v10

--- a/solution.py
+++ b/solution.py
@@ -172,7 +172,7 @@
         rs_o[r, :] = pack_state(dot(fqt[c, :], d_hi) + dot(fqt[c, :], d_lo))
 
 
-def dq_kernel(me_ref, dn, st, fk, fv, sq, gp, dq_o, *send):
+def dq_kernel(me_ref, dn, st, fk, fv, sq, gp, dq_o, mine, near, far):
     n = dn.shape[0]
 
     def body(step):
@@ -188,8 +188,9 @@
                 total = total + dot(w, pick(m, keys))
             dq = (total * sq[:, c]).astype(BF)
             dq_o[:, c] = dq
-            send[k][0:n, :] = dq.astype(F32)
-            send[k][n:n + 8, :] = gp[:, c]
+            out = (mine, far.at[0], near, far.at[1])[k]
+            out[0:n, :] = dq.astype(F32)
+            out[n:n + 8, :] = gp[:, c]
 
     each_step(body)
 
@@ -254,6 +255,7 @@
 
 
 def wgrad_q_kernel(y_ref, t0, t1, t2, t3, d0, d1, d2, d3, all_o, *send):
+    d1, d3 = d1.at[0], d3.at[0]
     n = t0.shape[3]
     blocks, m = t0.shape[0], t0.shape[2]
 
@@ -468,14 +470,16 @@
     parts = to_parts(rs)
     dn_3, _ = tie((dn, rs))
     mine_act = ((n, d), BF, col_mine(n, w))
-    dq, *dq_send = call_mine(
+    one = ((n + 8, GL), F32, whole((n + 8, GL)))
+    two = ((2, n + 8, GL), F32, whole((2, n + 8, GL)))
+    dq, dq_own, dq_near, dq_far = call_mine(
         dq_kernel,
         [col_mine(n, w), row_mine(w // 2, 128)] + [col_mine(n, w)] * 3 + [col_mine(8, w)],
-        [mine_act] + [((n + 8, GL), F32, whole((n + 8, GL)))] * ngroup,
-        "dquery", 2 * big,
+        [mine_act, one, one, two], "dquery", 2 * big,
     )(me, dn_3, st_in, fk, fv, sq, gp)
     parts, dq = tie((parts, dq))
-    dq_got = [dq_send[0]] + [swap(dq_send[k], k) for k in range(1, ngroup)]
+    dq_far = swap(dq_far, 1)
+    dq_near = swap(dq_near, 2)
     mine = run(parts, True, "suffix")
 
     r_in = from_parts(mine)
@@ -484,6 +488,7 @@
     (lk,) = call(
         local_k_kernel, (halves,), [col(n, w), col(n, w), col(n, w)], [act(F32)], "localk", 1,
     )(dn_4, fq, fv)
+    lk, dq_near, t2, t3 = tie((lk, dq_near, t2, t3))
     dk, *dk_send = call_mine(
         dk_kernel,
         [col_mine(n, w), col_mine(n, w), row_mine(w // 2, 128), col_mine(n, w)],
@@ -494,7 +499,8 @@
     dk_got = [dk_send[0]] + [swap(dk_send[k], k) for k in range(1, ngroup)]
     side = lax.axis_size("x")
     per = d // nxy
-    dq_got, _ = tie((dq_got, dk))
+    dq_far, _ = tie((dq_far, dk))
+    dq_got = [dq_own, dq_far, dq_near, swap(dq_far, 2)]
     at_y = lambda depth: pl.BlockSpec(
         (side, 2, per, depth), lambda step, y: (0, pair_at(step, y), 0, 0)
     )
@@ -502,7 +508,12 @@
     qshape = (side, per + 8, GL)
     tall, *gq_send = call_mine(
         wgrad_q_kernel,
-        [at_y(n)] * 4 + [whole((n + 8, GL))] * 4,
+        [at_y(n)] * 4 + [
+            whole((n + 8, GL)),
+            pl.BlockSpec((1, n + 8, GL), lambda *_: (0, 0, 0)),
+            whole((n + 8, GL)),
+            pl.BlockSpec((1, n + 8, GL), lambda *_: (1, 0, 0)),
+        ],
         [((side, side, per, 4 * n), BF, at_y(4 * n))] + [(qshape, F32, whole(qshape))] * side,
         "wgradq", 2 * big,
     )(own("y"), by_xy(t0), by_xy(t1), by_xy(t2), by_xy(t3), *dq_got)

time: 140 us -> 139 us (level)
  no operation moved by 1% of the time
where the time goes in v11:
time: 139 us
  Pallas kernels  60.4 us (43%)
  starting transfers between devices  48.3 us (35%)
  waiting for transfers between devices  28.4 us (20%)
  between operations  1.4 us (1%)
    all_to_all x2, starting transfers between devices, to_parts(): lax.all_to_all(st.reshape(nseq, st_rows // nseq, 128), SEQ, 0, 0, tiled=T...  12.3 us
    all_to_all x2, starting transfers between devices, from_parts(): return lax.all_to_all(mine, SEQ, 0, 0, tiled=True).reshape(st_rows, 128)  9.58 us
    all_to_all x1, starting transfers between devices, on_device(): both = lax.all_to_all(both, last, 0, 0, tiled=True)  9.1 us
    all_to_all x2, waiting for transfers between devices, from_parts(): return lax.all_to_all(mine, SEQ, 0, 0, tiled=True).reshape(st_rows, 128)  8.6 us
    ppermute x6, starting transfers between devices, turn_about(): lax.ppermute(v, axis, [(i, i ^ k) for i in range(lax.axis_size(axis))])  7.8 us
    ppermute x6, waiting for transfers between devices, turn_about(): lax.ppermute(v, axis, [(i, i ^ k) for i in range(lax.axis_size(axis))])  7.74 us
    pallas_call x1, Pallas kernels, on_device(): call_mine(dq_kernel, [col_mine(n, w), row_mine(w // 2, 128)] + [col_mine(...  5.99 us
    pallas_call x1, Pallas kernels, on_device(): call(dtok_kernel, (halves,), [col(n, w), col(n, w), st_spec, col(n, w), c...  5.83 us
  transfers between devices with their start and end apart: 21, of which 10 were waited for; matrix products, arithmetic and copies ran while one was open for 0% of the time, Pallas kernels for 37%

profile of v11, /device:TPU:1, one launch (start us, length us, event | category | flops | bytes accessed | tf_op | source)
XLA Modules:
  0.0 138.5 jit_solution(18023845442136268605)
XLA Ops:
  1.3 4.7 %kv.1 = (bf16[256,1024]{1,0:T(8,128)(2,1)}, bf16[256,1024]{1,0:T(8,128)(2,1)}, f32[256,1024]{1,0:T(8,128)}, f32[512,128]{1,0:T(8,128)}) custom-call(s32[1]{0:T(128)S(6)} %sub.7.nv_ref, bf16[256,1024]{1,0:T(8,128)(2,1)} %bitcast.19, bf16[1024,1024]{1,0:T(8,128)(2,1)} %wk.3, bf16[1024,1024]{1,0:T(8,128)(2,1)} %wv.3), custom_call_target="tpu_custom_call" | custom-call | flops 1073741824 | bytes 4194304 | tf_op jit(solution)/shard_map/kv/pallas_call | solution.py:412
  6.0 8.6 %all-to-all-start = ((f32[32,16,128]{2,1,0:T(8,128)}), f32[32,16,128]{2,1,0:T(8,128)S(1)}, u32[]{:S(2)}, u32[]{:S(2)}) async-start(f32[32,16,128]{2,1,0:T(8,128)} %bitcast.26), calls=%async_computation | async-start | bytes 524288 | tf_op jit(solution)/shard_map/all_to_all | solution.py:420
  17.1 3.7 %query.1 = (bf16[256,1024]{1,0:T(8,128)(2,1)}, bf16[1024,256]{1,0:T(8,128)(2,1)}, f32[256,1024]{1,0:T(8,128)}) custom-call(bf16[256,1024]{1,0:T(8,128)(2,1)} %bitcast.21, bf16[1024,1024]{1,0:T(8,128)(2,1)} %wq.3), custom_call_target="tpu_custom_call" | custom-call | flops 536870912 | bytes 4194304 | tf_op jit(solution)/shard_map/query/pallas_call | solution.py:445
  20.8 2.8 %all-to-all-done.v = f32[32,16,128]{2,1,0:T(8,128)S(1)} async-done(((f32[32,16,128]{2,1,0:T(8,128)}), f32[32,16,128]{2,1,0:T(8,128)S(1)}, u32[]{:S(2)}, u32[]{:S(2)}) %all-to-all-start) | async-done | bytes 262176 | tf_op jit(solution)/shard_map/all_to_all | solution.py:420
  26.0 4.9 %all-to-all-start.1 = ((f32[32,16,128]{2,1,0:T(8,128)}), f32[32,16,128]{2,1,0:T(8,128)}, u32[]{:S(2)}, u32[]{:S(2)}) async-start(f32[32,16,128]{2,1,0:T(8,128)} %prefix.1), calls=%async_computation.1 | async-start | bytes 524288 | tf_op jit(solution)/shard_map/all_to_all | solution.py:431
  31.0 5.1 %numer.1 = (f32[256,1024]{1,0:T(8,128)}, f32[256,1024]{1,0:T(8,128)}) custom-call(bf16[256,1024]{1,0:T(8,128)(2,1)} %get-tuple-element.77.fq, bf16[256,1024]{1,0:T(8,128)(2,1)} %get-tuple-element.78.fk, bf16[256,1024]{1,0:T(8,128)(2,1)} %get-tuple-element.79.fv, bf16[256,1024]{1,0:T(8,128)(2,1)} %bitcast.23, bf16[1024,1024]{1,0:T(8,128)(2,1)} %wo.3), custom_call_target="tpu_custom_call" | custom-call | flops 1073741824 | bytes 4194304 | tf_op jit(solution)/shard_map/numer/pallas_call | solution.py:458
  36.1 3.9 %all-to-all-done.1 = f32[32,16,128]{2,1,0:T(8,128)} async-done(((f32[32,16,128]{2,1,0:T(8,128)}), f32[32,16,128]{2,1,0:T(8,128)}, u32[]{:S(2)}, u32[]{:S(2)}) %all-to-all-start.1) | async-done | bytes 262176 | tf_op jit(solution)/shard_map/all_to_all | solution.py:431
  40.0 5.1 %norm.1 = (bf16[256,1024]{1,0:T(8,128)(2,1)}, f32[256,1024]{1,0:T(8,128)}, f32[512,128]{1,0:T(8,128)}, f32[8,1024]{1,0:T(8,128)}) custom-call(s32[1]{0:T(128)S(6)} %sub.7.nv_ref, f32[256,1024]{1,0:T(8,128)} %get-tuple-element.80.nl, f32[512,128]{1,0:T(8,128)} %bitcast.6.st, bf16[256,1024]{1,0:T(8,128)(2,1)} %get-tuple-element.77.fq, ...), custom_call_target="tpu_custom_call" | custom-call | flops 536870912 | bytes 4194304 | tf_op jit(solution)/shard_map/norm/pallas_call | solution.py:464
  45.1 3.7 %all-to-all-start.2 = ((f32[32,16,128]{2,1,0:T(8,128)}), f32[32,16,128]{2,1,0:T(8,128)S(1)}, u32[]{:S(2)}, u32[]{:S(2)}) async-start(f32[32,16,128]{2,1,0:T(8,128)} %bitcast.25), calls=%async_computation.2 | async-start | bytes 524288 | tf_op jit(solution)/shard_map/all_to_all | solution.py:420
  49.3 6.0 %dquery.1 = (bf16[256,1024]{1,0:T(8,128)(2,1)}, f32[264,256]{1,0:T(8,128)}, f32[264,256]{1,0:T(8,128)}, f32[2,264,256]{2,1,0:T(8,128)}) custom-call(s32[1]{0:T(128)} %bitcast.9.me_ref, f32[256,1024]{1,0:T(8,128)} %get-tuple-element.110.dn, f32[512,128]{1,0:T(8,128)} %bitcast.6.st, bf16[256,1024]{1,0:T(8,128)(2,1)} %get-tuple-element.78.fk, ...), custom_call_target="tpu_custom_call" | custom-call | flops 1073741824 | bytes 4194304 | tf_op jit(solution)/shard_map/dquery/pallas_call | solution.py:475
  55.3 2.7 %all-to-all-done.2.v = f32[32,16,128]{2,1,0:T(8,128)S(1)} async-done(((f32[32,16,128]{2,1,0:T(8,128)}), f32[32,16,128]{2,1,0:T(8,128)S(1)}, u32[]{:S(2)}, u32[]{:S(2)}) %all-to-all-start.2) | async-done | bytes 262176 | tf_op jit(solution)/shard_map/all_to_all | solution.py:420
  59.3 4.7 %all-to-all-start.3 = ((f32[32,16,128]{2,1,0:T(8,128)}), f32[32,16,128]{2,1,0:T(8,128)}, u32[]{:S(2)}, u32[]{:S(2)}) async-start(f32[32,16,128]{2,1,0:T(8,128)} %suffix.1), calls=%async_computation.3 | async-start | bytes 524288 | tf_op jit(solution)/shard_map/all_to_all | solution.py:431
  64.0 4.3 %localk.1.lk = f32[256,1024]{1,0:T(8,128)} custom-call(f32[256,1024]{1,0:T(8,128)} %get-tuple-element.110.dn, bf16[256,1024]{1,0:T(8,128)(2,1)} %get-tuple-element.77.fq, bf16[256,1024]{1,0:T(8,128)(2,1)} %get-tuple-element.79.fv), custom_call_target="tpu_custom_call" | custom-call | flops 1 | bytes 4194304 | tf_op jit(solution)/shard_map/localk/pallas_call | solution.py:488
  68.4 4.7 %all-to-all-done.3 = f32[32,16,128]{2,1,0:T(8,128)} async-done(((f32[32,16,128]{2,1,0:T(8,128)}), f32[32,16,128]{2,1,0:T(8,128)}, u32[]{:S(2)}, u32[]{:S(2)}) %all-to-all-start.3) | async-done | bytes 262176 | tf_op jit(solution)/shard_map/all_to_all | solution.py:431
  73.0 3.2 %dkey.1 = (bf16[256,1024]{1,0:T(8,128)(2,1)}, f32[256,256]{1,0:T(8,128)}, f32[256,256]{1,0:T(8,128)}, f32[256,256]{1,0:T(8,128)}, f32[256,256]{1,0:T(8,128)}) custom-call(s32[1]{0:T(128)} %bitcast.9.me_ref, f32[256,1024]{1,0:T(8,128)} %localk.1.lk, bf16[256,1024]{1,0:T(8,128)(2,1)} %get-tuple-element.79.fv, f32[512,128]{1,0:T(8,128)} %bitcast.13.st, ...), custom_call_target="tpu_custom_call" | custom-call | flops 1 | bytes 4194304 | tf_op jit(solution)/shard_map/dkey/pallas_call | solution.py:492
  78.8 4.3 %wgradq.1 = (bf16[4,4,64,1024]{3,2,1,0:T(8,128)(2,1)}, f32[4,72,256]{2,1,0:T(8,128)}, f32[4,72,256]{2,1,0:T(8,128)}, f32[4,72,256]{2,1,0:T(8,128)}, f32[4,72,256]{2,1,0:T(8,128)}) custom-call(s32[1]{0:T(128)} %bitcast.y_ref, bf16[4,4,64,256]{3,2,1,0:T(8,128)(2,1)} %bitcast.24, f32[4,4,64,256]{3,2,1,0:T(8,128)} %bitcast.10.t1, f32[4,4,64,256]{3,2,1,0:T(8,128)} %bitcast.11.t2, ...), custom_call_target="tpu_custom_call" | custom-call | flops 1073741824 | bytes 4194304 | tf_op jit(solution)/shard_map/wgradq/pallas_call | solution.py:509
  87.1 4.0 %collective-permute-done.8.d3 = f32[256,256]{1,0:T(8,128)} collective-permute-done((f32[256,256]{1,0:T(8,128)}, f32[256,256]{1,0:T(8,128)}, u32[]{:S(2)}, u32[]{:S(2)}) %collective-permute-start.8) | collective-permute-done | bytes 262176 | tf_op jit(solution)/shard_map/ppermute | solution.py:434
  91.1 3.2 %wgradk.1 = f32[16,64,256]{2,1,0:T(8,128)} custom-call(bf16[1024,1024]{1,0:T(8,128)(2,1)} %bitcast.28, f32[256,256]{1,0:T(8,128)} %get-tuple-element.105.d0, f32[256,256]{1,0:T(8,128)} %collective-permute-done.6.d1, f32[256,256]{1,0:T(8,128)} %collective-permute-done.7.d2, f32[256,256]{1,0:T(8,128)} %collective-permute-done.8.d3), custom_call_target="tpu_custom_call" | custom-call | flops 214748364800 | bytes 4194304 | tf_op jit(solution)/shard_map/wgradk/pallas_call | solution.py:524
  94.3 4.3 %all-to-all-start.4 = ((f32[16,64,256]{2,1,0:T(8,128)}), f32[16,64,256]{2,1,0:T(8,128)}, u32[]{:S(2)}, u32[]{:S(2)}) async-start(f32[16,64,256]{2,1,0:T(8,128)} %wgradk.1), calls=%async_computation.4 | async-start | bytes 2097152 | tf_op jit(solution)/shard_map/all_to_all | solution.py:529
  106.6 5.1 %localv.1 = (bf16[256,1024]{1,0:T(8,128)(2,1)}, f32[256,1024]{1,0:T(8,128)}) custom-call(bf16[256,1024]{1,0:T(8,128)(2,1)} %get-tuple-element.109.at, bf16[1024,1024]{1,0:T(8,128)(2,1)} %wo.3, f32[256,1024]{1,0:T(8,128)} %get-tuple-element.110.dn, bf16[256,1024]{1,0:T(8,128)(2,1)} %get-tuple-element.77.fq, bf16[256,1024]{1,0:T(8,128)(2,1)} %get-tuple-element.78.fk), custom_call_target="tpu_custom_call" | custom-call | flops 214748364800 | bytes 4194304 | tf_op jit(solution)/shard_map/localv/pallas_call | solution.py:532
  114.0 3.4 %collective-permute-done.13.q2 = f32[72,256]{1,0:T(8,128)} collective-permute-done((f32[72,256]{1,0:T(8,128)}, f32[72,256]{1,0:T(8,128)}, u32[]{:S(2)}, u32[]{:S(2)}) %collective-permute-start.13) | collective-permute-done | bytes 73760 | tf_op jit(solution)/shard_map/ppermute | solution.py:437
  119.5 9.1 %all-to-all-start.5 = ((f32[16,8,384]{2,1,0:T(8,128)}), f32[16,8,384]{2,1,0:T(8,128)}, u32[]{:S(2)}, u32[]{:S(2)}) async-start(f32[16,8,384]{2,1,0:T(8,128)} %join.1), calls=%async_computation.5 | async-start | bytes 393216 | tf_op jit(solution)/shard_map/all_to_all | solution.py:553
  128.6 5.8 %dtok.1 = bf16[256,1024]{1,0:T(8,128)(2,1)} custom-call(f32[256,1024]{1,0:T(8,128)} %get-tuple-element.126.lv, bf16[256,1024]{1,0:T(8,128)(2,1)} %get-tuple-element.78.fk, f32[512,128]{1,0:T(8,128)} %bitcast.13.st, bf16[256,1024]{1,0:T(8,128)(2,1)} %get-tuple-element.127.dq, bf16[256,1024]{1,0:T(8,128)(2,1)} %get-tuple-element.133.dk, ...), custom_call_target="tpu_custom_call" | custom-call | flops 1 | bytes 4194304 | tf_op jit(solution)/shard_map/dtok/pallas_call | solution.py:555
  134.4 2.6 %all-to-all-done.5.v = f32[16,8,384]{2,1,0:T(8,128)} async-done(((f32[16,8,384]{2,1,0:T(8,128)}), f32[16,8,384]{2,1,0:T(8,128)}, u32[]{:S(2)}, u32[]{:S(2)}) %all-to-all-start.5) | async-done | bytes 196640 | tf_op jit(solution)/shard_map/all_to_all | solution.py:553
  (35 shorter events, 27.1 us)
Async XLA Ops:
  6.0 17.6 %all-to-all-start = ((f32[32,16,128]{2,1,0:T(8,128)}), f32[32,16,128]{2,1,0:T(8,128)S(1)}, u32[]{:S(2)}, u32[]{:S(2)}) async-start(f32[32,16,128]{2,1,0:T(8,128)} %bitcast.26), calls=%async_computation | async-start | bytes 524288 | tf_op jit(solution)/shard_map/all_to_all | solution.py:420
  24.4 34.3 %collective-permute-start = (f32[1024,256]{1,0:T(8,128)}, f32[1024,256]{1,0:T(8,128)}, u32[]{:S(2)}, u32[]{:S(2)}) collective-permute-start(f32[1024,256]{1,0:T(8,128)} %get-tuple-element.85), channel_id=1, source_target_pairs={{0,1},{1,0},{8,9},{9,8},{2,3},{3,2},{10,11},{11,10},{4,5},{5,4},{1... | collective-permute-start | bytes 3145736 | tf_op jit(solution)/shard_map/ppermute | solution.py:434
  26.0 14.0 %all-to-all-start.1 = ((f32[32,16,128]{2,1,0:T(8,128)}), f32[32,16,128]{2,1,0:T(8,128)}, u32[]{:S(2)}, u32[]{:S(2)}) async-start(f32[32,16,128]{2,1,0:T(8,128)} %prefix.1), calls=%async_computation.1 | async-start | bytes 524288 | tf_op jit(solution)/shard_map/all_to_all | solution.py:431
  45.1 12.8 %all-to-all-start.2 = ((f32[32,16,128]{2,1,0:T(8,128)}), f32[32,16,128]{2,1,0:T(8,128)S(1)}, u32[]{:S(2)}, u32[]{:S(2)}) async-start(f32[32,16,128]{2,1,0:T(8,128)} %bitcast.25), calls=%async_computation.2 | async-start | bytes 524288 | tf_op jit(solution)/shard_map/all_to_all | solution.py:420
  48.9 19.5 %collective-permute-start.2 = (f32[1024,256]{1,0:T(8,128)}, f32[1024,256]{1,0:T(8,128)}, u32[]{:S(2)}, u32[]{:S(2)}) collective-permute-start(f32[1024,256]{1,0:T(8,128)} %get-tuple-element.85), channel_id=1, source_target_pairs={{0,8},{1,9},{8,0},{9,1},{2,10},{3,11},{10,2},{11,3},{4,12},{5,13},... | collective-permute-start | bytes 3145736 | tf_op jit(solution)/shard_map/ppermute | solution.py:434
  58.7 9.7 %collective-permute-start.3 = (f32[1024,256]{1,0:T(8,128)}, f32[1024,256]{1,0:T(8,128)}, u32[]{:S(2)}, u32[]{:S(2)}) collective-permute-start(f32[1024,256]{1,0:T(8,128)} %collective-permute-done), channel_id=1, source_target_pairs={{0,8},{1,9},{8,0},{9,1},{2,10},{3,11},{10,2},{11,3},{4,12},{5,13},... | collective-permute-start | bytes 3145736 | tf_op jit(solution)/shard_map/ppermute | solution.py:434
  58.9 17.4 %collective-permute-start.4 = (f32[2,264,256]{2,1,0:T(8,128)}, f32[2,264,256]{2,1,0:T(8,128)}, u32[]{:S(2)}, u32[]{:S(2)}) collective-permute-start(f32[2,264,256]{2,1,0:T(8,128)} %get-tuple-element.98), channel_id=1, source_target_pairs={{0,1},{1,0},{8,9},{9,8},{2,3},{3,2},{10,11},{11,10},{4,5},{5,4},{1... | collective-permute-start | bytes 1622024 | tf_op jit(solution)/shard_map/ppermute | solution.py:434
  58.9 9.5 %collective-permute-start.1 = (f32[264,256]{1,0:T(8,128)}, f32[264,256]{1,0:T(8,128)}, u32[]{:S(2)}, u32[]{:S(2)}) collective-permute-start(f32[264,256]{1,0:T(8,128)} %get-tuple-element.94), channel_id=1, source_target_pairs={{0,8},{1,9},{8,0},{9,1},{2,10},{3,11},{10,2},{11,3},{4,12},{5,13},... | collective-permute-start | bytes 811016 | tf_op jit(solution)/shard_map/ppermute | solution.py:434
  59.3 13.7 %all-to-all-start.3 = ((f32[32,16,128]{2,1,0:T(8,128)}), f32[32,16,128]{2,1,0:T(8,128)}, u32[]{:S(2)}, u32[]{:S(2)}) async-start(f32[32,16,128]{2,1,0:T(8,128)} %suffix.1), calls=%async_computation.3 | async-start | bytes 524288 | tf_op jit(solution)/shard_map/all_to_all | solution.py:431
  76.3 2.5 %collective-permute-start.5 = (f32[2,264,256]{2,1,0:T(8,128)}, f32[2,264,256]{2,1,0:T(8,128)}, u32[]{:S(2)}, u32[]{:S(2)}) collective-permute-start(f32[2,264,256]{2,1,0:T(8,128)} %collective-permute-done.4.d1), channel_id=1, source_target_pairs={{0,8},{1,9},{8,0},{9,1},{2,10},{3,11},{10,2},{11,3},{4,12},{5,13},... | collective-permute-start | bytes 1622024 | tf_op jit(solution)/shard_map/ppermute | solution.py:434
  76.6 8.7 %collective-permute-start.6 = (f32[256,256]{1,0:T(8,128)}, f32[256,256]{1,0:T(8,128)}, u32[]{:S(2)}, u32[]{:S(2)}) collective-permute-start(f32[256,256]{1,0:T(8,128)} %get-tuple-element.106), channel_id=1, source_target_pairs={{0,1},{1,0},{8,9},{9,8},{2,3},{3,2},{10,11},{11,10},{4,5},{5,4},{1... | collective-permute-start | bytes 786440 | tf_op jit(solution)/shard_map/ppermute | solution.py:434
  78.3 8.8 %collective-permute-start.7 = (f32[256,256]{1,0:T(8,128)}, f32[256,256]{1,0:T(8,128)}, u32[]{:S(2)}, u32[]{:S(2)}) collective-permute-start(f32[256,256]{1,0:T(8,128)} %get-tuple-element.107), channel_id=1, source_target_pairs={{0,8},{1,9},{8,0},{9,1},{2,10},{3,11},{10,2},{11,3},{4,12},{5,13},... | collective-permute-start | bytes 786440 | tf_op jit(solution)/shard_map/ppermute | solution.py:434
  78.8 12.3 %collective-permute-start.8 = (f32[256,256]{1,0:T(8,128)}, f32[256,256]{1,0:T(8,128)}, u32[]{:S(2)}, u32[]{:S(2)}) collective-permute-start(f32[256,256]{1,0:T(8,128)} %get-tuple-element.108), channel_id=1, source_target_pairs={{0,9},{1,8},{8,1},{9,0},{2,11},{3,10},{10,3},{11,2},{4,13},{5,12},... | collective-permute-start | bytes 786440 | tf_op jit(solution)/shard_map/ppermute | solution.py:434
  83.1 15.5 %collective-permute-start.9 = (f32[4,72,256]{2,1,0:T(8,128)}, f32[4,72,256]{2,1,0:T(8,128)}, u32[]{:S(2)}, u32[]{:S(2)}) collective-permute-start(f32[4,72,256]{2,1,0:T(8,128)} %get-tuple-element.114), channel_id=1, source_target_pairs={{0,16},{16,0},{32,48},{48,32},{1,17},{17,1},{33,49},{49,33},{2,18}... | collective-permute-start | bytes 884744 | tf_op jit(solution)/shard_map/ppermute | solution.py:437
  83.4 15.5 %collective-permute-start.10 = (f32[4,72,256]{2,1,0:T(8,128)}, f32[4,72,256]{2,1,0:T(8,128)}, u32[]{:S(2)}, u32[]{:S(2)}) collective-permute-start(f32[4,72,256]{2,1,0:T(8,128)} %get-tuple-element.115), channel_id=1, source_target_pairs={{0,32},{16,48},{32,0},{48,16},{1,33},{17,49},{33,1},{49,17},{2,34}... | collective-permute-start | bytes 884744 | tf_op jit(solution)/shard_map/ppermute | solution.py:437
  85.4 15.4 %collective-permute-start.11 = (f32[4,72,256]{2,1,0:T(8,128)}, f32[4,72,256]{2,1,0:T(8,128)}, u32[]{:S(2)}, u32[]{:S(2)}) collective-permute-start(f32[4,72,256]{2,1,0:T(8,128)} %get-tuple-element.116), channel_id=1, source_target_pairs={{0,48},{16,32},{32,16},{48,0},{1,49},{17,33},{33,17},{49,1},{2,50}... | collective-permute-start | bytes 884744 | tf_op jit(solution)/shard_map/ppermute | solution.py:437
  94.3 23.1 %all-to-all-start.4 = ((f32[16,64,256]{2,1,0:T(8,128)}), f32[16,64,256]{2,1,0:T(8,128)}, u32[]{:S(2)}, u32[]{:S(2)}) async-start(f32[16,64,256]{2,1,0:T(8,128)} %wgradk.1), calls=%async_computation.4 | async-start | bytes 2097152 | tf_op jit(solution)/shard_map/all_to_all | solution.py:529
  102.8 11.2 %collective-permute-start.12 = (f32[72,256]{1,0:T(8,128)}, f32[72,256]{1,0:T(8,128)}, u32[]{:S(2)}, u32[]{:S(2)}) collective-permute-start(f32[72,256]{1,0:T(8,128)} %get-tuple-element.122), channel_id=1, source_target_pairs={{0,64},{64,0},{128,192},{192,128},{1,65},{65,1},{129,193},{193,129... | collective-permute-start | bytes 221192 | tf_op jit(solution)/shard_map/ppermute | solution.py:437
  103.2 14.1 %collective-permute-start.13 = (f32[72,256]{1,0:T(8,128)}, f32[72,256]{1,0:T(8,128)}, u32[]{:S(2)}, u32[]{:S(2)}) collective-permute-start(f32[72,256]{1,0:T(8,128)} %get-tuple-element.123), channel_id=1, source_target_pairs={{0,128},{64,192},{128,0},{192,64},{1,129},{65,193},{129,1},{193,65... | collective-permute-start | bytes 221192 | tf_op jit(solution)/shard_map/ppermute | solution.py:437
  105.0 12.4 %collective-permute-start.14 = (f32[72,256]{1,0:T(8,128)}, f32[72,256]{1,0:T(8,128)}, u32[]{:S(2)}, u32[]{:S(2)}) collective-permute-start(f32[72,256]{1,0:T(8,128)} %get-tuple-element.124), channel_id=1, source_target_pairs={{0,192},{64,128},{128,64},{192,0},{1,193},{65,129},{129,65},{193,1... | collective-permute-start | bytes 221192 | tf_op jit(solution)/shard_map/ppermute | solution.py:437
  119.5 17.5 %all-to-all-start.5 = ((f32[16,8,384]{2,1,0:T(8,128)}), f32[16,8,384]{2,1,0:T(8,128)}, u32[]{:S(2)}, u32[]{:S(2)}) async-start(f32[16,8,384]{2,1,0:T(8,128)} %join.1), calls=%async_computation.5 | async-start | bytes 393216 | tf_op jit(solution)/shard_map/all_to_all | solution.py:553

commit v12 on v11

--- a/solution.py
+++ b/solution.py
@@ -303,21 +303,21 @@
     for i in range(1, k.shape[0]):
         total = total + k[i]
     height, width = total.shape
-    each = out.shape[1] // 2
+    each = height // out.shape[0]
     q = q0[...] + q1[...] + q2[...] + q3[...]
     gain = jnp.sum(q[height:height + 8], axis=0, keepdims=True)
-    parts = [gain[:, 128 * i:128 * i + 128] for i in range(width // 128)]
-    parts.append(jnp.zeros((2 * each - len(parts), 128), F32))
-    tile = jnp.concatenate(parts, axis=0)
     for j in range(out.shape[0]):
-        out[j, 0:each, 0:width] = q[each * j:each * j + each]
-        out[j, each:2 * each, 0:width] = total[each * j:each * j + each]
-        out[j, :, width:width + 128] = tile
+        for i in range(each):
+            r = each * j + i
+            out[j, :, width * i:width * i + width] = q[r:r + 1]
+            at = width * (each + i)
+            out[j, :, at:at + width] = total[r:r + 1]
+        out[j, :, 2 * each * width:] = gain
 
 
 def final_kernel(v, dw_o, dg_o):
-    width = v.shape[2] - 128
-    each = v.shape[1] // 2
+    width = GL
+    each = (v.shape[2] // width - 1) // 2
     for c in range(2):
         for b in range(2):
             g = 2 * c + b
@@ -326,10 +326,12 @@
                 total = total + v[8 * c + 2 * w + b]
             for which in range(2):
                 for i in range(each):
-                    r = which * each + i
+                    r = width * (which * each + i)
                     at = 4 * width * i + width * g
-                    dw_o[which:which + 1, at:at + width] = total[r:r + 1, 0:width]
-            dg_o[2 * g:2 * g + 2, :] = total[0:2, width:width + 128]
+                    dw_o[which:which + 1, at:at + width] = total[:, r:r + width]
+            for i in range(2):
+                r = width * 2 * each + 128 * i
+                dg_o[2 * g + i:2 * g + i + 1, :] = total[:, r:r + 128]
 
 
 def call(kernel, grid, in_specs, outs, name, flops, scratch=()):
@@ -544,7 +546,7 @@
     last = ("c", "w", "b")
     nlast = lax.axis_size(last)
     each = per // nlast
-    jshape = (nlast, 2 * each, GL + 128)
+    jshape = (nlast, 1, (2 * each + 1) * GL)
     (both,) = call(
         join_kernel, (), [whole(qshape[1:])] * side + [whole(kshape)],
         [(jshape, F32, whole(jshape))], "join", 1 << 22,

time: 139 us -> 139 us (level)
  no operation moved by 1% of the time
where the time goes in v12:
time: 139 us; the launch traced here: 138 us
  Pallas kernels  60.4 us (43%)
  starting transfers between devices  48.3 us (35%)
  waiting for transfers between devices  27.6 us (20%)
  between operations  1.4 us (1%)
    all_to_all x2, starting transfers between devices, to_parts(): lax.all_to_all(st.reshape(nseq, st_rows // nseq, 128), SEQ, 0, 0, tiled=T...  12.3 us
    all_to_all x2, starting transfers between devices, from_parts(): return lax.all_to_all(mine, SEQ, 0, 0, tiled=True).reshape(st_rows, 128)  9.58 us
    all_to_all x1, starting transfers between devices, on_device(): both = lax.all_to_all(both, last, 0, 0, tiled=True)  9.1 us
    all_to_all x2, waiting for transfers between devices, from_parts(): return lax.all_to_all(mine, SEQ, 0, 0, tiled=True).reshape(st_rows, 128)  8.6 us
    ppermute x6, starting transfers between devices, turn_about(): lax.ppermute(v, axis, [(i, i ^ k) for i in range(lax.axis_size(axis))])  7.8 us
    ppermute x6, waiting for transfers between devices, turn_about(): lax.ppermute(v, axis, [(i, i ^ k) for i in range(lax.axis_size(axis))])  7.74 us
    pallas_call x1, Pallas kernels, on_device(): call_mine(dq_kernel, [col_mine(n, w), row_mine(w // 2, 128)] + [col_mine(...  5.99 us
    pallas_call x1, Pallas kernels, on_device(): call(dtok_kernel, (halves,), [col(n, w), col(n, w), st_spec, col(n, w), c...  5.83 us
  transfers between devices with their start and end apart: 21, of which 10 were waited for; matrix products, arithmetic and copies ran while one was open for 0% of the time, Pallas kernels for 37%

profile of v12, /device:TPU:1, one launch (start us, length us, event | category | flops | bytes accessed | tf_op | source)
XLA Modules:
  0.0 137.8 jit_solution(6238289771885916205)
XLA Ops:
  1.3 4.7 %kv.1 = (bf16[256,1024]{1,0:T(8,128)(2,1)}, bf16[256,1024]{1,0:T(8,128)(2,1)}, f32[256,1024]{1,0:T(8,128)}, f32[512,128]{1,0:T(8,128)}) custom-call(s32[1]{0:T(128)S(6)} %sub.7.nv_ref, bf16[256,1024]{1,0:T(8,128)(2,1)} %bitcast.19, bf16[1024,1024]{1,0:T(8,128)(2,1)} %wk.3, bf16[1024,1024]{1,0:T(8,128)(2,1)} %wv.3), custom_call_target="tpu_custom_call" | custom-call | flops 1073741824 | bytes 4194304 | tf_op jit(solution)/shard_map/kv/pallas_call | solution.py:414
  6.0 8.6 %all-to-all-start = ((f32[32,16,128]{2,1,0:T(8,128)}), f32[32,16,128]{2,1,0:T(8,128)S(1)}, u32[]{:S(2)}, u32[]{:S(2)}) async-start(f32[32,16,128]{2,1,0:T(8,128)} %bitcast.26), calls=%async_computation | async-start | bytes 524288 | tf_op jit(solution)/shard_map/all_to_all | solution.py:422
  14.6 2.5 %turn.1 = (bf16[1024,256]{1,0:T(8,128)(2,1)}, f32[1024,256]{1,0:T(8,128)}) custom-call(bf16[256,1024]{1,0:T(8,128)(2,1)} %bitcast.20), custom_call_target="tpu_custom_call" | custom-call | flops 134217728 | bytes 4194304 | tf_op jit(solution)/shard_map/turn/pallas_call | solution.py:443
  17.1 3.7 %query.1 = (bf16[256,1024]{1,0:T(8,128)(2,1)}, bf16[1024,256]{1,0:T(8,128)(2,1)}, f32[256,1024]{1,0:T(8,128)}) custom-call(bf16[256,1024]{1,0:T(8,128)(2,1)} %bitcast.21, bf16[1024,1024]{1,0:T(8,128)(2,1)} %wq.3), custom_call_target="tpu_custom_call" | custom-call | flops 536870912 | bytes 4194304 | tf_op jit(solution)/shard_map/query/pallas_call | solution.py:447
  20.8 2.8 %all-to-all-done.v = f32[32,16,128]{2,1,0:T(8,128)S(1)} async-done(((f32[32,16,128]{2,1,0:T(8,128)}), f32[32,16,128]{2,1,0:T(8,128)S(1)}, u32[]{:S(2)}, u32[]{:S(2)}) %all-to-all-start) | async-done | bytes 262176 | tf_op jit(solution)/shard_map/all_to_all | solution.py:422
  26.0 4.9 %all-to-all-start.1 = ((f32[32,16,128]{2,1,0:T(8,128)}), f32[32,16,128]{2,1,0:T(8,128)}, u32[]{:S(2)}, u32[]{:S(2)}) async-start(f32[32,16,128]{2,1,0:T(8,128)} %prefix.1), calls=%async_computation.1 | async-start | bytes 524288 | tf_op jit(solution)/shard_map/all_to_all | solution.py:433
  31.0 5.1 %numer.1 = (f32[256,1024]{1,0:T(8,128)}, f32[256,1024]{1,0:T(8,128)}) custom-call(bf16[256,1024]{1,0:T(8,128)(2,1)} %get-tuple-element.77.fq, bf16[256,1024]{1,0:T(8,128)(2,1)} %get-tuple-element.78.fk, bf16[256,1024]{1,0:T(8,128)(2,1)} %get-tuple-element.79.fv, bf16[256,1024]{1,0:T(8,128)(2,1)} %bitcast.23, bf16[1024,1024]{1,0:T(8,128)(2,1)} %wo.3), custom_call_target="tpu_custom_call" | custom-call | flops 1073741824 | bytes 4194304 | tf_op jit(solution)/shard_map/numer/pallas_call | solution.py:460
  36.1 3.9 %all-to-all-done.1 = f32[32,16,128]{2,1,0:T(8,128)} async-done(((f32[32,16,128]{2,1,0:T(8,128)}), f32[32,16,128]{2,1,0:T(8,128)}, u32[]{:S(2)}, u32[]{:S(2)}) %all-to-all-start.1) | async-done | bytes 262176 | tf_op jit(solution)/shard_map/all_to_all | solution.py:433
  40.0 5.1 %norm.1 = (bf16[256,1024]{1,0:T(8,128)(2,1)}, f32[256,1024]{1,0:T(8,128)}, f32[512,128]{1,0:T(8,128)}, f32[8,1024]{1,0:T(8,128)}) custom-call(s32[1]{0:T(128)S(6)} %sub.7.nv_ref, f32[256,1024]{1,0:T(8,128)} %get-tuple-element.80.nl, f32[512,128]{1,0:T(8,128)} %bitcast.6.st, bf16[256,1024]{1,0:T(8,128)(2,1)} %get-tuple-element.77.fq, ...), custom_call_target="tpu_custom_call" | custom-call | flops 536870912 | bytes 4194304 | tf_op jit(solution)/shard_map/norm/pallas_call | solution.py:466
  45.1 3.7 %all-to-all-start.2 = ((f32[32,16,128]{2,1,0:T(8,128)}), f32[32,16,128]{2,1,0:T(8,128)S(1)}, u32[]{:S(2)}, u32[]{:S(2)}) async-start(f32[32,16,128]{2,1,0:T(8,128)} %bitcast.25), calls=%async_computation.2 | async-start | bytes 524288 | tf_op jit(solution)/shard_map/all_to_all | solution.py:422
  49.3 6.0 %dquery.1 = (bf16[256,1024]{1,0:T(8,128)(2,1)}, f32[264,256]{1,0:T(8,128)}, f32[264,256]{1,0:T(8,128)}, f32[2,264,256]{2,1,0:T(8,128)}) custom-call(s32[1]{0:T(128)} %bitcast.9.me_ref, f32[256,1024]{1,0:T(8,128)} %get-tuple-element.110.dn, f32[512,128]{1,0:T(8,128)} %bitcast.6.st, bf16[256,1024]{1,0:T(8,128)(2,1)} %get-tuple-element.78.fk, ...), custom_call_target="tpu_custom_call" | custom-call | flops 1073741824 | bytes 4194304 | tf_op jit(solution)/shard_map/dquery/pallas_call | solution.py:477
  55.3 2.7 %all-to-all-done.2.v = f32[32,16,128]{2,1,0:T(8,128)S(1)} async-done(((f32[32,16,128]{2,1,0:T(8,128)}), f32[32,16,128]{2,1,0:T(8,128)S(1)}, u32[]{:S(2)}, u32[]{:S(2)}) %all-to-all-start.2) | async-done | bytes 262176 | tf_op jit(solution)/shard_map/all_to_all | solution.py:422
  59.3 4.7 %all-to-all-start.3 = ((f32[32,16,128]{2,1,0:T(8,128)}), f32[32,16,128]{2,1,0:T(8,128)}, u32[]{:S(2)}, u32[]{:S(2)}) async-start(f32[32,16,128]{2,1,0:T(8,128)} %suffix.1), calls=%async_computation.3 | async-start | bytes 524288 | tf_op jit(solution)/shard_map/all_to_all | solution.py:433
  64.0 4.3 %localk.1.lk = f32[256,1024]{1,0:T(8,128)} custom-call(f32[256,1024]{1,0:T(8,128)} %get-tuple-element.110.dn, bf16[256,1024]{1,0:T(8,128)(2,1)} %get-tuple-element.77.fq, bf16[256,1024]{1,0:T(8,128)(2,1)} %get-tuple-element.79.fv), custom_call_target="tpu_custom_call" | custom-call | flops 1 | bytes 4194304 | tf_op jit(solution)/shard_map/localk/pallas_call | solution.py:490
  68.4 4.7 %all-to-all-done.3 = f32[32,16,128]{2,1,0:T(8,128)} async-done(((f32[32,16,128]{2,1,0:T(8,128)}), f32[32,16,128]{2,1,0:T(8,128)}, u32[]{:S(2)}, u32[]{:S(2)}) %all-to-all-start.3) | async-done | bytes 262176 | tf_op jit(solution)/shard_map/all_to_all | solution.py:433
  73.0 3.2 %dkey.1 = (bf16[256,1024]{1,0:T(8,128)(2,1)}, f32[256,256]{1,0:T(8,128)}, f32[256,256]{1,0:T(8,128)}, f32[256,256]{1,0:T(8,128)}, f32[256,256]{1,0:T(8,128)}) custom-call(s32[1]{0:T(128)} %bitcast.9.me_ref, f32[256,1024]{1,0:T(8,128)} %localk.1.lk, bf16[256,1024]{1,0:T(8,128)(2,1)} %get-tuple-element.79.fv, f32[512,128]{1,0:T(8,128)} %bitcast.13.st, ...), custom_call_target="tpu_custom_call" | custom-call | flops 1 | bytes 4194304 | tf_op jit(solution)/shard_map/dkey/pallas_call | solution.py:494
  78.8 4.3 %wgradq.1 = (bf16[4,4,64,1024]{3,2,1,0:T(8,128)(2,1)}, f32[4,72,256]{2,1,0:T(8,128)}, f32[4,72,256]{2,1,0:T(8,128)}, f32[4,72,256]{2,1,0:T(8,128)}, f32[4,72,256]{2,1,0:T(8,128)}) custom-call(s32[1]{0:T(128)} %bitcast.y_ref, bf16[4,4,64,256]{3,2,1,0:T(8,128)(2,1)} %bitcast.24, f32[4,4,64,256]{3,2,1,0:T(8,128)} %bitcast.10.t1, f32[4,4,64,256]{3,2,1,0:T(8,128)} %bitcast.11.t2, ...), custom_call_target="tpu_custom_call" | custom-call | flops 1073741824 | bytes 4194304 | tf_op jit(solution)/shard_map/wgradq/pallas_call | solution.py:511
  87.1 4.0 %collective-permute-done.8.d3 = f32[256,256]{1,0:T(8,128)} collective-permute-done((f32[256,256]{1,0:T(8,128)}, f32[256,256]{1,0:T(8,128)}, u32[]{:S(2)}, u32[]{:S(2)}) %collective-permute-start.8) | collective-permute-done | bytes 262176 | tf_op jit(solution)/shard_map/ppermute | solution.py:436
  91.1 3.2 %wgradk.1 = f32[16,64,256]{2,1,0:T(8,128)} custom-call(bf16[1024,1024]{1,0:T(8,128)(2,1)} %bitcast.28, f32[256,256]{1,0:T(8,128)} %get-tuple-element.105.d0, f32[256,256]{1,0:T(8,128)} %collective-permute-done.6.d1, f32[256,256]{1,0:T(8,128)} %collective-permute-done.7.d2, f32[256,256]{1,0:T(8,128)} %collective-permute-done.8.d3), custom_call_target="tpu_custom_call" | custom-call | flops 214748364800 | bytes 4194304 | tf_op jit(solution)/shard_map/wgradk/pallas_call | solution.py:526
  94.3 4.3 %all-to-all-start.4 = ((f32[16,64,256]{2,1,0:T(8,128)}), f32[16,64,256]{2,1,0:T(8,128)}, u32[]{:S(2)}, u32[]{:S(2)}) async-start(f32[16,64,256]{2,1,0:T(8,128)} %wgradk.1), calls=%async_computation.4 | async-start | bytes 2097152 | tf_op jit(solution)/shard_map/all_to_all | solution.py:531
  106.6 5.1 %localv.1 = (bf16[256,1024]{1,0:T(8,128)(2,1)}, f32[256,1024]{1,0:T(8,128)}) custom-call(bf16[256,1024]{1,0:T(8,128)(2,1)} %get-tuple-element.109.at, bf16[1024,1024]{1,0:T(8,128)(2,1)} %wo.3, f32[256,1024]{1,0:T(8,128)} %get-tuple-element.110.dn, bf16[256,1024]{1,0:T(8,128)(2,1)} %get-tuple-element.77.fq, bf16[256,1024]{1,0:T(8,128)(2,1)} %get-tuple-element.78.fk), custom_call_target="tpu_custom_call" | custom-call | flops 214748364800 | bytes 4194304 | tf_op jit(solution)/shard_map/localv/pallas_call | solution.py:534
  114.0 3.4 %collective-permute-done.13.q2 = f32[72,256]{1,0:T(8,128)} collective-permute-done((f32[72,256]{1,0:T(8,128)}, f32[72,256]{1,0:T(8,128)}, u32[]{:S(2)}, u32[]{:S(2)}) %collective-permute-start.13) | collective-permute-done | bytes 73760 | tf_op jit(solution)/shard_map/ppermute | solution.py:439
  119.5 9.1 %all-to-all-start.5 = ((f32[16,1,2304]{2,1,0:T(1,128)}), f32[16,1,2304]{2,1,0:T(1,128)}, u32[]{:S(2)}, u32[]{:S(2)}) async-start(f32[16,1,2304]{2,1,0:T(1,128)} %join.1), calls=%async_computation.5 | async-start | bytes 294912 | tf_op jit(solution)/shard_map/all_to_all | solution.py:555
  128.6 5.8 %dtok.1 = bf16[256,1024]{1,0:T(8,128)(2,1)} custom-call(f32[256,1024]{1,0:T(8,128)} %get-tuple-element.126.lv, bf16[256,1024]{1,0:T(8,128)(2,1)} %get-tuple-element.78.fk, f32[512,128]{1,0:T(8,128)} %bitcast.13.st, bf16[256,1024]{1,0:T(8,128)(2,1)} %get-tuple-element.127.dq, bf16[256,1024]{1,0:T(8,128)(2,1)} %get-tuple-element.133.dk, ...), custom_call_target="tpu_custom_call" | custom-call | flops 1 | bytes 4194304 | tf_op jit(solution)/shard_map/dtok/pallas_call | solution.py:557
  (35 shorter events, 26.4 us)
Async XLA Ops:
  6.0 17.6 %all-to-all-start = ((f32[32,16,128]{2,1,0:T(8,128)}), f32[32,16,128]{2,1,0:T(8,128)S(1)}, u32[]{:S(2)}, u32[]{:S(2)}) async-start(f32[32,16,128]{2,1,0:T(8,128)} %bitcast.26), calls=%async_computation | async-start | bytes 524288 | tf_op jit(solution)/shard_map/all_to_all | solution.py:422
  24.4 34.3 %collective-permute-start = (f32[1024,256]{1,0:T(8,128)}, f32[1024,256]{1,0:T(8,128)}, u32[]{:S(2)}, u32[]{:S(2)}) collective-permute-start(f32[1024,256]{1,0:T(8,128)} %get-tuple-element.85), channel_id=1, source_target_pairs={{0,1},{1,0},{8,9},{9,8},{2,3},{3,2},{10,11},{11,10},{4,5},{5,4},{1... | collective-permute-start | bytes 3145736 | tf_op jit(solution)/shard_map/ppermute | solution.py:436
  26.0 14.0 %all-to-all-start.1 = ((f32[32,16,128]{2,1,0:T(8,128)}), f32[32,16,128]{2,1,0:T(8,128)}, u32[]{:S(2)}, u32[]{:S(2)}) async-start(f32[32,16,128]{2,1,0:T(8,128)} %prefix.1), calls=%async_computation.1 | async-start | bytes 524288 | tf_op jit(solution)/shard_map/all_to_all | solution.py:433
  45.1 12.8 %all-to-all-start.2 = ((f32[32,16,128]{2,1,0:T(8,128)}), f32[32,16,128]{2,1,0:T(8,128)S(1)}, u32[]{:S(2)}, u32[]{:S(2)}) async-start(f32[32,16,128]{2,1,0:T(8,128)} %bitcast.25), calls=%async_computation.2 | async-start | bytes 524288 | tf_op jit(solution)/shard_map/all_to_all | solution.py:422
  48.9 19.5 %collective-permute-start.2 = (f32[1024,256]{1,0:T(8,128)}, f32[1024,256]{1,0:T(8,128)}, u32[]{:S(2)}, u32[]{:S(2)}) collective-permute-start(f32[1024,256]{1,0:T(8,128)} %get-tuple-element.85), channel_id=1, source_target_pairs={{0,8},{1,9},{8,0},{9,1},{2,10},{3,11},{10,2},{11,3},{4,12},{5,13},... | collective-permute-start | bytes 3145736 | tf_op jit(solution)/shard_map/ppermute | solution.py:436
  58.7 9.7 %collective-permute-start.3 = (f32[1024,256]{1,0:T(8,128)}, f32[1024,256]{1,0:T(8,128)}, u32[]{:S(2)}, u32[]{:S(2)}) collective-permute-start(f32[1024,256]{1,0:T(8,128)} %collective-permute-done), channel_id=1, source_target_pairs={{0,8},{1,9},{8,0},{9,1},{2,10},{3,11},{10,2},{11,3},{4,12},{5,13},... | collective-permute-start | bytes 3145736 | tf_op jit(solution)/shard_map/ppermute | solution.py:436
  58.9 17.4 %collective-permute-start.4 = (f32[2,264,256]{2,1,0:T(8,128)}, f32[2,264,256]{2,1,0:T(8,128)}, u32[]{:S(2)}, u32[]{:S(2)}) collective-permute-start(f32[2,264,256]{2,1,0:T(8,128)} %get-tuple-element.98), channel_id=1, source_target_pairs={{0,1},{1,0},{8,9},{9,8},{2,3},{3,2},{10,11},{11,10},{4,5},{5,4},{1... | collective-permute-start | bytes 1622024 | tf_op jit(solution)/shard_map/ppermute | solution.py:436
  58.9 9.5 %collective-permute-start.1 = (f32[264,256]{1,0:T(8,128)}, f32[264,256]{1,0:T(8,128)}, u32[]{:S(2)}, u32[]{:S(2)}) collective-permute-start(f32[264,256]{1,0:T(8,128)} %get-tuple-element.94), channel_id=1, source_target_pairs={{0,8},{1,9},{8,0},{9,1},{2,10},{3,11},{10,2},{11,3},{4,12},{5,13},... | collective-permute-start | bytes 811016 | tf_op jit(solution)/shard_map/ppermute | solution.py:436
  59.3 13.7 %all-to-all-start.3 = ((f32[32,16,128]{2,1,0:T(8,128)}), f32[32,16,128]{2,1,0:T(8,128)}, u32[]{:S(2)}, u32[]{:S(2)}) async-start(f32[32,16,128]{2,1,0:T(8,128)} %suffix.1), calls=%async_computation.3 | async-start | bytes 524288 | tf_op jit(solution)/shard_map/all_to_all | solution.py:433
  76.3 2.5 %collective-permute-start.5 = (f32[2,264,256]{2,1,0:T(8,128)}, f32[2,264,256]{2,1,0:T(8,128)}, u32[]{:S(2)}, u32[]{:S(2)}) collective-permute-start(f32[2,264,256]{2,1,0:T(8,128)} %collective-permute-done.4.d1), channel_id=1, source_target_pairs={{0,8},{1,9},{8,0},{9,1},{2,10},{3,11},{10,2},{11,3},{4,12},{5,13},... | collective-permute-start | bytes 1622024 | tf_op jit(solution)/shard_map/ppermute | solution.py:436
  76.6 8.7 %collective-permute-start.6 = (f32[256,256]{1,0:T(8,128)}, f32[256,256]{1,0:T(8,128)}, u32[]{:S(2)}, u32[]{:S(2)}) collective-permute-start(f32[256,256]{1,0:T(8,128)} %get-tuple-element.106), channel_id=1, source_target_pairs={{0,1},{1,0},{8,9},{9,8},{2,3},{3,2},{10,11},{11,10},{4,5},{5,4},{1... | collective-permute-start | bytes 786440 | tf_op jit(solution)/shard_map/ppermute | solution.py:436
  78.3 8.8 %collective-permute-start.7 = (f32[256,256]{1,0:T(8,128)}, f32[256,256]{1,0:T(8,128)}, u32[]{:S(2)}, u32[]{:S(2)}) collective-permute-start(f32[256,256]{1,0:T(8,128)} %get-tuple-element.107), channel_id=1, source_target_pairs={{0,8},{1,9},{8,0},{9,1},{2,10},{3,11},{10,2},{11,3},{4,12},{5,13},... | collective-permute-start | bytes 786440 | tf_op jit(solution)/shard_map/ppermute | solution.py:436
  78.8 12.3 %collective-permute-start.8 = (f32[256,256]{1,0:T(8,128)}, f32[256,256]{1,0:T(8,128)}, u32[]{:S(2)}, u32[]{:S(2)}) collective-permute-start(f32[256,256]{1,0:T(8,128)} %get-tuple-element.108), channel_id=1, source_target_pairs={{0,9},{1,8},{8,1},{9,0},{2,11},{3,10},{10,3},{11,2},{4,13},{5,12},... | collective-permute-start | bytes 786440 | tf_op jit(solution)/shard_map/ppermute | solution.py:436
  83.1 15.5 %collective-permute-start.9 = (f32[4,72,256]{2,1,0:T(8,128)}, f32[4,72,256]{2,1,0:T(8,128)}, u32[]{:S(2)}, u32[]{:S(2)}) collective-permute-start(f32[4,72,256]{2,1,0:T(8,128)} %get-tuple-element.114), channel_id=1, source_target_pairs={{0,16},{16,0},{32,48},{48,32},{1,17},{17,1},{33,49},{49,33},{2,18}... | collective-permute-start | bytes 884744 | tf_op jit(solution)/shard_map/ppermute | solution.py:439
  83.4 15.5 %collective-permute-start.10 = (f32[4,72,256]{2,1,0:T(8,128)}, f32[4,72,256]{2,1,0:T(8,128)}, u32[]{:S(2)}, u32[]{:S(2)}) collective-permute-start(f32[4,72,256]{2,1,0:T(8,128)} %get-tuple-element.115), channel_id=1, source_target_pairs={{0,32},{16,48},{32,0},{48,16},{1,33},{17,49},{33,1},{49,17},{2,34}... | collective-permute-start | bytes 884744 | tf_op jit(solution)/shard_map/ppermute | solution.py:439
  85.4 15.4 %collective-permute-start.11 = (f32[4,72,256]{2,1,0:T(8,128)}, f32[4,72,256]{2,1,0:T(8,128)}, u32[]{:S(2)}, u32[]{:S(2)}) collective-permute-start(f32[4,72,256]{2,1,0:T(8,128)} %get-tuple-element.116), channel_id=1, source_target_pairs={{0,48},{16,32},{32,16},{48,0},{1,49},{17,33},{33,17},{49,1},{2,50}... | collective-permute-start | bytes 884744 | tf_op jit(solution)/shard_map/ppermute | solution.py:439
  94.3 23.1 %all-to-all-start.4 = ((f32[16,64,256]{2,1,0:T(8,128)}), f32[16,64,256]{2,1,0:T(8,128)}, u32[]{:S(2)}, u32[]{:S(2)}) async-start(f32[16,64,256]{2,1,0:T(8,128)} %wgradk.1), calls=%async_computation.4 | async-start | bytes 2097152 | tf_op jit(solution)/shard_map/all_to_all | solution.py:531
  102.8 11.2 %collective-permute-start.12 = (f32[72,256]{1,0:T(8,128)}, f32[72,256]{1,0:T(8,128)}, u32[]{:S(2)}, u32[]{:S(2)}) collective-permute-start(f32[72,256]{1,0:T(8,128)} %get-tuple-element.122), channel_id=1, source_target_pairs={{0,64},{64,0},{128,192},{192,128},{1,65},{65,1},{129,193},{193,129... | collective-permute-start | bytes 221192 | tf_op jit(solution)/shard_map/ppermute | solution.py:439
  103.2 14.1 %collective-permute-start.13 = (f32[72,256]{1,0:T(8,128)}, f32[72,256]{1,0:T(8,128)}, u32[]{:S(2)}, u32[]{:S(2)}) collective-permute-start(f32[72,256]{1,0:T(8,128)} %get-tuple-element.123), channel_id=1, source_target_pairs={{0,128},{64,192},{128,0},{192,64},{1,129},{65,193},{129,1},{193,65... | collective-permute-start | bytes 221192 | tf_op jit(solution)/shard_map/ppermute | solution.py:439
  105.0 12.4 %collective-permute-start.14 = (f32[72,256]{1,0:T(8,128)}, f32[72,256]{1,0:T(8,128)}, u32[]{:S(2)}, u32[]{:S(2)}) collective-permute-start(f32[72,256]{1,0:T(8,128)} %get-tuple-element.124), channel_id=1, source_target_pairs={{0,192},{64,128},{128,64},{192,0},{1,193},{65,129},{129,65},{193,1... | collective-permute-start | bytes 221192 | tf_op jit(solution)/shard_map/ppermute | solution.py:439
  119.5 16.8 %all-to-all-start.5 = ((f32[16,1,2304]{2,1,0:T(1,128)}), f32[16,1,2304]{2,1,0:T(1,128)}, u32[]{:S(2)}, u32[]{:S(2)}) async-start(f32[16,1,2304]{2,1,0:T(1,128)} %join.1), calls=%async_computation.5 | async-start | bytes 294912 | tf_op jit(solution)/shard_map/all_to_all | solution.py:555

commit v13 on v12

--- a/solution.py
+++ b/solution.py
@@ -254,21 +254,21 @@
         dt_o[...] = acc[...].astype(BF)
 
 
-def wgrad_q_kernel(y_ref, t0, t1, t2, t3, d0, d1, d2, d3, all_o, *send):
+def wgrad_q_kernel(x_ref, t0, t1, t2, t3, d0, d1, d2, d3, all_o, *send):
     d1, d3 = d1.at[0], d3.at[0]
     n = t0.shape[3]
-    blocks, m = t0.shape[0], t0.shape[2]
+    blocks, m = t0.shape[1], t0.shape[2]
 
     def body(step):
         parts = [d[0:n, :].astype(BF) for d in (d0, d1, d2, d3)]
         gain = d0[n:n + 8, :] + d1[n:n + 8, :] + d2[n:n + 8, :] + d3[n:n + 8, :]
         for i in range(2):
             out = send[2 * step + i]
-            at = jnp.bitwise_xor(jnp.bitwise_and(y_ref[0], 1), i)
+            at = jnp.bitwise_xor(jnp.bitwise_and(x_ref[0], 1), i)
             res = jnp.zeros((blocks * m, d0.shape[1]), F32)
             for j, t in enumerate((t0, t1, t2, t3)):
-                turned = t[:, at].reshape(blocks * m, n).astype(BF)
-                all_o[:, at, :, n * j:n * j + n] = turned.reshape(blocks, m, n)
+                turned = t[at].reshape(blocks * m, n).astype(BF)
+                all_o[at, :, :, n * j:n * j + n] = turned.reshape(blocks, m, n)
                 res = res + dot(turned, parts[j])
             out[:, 0:m, :] = res.reshape(blocks, m, res.shape[1])
             for block in range(blocks):
@@ -277,9 +277,9 @@
     each_step(body)
 
 
-def sum_y_kernel(x_ref, v0, v1, v2, v3, *send):
+def sum_x_kernel(y_ref, v0, v1, v2, v3, *send):
     for k, out in enumerate(send):
-        at = jnp.bitwise_xor(x_ref[0], k)
+        at = jnp.bitwise_xor(y_ref[0], k)
         out[...] = v0[at] + v1[at] + v2[at] + v3[at]
 
 
@@ -503,23 +503,23 @@
     per = d // nxy
     dq_far, _ = tie((dq_far, dk))
     dq_got = [dq_own, dq_far, dq_near, swap(dq_far, 2)]
-    at_y = lambda depth: pl.BlockSpec(
-        (side, 2, per, depth), lambda step, y: (0, pair_at(step, y), 0, 0)
+    at_x = lambda depth: pl.BlockSpec(
+        (2, side, per, depth), lambda step, x: (pair_at(step, x), 0, 0, 0)
     )
     by_xy = lambda v: v.reshape(side, side, per, v.shape[-1])
     qshape = (side, per + 8, GL)
     tall, *gq_send = call_mine(
         wgrad_q_kernel,
-        [at_y(n)] * 4 + [
+        [at_x(n)] * 4 + [
             whole((n + 8, GL)),
             pl.BlockSpec((1, n + 8, GL), lambda *_: (0, 0, 0)),
             whole((n + 8, GL)),
             pl.BlockSpec((1, n + 8, GL), lambda *_: (1, 0, 0)),
         ],
-        [((side, side, per, 4 * n), BF, at_y(4 * n))] + [(qshape, F32, whole(qshape))] * side,
+        [((side, side, per, 4 * n), BF, at_x(4 * n))] + [(qshape, F32, whole(qshape))] * side,
         "wgradq", 2 * big,
-    )(own("y"), by_xy(t0), by_xy(t1), by_xy(t2), by_xy(t3), *dq_got)
-    gq_got = [gq_send[0]] + [turn_about("y", gq_send[k], k) for k in range(1, side)]
+    )(own("x"), by_xy(t0), by_xy(t1), by_xy(t2), by_xy(t3), *dq_got)
+    gq_got = [gq_send[0]] + [turn_about("x", gq_send[k], k) for k in range(1, side)]
 
     steps = 2
     kshape = (nxy, per, GL)
@@ -537,10 +537,10 @@
     )(at, w_out, dn_5, fq, fk)
     gq_got, _ = tie((gq_got, gk))
     gq_send = call(
-        sum_y_kernel, (), [SMEM] + [whole(qshape)] * side,
-        [(qshape[1:], F32, whole(qshape[1:]))] * side, "sumy", 1 << 22,
-    )(own("x"), *gq_got)
-    gq_got = [gq_send[0]] + [turn_about("x", gq_send[k], k) for k in range(1, side)]
+        sum_x_kernel, (), [SMEM] + [whole(qshape)] * side,
+        [(qshape[1:], F32, whole(qshape[1:]))] * side, "sumx", 1 << 22,
+    )(own("y"), *gq_got)
+    gq_got = [gq_send[0]] + [turn_about("y", gq_send[k], k) for k in range(1, side)]
     gk_parts, mo, lv, gq_got = tie((gk_parts, mo, lv, gq_got))
 
     last = ("c", "w", "b")

time: 139 us -> 139 us (level)
  no operation moved by 1% of the time
where the time goes in v13:
time: 139 us; the launch traced here: 138 us
  Pallas kernels  60.4 us (43%)
  starting transfers between devices  48.4 us (35%)
  waiting for transfers between devices  28.2 us (20%)
  between operations  1.4 us (1%)
    all_to_all x2, starting transfers between devices, to_parts(): lax.all_to_all(st.reshape(nseq, st_rows // nseq, 128), SEQ, 0, 0, tiled=T...  12.3 us
    all_to_all x2, starting transfers between devices, from_parts(): return lax.all_to_all(mine, SEQ, 0, 0, tiled=True).reshape(st_rows, 128)  9.57 us
    all_to_all x1, starting transfers between devices, on_device(): both = lax.all_to_all(both, last, 0, 0, tiled=True)  9.19 us
    all_to_all x2, waiting for transfers between devices, from_parts(): return lax.all_to_all(mine, SEQ, 0, 0, tiled=True).reshape(st_rows, 128)  8.62 us
    ppermute x6, waiting for transfers between devices, turn_about(): lax.ppermute(v, axis, [(i, i ^ k) for i in range(lax.axis_size(axis))])  8.5 us
    ppermute x6, starting transfers between devices, turn_about(): lax.ppermute(v, axis, [(i, i ^ k) for i in range(lax.axis_size(axis))])  7.8 us
    pallas_call x1, Pallas kernels, on_device(): call_mine(dq_kernel, [col_mine(n, w), row_mine(w // 2, 128)] + [col_mine(...  5.98 us
    pallas_call x1, Pallas kernels, on_device(): call(dtok_kernel, (halves,), [col(n, w), col(n, w), st_spec, col(n, w), c...  5.83 us
  transfers between devices with their start and end apart: 21, of which 10 were waited for; matrix products, arithmetic and copies ran while one was open for 0% of the time, Pallas kernels for 37%

profile of v13, /device:TPU:1, one launch (start us, length us, event | category | flops | bytes accessed | tf_op | source)
XLA Modules:
  0.0 138.5 jit_solution(11467948892124125073)
XLA Ops:
  1.3 4.7 %kv.1 = (bf16[256,1024]{1,0:T(8,128)(2,1)}, bf16[256,1024]{1,0:T(8,128)(2,1)}, f32[256,1024]{1,0:T(8,128)}, f32[512,128]{1,0:T(8,128)}) custom-call(s32[1]{0:T(128)S(6)} %sub.7.nv_ref, bf16[256,1024]{1,0:T(8,128)(2,1)} %bitcast.19, bf16[1024,1024]{1,0:T(8,128)(2,1)} %wk.3, bf16[1024,1024]{1,0:T(8,128)(2,1)} %wv.3), custom_call_target="tpu_custom_call" | custom-call | flops 1073741824 | bytes 4194304 | tf_op jit(solution)/shard_map/kv/pallas_call | solution.py:414
  6.0 8.6 %all-to-all-start = ((f32[32,16,128]{2,1,0:T(8,128)}), f32[32,16,128]{2,1,0:T(8,128)S(1)}, u32[]{:S(2)}, u32[]{:S(2)}) async-start(f32[32,16,128]{2,1,0:T(8,128)} %bitcast.26), calls=%async_computation | async-start | bytes 524288 | tf_op jit(solution)/shard_map/all_to_all | solution.py:422
  17.1 3.7 %query.1 = (bf16[256,1024]{1,0:T(8,128)(2,1)}, bf16[1024,256]{1,0:T(8,128)(2,1)}, f32[256,1024]{1,0:T(8,128)}) custom-call(bf16[256,1024]{1,0:T(8,128)(2,1)} %bitcast.21, bf16[1024,1024]{1,0:T(8,128)(2,1)} %wq.3), custom_call_target="tpu_custom_call" | custom-call | flops 536870912 | bytes 4194304 | tf_op jit(solution)/shard_map/query/pallas_call | solution.py:447
  20.8 2.8 %all-to-all-done.v = f32[32,16,128]{2,1,0:T(8,128)S(1)} async-done(((f32[32,16,128]{2,1,0:T(8,128)}), f32[32,16,128]{2,1,0:T(8,128)S(1)}, u32[]{:S(2)}, u32[]{:S(2)}) %all-to-all-start) | async-done | bytes 262176 | tf_op jit(solution)/shard_map/all_to_all | solution.py:422
  26.0 4.9 %all-to-all-start.1 = ((f32[32,16,128]{2,1,0:T(8,128)}), f32[32,16,128]{2,1,0:T(8,128)}, u32[]{:S(2)}, u32[]{:S(2)}) async-start(f32[32,16,128]{2,1,0:T(8,128)} %prefix.1), calls=%async_computation.1 | async-start | bytes 524288 | tf_op jit(solution)/shard_map/all_to_all | solution.py:433
  31.0 5.1 %numer.1 = (f32[256,1024]{1,0:T(8,128)}, f32[256,1024]{1,0:T(8,128)}) custom-call(bf16[256,1024]{1,0:T(8,128)(2,1)} %get-tuple-element.77.fq, bf16[256,1024]{1,0:T(8,128)(2,1)} %get-tuple-element.78.fk, bf16[256,1024]{1,0:T(8,128)(2,1)} %get-tuple-element.79.fv, bf16[256,1024]{1,0:T(8,128)(2,1)} %bitcast.23, bf16[1024,1024]{1,0:T(8,128)(2,1)} %wo.3), custom_call_target="tpu_custom_call" | custom-call | flops 1073741824 | bytes 4194304 | tf_op jit(solution)/shard_map/numer/pallas_call | solution.py:460
  36.0 4.0 %all-to-all-done.1 = f32[32,16,128]{2,1,0:T(8,128)} async-done(((f32[32,16,128]{2,1,0:T(8,128)}), f32[32,16,128]{2,1,0:T(8,128)}, u32[]{:S(2)}, u32[]{:S(2)}) %all-to-all-start.1) | async-done | bytes 262176 | tf_op jit(solution)/shard_map/all_to_all | solution.py:433
  40.0 5.1 %norm.1 = (bf16[256,1024]{1,0:T(8,128)(2,1)}, f32[256,1024]{1,0:T(8,128)}, f32[512,128]{1,0:T(8,128)}, f32[8,1024]{1,0:T(8,128)}) custom-call(s32[1]{0:T(128)S(6)} %sub.7.nv_ref, f32[256,1024]{1,0:T(8,128)} %get-tuple-element.80.nl, f32[512,128]{1,0:T(8,128)} %bitcast.6.st, bf16[256,1024]{1,0:T(8,128)(2,1)} %get-tuple-element.77.fq, ...), custom_call_target="tpu_custom_call" | custom-call | flops 536870912 | bytes 4194304 | tf_op jit(solution)/shard_map/norm/pallas_call | solution.py:466
  45.1 3.7 %all-to-all-start.2 = ((f32[32,16,128]{2,1,0:T(8,128)}), f32[32,16,128]{2,1,0:T(8,128)S(1)}, u32[]{:S(2)}, u32[]{:S(2)}) async-start(f32[32,16,128]{2,1,0:T(8,128)} %bitcast.25), calls=%async_computation.2 | async-start | bytes 524288 | tf_op jit(solution)/shard_map/all_to_all | solution.py:422
  49.3 6.0 %dquery.1 = (bf16[256,1024]{1,0:T(8,128)(2,1)}, f32[264,256]{1,0:T(8,128)}, f32[264,256]{1,0:T(8,128)}, f32[2,264,256]{2,1,0:T(8,128)}) custom-call(s32[1]{0:T(128)} %bitcast.9.me_ref, f32[256,1024]{1,0:T(8,128)} %get-tuple-element.110.dn, f32[512,128]{1,0:T(8,128)} %bitcast.6.st, bf16[256,1024]{1,0:T(8,128)(2,1)} %get-tuple-element.78.fk, ...), custom_call_target="tpu_custom_call" | custom-call | flops 1073741824 | bytes 4194304 | tf_op jit(solution)/shard_map/dquery/pallas_call | solution.py:477
  55.3 2.7 %all-to-all-done.2.v = f32[32,16,128]{2,1,0:T(8,128)S(1)} async-done(((f32[32,16,128]{2,1,0:T(8,128)}), f32[32,16,128]{2,1,0:T(8,128)S(1)}, u32[]{:S(2)}, u32[]{:S(2)}) %all-to-all-start.2) | async-done | bytes 262176 | tf_op jit(solution)/shard_map/all_to_all | solution.py:422
  59.3 4.7 %all-to-all-start.3 = ((f32[32,16,128]{2,1,0:T(8,128)}), f32[32,16,128]{2,1,0:T(8,128)}, u32[]{:S(2)}, u32[]{:S(2)}) async-start(f32[32,16,128]{2,1,0:T(8,128)} %suffix.1), calls=%async_computation.3 | async-start | bytes 524288 | tf_op jit(solution)/shard_map/all_to_all | solution.py:433
  64.0 4.4 %localk.1.lk = f32[256,1024]{1,0:T(8,128)} custom-call(f32[256,1024]{1,0:T(8,128)} %get-tuple-element.110.dn, bf16[256,1024]{1,0:T(8,128)(2,1)} %get-tuple-element.77.fq, bf16[256,1024]{1,0:T(8,128)(2,1)} %get-tuple-element.79.fv), custom_call_target="tpu_custom_call" | custom-call | flops 1 | bytes 4194304 | tf_op jit(solution)/shard_map/localk/pallas_call | solution.py:490
  68.4 4.6 %all-to-all-done.3 = f32[32,16,128]{2,1,0:T(8,128)} async-done(((f32[32,16,128]{2,1,0:T(8,128)}), f32[32,16,128]{2,1,0:T(8,128)}, u32[]{:S(2)}, u32[]{:S(2)}) %all-to-all-start.3) | async-done | bytes 262176 | tf_op jit(solution)/shard_map/all_to_all | solution.py:433
  73.0 3.2 %dkey.1 = (bf16[256,1024]{1,0:T(8,128)(2,1)}, f32[256,256]{1,0:T(8,128)}, f32[256,256]{1,0:T(8,128)}, f32[256,256]{1,0:T(8,128)}, f32[256,256]{1,0:T(8,128)}) custom-call(s32[1]{0:T(128)} %bitcast.9.me_ref, f32[256,1024]{1,0:T(8,128)} %localk.1.lk, bf16[256,1024]{1,0:T(8,128)(2,1)} %get-tuple-element.79.fv, f32[512,128]{1,0:T(8,128)} %bitcast.13.st, ...), custom_call_target="tpu_custom_call" | custom-call | flops 1 | bytes 4194304 | tf_op jit(solution)/shard_map/dkey/pallas_call | solution.py:494
  78.8 4.4 %wgradq.1 = (bf16[4,4,64,1024]{3,2,1,0:T(8,128)(2,1)}, f32[4,72,256]{2,1,0:T(8,128)}, f32[4,72,256]{2,1,0:T(8,128)}, f32[4,72,256]{2,1,0:T(8,128)}, f32[4,72,256]{2,1,0:T(8,128)}) custom-call(s32[1]{0:T(128)} %bitcast.x_ref, bf16[4,4,64,256]{3,2,1,0:T(8,128)(2,1)} %bitcast.24, f32[4,4,64,256]{3,2,1,0:T(8,128)} %bitcast.10.t1, f32[4,4,64,256]{3,2,1,0:T(8,128)} %bitcast.11.t2, ...), custom_call_target="tpu_custom_call" | custom-call | flops 1073741824 | bytes 4194304 | tf_op jit(solution)/shard_map/wgradq/pallas_call | solution.py:511
  87.2 3.8 %collective-permute-done.8.d3 = f32[256,256]{1,0:T(8,128)} collective-permute-done((f32[256,256]{1,0:T(8,128)}, f32[256,256]{1,0:T(8,128)}, u32[]{:S(2)}, u32[]{:S(2)}) %collective-permute-start.8) | collective-permute-done | bytes 262176 | tf_op jit(solution)/shard_map/ppermute | solution.py:436
  91.0 3.2 %wgradk.1 = f32[16,64,256]{2,1,0:T(8,128)} custom-call(bf16[1024,1024]{1,0:T(8,128)(2,1)} %bitcast.28, f32[256,256]{1,0:T(8,128)} %get-tuple-element.105.d0, f32[256,256]{1,0:T(8,128)} %collective-permute-done.6.d1, f32[256,256]{1,0:T(8,128)} %collective-permute-done.7.d2, f32[256,256]{1,0:T(8,128)} %collective-permute-done.8.d3), custom_call_target="tpu_custom_call" | custom-call | flops 214748364800 | bytes 4194304 | tf_op jit(solution)/shard_map/wgradk/pallas_call | solution.py:526
  94.2 4.3 %all-to-all-start.4 = ((f32[16,64,256]{2,1,0:T(8,128)}), f32[16,64,256]{2,1,0:T(8,128)}, u32[]{:S(2)}, u32[]{:S(2)}) async-start(f32[16,64,256]{2,1,0:T(8,128)} %wgradk.1), calls=%async_computation.4 | async-start | bytes 2097152 | tf_op jit(solution)/shard_map/all_to_all | solution.py:531
  106.5 5.1 %localv.1 = (bf16[256,1024]{1,0:T(8,128)(2,1)}, f32[256,1024]{1,0:T(8,128)}) custom-call(bf16[256,1024]{1,0:T(8,128)(2,1)} %get-tuple-element.109.at, bf16[1024,1024]{1,0:T(8,128)(2,1)} %wo.3, f32[256,1024]{1,0:T(8,128)} %get-tuple-element.110.dn, bf16[256,1024]{1,0:T(8,128)(2,1)} %get-tuple-element.77.fq, bf16[256,1024]{1,0:T(8,128)(2,1)} %get-tuple-element.78.fk), custom_call_target="tpu_custom_call" | custom-call | flops 214748364800 | bytes 4194304 | tf_op jit(solution)/shard_map/localv/pallas_call | solution.py:534
  111.5 3.2 %collective-permute-done.12.q1 = f32[72,256]{1,0:T(8,128)} collective-permute-done((f32[72,256]{1,0:T(8,128)}, f32[72,256]{1,0:T(8,128)}, u32[]{:S(2)}, u32[]{:S(2)}) %collective-permute-start.12) | collective-permute-done | bytes 73760 | tf_op jit(solution)/shard_map/ppermute | solution.py:439
  114.7 3.2 %collective-permute-done.13.q2 = f32[72,256]{1,0:T(8,128)} collective-permute-done((f32[72,256]{1,0:T(8,128)}, f32[72,256]{1,0:T(8,128)}, u32[]{:S(2)}, u32[]{:S(2)}) %collective-permute-start.13) | collective-permute-done | bytes 73760 | tf_op jit(solution)/shard_map/ppermute | solution.py:439
  120.1 9.2 %all-to-all-start.5 = ((f32[16,1,2304]{2,1,0:T(1,128)}), f32[16,1,2304]{2,1,0:T(1,128)}, u32[]{:S(2)}, u32[]{:S(2)}) async-start(f32[16,1,2304]{2,1,0:T(1,128)} %join.1), calls=%async_computation.5 | async-start | bytes 294912 | tf_op jit(solution)/shard_map/all_to_all | solution.py:555
  129.3 5.8 %dtok.1 = bf16[256,1024]{1,0:T(8,128)(2,1)} custom-call(f32[256,1024]{1,0:T(8,128)} %get-tuple-element.126.lv, bf16[256,1024]{1,0:T(8,128)(2,1)} %get-tuple-element.78.fk, f32[512,128]{1,0:T(8,128)} %bitcast.13.st, bf16[256,1024]{1,0:T(8,128)(2,1)} %get-tuple-element.127.dq, bf16[256,1024]{1,0:T(8,128)(2,1)} %get-tuple-element.133.dk, ...), custom_call_target="tpu_custom_call" | custom-call | flops 1 | bytes 4194304 | tf_op jit(solution)/shard_map/dtok/pallas_call | solution.py:557
  (35 shorter events, 26.6 us)
Async XLA Ops:
  6.0 17.6 %all-to-all-start = ((f32[32,16,128]{2,1,0:T(8,128)}), f32[32,16,128]{2,1,0:T(8,128)S(1)}, u32[]{:S(2)}, u32[]{:S(2)}) async-start(f32[32,16,128]{2,1,0:T(8,128)} %bitcast.26), calls=%async_computation | async-start | bytes 524288 | tf_op jit(solution)/shard_map/all_to_all | solution.py:422
  24.4 34.3 %collective-permute-start = (f32[1024,256]{1,0:T(8,128)}, f32[1024,256]{1,0:T(8,128)}, u32[]{:S(2)}, u32[]{:S(2)}) collective-permute-start(f32[1024,256]{1,0:T(8,128)} %get-tuple-element.85), channel_id=1, source_target_pairs={{0,1},{1,0},{8,9},{9,8},{2,3},{3,2},{10,11},{11,10},{4,5},{5,4},{1... | collective-permute-start | bytes 3145736 | tf_op jit(solution)/shard_map/ppermute | solution.py:436
  26.0 14.0 %all-to-all-start.1 = ((f32[32,16,128]{2,1,0:T(8,128)}), f32[32,16,128]{2,1,0:T(8,128)}, u32[]{:S(2)}, u32[]{:S(2)}) async-start(f32[32,16,128]{2,1,0:T(8,128)} %prefix.1), calls=%async_computation.1 | async-start | bytes 524288 | tf_op jit(solution)/shard_map/all_to_all | solution.py:433
  45.1 12.8 %all-to-all-start.2 = ((f32[32,16,128]{2,1,0:T(8,128)}), f32[32,16,128]{2,1,0:T(8,128)S(1)}, u32[]{:S(2)}, u32[]{:S(2)}) async-start(f32[32,16,128]{2,1,0:T(8,128)} %bitcast.25), calls=%async_computation.2 | async-start | bytes 524288 | tf_op jit(solution)/shard_map/all_to_all | solution.py:422
  48.9 19.5 %collective-permute-start.2 = (f32[1024,256]{1,0:T(8,128)}, f32[1024,256]{1,0:T(8,128)}, u32[]{:S(2)}, u32[]{:S(2)}) collective-permute-start(f32[1024,256]{1,0:T(8,128)} %get-tuple-element.85), channel_id=1, source_target_pairs={{0,8},{1,9},{8,0},{9,1},{2,10},{3,11},{10,2},{11,3},{4,12},{5,13},... | collective-permute-start | bytes 3145736 | tf_op jit(solution)/shard_map/ppermute | solution.py:436
  58.7 9.7 %collective-permute-start.3 = (f32[1024,256]{1,0:T(8,128)}, f32[1024,256]{1,0:T(8,128)}, u32[]{:S(2)}, u32[]{:S(2)}) collective-permute-start(f32[1024,256]{1,0:T(8,128)} %collective-permute-done), channel_id=1, source_target_pairs={{0,8},{1,9},{8,0},{9,1},{2,10},{3,11},{10,2},{11,3},{4,12},{5,13},... | collective-permute-start | bytes 3145736 | tf_op jit(solution)/shard_map/ppermute | solution.py:436
  58.9 17.4 %collective-permute-start.4 = (f32[2,264,256]{2,1,0:T(8,128)}, f32[2,264,256]{2,1,0:T(8,128)}, u32[]{:S(2)}, u32[]{:S(2)}) collective-permute-start(f32[2,264,256]{2,1,0:T(8,128)} %get-tuple-element.98), channel_id=1, source_target_pairs={{0,1},{1,0},{8,9},{9,8},{2,3},{3,2},{10,11},{11,10},{4,5},{5,4},{1... | collective-permute-start | bytes 1622024 | tf_op jit(solution)/shard_map/ppermute | solution.py:436
  58.9 9.5 %collective-permute-start.1 = (f32[264,256]{1,0:T(8,128)}, f32[264,256]{1,0:T(8,128)}, u32[]{:S(2)}, u32[]{:S(2)}) collective-permute-start(f32[264,256]{1,0:T(8,128)} %get-tuple-element.94), channel_id=1, source_target_pairs={{0,8},{1,9},{8,0},{9,1},{2,10},{3,11},{10,2},{11,3},{4,12},{5,13},... | collective-permute-start | bytes 811016 | tf_op jit(solution)/shard_map/ppermute | solution.py:436
  59.3 13.7 %all-to-all-start.3 = ((f32[32,16,128]{2,1,0:T(8,128)}), f32[32,16,128]{2,1,0:T(8,128)}, u32[]{:S(2)}, u32[]{:S(2)}) async-start(f32[32,16,128]{2,1,0:T(8,128)} %suffix.1), calls=%async_computation.3 | async-start | bytes 524288 | tf_op jit(solution)/shard_map/all_to_all | solution.py:433
  76.3 2.5 %collective-permute-start.5 = (f32[2,264,256]{2,1,0:T(8,128)}, f32[2,264,256]{2,1,0:T(8,128)}, u32[]{:S(2)}, u32[]{:S(2)}) collective-permute-start(f32[2,264,256]{2,1,0:T(8,128)} %collective-permute-done.4.d1), channel_id=1, source_target_pairs={{0,8},{1,9},{8,0},{9,1},{2,10},{3,11},{10,2},{11,3},{4,12},{5,13},... | collective-permute-start | bytes 1622024 | tf_op jit(solution)/shard_map/ppermute | solution.py:436
  76.5 8.8 %collective-permute-start.6 = (f32[256,256]{1,0:T(8,128)}, f32[256,256]{1,0:T(8,128)}, u32[]{:S(2)}, u32[]{:S(2)}) collective-permute-start(f32[256,256]{1,0:T(8,128)} %get-tuple-element.106), channel_id=1, source_target_pairs={{0,1},{1,0},{8,9},{9,8},{2,3},{3,2},{10,11},{11,10},{4,5},{5,4},{1... | collective-permute-start | bytes 786440 | tf_op jit(solution)/shard_map/ppermute | solution.py:436
  78.2 9.0 %collective-permute-start.7 = (f32[256,256]{1,0:T(8,128)}, f32[256,256]{1,0:T(8,128)}, u32[]{:S(2)}, u32[]{:S(2)}) collective-permute-start(f32[256,256]{1,0:T(8,128)} %get-tuple-element.107), channel_id=1, source_target_pairs={{0,8},{1,9},{8,0},{9,1},{2,10},{3,11},{10,2},{11,3},{4,12},{5,13},... | collective-permute-start | bytes 786440 | tf_op jit(solution)/shard_map/ppermute | solution.py:436
  78.8 12.2 %collective-permute-start.8 = (f32[256,256]{1,0:T(8,128)}, f32[256,256]{1,0:T(8,128)}, u32[]{:S(2)}, u32[]{:S(2)}) collective-permute-start(f32[256,256]{1,0:T(8,128)} %get-tuple-element.108), channel_id=1, source_target_pairs={{0,9},{1,8},{8,1},{9,0},{2,11},{3,10},{10,3},{11,2},{4,13},{5,12},... | collective-permute-start | bytes 786440 | tf_op jit(solution)/shard_map/ppermute | solution.py:436
  83.2 15.3 %collective-permute-start.9 = (f32[4,72,256]{2,1,0:T(8,128)}, f32[4,72,256]{2,1,0:T(8,128)}, u32[]{:S(2)}, u32[]{:S(2)}) collective-permute-start(f32[4,72,256]{2,1,0:T(8,128)} %get-tuple-element.114), channel_id=1, source_target_pairs={{0,64},{64,0},{128,192},{192,128},{1,65},{65,1},{129,193},{193,129... | collective-permute-start | bytes 884744 | tf_op jit(solution)/shard_map/ppermute | solution.py:439
  83.6 15.3 %collective-permute-start.10 = (f32[4,72,256]{2,1,0:T(8,128)}, f32[4,72,256]{2,1,0:T(8,128)}, u32[]{:S(2)}, u32[]{:S(2)}) collective-permute-start(f32[4,72,256]{2,1,0:T(8,128)} %get-tuple-element.115), channel_id=1, source_target_pairs={{0,128},{64,192},{128,0},{192,64},{1,129},{65,193},{129,1},{193,65... | collective-permute-start | bytes 884744 | tf_op jit(solution)/shard_map/ppermute | solution.py:439
  85.3 15.3 %collective-permute-start.11 = (f32[4,72,256]{2,1,0:T(8,128)}, f32[4,72,256]{2,1,0:T(8,128)}, u32[]{:S(2)}, u32[]{:S(2)}) collective-permute-start(f32[4,72,256]{2,1,0:T(8,128)} %get-tuple-element.116), channel_id=1, source_target_pairs={{0,192},{64,128},{128,64},{192,0},{1,193},{65,129},{129,65},{193,1... | collective-permute-start | bytes 884744 | tf_op jit(solution)/shard_map/ppermute | solution.py:439
  94.2 23.8 %all-to-all-start.4 = ((f32[16,64,256]{2,1,0:T(8,128)}), f32[16,64,256]{2,1,0:T(8,128)}, u32[]{:S(2)}, u32[]{:S(2)}) async-start(f32[16,64,256]{2,1,0:T(8,128)} %wgradk.1), calls=%async_computation.4 | async-start | bytes 2097152 | tf_op jit(solution)/shard_map/all_to_all | solution.py:531
  102.6 12.1 %collective-permute-start.12 = (f32[72,256]{1,0:T(8,128)}, f32[72,256]{1,0:T(8,128)}, u32[]{:S(2)}, u32[]{:S(2)}) collective-permute-start(f32[72,256]{1,0:T(8,128)} %get-tuple-element.122), channel_id=1, source_target_pairs={{0,16},{16,0},{32,48},{48,32},{1,17},{17,1},{33,49},{49,33},{2,18}... | collective-permute-start | bytes 221192 | tf_op jit(solution)/shard_map/ppermute | solution.py:439
  103.2 14.7 %collective-permute-start.13 = (f32[72,256]{1,0:T(8,128)}, f32[72,256]{1,0:T(8,128)}, u32[]{:S(2)}, u32[]{:S(2)}) collective-permute-start(f32[72,256]{1,0:T(8,128)} %get-tuple-element.123), channel_id=1, source_target_pairs={{0,32},{16,48},{32,0},{48,16},{1,33},{17,49},{33,1},{49,17},{2,34}... | collective-permute-start | bytes 221192 | tf_op jit(solution)/shard_map/ppermute | solution.py:439
  105.0 13.0 %collective-permute-start.14 = (f32[72,256]{1,0:T(8,128)}, f32[72,256]{1,0:T(8,128)}, u32[]{:S(2)}, u32[]{:S(2)}) collective-permute-start(f32[72,256]{1,0:T(8,128)} %get-tuple-element.124), channel_id=1, source_target_pairs={{0,48},{16,32},{32,16},{48,0},{1,49},{17,33},{33,17},{49,1},{2,50}... | collective-permute-start | bytes 221192 | tf_op jit(solution)/shard_map/ppermute | solution.py:439
  120.1 16.8 %all-to-all-start.5 = ((f32[16,1,2304]{2,1,0:T(1,128)}), f32[16,1,2304]{2,1,0:T(1,128)}, u32[]{:S(2)}, u32[]{:S(2)}) async-start(f32[16,1,2304]{2,1,0:T(1,128)} %join.1), calls=%async_computation.5 | async-start | bytes 294912 | tf_op jit(solution)/shard_map/all_to_all | solution.py:555

commit v14 on v12

--- a/solution.py
+++ b/solution.py
@@ -18,8 +18,9 @@
 SEQ = ("x", "y", "c")
 GROUP = ("c", "b")
 VMEM_LIMIT = 64 * 1024 * 1024
-GRANT = {name: 58 << 20 for name in ("turn", "query", "dquery")}
+GRANT = {name: 58 << 20 for name in ("turn", "query", "dquery", "localv", "sumy")}
 GRANT.update({name: 4 << 20 for name in ("prefix", "suffix", "final")})
+GRANT["join"] = 8 << 20
 
 
 def dot(a, b, dims=NN):

time: 139 us -> 138 us (level)
  no operation moved by 1% of the time
where the time goes in v14:
time: 138 us
  Pallas kernels  60.3 us (44%)
  starting transfers between devices  48.4 us (35%)
  waiting for transfers between devices  27.6 us (20%)
  between operations  1.4 us (1%)
    all_to_all x2, starting transfers between devices, to_parts(): lax.all_to_all(st.reshape(nseq, st_rows // nseq, 128), SEQ, 0, 0, tiled=T...  12.3 us
    all_to_all x2, starting transfers between devices, from_parts(): return lax.all_to_all(mine, SEQ, 0, 0, tiled=True).reshape(st_rows, 128)  9.61 us
    all_to_all x1, starting transfers between devices, on_device(): both = lax.all_to_all(both, last, 0, 0, tiled=True)  9.13 us
    all_to_all x2, waiting for transfers between devices, from_parts(): return lax.all_to_all(mine, SEQ, 0, 0, tiled=True).reshape(st_rows, 128)  8.63 us
    ppermute x6, starting transfers between devices, turn_about(): lax.ppermute(v, axis, [(i, i ^ k) for i in range(lax.axis_size(axis))])  7.8 us
    ppermute x6, waiting for transfers between devices, turn_about(): lax.ppermute(v, axis, [(i, i ^ k) for i in range(lax.axis_size(axis))])  7.67 us
    pallas_call x1, Pallas kernels, on_device(): call_mine(dq_kernel, [col_mine(n, w), row_mine(w // 2, 128)] + [col_mine(...  5.99 us
    pallas_call x1, Pallas kernels, on_device(): call(dtok_kernel, (halves,), [col(n, w), col(n, w), st_spec, col(n, w), c...  5.83 us
  transfers between devices with their start and end apart: 21, of which 10 were waited for; matrix products, arithmetic and copies ran while one was open for 0% of the time, Pallas kernels for 37%

profile of v14, /device:TPU:1, one launch (start us, length us, event | category | flops | bytes accessed | tf_op | source)
XLA Modules:
  0.0 137.7 jit_solution(4105088767175656392)
XLA Ops:
  1.3 4.7 %kv.1 = (bf16[256,1024]{1,0:T(8,128)(2,1)}, bf16[256,1024]{1,0:T(8,128)(2,1)}, f32[256,1024]{1,0:T(8,128)}, f32[512,128]{1,0:T(8,128)}) custom-call(s32[1]{0:T(128)S(6)} %sub.7.nv_ref, bf16[256,1024]{1,0:T(8,128)(2,1)} %bitcast.19, bf16[1024,1024]{1,0:T(8,128)(2,1)} %wk.3, bf16[1024,1024]{1,0:T(8,128)(2,1)} %wv.3), custom_call_target="tpu_custom_call" | custom-call | flops 1073741824 | bytes 4194304 | tf_op jit(solution)/shard_map/kv/pallas_call | solution.py:415
  6.0 8.6 %all-to-all-start = ((f32[32,16,128]{2,1,0:T(8,128)}), f32[32,16,128]{2,1,0:T(8,128)S(1)}, u32[]{:S(2)}, u32[]{:S(2)}) async-start(f32[32,16,128]{2,1,0:T(8,128)} %bitcast.26), calls=%async_computation | async-start | bytes 524288 | tf_op jit(solution)/shard_map/all_to_all | solution.py:423
  14.6 2.5 %turn.1 = (bf16[1024,256]{1,0:T(8,128)(2,1)}, f32[1024,256]{1,0:T(8,128)}) custom-call(bf16[256,1024]{1,0:T(8,128)(2,1)} %bitcast.20), custom_call_target="tpu_custom_call" | custom-call | flops 134217728 | bytes 4194304 | tf_op jit(solution)/shard_map/turn/pallas_call | solution.py:444
  17.1 3.7 %query.1 = (bf16[256,1024]{1,0:T(8,128)(2,1)}, bf16[1024,256]{1,0:T(8,128)(2,1)}, f32[256,1024]{1,0:T(8,128)}) custom-call(bf16[256,1024]{1,0:T(8,128)(2,1)} %bitcast.21, bf16[1024,1024]{1,0:T(8,128)(2,1)} %wq.3), custom_call_target="tpu_custom_call" | custom-call | flops 536870912 | bytes 4194304 | tf_op jit(solution)/shard_map/query/pallas_call | solution.py:448
  20.8 2.8 %all-to-all-done.v = f32[32,16,128]{2,1,0:T(8,128)S(1)} async-done(((f32[32,16,128]{2,1,0:T(8,128)}), f32[32,16,128]{2,1,0:T(8,128)S(1)}, u32[]{:S(2)}, u32[]{:S(2)}) %all-to-all-start) | async-done | bytes 262176 | tf_op jit(solution)/shard_map/all_to_all | solution.py:423
  26.0 4.9 %all-to-all-start.1 = ((f32[32,16,128]{2,1,0:T(8,128)}), f32[32,16,128]{2,1,0:T(8,128)}, u32[]{:S(2)}, u32[]{:S(2)}) async-start(f32[32,16,128]{2,1,0:T(8,128)} %prefix.1), calls=%async_computation.1 | async-start | bytes 524288 | tf_op jit(solution)/shard_map/all_to_all | solution.py:434
  31.0 5.1 %numer.1 = (f32[256,1024]{1,0:T(8,128)}, f32[256,1024]{1,0:T(8,128)}) custom-call(bf16[256,1024]{1,0:T(8,128)(2,1)} %get-tuple-element.77.fq, bf16[256,1024]{1,0:T(8,128)(2,1)} %get-tuple-element.78.fk, bf16[256,1024]{1,0:T(8,128)(2,1)} %get-tuple-element.79.fv, bf16[256,1024]{1,0:T(8,128)(2,1)} %bitcast.23, bf16[1024,1024]{1,0:T(8,128)(2,1)} %wo.3), custom_call_target="tpu_custom_call" | custom-call | flops 1073741824 | bytes 4194304 | tf_op jit(solution)/shard_map/numer/pallas_call | solution.py:461
  36.0 4.0 %all-to-all-done.1 = f32[32,16,128]{2,1,0:T(8,128)} async-done(((f32[32,16,128]{2,1,0:T(8,128)}), f32[32,16,128]{2,1,0:T(8,128)}, u32[]{:S(2)}, u32[]{:S(2)}) %all-to-all-start.1) | async-done | bytes 262176 | tf_op jit(solution)/shard_map/all_to_all | solution.py:434
  40.0 5.1 %norm.1 = (bf16[256,1024]{1,0:T(8,128)(2,1)}, f32[256,1024]{1,0:T(8,128)}, f32[512,128]{1,0:T(8,128)}, f32[8,1024]{1,0:T(8,128)}) custom-call(s32[1]{0:T(128)S(6)} %sub.7.nv_ref, f32[256,1024]{1,0:T(8,128)} %get-tuple-element.80.nl, f32[512,128]{1,0:T(8,128)} %bitcast.6.st, bf16[256,1024]{1,0:T(8,128)(2,1)} %get-tuple-element.77.fq, ...), custom_call_target="tpu_custom_call" | custom-call | flops 536870912 | bytes 4194304 | tf_op jit(solution)/shard_map/norm/pallas_call | solution.py:467
  45.1 3.7 %all-to-all-start.2 = ((f32[32,16,128]{2,1,0:T(8,128)}), f32[32,16,128]{2,1,0:T(8,128)S(1)}, u32[]{:S(2)}, u32[]{:S(2)}) async-start(f32[32,16,128]{2,1,0:T(8,128)} %bitcast.25), calls=%async_computation.2 | async-start | bytes 524288 | tf_op jit(solution)/shard_map/all_to_all | solution.py:423
  49.3 6.0 %dquery.1 = (bf16[256,1024]{1,0:T(8,128)(2,1)}, f32[264,256]{1,0:T(8,128)}, f32[264,256]{1,0:T(8,128)}, f32[2,264,256]{2,1,0:T(8,128)}) custom-call(s32[1]{0:T(128)} %bitcast.9.me_ref, f32[256,1024]{1,0:T(8,128)} %get-tuple-element.110.dn, f32[512,128]{1,0:T(8,128)} %bitcast.6.st, bf16[256,1024]{1,0:T(8,128)(2,1)} %get-tuple-element.78.fk, ...), custom_call_target="tpu_custom_call" | custom-call | flops 1073741824 | bytes 4194304 | tf_op jit(solution)/shard_map/dquery/pallas_call | solution.py:478
  55.3 2.7 %all-to-all-done.2.v = f32[32,16,128]{2,1,0:T(8,128)S(1)} async-done(((f32[32,16,128]{2,1,0:T(8,128)}), f32[32,16,128]{2,1,0:T(8,128)S(1)}, u32[]{:S(2)}, u32[]{:S(2)}) %all-to-all-start.2) | async-done | bytes 262176 | tf_op jit(solution)/shard_map/all_to_all | solution.py:423
  59.3 4.7 %all-to-all-start.3 = ((f32[32,16,128]{2,1,0:T(8,128)}), f32[32,16,128]{2,1,0:T(8,128)}, u32[]{:S(2)}, u32[]{:S(2)}) async-start(f32[32,16,128]{2,1,0:T(8,128)} %suffix.1), calls=%async_computation.3 | async-start | bytes 524288 | tf_op jit(solution)/shard_map/all_to_all | solution.py:434
  63.9 4.3 %localk.1.lk = f32[256,1024]{1,0:T(8,128)} custom-call(f32[256,1024]{1,0:T(8,128)} %get-tuple-element.110.dn, bf16[256,1024]{1,0:T(8,128)(2,1)} %get-tuple-element.77.fq, bf16[256,1024]{1,0:T(8,128)(2,1)} %get-tuple-element.79.fv), custom_call_target="tpu_custom_call" | custom-call | flops 1 | bytes 4194304 | tf_op jit(solution)/shard_map/localk/pallas_call | solution.py:491
  68.3 4.7 %all-to-all-done.3 = f32[32,16,128]{2,1,0:T(8,128)} async-done(((f32[32,16,128]{2,1,0:T(8,128)}), f32[32,16,128]{2,1,0:T(8,128)}, u32[]{:S(2)}, u32[]{:S(2)}) %all-to-all-start.3) | async-done | bytes 262176 | tf_op jit(solution)/shard_map/all_to_all | solution.py:434
  73.0 3.2 %dkey.1 = (bf16[256,1024]{1,0:T(8,128)(2,1)}, f32[256,256]{1,0:T(8,128)}, f32[256,256]{1,0:T(8,128)}, f32[256,256]{1,0:T(8,128)}, f32[256,256]{1,0:T(8,128)}) custom-call(s32[1]{0:T(128)} %bitcast.9.me_ref, f32[256,1024]{1,0:T(8,128)} %localk.1.lk, bf16[256,1024]{1,0:T(8,128)(2,1)} %get-tuple-element.79.fv, f32[512,128]{1,0:T(8,128)} %bitcast.13.st, ...), custom_call_target="tpu_custom_call" | custom-call | flops 1 | bytes 4194304 | tf_op jit(solution)/shard_map/dkey/pallas_call | solution.py:495
  78.7 4.3 %wgradq.1 = (bf16[4,4,64,1024]{3,2,1,0:T(8,128)(2,1)}, f32[4,72,256]{2,1,0:T(8,128)}, f32[4,72,256]{2,1,0:T(8,128)}, f32[4,72,256]{2,1,0:T(8,128)}, f32[4,72,256]{2,1,0:T(8,128)}) custom-call(s32[1]{0:T(128)} %bitcast.y_ref, bf16[4,4,64,256]{3,2,1,0:T(8,128)(2,1)} %bitcast.24, f32[4,4,64,256]{3,2,1,0:T(8,128)} %bitcast.10.t1, f32[4,4,64,256]{3,2,1,0:T(8,128)} %bitcast.11.t2, ...), custom_call_target="tpu_custom_call" | custom-call | flops 1073741824 | bytes 4194304 | tf_op jit(solution)/shard_map/wgradq/pallas_call | solution.py:512
  87.0 4.0 %collective-permute-done.8.d3 = f32[256,256]{1,0:T(8,128)} collective-permute-done((f32[256,256]{1,0:T(8,128)}, f32[256,256]{1,0:T(8,128)}, u32[]{:S(2)}, u32[]{:S(2)}) %collective-permute-start.8) | collective-permute-done | bytes 262176 | tf_op jit(solution)/shard_map/ppermute | solution.py:437
  91.0 3.2 %wgradk.1 = f32[16,64,256]{2,1,0:T(8,128)} custom-call(bf16[1024,1024]{1,0:T(8,128)(2,1)} %bitcast.28, f32[256,256]{1,0:T(8,128)} %get-tuple-element.105.d0, f32[256,256]{1,0:T(8,128)} %collective-permute-done.6.d1, f32[256,256]{1,0:T(8,128)} %collective-permute-done.7.d2, f32[256,256]{1,0:T(8,128)} %collective-permute-done.8.d3), custom_call_target="tpu_custom_call" | custom-call | flops 214748364800 | bytes 4194304 | tf_op jit(solution)/shard_map/wgradk/pallas_call | solution.py:527
  94.2 4.3 %all-to-all-start.4 = ((f32[16,64,256]{2,1,0:T(8,128)}), f32[16,64,256]{2,1,0:T(8,128)}, u32[]{:S(2)}, u32[]{:S(2)}) async-start(f32[16,64,256]{2,1,0:T(8,128)} %wgradk.1), calls=%async_computation.4 | async-start | bytes 2097152 | tf_op jit(solution)/shard_map/all_to_all | solution.py:532
  106.6 5.1 %localv.1 = (bf16[256,1024]{1,0:T(8,128)(2,1)}, f32[256,1024]{1,0:T(8,128)}) custom-call(bf16[256,1024]{1,0:T(8,128)(2,1)} %get-tuple-element.109.at, bf16[1024,1024]{1,0:T(8,128)(2,1)} %wo.3, f32[256,1024]{1,0:T(8,128)} %get-tuple-element.110.dn, bf16[256,1024]{1,0:T(8,128)(2,1)} %get-tuple-element.77.fq, bf16[256,1024]{1,0:T(8,128)(2,1)} %get-tuple-element.78.fk), custom_call_target="tpu_custom_call" | custom-call | flops 214748364800 | bytes 4194304 | tf_op jit(solution)/shard_map/localv/pallas_call | solution.py:535
  113.9 3.4 %collective-permute-done.13.q2 = f32[72,256]{1,0:T(8,128)} collective-permute-done((f32[72,256]{1,0:T(8,128)}, f32[72,256]{1,0:T(8,128)}, u32[]{:S(2)}, u32[]{:S(2)}) %collective-permute-start.13) | collective-permute-done | bytes 73760 | tf_op jit(solution)/shard_map/ppermute | solution.py:440
  119.3 9.1 %all-to-all-start.5 = ((f32[16,1,2304]{2,1,0:T(1,128)}), f32[16,1,2304]{2,1,0:T(1,128)}, u32[]{:S(2)}, u32[]{:S(2)}) async-start(f32[16,1,2304]{2,1,0:T(1,128)} %join.1), calls=%async_computation.5 | async-start | bytes 294912 | tf_op jit(solution)/shard_map/all_to_all | solution.py:556
  128.5 5.8 %dtok.1 = bf16[256,1024]{1,0:T(8,128)(2,1)} custom-call(f32[256,1024]{1,0:T(8,128)} %get-tuple-element.126.lv, bf16[256,1024]{1,0:T(8,128)(2,1)} %get-tuple-element.78.fk, f32[512,128]{1,0:T(8,128)} %bitcast.13.st, bf16[256,1024]{1,0:T(8,128)(2,1)} %get-tuple-element.127.dq, bf16[256,1024]{1,0:T(8,128)(2,1)} %get-tuple-element.133.dk, ...), custom_call_target="tpu_custom_call" | custom-call | flops 1 | bytes 4194304 | tf_op jit(solution)/shard_map/dtok/pallas_call | solution.py:558
  (37 shorter events, 26.3 us)
Async XLA Ops:
  6.0 17.6 %all-to-all-start = ((f32[32,16,128]{2,1,0:T(8,128)}), f32[32,16,128]{2,1,0:T(8,128)S(1)}, u32[]{:S(2)}, u32[]{:S(2)}) async-start(f32[32,16,128]{2,1,0:T(8,128)} %bitcast.26), calls=%async_computation | async-start | bytes 524288 | tf_op jit(solution)/shard_map/all_to_all | solution.py:423
  24.4 34.3 %collective-permute-start = (f32[1024,256]{1,0:T(8,128)}, f32[1024,256]{1,0:T(8,128)}, u32[]{:S(2)}, u32[]{:S(2)}) collective-permute-start(f32[1024,256]{1,0:T(8,128)} %get-tuple-element.85), channel_id=1, source_target_pairs={{0,1},{1,0},{8,9},{9,8},{2,3},{3,2},{10,11},{11,10},{4,5},{5,4},{1... | collective-permute-start | bytes 3145736 | tf_op jit(solution)/shard_map/ppermute | solution.py:437
  26.0 14.0 %all-to-all-start.1 = ((f32[32,16,128]{2,1,0:T(8,128)}), f32[32,16,128]{2,1,0:T(8,128)}, u32[]{:S(2)}, u32[]{:S(2)}) async-start(f32[32,16,128]{2,1,0:T(8,128)} %prefix.1), calls=%async_computation.1 | async-start | bytes 524288 | tf_op jit(solution)/shard_map/all_to_all | solution.py:434
  45.1 12.8 %all-to-all-start.2 = ((f32[32,16,128]{2,1,0:T(8,128)}), f32[32,16,128]{2,1,0:T(8,128)S(1)}, u32[]{:S(2)}, u32[]{:S(2)}) async-start(f32[32,16,128]{2,1,0:T(8,128)} %bitcast.25), calls=%async_computation.2 | async-start | bytes 524288 | tf_op jit(solution)/shard_map/all_to_all | solution.py:423
  48.8 19.5 %collective-permute-start.2 = (f32[1024,256]{1,0:T(8,128)}, f32[1024,256]{1,0:T(8,128)}, u32[]{:S(2)}, u32[]{:S(2)}) collective-permute-start(f32[1024,256]{1,0:T(8,128)} %get-tuple-element.85), channel_id=1, source_target_pairs={{0,8},{1,9},{8,0},{9,1},{2,10},{3,11},{10,2},{11,3},{4,12},{5,13},... | collective-permute-start | bytes 3145736 | tf_op jit(solution)/shard_map/ppermute | solution.py:437
  58.6 9.7 %collective-permute-start.3 = (f32[1024,256]{1,0:T(8,128)}, f32[1024,256]{1,0:T(8,128)}, u32[]{:S(2)}, u32[]{:S(2)}) collective-permute-start(f32[1024,256]{1,0:T(8,128)} %collective-permute-done), channel_id=1, source_target_pairs={{0,8},{1,9},{8,0},{9,1},{2,10},{3,11},{10,2},{11,3},{4,12},{5,13},... | collective-permute-start | bytes 3145736 | tf_op jit(solution)/shard_map/ppermute | solution.py:437
  58.8 17.4 %collective-permute-start.4 = (f32[2,264,256]{2,1,0:T(8,128)}, f32[2,264,256]{2,1,0:T(8,128)}, u32[]{:S(2)}, u32[]{:S(2)}) collective-permute-start(f32[2,264,256]{2,1,0:T(8,128)} %get-tuple-element.98), channel_id=1, source_target_pairs={{0,1},{1,0},{8,9},{9,8},{2,3},{3,2},{10,11},{11,10},{4,5},{5,4},{1... | collective-permute-start | bytes 1622024 | tf_op jit(solution)/shard_map/ppermute | solution.py:437
  58.8 9.5 %collective-permute-start.1 = (f32[264,256]{1,0:T(8,128)}, f32[264,256]{1,0:T(8,128)}, u32[]{:S(2)}, u32[]{:S(2)}) collective-permute-start(f32[264,256]{1,0:T(8,128)} %get-tuple-element.94), channel_id=1, source_target_pairs={{0,8},{1,9},{8,0},{9,1},{2,10},{3,11},{10,2},{11,3},{4,12},{5,13},... | collective-permute-start | bytes 811016 | tf_op jit(solution)/shard_map/ppermute | solution.py:437
  59.3 13.7 %all-to-all-start.3 = ((f32[32,16,128]{2,1,0:T(8,128)}), f32[32,16,128]{2,1,0:T(8,128)}, u32[]{:S(2)}, u32[]{:S(2)}) async-start(f32[32,16,128]{2,1,0:T(8,128)} %suffix.1), calls=%async_computation.3 | async-start | bytes 524288 | tf_op jit(solution)/shard_map/all_to_all | solution.py:434
  76.2 2.5 %collective-permute-start.5 = (f32[2,264,256]{2,1,0:T(8,128)}, f32[2,264,256]{2,1,0:T(8,128)}, u32[]{:S(2)}, u32[]{:S(2)}) collective-permute-start(f32[2,264,256]{2,1,0:T(8,128)} %collective-permute-done.4.d1), channel_id=1, source_target_pairs={{0,8},{1,9},{8,0},{9,1},{2,10},{3,11},{10,2},{11,3},{4,12},{5,13},... | collective-permute-start | bytes 1622024 | tf_op jit(solution)/shard_map/ppermute | solution.py:437
  76.6 8.8 %collective-permute-start.6 = (f32[256,256]{1,0:T(8,128)}, f32[256,256]{1,0:T(8,128)}, u32[]{:S(2)}, u32[]{:S(2)}) collective-permute-start(f32[256,256]{1,0:T(8,128)} %get-tuple-element.106), channel_id=1, source_target_pairs={{0,1},{1,0},{8,9},{9,8},{2,3},{3,2},{10,11},{11,10},{4,5},{5,4},{1... | collective-permute-start | bytes 786440 | tf_op jit(solution)/shard_map/ppermute | solution.py:437
  78.2 8.8 %collective-permute-start.7 = (f32[256,256]{1,0:T(8,128)}, f32[256,256]{1,0:T(8,128)}, u32[]{:S(2)}, u32[]{:S(2)}) collective-permute-start(f32[256,256]{1,0:T(8,128)} %get-tuple-element.107), channel_id=1, source_target_pairs={{0,8},{1,9},{8,0},{9,1},{2,10},{3,11},{10,2},{11,3},{4,12},{5,13},... | collective-permute-start | bytes 786440 | tf_op jit(solution)/shard_map/ppermute | solution.py:437
  78.7 12.3 %collective-permute-start.8 = (f32[256,256]{1,0:T(8,128)}, f32[256,256]{1,0:T(8,128)}, u32[]{:S(2)}, u32[]{:S(2)}) collective-permute-start(f32[256,256]{1,0:T(8,128)} %get-tuple-element.108), channel_id=1, source_target_pairs={{0,9},{1,8},{8,1},{9,0},{2,11},{3,10},{10,3},{11,2},{4,13},{5,12},... | collective-permute-start | bytes 786440 | tf_op jit(solution)/shard_map/ppermute | solution.py:437
  83.1 15.5 %collective-permute-start.9 = (f32[4,72,256]{2,1,0:T(8,128)}, f32[4,72,256]{2,1,0:T(8,128)}, u32[]{:S(2)}, u32[]{:S(2)}) collective-permute-start(f32[4,72,256]{2,1,0:T(8,128)} %get-tuple-element.114), channel_id=1, source_target_pairs={{0,16},{16,0},{32,48},{48,32},{1,17},{17,1},{33,49},{49,33},{2,18}... | collective-permute-start | bytes 884744 | tf_op jit(solution)/shard_map/ppermute | solution.py:440
  83.4 15.5 %collective-permute-start.10 = (f32[4,72,256]{2,1,0:T(8,128)}, f32[4,72,256]{2,1,0:T(8,128)}, u32[]{:S(2)}, u32[]{:S(2)}) collective-permute-start(f32[4,72,256]{2,1,0:T(8,128)} %get-tuple-element.115), channel_id=1, source_target_pairs={{0,32},{16,48},{32,0},{48,16},{1,33},{17,49},{33,1},{49,17},{2,34}... | collective-permute-start | bytes 884744 | tf_op jit(solution)/shard_map/ppermute | solution.py:440
  85.3 15.4 %collective-permute-start.11 = (f32[4,72,256]{2,1,0:T(8,128)}, f32[4,72,256]{2,1,0:T(8,128)}, u32[]{:S(2)}, u32[]{:S(2)}) collective-permute-start(f32[4,72,256]{2,1,0:T(8,128)} %get-tuple-element.116), channel_id=1, source_target_pairs={{0,48},{16,32},{32,16},{48,0},{1,49},{17,33},{33,17},{49,1},{2,50}... | collective-permute-start | bytes 884744 | tf_op jit(solution)/shard_map/ppermute | solution.py:440
  94.2 23.0 %all-to-all-start.4 = ((f32[16,64,256]{2,1,0:T(8,128)}), f32[16,64,256]{2,1,0:T(8,128)}, u32[]{:S(2)}, u32[]{:S(2)}) async-start(f32[16,64,256]{2,1,0:T(8,128)} %wgradk.1), calls=%async_computation.4 | async-start | bytes 2097152 | tf_op jit(solution)/shard_map/all_to_all | solution.py:532
  102.8 11.1 %collective-permute-start.12 = (f32[72,256]{1,0:T(8,128)}, f32[72,256]{1,0:T(8,128)}, u32[]{:S(2)}, u32[]{:S(2)}) collective-permute-start(f32[72,256]{1,0:T(8,128)} %get-tuple-element.122), channel_id=1, source_target_pairs={{0,64},{64,0},{128,192},{192,128},{1,65},{65,1},{129,193},{193,129... | collective-permute-start | bytes 221192 | tf_op jit(solution)/shard_map/ppermute | solution.py:440
  103.2 14.1 %collective-permute-start.13 = (f32[72,256]{1,0:T(8,128)}, f32[72,256]{1,0:T(8,128)}, u32[]{:S(2)}, u32[]{:S(2)}) collective-permute-start(f32[72,256]{1,0:T(8,128)} %get-tuple-element.123), channel_id=1, source_target_pairs={{0,128},{64,192},{128,0},{192,64},{1,129},{65,193},{129,1},{193,65... | collective-permute-start | bytes 221192 | tf_op jit(solution)/shard_map/ppermute | solution.py:440
  105.0 12.3 %collective-permute-start.14 = (f32[72,256]{1,0:T(8,128)}, f32[72,256]{1,0:T(8,128)}, u32[]{:S(2)}, u32[]{:S(2)}) collective-permute-start(f32[72,256]{1,0:T(8,128)} %get-tuple-element.124), channel_id=1, source_target_pairs={{0,192},{64,128},{128,64},{192,0},{1,193},{65,129},{129,65},{193,1... | collective-permute-start | bytes 221192 | tf_op jit(solution)/shard_map/ppermute | solution.py:440
  106.6 10.6 %copy-start = (f32[72,256]{1,0:T(8,128)S(1)}, f32[72,256]{1,0:T(8,128)}, u32[]{:S(2)}) copy-start(f32[72,256]{1,0:T(8,128)} %get-tuple-element.128.q0) | copy-start | bytes 221188
  119.3 16.8 %all-to-all-start.5 = ((f32[16,1,2304]{2,1,0:T(1,128)}), f32[16,1,2304]{2,1,0:T(1,128)}, u32[]{:S(2)}, u32[]{:S(2)}) async-start(f32[16,1,2304]{2,1,0:T(1,128)} %join.1), calls=%async_computation.5 | async-start | bytes 294912 | tf_op jit(solution)/shard_map/all_to_all | solution.py:556
